TPU v7x, 32 devices: a whole 2x2x4 slice. The times are simulated.
32 devices in a mesh: cfg: 2 (over y), rows: 8 (over z, x), tp: 2 (over core).
Axes of the slice: x: 2, y: 2, z: 4, core: 2. Of those that a mesh axis runs over, the one named last changes fastest.
Arguments:
- latent: bfloat16 [2, 32, 1280, 128], P('cfg', 'rows', 'tp'), may hold values from -60 to 60
- stale_kv: bfloat16 [2, 2, 32, 128, 1024], P('cfg', None, 'rows', None, 'tp'), may hold values from -60 to 60
- timestep: int32 [1], replicated, may hold values from 0 to 999
- w_time: bfloat16 [320, 1280], P(None, 'tp'), may hold values from -0.3125 to 0.3125
- gn_gain: bfloat16 [1280], P('tp'), may hold values from 0.5 to 1.5
- gn_bias: bfloat16 [1280], P('tp'), may hold values from -3 to 3
- conv_w: bfloat16 [3, 3, 1280, 1280], P(None, None, 'tp', 'cfg'), may hold values from -0.0546875 to 0.0546875
- conv_b: bfloat16 [1280], P('tp'), may hold values from -3 to 3
- ln_gain: bfloat16 [1280], P('tp'), may hold values from 0.5 to 1.5
- ln_bias: bfloat16 [1280], P('tp'), may hold values from -3 to 3
- w_qkv: bfloat16 [1280, 3, 1024], P(None, None, 'tp'), may hold values from -0.15625 to 0.15625
- w_out: bfloat16 [1024, 1280], P('tp'), may hold values from -0.25 to 0.25
Outputs:
- guided: bfloat16 [32, 640, 2, 128], P('rows', 'tp', 'cfg')
- fresh_kv: bfloat16 [2, 2, 32, 128, 1024], P('cfg', None, 'rows', None, 'tp')
All inputs are finite; a program needn't handle non-finite values.
Results may differ from a plain program's by a relative error of at most 0.029.
Values may be sent and summed in bfloat16 or wider, within the bound.
No kernel may reach another device: no remote copies, remote signals or barrier semaphores. Data moves between devices by JAX's collectives and lax.ppermute only.
A program may use at most 128 MiB of HBM per device.

v0:
```python
import math

import jax
import jax.numpy as jnp
from jax import lax
from jax.sharding import PartitionSpec as P

D = 1280
HD = 64
GROUPS = 32
TEMB = 320


epsilon = 1e-05
guidance = 5.0


def padded(array, sides, width):
    for axis, dim in sides:
        count, length = (lax.axis_size(axis), array.shape[dim])
        up = [(i, (i + 1) % count) for i in range(count - 1)]
        down = [(j, i) for i, j in up]
        last = lax.slice_in_dim(array, length - width, length, axis=dim)
        leading = lax.slice_in_dim(array, 0, width, axis=dim)
        before = lax.ppermute(last, axis, up)
        after = lax.ppermute(leading, axis, down)
        array = jnp.concatenate([before, array, after], axis=dim)
    return array


def swapped(array, axis, distance):
    return lax.ppermute(array, axis, [(i, i ^ 1 << distance) for i in range(lax.axis_size(axis))])


def block_state(query_heads, key_heads, value_heads, score_scale):
    scores = (
        jnp.einsum("qhd,khd->hqk", query_heads, key_heads, preferred_element_type=jnp.float32)
        * score_scale
    )
    maxima = jnp.max(scores, axis=-1)
    weights = jnp.exp(scores - maxima[..., None])
    totals = jnp.sum(weights, axis=-1)
    weighted = jnp.einsum(
        "hqk,khd->qhd",
        weights.astype(jnp.bfloat16),
        value_heads,
        preferred_element_type=jnp.float32,
    )
    return (maxima, totals, weighted)


def absorb(first, second):
    peak = jnp.maximum(first[0], second[0])
    factor_one = jnp.exp(first[0] - peak)
    factor_two = jnp.exp(second[0] - peak)
    totals = first[1] * factor_one + second[1] * factor_two
    weighted = first[2] * factor_one.T[:, :, None] + second[2] * factor_two.T[:, :, None]
    return (peak, totals, weighted)


def per_device(
    latent,
    stale_kv,
    timestep,
    w_time,
    gn_gain,
    gn_bias,
    conv_w,
    conv_b,
    ln_gain,
    ln_bias,
    w_qkv,
    w_out,
):
    latent_rows = latent[0]
    rows_count = lax.axis_size("rows")
    span_rows, local_channels, grid_width = latent_rows.shape
    positions = span_rows * grid_width
    group_width = D // GROUPS
    local_groups = local_channels // group_width
    my_block = lax.axis_index("rows")
    half_width = TEMB // 2
    frequencies = jnp.exp(
        -math.log(10000.0) * jnp.arange(half_width, dtype=jnp.float32) / half_width
    )
    angles = timestep.astype(jnp.float32)[0] * frequencies
    embedding = jnp.concatenate([jnp.cos(angles), jnp.sin(angles)])
    time_bias = jnp.dot(
        jax.nn.silu(embedding)[None, :], w_time.astype(jnp.float32), precision=lax.Precision.HIGHEST
    )[0]
    latent32 = latent_rows.astype(jnp.float32)
    values32 = latent32.reshape(span_rows, local_groups, group_width, grid_width)
    group_total, group_square = lax.psum(
        (jnp.sum(values32, axis=(0, 2, 3)), jnp.sum(values32 * values32, axis=(0, 2, 3))), "rows"
    )
    amount = span_rows * rows_count * grid_width * group_width
    group_mean = group_total / amount
    variance = group_square / amount - group_mean * group_mean
    scaled = (
        (values32 - group_mean[None, :, None, None])
        * lax.rsqrt(variance + epsilon)[None, :, None, None]
    ).reshape(span_rows, local_channels, grid_width)
    scaled = (
        scaled * gn_gain.astype(jnp.float32)[None, :, None]
        + gn_bias.astype(jnp.float32)[None, :, None]
    )
    activated = jax.nn.silu(scaled).astype(jnp.bfloat16)
    rimmed = padded(activated, (("rows", 0),), 1)
    framed = jnp.pad(rimmed, ((0, 0), (0, 0), (1, 1)))
    kernel_full = lax.all_gather(conv_w, "cfg", axis=3, tiled=True)
    running = jnp.zeros((span_rows, local_channels, grid_width), jnp.float32)
    shard_piece = lax.all_gather(framed, "tp", axis=1, tiled=True)
    for row_tap in range(3):
        for col_tap in range(3):
            window = shard_piece[row_tap : row_tap + span_rows, :, col_tap : col_tap + grid_width]
            running = running + jnp.einsum(
                "oi,riw->row",
                kernel_full[row_tap, col_tap],
                window,
                preferred_element_type=jnp.float32,
            )
    hidden = running + conv_b.astype(jnp.float32)[None, :, None] + time_bias[None, :, None]
    resid = (latent32 + hidden).astype(jnp.bfloat16)
    resid32 = resid.astype(jnp.float32)
    sum_plain, sum_square = lax.psum(
        (jnp.sum(resid32, axis=1), jnp.sum(resid32 * resid32, axis=1)), "tp"
    )
    token_mean = sum_plain / D
    token_var = sum_square / D - token_mean * token_mean
    normed_part = (resid32 - token_mean[:, None, :]) * lax.rsqrt(token_var + epsilon)[:, None, :]
    normed_part = (
        normed_part * ln_gain.astype(jnp.float32)[None, :, None]
        + ln_bias.astype(jnp.float32)[None, :, None]
    ).astype(jnp.bfloat16)
    normed = lax.all_gather(normed_part, "tp", axis=1, tiled=True)
    local_features = w_qkv.shape[2]
    local_heads = local_features // HD
    projected = jnp.einsum(
        "rdw,df->rwf",
        normed,
        w_qkv.reshape(D, 3 * local_features),
        preferred_element_type=jnp.float32,
    ).reshape(positions, 3, local_features)
    queries = projected[:, 0].astype(jnp.bfloat16)
    keys_new = projected[:, 1].astype(jnp.bfloat16)
    values_new = projected[:, 2].astype(jnp.bfloat16)
    fresh_kv = jnp.stack([keys_new, values_new]).reshape(
        1, 2, span_rows, grid_width, local_features
    )
    score_scale = 1.0 / math.sqrt(HD)
    query_heads = queries.reshape(positions, local_heads, HD)
    near_state = block_state(
        query_heads,
        keys_new.reshape(positions, local_heads, HD),
        values_new.reshape(positions, local_heads, HD),
        score_scale,
    )
    stale_pair = stale_kv[0]
    shard_piece = lax.all_gather(stale_pair, "rows", axis=1, tiled=True)

    def take_block(block_number, inner_state):
        block_rows = lax.dynamic_slice_in_dim(shard_piece, block_number * span_rows, span_rows, 1)
        key_heads = block_rows[0].reshape(positions, local_heads, HD)
        value_heads = block_rows[1].reshape(positions, local_heads, HD)
        merged = absorb(inner_state, block_state(query_heads, key_heads, value_heads, score_scale))
        is_mine = block_number * span_rows == my_block * span_rows
        return jax.tree.map(
            lambda kept, fresh: jnp.where(is_mine, kept, fresh), inner_state, merged
        )

    final_state = lax.fori_loop(0, shard_piece.shape[1] // span_rows, take_block, near_state)
    attended = (
        (final_state[2] / final_state[1].T[:, :, None])
        .astype(jnp.bfloat16)
        .reshape(span_rows, grid_width, local_features)
    )
    head_terms = jnp.einsum("rwf,fd->rdw", attended, w_out, preferred_element_type=jnp.float32)
    projected_back = lax.psum_scatter(
        head_terms.astype(jnp.bfloat16), "tp", scatter_dimension=1, tiled=True
    ).astype(jnp.float32)
    branch_out = (resid.astype(jnp.float32) + projected_back).astype(jnp.bfloat16)
    paired = branch_out.reshape(span_rows, local_channels // 2, 2, grid_width)
    branch_index = lax.axis_index("cfg")
    kept_half = lax.dynamic_slice_in_dim(paired, branch_index, 1, 2)
    sent_half = lax.dynamic_slice_in_dim(paired, 1 - branch_index, 1, 2)
    other_branch = swapped(sent_half, "cfg", 0)
    is_cond = branch_index == 0
    cond_out = jnp.where(is_cond, kept_half, other_branch).astype(jnp.float32)
    uncond_out = jnp.where(is_cond, other_branch, kept_half).astype(jnp.float32)
    guided = (uncond_out + guidance * (cond_out - uncond_out)).astype(jnp.bfloat16)
    return (guided, fresh_kv)


def solution(mesh):
    in_specs = (
        P("cfg", "rows", "tp", None),
        P("cfg", None, "rows", None, "tp"),
        P(),
        P(None, "tp"),
        P("tp"),
        P("tp"),
        P(None, None, "tp", "cfg"),
        P("tp"),
        P("tp"),
        P("tp"),
        P(None, None, "tp"),
        P("tp", None),
    )
    out_specs = (P("rows", "tp", "cfg", None), P("cfg", None, "rows", None, "tp"))
    return jax.shard_map(
        per_device, mesh=mesh, in_specs=in_specs, out_specs=out_specs, check_vma=False
    )
```

profile of v0, /device:TPU:0, one launch (start us, length us, event | category | flops | bytes accessed | tf_op | source)
XLA Modules:
  0.0 589.8 jit_solution(2722258485959840039)
XLA Ops:
  7.2 1.5 copy.48
  10.0 23.1 %all-reduce.1 = (f32[16]{0:T(128)S(1)}, f32[16]{0:T(128)S(1)}) all-reduce(f32[16]{0:T(128)S(1)} %reduce_sum.79, f32[16]{0:T(128)S(1)} %reduce_sum.76), channel_id=1, replica_groups=mesh['cfg'=2,'rows'=8,'tp'=2] {'rows'}, use_global_device_ids=true, to_apply=%region_5.6 | all-reduce | flops 32 | bytes 256 | tf_op jit(solution)/shard_map/psum | solution.py:93
  34.0 1.3 collective-permute-start.1
  35.3 4.6 collective-permute-start
  39.8 1.3 collective-permute-done.1
  41.2 1.5 collective-permute-done
  45.9 7.9 %all-gather.6.cloned.1.call-done = bf16[6,1280,130]{1,2,0:T(8,128)(2,1)} async-done(((bf16[6,640,130]{1,2,0:T(8,128)(2,1)}), bf16[6,1280,130]{1,2,0:T(8,128)(2,1)}) %all-gather.6.cloned.1.call-update) | async-done | bytes 1996816 | tf_op jit(solution)/shard_map/all_gather | solution.py:112
  53.8 179.0 %all-gather.8.cloned.1.call-done = bf16[3,3,640,1280]{3,2,1,0:T(8,128)(2,1)} async-done(((bf16[3,3,640,640]{3,2,1,0:T(8,128)(2,1)}), bf16[3,3,640,1280]{3,2,1,0:T(8,128)(2,1)}) %all-gather.8.cloned.1.call-update) | async-done | bytes 14745616 | tf_op jit(solution)/shard_map/all_gather | solution.py:110
  232.8 3.2 fusion.41
  236.0 3.8 fusion.45
  239.9 3.2 fusion.46
  243.1 1.2 fusion.47
  244.4 1.2 fusion.48
  249.4 1.4 convert_reduce_fusion
  250.8 2.7 all-reduce.2
  254.7 2.3 copy.51
  257.0 6.4 %copy.49 = bf16[1280,3,512]{0,2,1:T(8,128)(2,1)} copy(bf16[1280,3,512]{2,0,1:T(8,128)(2,1)} %param.24) | data formatting | bytes 7864320 | tf_op args[10]
  264.2 4.8 fusion.30
  269.9 2.7 multiply_reduce_fusion
  272.6 2.5 fusion.53
  275.1 1.4 fusion.25
  276.5 115.8 %all-gather.12.cloned.1.call-done = bf16[1,2,32,128,512]{4,3,1,0,2:T(8,128)(2,1)} async-done(((bf16[1,2,4,128,512]{4,3,1,0,2:T(8,128)(2,1)}), bf16[1,2,32,128,512]{4,3,1,0,2:T(8,128)(2,1)}) %all-gather.12.cloned.1.call-update) | async-done | bytes 8388624 | tf_op jit(solution)/shard_map/all_gather | solution.py:159
  392.3 156.5 %while.19 = (s32[]{:T(128)}, f32[8,512]{1,0:T(8,128)S(1)}, f32[8,512]{1,0:T(8,128)S(1)}, f32[512,8,64]{0,2,1:T(8,128)}, s32[]{:T(128)}, /*index=5*/bf16[2,32,128...) while((s32[]{:T(128)}, f32[8,512]{1,0:T(8,128)S(1)}, ...), condition=%wide.region_15.16_spmd, body=%wide.region_12.0_spmd.sunk | while | flops 554721280 | bytes 43745536 | solution.py:171
  392.3 1.3 constant_dynamic-slice_fusion.4
  394.2 5.6 bitcast_reduce_fusion.2
  399.7 4.8 fusion.123
  405.7 5.2 fusion.125
  411.9 1.3 constant_dynamic-slice_fusion.4
  413.7 5.6 bitcast_reduce_fusion.2
  419.3 4.8 fusion.123
  425.3 5.2 fusion.125
  431.4 1.3 constant_dynamic-slice_fusion.4
  433.3 5.6 bitcast_reduce_fusion.2
  438.8 4.8 fusion.123
  444.8 5.2 fusion.125
  451.0 1.3 constant_dynamic-slice_fusion.4
  452.8 5.6 bitcast_reduce_fusion.2
  458.4 4.8 fusion.123
  464.4 5.2 fusion.125
  470.6 1.3 constant_dynamic-slice_fusion.4
  472.4 5.6 bitcast_reduce_fusion.2
  478.0 4.8 fusion.123
  484.0 5.2 fusion.125
  490.1 1.3 constant_dynamic-slice_fusion.4
  492.0 5.6 bitcast_reduce_fusion.2
  497.5 4.8 fusion.123
  503.5 5.2 fusion.125
  509.7 1.3 constant_dynamic-slice_fusion.4
  511.5 5.6 bitcast_reduce_fusion.2
  517.1 4.8 fusion.123
  523.1 5.2 fusion.125
  529.2 1.3 constant_dynamic-slice_fusion.4
  531.1 5.6 bitcast_reduce_fusion.2
  536.6 4.8 fusion.123
  542.6 5.2 fusion.125
  548.8 1.3 divide_convert_fusion
  551.2 2.2 copy.65
  553.3 2.6 copy.77
  556.0 7.1 %reduce-scatter.4.cloned.1.call-done = bf16[640,512]{1,0:T(8,128)(2,1)} async-done(((bf16[1280,512]{1,0:T(8,128)(2,1)}), bf16[640,512]{1,0:T(8,128)(2,1)}) %reduce-scatter.4.cloned.1.call-update) | async-done | bytes 655376
  563.1 1.6 reshape.105
  566.7 1.5 copy.54
  569.6 1.8 collective-permute-start.2
  572.9 7.0 %collective-permute-done.2 = bf16[4,320,1,128]{3,1,2,0:T(8,128)(2,1)} collective-permute-done((bf16[4,320,1,128]{3,1,2,0:T(8,128)(2,1)}, bf16[4,320,1,128]{3,1,2,0:T(8,128)(2,1)}, u32[]{:S(2)}, u32[]{:S(2)}) %collective-permute-start.2) | collective-permute-done | bytes 327712 | tf_op jit(solution)/shard_map/ppermute | solution.py:32
  579.8 2.7 fusion.96
  (149 shorter events, 39.4 us)
Async XLA Ops:
  7.2 543.1 %copy-start = (bf16[512,1280]{1,0:T(8,128)(2,1)S(1)}, bf16[512,1280]{1,0:T(8,128)(2,1)}, u32[]{:S(2)}) copy-start(bf16[512,1280]{1,0:T(8,128)(2,1)} %param.25) | copy-start | bytes 3932164
  7.2 2.8 copy-start.10
  7.2 46.6 %all-gather.6.cloned.1.call-start = ((), (), s32[]{:S(2)}) async-start(), calls=%async_computation.1 | async-start | bytes 3133440 | tf_op jit(solution)/shard_map/all_gather | solution.py:112
  34.0 7.2 %collective-permute-start.1 = (bf16[1,640,128]{1,2,0:T(8,128)(2,1)S(1)}, bf16[1,640,128]{1,2,0:T(8,128)(2,1)S(1)}, u32[]{:S(2)}, u32[]{:S(2)}) collective-permute-start(bf16[1,640,128]{1,2,0:T(8,128)(2,1)S(1)} %get-tuple-element.229), channel_id=1, source_target_pairs={{2,0},{4,2},{6,4},{8,6},{10,8},{12,10},{14,12},{3,1},{5,3},{7,5},{... | collective-permute-start | bytes 491528 | tf_op jit(solution)/shard_map/ppermute | solution.py:26
  35.3 7.4 %collective-permute-start = (bf16[1,640,128]{1,2,0:T(8,128)(2,1)S(1)}, bf16[1,640,128]{1,2,0:T(8,128)(2,1)S(1)}, u32[]{:S(2)}, u32[]{:S(2)}) collective-permute-start(bf16[1,640,128]{1,2,0:T(8,128)(2,1)S(1)} %get-tuple-element.228), channel_id=1, source_target_pairs={{0,2},{2,4},{4,6},{6,8},{8,10},{10,12},{12,14},{1,3},{3,5},{5,7},{... | collective-permute-start | bytes 491528 | tf_op jit(solution)/shard_map/ppermute | solution.py:25
  43.9 1.6 copy-start.11
  43.9 1.6 copy-start.12
  43.9 1.7 copy-start.13
  43.9 1.7 copy-start.9
  44.0 188.8 %all-gather.8.cloned.1.call-start = ((), (), s32[]{:S(2)}) async-start(), calls=%async_computation.2 | async-start | bytes 22118400 | tf_op jit(solution)/shard_map/all_gather | solution.py:110
  44.7 219.5 %all-gather.10.cloned.1.call-start = ((), (), s32[]{:S(2)}) async-start(), calls=%async_computation.3 | async-start | bytes 1966080 | tf_op jit(solution)/shard_map/all_gather | solution.py:135
  232.8 10.3 %copy-start.14 = (bf16[3,3,640,1280]{3,2,1,0:T(8,128)(2,1)S(1)}, bf16[3,3,640,1280]{3,2,1,0:T(8,128)(2,1)}, u32[]{:S(2)}) copy-start(bf16[3,3,640,1280]{3,2,1,0:T(8,128)(2,1)} %all-gather.8.cloned.1.call-done) | copy-start | bytes 44236804
  239.9 3.3 copy-start.15
  250.8 6.2 %copy-start.7 = (bf16[4,640,128]{1,2,0:T(8,128)(2,1)}, bf16[4,640,128]{1,2,0:T(8,128)(2,1)S(1)}, u32[]{:S(2)}) copy-start(bf16[4,640,128]{1,2,0:T(8,128)(2,1)S(1)} %get-tuple-element.234) | copy-start | bytes 1966084
  254.6 137.7 %all-gather.12.cloned.1.call-start = ((), (), s32[]{:S(2)}) async-start(), calls=%async_computation.4 | async-start | bytes 9437184 | tf_op jit(solution)/shard_map/all_gather | solution.py:159
  257.0 306.1 %reduce-scatter.4.cloned.1.call-start = ((), (), s32[]{:S(2)}) async-start(), calls=%async_computation.5 | async-start | bytes 1966080
  269.9 2.7 copy-start.3
  269.9 2.7 copy-start.5
  404.5 1.2 copy-start.1
  410.9 1.0 copy-start.2
  424.1 1.2 copy-start.1
  430.5 1.0 copy-start.2
  443.6 1.2 copy-start.1
  450.0 1.0 copy-start.2
  463.2 1.2 copy-start.1
  469.6 1.0 copy-start.2
  482.7 1.2 copy-start.1
  489.1 1.0 copy-start.2
  502.3 1.2 copy-start.1
  508.7 1.0 copy-start.2
  521.9 1.2 copy-start.1
  528.3 1.0 copy-start.2
  541.4 1.2 copy-start.1
  547.8 1.0 copy-start.2
  556.0 9.7 %copy-start.8 = (bf16[4,640,128]{1,2,0:T(8,128)(2,1)S(1)}, bf16[4,640,128]{1,2,0:T(8,128)(2,1)}, u32[]{:S(2)}) copy-start(bf16[4,640,128]{1,2,0:T(8,128)(2,1)} %copy-done.7) | copy-start | bytes 1966084
  566.7 4.7 copy-start.6
  568.1 3.4 copy-start.4
  569.6 10.2 %collective-permute-start.2 = (bf16[4,320,1,128]{3,1,2,0:T(8,128)(2,1)}, bf16[4,320,1,128]{3,1,2,0:T(8,128)(2,1)}, u32[]{:S(2)}, u32[]{:S(2)}) collective-permute-start(bf16[4,320,1,128]{3,1,2,0:T(8,128)(2,1)} %copy.55), channel_id=1, source_target_pairs={{0,16},{16,0},{1,17},{17,1},{2,18},{18,2},{3,19},{19,3},{4,20},{20... | collective-permute-start | bytes 983048 | tf_op jit(solution)/shard_map/ppermute | solution.py:32
Sparse Core Ops, SparseCore 0:
  44.0 9.7 all-gather.5
  55.4 177.4 all-gather.7
  254.7 9.4 all-gather.9
  266.2 126.0 all-gather.11
  556.1 6.9 reduce-scatter.3
where the time goes:
time: 592 us; the launch traced here: 590 us
  waiting for transfers between devices  321 us (54%)
  matrix products  115 us (19%)
  local copies, waits for them, and re-layouts  54.8 us (9%)
  other arithmetic  49.9 us (8%)
  blocking collectives  25.7 us (4%)
  between operations  14.8 us (2%)
  starting transfers between devices  7.81 us (1%)
    all_gather x1, waiting for transfers between devices, per_device(): kernel_full = lax.all_gather(conv_w, 'cfg', axis=3, tiled=True)  179 us
    all_gather x1, waiting for transfers between devices, per_device(): shard_piece = lax.all_gather(stale_pair, 'rows', axis=1, tiled=True)  116 us
    dot_general x9, matrix products, block_state(): jnp.einsum('qhd,khd->hqk', query_heads, key_heads, preferred_element_type...  47.3 us
    dot_general x9, matrix products, block_state(): jnp.einsum('hqk,khd->qhd', weights.astype(jnp.bfloat16), value_heads, pre...  44 us
    reduce_sum x9, other arithmetic, block_state(): totals = jnp.sum(weights, axis=-1)  39.5 us
    psum x1, blocking collectives, per_device(): lax.psum((jnp.sum(values32, axis=(0, 2, 3)), jnp.sum(values32 * values32,...  23.1 us
    unnamed x36, local copies, waits for them, and re-layouts  18.3 us
    while x48, local copies, waits for them, and re-layouts  18.1 us
  transfers between devices with their start and end apart: 8, of which 8 were waited for; matrix products, arithmetic and copies ran while one was open for 4% of the time, Pallas kernels for 0%

commit v1 on v0

v1 whole, which is shorter than its diff:
```python
import functools
import math

import jax
import jax.numpy as jnp
from jax import lax
from jax.experimental import pallas as pl
from jax.experimental.pallas import tpu as pltpu
from jax.sharding import PartitionSpec as P

D = 1280
HD = 64
GROUPS = 32
TEMB = 320
LANES = 128

epsilon = 1e-05
guidance = 5.0
EXP2_SCALE = math.log2(math.e) / math.sqrt(HD)
VMEM_LIMIT = 50 * 1024 * 1024


def swapped(array, axis):
    return lax.ppermute(array, axis, [(i, i ^ 1) for i in range(lax.axis_size(axis))])


def ring_pairs(count):
    order = list(range(0, count, 2)) + list(range(count - 1, 0, -2))
    forward = [(order[i], order[(i + 1) % count]) for i in range(count)]
    backward = [(j, i) for i, j in forward]
    return forward, backward


def gather_tp(array, axis):
    if lax.axis_size("tp") != 2:
        return lax.all_gather(array, "tp", axis=axis, tiled=True)
    other = swapped(array, "tp")
    first = lax.axis_index("tp") == 0
    return jnp.concatenate(
        [jnp.where(first, array, other), jnp.where(first, other, array)], axis=axis
    )


def halves_of_inputs(own):
    cfg = lax.axis_index("cfg")
    if lax.axis_size("tp") != 2:
        full = lax.all_gather(own, "tp", axis=1, tiled=True)
        half = full.shape[1] // 2
        mine = lax.dynamic_slice_in_dim(full, cfg * half, half, 1)
        sent = lax.dynamic_slice_in_dim(full, (1 - cfg) * half, half, 1)
        return mine, swapped(sent, "cfg")
    at = lax.axis_index("tp") == cfg
    across = lax.ppermute(own, ("cfg", "tp"), [(1, 3), (2, 0)])
    pairs = [(0, 1), (3, 2)]
    own_side = lax.ppermute(own, ("cfg", "tp"), pairs)
    across_side = lax.ppermute(across, ("cfg", "tp"), pairs)
    return jnp.where(at, own, own_side), jnp.where(at, across, across_side)


def conv_kernel(flags_ref, x_ref, coef_ref, w_ref, out_ref, act_ref, acc_ref):
    rows = out_ref.shape[0]
    step = pl.program_id(0)

    @pl.when(step == 0)
    def _():
        mean = coef_ref[:, 0:1]
        scale = coef_ref[:, 1:2]
        shift = coef_ref[:, 2:3]
        for r in range(rows + 2):
            x = x_ref[r].astype(jnp.float32)
            z = (x - mean) * scale + shift
            z = z * jax.nn.sigmoid(z)
            if r == 0:
                z = jnp.where(flags_ref[0] == 1, z, 0.0)
            if r == rows + 1:
                z = jnp.where(flags_ref[1] == 1, z, 0.0)
            act_ref[:, r * LANES : (r + 1) * LANES] = z.astype(jnp.bfloat16)

    def product(row_tap):
        return jnp.dot(
            w_ref[row_tap, 0],
            act_ref[:, row_tap * LANES : (row_tap + rows) * LANES],
            preferred_element_type=jnp.float32,
        )

    y = product(0) + product(1) + product(2)
    lane = lax.broadcasted_iota(jnp.int32, (y.shape[0], LANES), 1)

    @pl.when(step == 0)
    def _():
        for r in range(rows):
            part = pltpu.roll(y[:, r * LANES : (r + 1) * LANES], 1, axis=1)
            acc_ref[r] = jnp.where(lane == 0, 0.0, part)

    @pl.when(step == 1)
    def _():
        for r in range(rows):
            acc_ref[r] += y[:, r * LANES : (r + 1) * LANES]

    @pl.when(step == 2)
    def _():
        for r in range(rows):
            part = pltpu.roll(y[:, r * LANES : (r + 1) * LANES], LANES - 1, axis=1)
            total = acc_ref[r] + jnp.where(lane == LANES - 1, 0.0, part)
            out_ref[r] = total.astype(out_ref.dtype)


def conv_call(flags, x, coef, conv_w, out_dtype):
    rows = x.shape[0] - 2
    outs, ins = conv_w.shape[2:]
    return pl.pallas_call(
        conv_kernel,
        grid=(3,),
        in_specs=[
            pl.BlockSpec(memory_space=pltpu.SMEM),
            pl.BlockSpec(x.shape, lambda i: (0, 0, 0)),
            pl.BlockSpec(coef.shape, lambda i: (0, 0)),
            pl.BlockSpec((3, 1, outs, ins), lambda i: (0, i, 0, 0)),
        ],
        out_specs=pl.BlockSpec((rows, outs, LANES), lambda i: (0, 0, 0)),
        out_shape=jax.ShapeDtypeStruct((rows, outs, LANES), out_dtype),
        scratch_shapes=[
            pltpu.VMEM((ins, (rows + 2) * LANES), jnp.bfloat16),
            pltpu.VMEM((rows, outs, LANES), jnp.float32),
        ],
        compiler_params=pltpu.CompilerParams(vmem_limit_bytes=VMEM_LIMIT),
        cost_estimate=pl.CostEstimate(
            flops=2 * 9 * outs * ins * rows * LANES,
            bytes_accessed=2 * 9 * outs * ins,
            transcendentals=ins * rows * LANES,
        ),
        name="norm_conv",
    )(flags, x, coef, conv_w)


def attention_kernel(blocks, carried, final, *refs):
    q_ref = refs[0]
    kv_refs = refs[1 : 1 + 2 * blocks]
    at = 1 + 2 * blocks
    if carried:
        m_in, acc_in = refs[at : at + 2]
        at += 2
    outs = refs[at:]
    positions = q_ref.shape[0]
    tile = min(256, positions)
    for start in range(0, positions, tile):
        rows = pl.ds(start, tile)
        q = q_ref[rows, :]
        low_q = lax.broadcasted_iota(jnp.int32, q.shape, 1) < HD
        results = []
        for head in range(2):
            sel_q = low_q if head == 0 else jnp.logical_not(low_q)
            qh = jnp.where(sel_q, q, jnp.zeros_like(q))
            peak = m_in[0, head, rows, :] if carried else None
            acc = acc_in[0, head, rows, :] if carried else None
            for block in range(blocks):
                keys = kv_refs[2 * block]
                values = kv_refs[2 * block + 1]
                k = keys[...]
                v = values[...]
                low_v = lax.broadcasted_iota(jnp.int32, v.shape, 1) < HD
                sel_v = low_v if head == 0 else jnp.logical_not(low_v)
                v = jnp.where(sel_v, v, jnp.ones_like(v))
                s = lax.dot_general(
                    qh, k, (((1,), (1,)), ((), ())), preferred_element_type=jnp.float32
                )
                top = jnp.broadcast_to(jnp.max(s, axis=1, keepdims=True), (tile, LANES))
                new_peak = top if peak is None else jnp.maximum(peak, top)
                wide = jnp.concatenate([new_peak] * (s.shape[1] // LANES), axis=1)
                p = jnp.exp2((s - wide) * EXP2_SCALE).astype(jnp.bfloat16)
                term = jnp.dot(p, v, preferred_element_type=jnp.float32)
                if acc is None:
                    acc = term
                else:
                    acc = acc * jnp.exp2((peak - new_peak) * EXP2_SCALE) + term
                peak = new_peak
            if final:
                results.append(acc / pltpu.roll(acc, HD, axis=1))
            else:
                outs[0][0, head, rows, :] = peak
                outs[1][0, head, rows, :] = acc
        if final:
            outs[0][rows, :] = jnp.where(low_q, results[0], results[1]).astype(jnp.bfloat16)


def attention_call(q, pairs, state, final):
    positions, features = q.shape
    tiles = features // LANES
    column = pl.BlockSpec((positions, LANES), lambda i: (0, i))
    carry = pl.BlockSpec((1, 2, positions, LANES), lambda i: (i, 0, 0, 0))
    carry_shape = jax.ShapeDtypeStruct((tiles, 2, positions, LANES), jnp.float32)
    operands = [q]
    specs = [column]
    for k, v in pairs:
        operands += [k, v]
        specs += [column, column]
    if state is not None:
        operands += list(state)
        specs += [carry, carry]
    if final:
        out_shape = jax.ShapeDtypeStruct((positions, features), jnp.bfloat16)
        out_specs = column
    else:
        out_shape = (carry_shape, carry_shape)
        out_specs = (carry, carry)
    keys = positions * len(pairs)
    return pl.pallas_call(
        functools.partial(attention_kernel, len(pairs), state is not None, final),
        grid=(tiles,),
        in_specs=specs,
        out_specs=out_specs,
        out_shape=out_shape,
        compiler_params=pltpu.CompilerParams(vmem_limit_bytes=VMEM_LIMIT),
        cost_estimate=pl.CostEstimate(
            flops=16 * positions * keys * features,
            bytes_accessed=4 * keys * features,
            transcendentals=positions * keys * features // HD,
        ),
        name="attend",
    )(*operands)


def per_device(
    latent,
    stale_kv,
    timestep,
    w_time,
    gn_gain,
    gn_bias,
    conv_w,
    conv_b,
    ln_gain,
    ln_bias,
    w_qkv,
    w_out,
):
    latent_rows = latent[0]
    rows_count = lax.axis_size("rows")
    tp_count = lax.axis_size("tp")
    span_rows, local_channels, grid_width = latent_rows.shape
    positions = span_rows * grid_width
    group_width = D // GROUPS
    local_groups = local_channels // group_width
    my_block = lax.axis_index("rows")
    cfg = lax.axis_index("cfg")
    tp = lax.axis_index("tp")

    up_pairs = [(i, i + 1) for i in range(rows_count - 1)]
    down_pairs = [(i + 1, i) for i in range(rows_count - 1)]
    before = lax.ppermute(latent_rows[span_rows - 1 :], "rows", up_pairs)
    after = lax.ppermute(latent_rows[:1], "rows", down_pairs)
    rimmed = jnp.concatenate([before, latent_rows, after], axis=0)
    x_mine, x_other = halves_of_inputs(rimmed)

    forward, backward = ring_pairs(rows_count)
    stale_k = stale_kv[0, 0].reshape(positions, -1)
    stale_v = stale_kv[0, 1].reshape(positions, -1)
    kf = vf = None
    kb = vb = None
    kf, vf, kb, vb = stale_k, stale_v, stale_k, stale_v
    arrived = []
    for hop in range(1, rows_count // 2 + 1):
        last = hop == rows_count // 2
        kf = lax.ppermute(kf, "rows", forward)
        vb = lax.ppermute(vb, "rows", backward)
        if last:
            arrived.append([(kf, vb)])
        else:
            vf = lax.ppermute(vf, "rows", forward)
            kb = lax.ppermute(kb, "rows", backward)
            arrived.append([(kf, vf), (kb, vb)])

    latent32 = latent_rows.astype(jnp.float32)
    values32 = latent32.reshape(span_rows, local_groups, group_width, grid_width)
    sums = jnp.stack(
        [jnp.sum(values32, axis=(0, 2, 3)), jnp.sum(values32 * values32, axis=(0, 2, 3))]
    )
    table = jnp.zeros((2, 2, GROUPS), jnp.float32)
    table = lax.dynamic_update_slice(table, sums[None], (cfg, 0, tp * local_groups))
    table = lax.psum(table, ("cfg", "rows", "tp"))
    vectors = gather_tp(jnp.stack([gn_gain, gn_bias, ln_gain, ln_bias]), 1).astype(jnp.float32)

    amount = span_rows * rows_count * grid_width * group_width
    table = lax.dynamic_slice_in_dim(table, cfg * (GROUPS // 2), GROUPS // 2, 2)
    group_mean = table[:, 0] / amount
    variance = table[:, 1] / amount - group_mean * group_mean
    inverse = lax.rsqrt(variance + epsilon)
    half = D // 2
    gain_half = lax.dynamic_slice_in_dim(vectors[0], cfg * half, half)
    bias_half = lax.dynamic_slice_in_dim(vectors[1], cfg * half, half)
    mean_c = jnp.repeat(group_mean, group_width, axis=1)
    scale_c = jnp.repeat(inverse, group_width, axis=1) * gain_half[None]
    coef = jnp.stack(
        [mean_c, scale_c, jnp.broadcast_to(bias_half[None], mean_c.shape)], axis=2
    )
    coef_mine = lax.dynamic_index_in_dim(coef, cfg, 0, keepdims=False)
    coef_other = lax.dynamic_index_in_dim(coef, 1 - cfg, 0, keepdims=False)
    flags = jnp.stack([my_block > 0, my_block < rows_count - 1]).astype(jnp.int32)

    conv_sent = conv_call(flags, x_other, coef_other, conv_w, jnp.bfloat16)
    conv_received = swapped(conv_sent, "cfg")
    conv_own = conv_call(flags, x_mine, coef_mine, conv_w, jnp.float32)

    half_width = TEMB // 2
    frequencies = jnp.exp(
        -math.log(10000.0) * jnp.arange(half_width, dtype=jnp.float32) / half_width
    )
    angles = timestep.astype(jnp.float32)[0] * frequencies
    embedding = jnp.concatenate([jnp.cos(angles), jnp.sin(angles)])
    time_bias = jnp.dot(
        jax.nn.silu(embedding)[None, :], w_time.astype(jnp.float32), precision=lax.Precision.HIGHEST
    )[0]
    bias = conv_b.astype(jnp.float32) + time_bias
    resid = (
        latent32 + (conv_own + conv_received.astype(jnp.float32) + bias[None, :, None])
    ).astype(jnp.bfloat16)

    full = gather_tp(resid, 1).astype(jnp.float32)
    token_mean = jnp.mean(full, axis=1)
    token_var = jnp.mean(full * full, axis=1) - token_mean * token_mean
    normed = (full - token_mean[:, None, :]) * lax.rsqrt(token_var + epsilon)[:, None, :]
    normed = (normed * vectors[2][None, :, None] + vectors[3][None, :, None]).astype(jnp.bfloat16)
    local_features = w_qkv.shape[2]
    projected = (
        jnp.einsum(
            "rdw,df->rwf",
            normed,
            w_qkv.reshape(D, 3 * local_features),
            preferred_element_type=jnp.float32,
        )
        .reshape(positions, 3 * local_features)
        .astype(jnp.bfloat16)
    )
    queries = projected[:, :local_features]
    keys_new = projected[:, local_features : 2 * local_features]
    values_new = projected[:, 2 * local_features :]
    fresh_kv = jnp.stack([keys_new, values_new]).reshape(
        1, 2, span_rows, grid_width, local_features
    )

    state = attention_call(queries, [(keys_new, values_new)] + arrived[0], None, False)
    for group in arrived[1:-1]:
        state = attention_call(queries, group, state, False)
    attended = attention_call(queries, arrived[-1], state, True)

    attended_full = gather_tp(attended, 1)
    if tp_count == 2:
        w_split = w_out.reshape(-1, tp_count, local_channels)
        first = tp == 0
        w_mine = lax.dynamic_index_in_dim(w_split, tp, 1, keepdims=False)
        w_side = swapped(lax.dynamic_index_in_dim(w_split, 1 - tp, 1, keepdims=False), "tp")
        w_cols = jnp.concatenate(
            [jnp.where(first, w_mine, w_side), jnp.where(first, w_side, w_mine)], axis=0
        )
    else:
        w_cols = lax.all_to_all(w_out, "tp", 1, 0, tiled=True)
    w_pairs = w_cols.reshape(w_cols.shape[0], local_channels // 2, 2)
    att_rows = attended_full.reshape(span_rows, grid_width, -1)
    resid_pairs = resid.reshape(span_rows, local_channels // 2, 2, grid_width)

    def branch_out(parity):
        terms = jnp.einsum(
            "rwf,fd->rdw",
            att_rows,
            lax.dynamic_index_in_dim(w_pairs, parity, 2, keepdims=False),
            preferred_element_type=jnp.float32,
        )
        base = lax.dynamic_index_in_dim(resid_pairs, parity, 2, keepdims=False)
        return (base.astype(jnp.float32) + terms).astype(jnp.bfloat16)

    other_branch = swapped(branch_out(1 - cfg), "cfg")
    kept = branch_out(cfg)
    is_cond = cfg == 0
    cond_out = jnp.where(is_cond, kept, other_branch).astype(jnp.float32)
    uncond_out = jnp.where(is_cond, other_branch, kept).astype(jnp.float32)
    guided = (uncond_out + guidance * (cond_out - uncond_out)).astype(jnp.bfloat16)
    return (guided[:, :, None, :], fresh_kv)


def solution(mesh):
    in_specs = (
        P("cfg", "rows", "tp", None),
        P("cfg", None, "rows", None, "tp"),
        P(),
        P(None, "tp"),
        P("tp"),
        P("tp"),
        P(None, None, "tp", "cfg"),
        P("tp"),
        P("tp"),
        P("tp"),
        P(None, None, "tp"),
        P("tp", None),
    )
    out_specs = (P("rows", "tp", "cfg", None), P("cfg", None, "rows", None, "tp"))
    return jax.shard_map(
        per_device, mesh=mesh, in_specs=in_specs, out_specs=out_specs, check_vma=False
    )
```

time: 592 us -> 228 us (0.39)
  waiting for transfers between devices: 321 us -> 22.3 us
  matrix products: 115 us -> 8.3 us
  Pallas kernels: 0 us -> 67.2 us
  other arithmetic: 49.9 us -> 12.7 us
  starting transfers between devices: 7.81 us -> 33.3 us
  blocking collectives: 25.7 us -> 47.5 us
  local copies, waits for them, and re-layouts: 54.8 us -> 33.6 us
  between operations: 14.8 us -> 1.8 us
    all_gather x4 -> x0, waiting for transfers between devices: 304 us -> none  [the longest x1 179 us: per_device(): kernel_full = lax.all_gather(conv_w, 'cfg', axis=3, tiled=True)]
    dot_general x28 -> x2, matrix products: 110 us -> 3.26 us  [branch_out(): jnp.einsum('rwf,fd->rdw', att_rows, lax.dynamic_index_in_dim(w_pairs, par...]
    pallas_call x0 -> x6, Pallas kernels: none -> 67.2 us  [the longest x4 50 us: attention_call(): pl.pallas_call(functools.partial(attention_kernel, len(pairs), state is n...]
    reduce_sum x9 -> x1, other arithmetic: 39.5 us -> 0.35 us  [per_device(): token_mean = jnp.mean(full, axis=1)]
    ppermute x3 -> x25, starting transfers between devices: 7.61 us -> 33.3 us  [the longest x4 6.06 us: per_device(): vb = lax.ppermute(vb, 'rows', backward)]
    psum x2 -> x1, blocking collectives: 25.7 us -> 47.5 us  [per_device(): table = lax.psum(table, ('cfg', 'rows', 'tp'))]
    while x48 -> x0, local copies, waits for them, and re-layouts: 18.1 us -> none
    ppermute x3 -> x25, waiting for transfers between devices: 9.76 us -> 22.3 us  [the longest x6 11.2 us: swapped(): lax.ppermute(array, axis, [(i, i ^ 1) for i in range(lax.axis_size(axis))])]
  transfers between devices with their start and end apart: 8 -> 25, of which waited for: 8 -> 5; matrix products, arithmetic and copies ran while one was open for 4% -> 21% of each run, Pallas kernels for 0% -> 30%
where the time goes in v1:
time: 228 us; the launch traced here: 227 us
  Pallas kernels  67.2 us (29%)
  blocking collectives  47.5 us (21%)
  local copies, waits for them, and re-layouts  33.6 us (15%)
  starting transfers between devices  33.3 us (15%)
  waiting for transfers between devices  22.3 us (10%)
  other arithmetic  12.7 us (6%)
  matrix products  8.3 us (4%)
    pallas_call x4, Pallas kernels, attention_call(): pl.pallas_call(functools.partial(attention_kernel, len(pairs), state is n...  50 us
    psum x1, blocking collectives, per_device(): table = lax.psum(table, ('cfg', 'rows', 'tp'))  47.5 us
    pallas_call x2, Pallas kernels, conv_call(): pl.pallas_call(conv_kernel, grid=(3,), in_specs=[pl.BlockSpec(memory_spac...  17.2 us
    ppermute x6, waiting for transfers between devices, swapped(): lax.ppermute(array, axis, [(i, i ^ 1) for i in range(lax.axis_size(axis))])  11.2 us
    ppermute x4, waiting for transfers between devices, per_device(): vb = lax.ppermute(vb, 'rows', backward)  10.7 us
    unnamed x32, local copies, waits for them, and re-layouts  9.15 us
    ppermute x4, starting transfers between devices, per_device(): vb = lax.ppermute(vb, 'rows', backward)  6.06 us
    ppermute x4, starting transfers between devices, per_device(): kf = lax.ppermute(kf, 'rows', forward)  5.62 us
  transfers between devices with their start and end apart: 25, of which 5 were waited for; matrix products, arithmetic and copies ran while one was open for 21% of the time, Pallas kernels for 30%

profile of v1, /device:TPU:0, one launch (start us, length us, event | category | flops | bytes accessed | tf_op | source)
XLA Modules:
  0.0 226.7 jit_solution(16585571862120011065)
XLA Ops:
  0.7 1.1 slice_bitcast_fusion.1
  1.8 4.9 %collective-permute-start = (bf16[1,640,128]{2,1,0:T(8,128)(2,1)S(1)}, bf16[1,640,128]{2,1,0:T(8,128)(2,1)S(1)}, u32[]{:S(2)}, u32[]{:S(2)}) collective-permute-start(bf16[1,640,128]{2,1,0:T(8,128)(2,1)S(1)} %get-tuple-element.45), channel_id=1, source_target_pairs={{0,2},{2,4},{4,6},{6,8},{8,10},{10,12},{12,14},{1,3},{3,5},{5,7},{... | collective-permute-start | bytes 491528 | tf_op jit(solution)/shard_map/ppermute | solution.py:250
  6.7 1.3 collective-permute-start.1
  8.0 2.3 fusion.30
  10.2 2.6 %collective-permute-start.13 = (bf16[512,512]{1,0:T(8,128)(2,1)}, bf16[512,512]{1,0:T(8,128)(2,1)S(1)}, u32[]{:S(2)}, u32[]{:S(2)}) collective-permute-start(bf16[512,512]{1,0:T(8,128)(2,1)} %bitcast.23), channel_id=1, source_target_pairs={{4,0},{8,4},{12,8},{14,12},{10,14},{6,10},{2,6},{0,2},{5,1},{9,5},... | collective-permute-start | bytes 1572872 | tf_op jit(solution)/shard_map/ppermute | solution.py:265
  12.9 1.0 collective-permute-start.17
  13.9 0.3 collective-permute-done.1
  14.2 1.1 pad_maximum_fusion.4
  15.3 1.3 collective-permute-start.4
  16.6 1.6 collective-permute-start.3
  18.2 4.1 %collective-permute-start.9 = (bf16[512,512]{1,0:T(8,128)(2,1)}, bf16[512,512]{1,0:T(8,128)(2,1)S(1)}, u32[]{:S(2)}, u32[]{:S(2)}) collective-permute-start(bf16[512,512]{1,0:T(8,128)(2,1)} %bitcast.22), channel_id=1, source_target_pairs={{0,4},{4,8},{8,12},{12,14},{14,10},{10,6},{6,2},{2,0},{1,5},{5,9},... | collective-permute-start | bytes 1572872 | tf_op jit(solution)/shard_map/ppermute | solution.py:264
  22.3 0.3 convert_reduce_fusion.1
  23.8 0.2 dynamic_update_slice.3
  24.0 47.5 %psum.7 = f32[2,2,32]{2,0,1:T(2,128)S(1)} all-reduce(f32[2,2,32]{2,0,1:T(2,128)S(1)} %dynamic_update_slice.3), channel_id=1, replica_groups=mesh['cfg'=2,'rows'=8,'tp'=2] {'cfg','rows','tp'}, use_global_device_ids=true, to_apply=%region_4.5 | all-reduce | flops 128 | bytes 1024 | tf_op jit(solution)/shard_map/psum | solution.py:280
  71.6 0.3 convolution_reduce_fusion
  72.4 1.4 collective-permute-start.5
  73.9 2.3 collective-permute-start.2
  76.2 0.2 copy.41
  76.4 1.3 broadcast_select_fusion.x_ref
  77.7 8.6 %norm_conv.3 = bf16[4,640,128]{2,1,0:T(8,128)(2,1)S(1)} custom-call(s32[2]{0:T(128)S(1)} %add_convert_fusion.1.flags_ref, bf16[6,640,128]{2,1,0:T(8,128)(2,1)S(1)} %broadcast_select_fusion.x_ref, f32[640,3]{1,0:T(8,128)S(1)} %bitcast.86, bf16[3,3,640,640]{3,2,1,0:T(8,128)(2,1)} %w_ref.3), custom_call_target="tpu_custom_call" | custom-call | flops 3774873600 | bytes 7372800 | tf_op jit(solution)/shard_map/norm_conv/pallas_call | solution.py:111
  86.3 1.8 collective-permute-start.6
  88.1 0.2 copy.40
  88.3 0.6 collective-permute-start.20
  88.9 1.4 collective-permute-start.10
  90.4 0.6 collective-permute-start.14
  90.9 1.2 broadcast_select_fusion.1.x_ref
  92.2 8.6 %norm_conv.2 = f32[4,640,128]{2,1,0:T(8,128)S(1)} custom-call(s32[2]{0:T(128)S(1)} %add_convert_fusion.1.flags_ref, bf16[6,640,128]{2,1,0:T(8,128)(2,1)S(1)} %broadcast_select_fusion.1.x_ref, f32[640,3]{1,0:T(8,128)S(1)} %bitcast.85, bf16[3,3,640,640]{3,2,1,0:T(8,128)(2,1)} %w_ref.3), custom_call_target="tpu_custom_call" | custom-call | flops 3774873600 | bytes 7372800 | tf_op jit(solution)/shard_map/norm_conv/pallas_call | solution.py:111
  100.8 2.6 %collective-permute-done.6 = bf16[4,640,128]{2,1,0:T(8,128)(2,1)} collective-permute-done((bf16[4,640,128]{2,1,0:T(8,128)(2,1)S(1)}, bf16[4,640,128]{2,1,0:T(8,128)(2,1)}, u32[]{:S(2)}, u32[]{:S(2)}) %collective-permute-start.6) | collective-permute-done | bytes 655392 | tf_op jit(solution)/shard_map/ppermute | solution.py:24
  103.4 1.4 add_convert_fusion
  104.8 0.8 collective-permute-start.8
  105.7 2.0 collective-permute-start.21
  107.7 6.6 %collective-permute-done.14.refs_4_ = bf16[512,512]{1,0:T(8,128)(2,1)} collective-permute-done((bf16[512,512]{1,0:T(8,128)(2,1)S(1)}, bf16[512,512]{1,0:T(8,128)(2,1)}, u32[]{:S(2)}, u32[]{:S(2)}) %collective-permute-start.14) | collective-permute-done | bytes 524320 | tf_op jit(solution)/shard_map/ppermute | solution.py:265
  114.3 0.8 collective-permute-start.15
  115.1 6.2 %copy.48 = bf16[1280,3,512]{0,2,1:T(8,128)(2,1)} copy(bf16[1280,3,512]{2,0,1:T(8,128)(2,1)} %param.22) | data formatting | bytes 7864320 | tf_op args[10]
  121.4 2.5 %copy.43 = bf16[512,1280]{0,1:T(8,128)(2,1)} copy(bf16[512,1280]{1,0:T(8,128)(2,1)} %param.23) | data formatting | bytes 2621440 | tf_op args[11]
  123.8 2.4 %constant_dynamic-slice_fusion.5 = (bf16[512,1,640]{0,2,1:T(8,128)(2,1)}, bf16[512,1,640]{0,2,1:T(8,128)(2,1)}) fusion(bf16[512,2,640]{0,2,1:T(8,128)(2,1)} %bitcast.90, s32[]{:T(128)S(6)} %select_n.116, s32[]{:T(128)S(6)} %select_n.117), kind=kLoop, calls=%fused_computation.58 | loop fusion | bytes 2621448 | tf_op jit(solution)/shard_map/jit(dynamic_index_in_dim)/dynamic_slice | solution.py:350
  126.2 2.2 copy.45
  128.4 2.2 copy.44
  130.7 1.7 collective-permute-start.19
  132.3 0.4 collective-permute-start.22
  132.7 4.1 %collective-permute-done.15.refs_4_ = bf16[512,512]{1,0:T(8,128)(2,1)} collective-permute-done((bf16[512,512]{1,0:T(8,128)(2,1)}, bf16[512,512]{1,0:T(8,128)(2,1)}, u32[]{:S(2)}, u32[]{:S(2)}) %collective-permute-start.15) | collective-permute-done | bytes 524320 | tf_op jit(solution)/shard_map/ppermute | solution.py:265
  136.8 2.0 collective-permute-start.16
  138.8 1.2 broadcast_select_fusion.3
  140.0 0.4 convert_reduce_fusion
  140.4 1.7 fusion.6
  142.0 2.5 %copy.47 = bf16[4,128,1280]{2,1,0:T(8,128)(2,1)} copy(bf16[4,128,1280]{1,2,0:T(8,128)(2,1)} %fusion.6) | data formatting | bytes 2621440 | tf_op jit(solution)/shard_map/rdw,df->rwf/dot_general | solution.py:325
  144.5 4.7 %convolution_convert_fusion = bf16[512,1536]{1,0:T(8,128)(2,1)S(1)} fusion(bf16[512,1280]{1,0:T(8,128)(2,1)} %bitcast.92, bf16[1280,1536]{0,1:T(8,128)(2,1)} %bitcast.91), kind=kOutput, calls=%fused_computation.3 | convolution fusion | flops 2014052352 | bytes 6815744 | tf_op jit(solution)/shard_map/rdw,df->rwf/dot_general | solution.py:325
  149.4 16.7 %attend.4 = (f32[4,2,512,128]{3,2,1,0:T(8,128)}, f32[4,2,512,128]{3,2,1,0:T(8,128)}) custom-call(bf16[512,512]{1,0:T(8,128)(2,1)S(1)} %get-tuple-element.30.refs_0_, bf16[512,512]{1,0:T(8,128)(2,1)S(1)} %get-tuple-element.29.refs_1_, bf16[512,512]{1,0:T(8,128)(2,1)S(1)} %get-tuple-element.28.refs_2_, bf16[512,512]{1,0:T(8,128)(2,1)S(1)} %collective-permute-done.9.refs_3_, ...), custom_call_target="tpu_custom_call" | custom-call | flops 6442450944 | bytes 3145728 | tf_op jit(solution)/shard_map/attend/pallas_call | solution.py:207
  166.1 12.9 %attend.5 = (f32[4,2,512,128]{3,2,1,0:T(8,128)}, f32[4,2,512,128]{3,2,1,0:T(8,128)}) custom-call(bf16[512,512]{1,0:T(8,128)(2,1)S(1)} %get-tuple-element.30.refs_0_, bf16[512,512]{1,0:T(8,128)(2,1)} %collective-permute-done.10.refs_1_, bf16[512,512]{1,0:T(8,128)(2,1)} %collective-permute-done.18.refs_2_, bf16[512,512]{1,0:T(8,128)(2,1)} %collective-permute-done.21.refs_3_, ...), custom_call_target="tpu_custom_call" | custom-call | flops 4294967296 | bytes 2097152 | tf_op jit(solution)/shard_map/attend/pallas_call | solution.py:207
  179.0 13.0 %attend.6 = (f32[4,2,512,128]{3,2,1,0:T(8,128)}, f32[4,2,512,128]{3,2,1,0:T(8,128)}) custom-call(bf16[512,512]{1,0:T(8,128)(2,1)S(1)} %get-tuple-element.30.refs_0_, bf16[512,512]{1,0:T(8,128)(2,1)} %collective-permute-done.11.refs_1_, bf16[512,512]{1,0:T(8,128)(2,1)} %collective-permute-done.19.refs_2_, bf16[512,512]{1,0:T(8,128)(2,1)} %collective-permute-done.22.refs_3_, ...), custom_call_target="tpu_custom_call" | custom-call | flops 4294967296 | bytes 2097152 | tf_op jit(solution)/shard_map/attend/pallas_call | solution.py:207
  192.0 7.4 %attend.7 = bf16[512,512]{1,0:T(8,128)(2,1)S(1)} custom-call(bf16[512,512]{1,0:T(8,128)(2,1)S(1)} %get-tuple-element.30.refs_0_, bf16[512,512]{1,0:T(8,128)(2,1)} %collective-permute-done.12.refs_1_, bf16[512,512]{1,0:T(8,128)(2,1)} %collective-permute-done.16.refs_2_, f32[4,2,512,128]{3,2,1,0:T(8,128)} %get-tuple-element.12.refs_3_, ...), custom_call_target="tpu_custom_call" | custom-call | flops 2147483648 | bytes 1048576 | tf_op jit(solution)/shard_map/attend/pallas_call | solution.py:207
  199.5 0.3 collective-permute-start.23
  199.8 1.2 bitcast_select_fusion.1
  201.1 1.5 copy.46
  202.6 3.1 %reshape.116 = bf16[1024,320,2]{0,2,1:T(2,128)(2,1)S(1)} reshape(bf16[1024,640]{0,1:T(8,128)(2,1)} %copy.46) | data formatting | bytes 2621440 | tf_op jit(solution)/shard_map/reshape | solution.py:357
  205.7 3.8 %constant_dynamic-slice_fusion.1 = (bf16[1024,320,1]{0,2,1:T(2,128)(2,1)}, bf16[1024,320,1]{0,2,1:T(2,128)(2,1)S(1)}) fusion(bf16[1024,320,2]{0,2,1:T(2,128)(2,1)S(1)} %reshape.116, s32[]{:T(128)S(6)} %select_n.106, s32[]{:T(128)S(6)} %select_n.114), kind=kLoop, calls=%fused_computation.54 | loop fusion | bytes 2621448 | tf_op jit(solution)/shard_map/jit(dynamic_index_in_dim)/dynamic_slice | solution.py:365
  209.5 2.2 constant_dynamic-slice_fusion.2
  211.7 1.1 broadcast_select_fusion.5
  213.0 0.6 fusion.10
  213.5 0.4 copy-done.8
  213.9 0.3 collective-permute-start.24
  214.2 1.1 pad_maximum_fusion.3
  215.3 8.6 %collective-permute-done.24 = bf16[4,320,128]{2,1,0:T(8,128)(2,1)} collective-permute-done((bf16[4,320,128]{2,1,0:T(8,128)(2,1)S(1)}, bf16[4,320,128]{2,1,0:T(8,128)(2,1)}, u32[]{:S(2)}, u32[]{:S(2)}) %collective-permute-start.24) | collective-permute-done | bytes 327712 | tf_op jit(solution)/shard_map/ppermute | solution.py:24
  223.9 2.7 %fusion.15 = bf16[4,320,1,128]{3,1,2,0:T(8,128)(2,1)} fusion(bf16[4,320,128]{2,1,0:T(8,128)(2,1)} %collective-permute-done.24, bf16[4,128,1024]{2,1,0:T(8,128)(2,1)} %bitcast.94, bf16[1024,320,1]{0,2,1:T(2,128)(2,1)S(1)} %copy-done.7, bf16[4,320,1,128]{3,2,1,0:T(2,128)(2,1)S(1)} %copy-done.9, pred[]{:T(512)S(6)} %eq.12), kind=kOutput, calls=%fused_computation.40 | convolution fusion | flops 337346560 | bytes 2686977 | tf_op jit(solution)/shard_map/rwf,fd->rdw/dot_general | solution.py:362
  (87 shorter events, 1.9 us)
Async XLA Ops:
  0.6 71.0 %copy-start = (bf16[320,640]{1,0:T(8,128)(2,1)S(1)}, bf16[320,640]{1,0:T(8,128)(2,1)}, u32[]{:S(2)}) copy-start(bf16[320,640]{1,0:T(8,128)(2,1)} %param.15) | copy-start | bytes 1228804
  0.6 13.6 %copy-start.2 = (bf16[1,4,640,128]{3,2,1,0:T(8,128)(2,1)S(1)}, bf16[1,4,640,128]{3,2,1,0:T(8,128)(2,1)}, u32[]{:S(2)}) copy-start(bf16[1,4,640,128]{3,2,1,0:T(8,128)(2,1)} %param.12) | copy-start | bytes 1966084
  0.7 13.2 %copy-start.11 = (bf16[640]{0:T(1024)(128)(2,1)S(1)}, bf16[640]{0:T(1024)(128)(2,1)}, u32[]{:S(2)}) copy-start(bf16[640]{0:T(1024)(128)(2,1)} %param.16) | copy-start | bytes 3844
  0.7 13.2 %copy-start.12 = (bf16[640]{0:T(1024)(128)(2,1)S(1)}, bf16[640]{0:T(1024)(128)(2,1)}, u32[]{:S(2)}) copy-start(bf16[640]{0:T(1024)(128)(2,1)} %param.17) | copy-start | bytes 3844
  0.7 13.2 %copy-start.13 = (bf16[640]{0:T(1024)(128)(2,1)S(1)}, bf16[640]{0:T(1024)(128)(2,1)}, u32[]{:S(2)}) copy-start(bf16[640]{0:T(1024)(128)(2,1)} %param.20) | copy-start | bytes 3844
  0.7 13.2 %copy-start.14 = (bf16[640]{0:T(1024)(128)(2,1)S(1)}, bf16[640]{0:T(1024)(128)(2,1)}, u32[]{:S(2)}) copy-start(bf16[640]{0:T(1024)(128)(2,1)} %param.21) | copy-start | bytes 3844
  1.8 12.1 %collective-permute-start = (bf16[1,640,128]{2,1,0:T(8,128)(2,1)S(1)}, bf16[1,640,128]{2,1,0:T(8,128)(2,1)S(1)}, u32[]{:S(2)}, u32[]{:S(2)}) collective-permute-start(bf16[1,640,128]{2,1,0:T(8,128)(2,1)S(1)} %get-tuple-element.45), channel_id=1, source_target_pairs={{0,2},{2,4},{4,6},{6,8},{8,10},{10,12},{12,14},{1,3},{3,5},{5,7},{... | collective-permute-start | bytes 491528 | tf_op jit(solution)/shard_map/ppermute | solution.py:250
  6.7 7.6 %collective-permute-start.1 = (bf16[1,640,128]{2,1,0:T(8,128)(2,1)S(1)}, bf16[1,640,128]{2,1,0:T(8,128)(2,1)S(1)}, u32[]{:S(2)}, u32[]{:S(2)}) collective-permute-start(bf16[1,640,128]{2,1,0:T(8,128)(2,1)S(1)} %get-tuple-element.46), channel_id=1, source_target_pairs={{2,0},{4,2},{6,4},{8,6},{10,8},{12,10},{14,12},{3,1},{5,3},{7,5},{... | collective-permute-start | bytes 491528 | tf_op jit(solution)/shard_map/ppermute | solution.py:251
  10.2 78.0 %collective-permute-start.13 = (bf16[512,512]{1,0:T(8,128)(2,1)}, bf16[512,512]{1,0:T(8,128)(2,1)S(1)}, u32[]{:S(2)}, u32[]{:S(2)}) collective-permute-start(bf16[512,512]{1,0:T(8,128)(2,1)} %bitcast.23), channel_id=1, source_target_pairs={{4,0},{8,4},{12,8},{14,12},{10,14},{6,10},{2,6},{0,2},{5,1},{9,5},... | collective-permute-start | bytes 1572872 | tf_op jit(solution)/shard_map/ppermute | solution.py:265
  12.9 92.8 %collective-permute-start.17 = (bf16[512,512]{1,0:T(8,128)(2,1)}, bf16[512,512]{1,0:T(8,128)(2,1)S(1)}, u32[]{:S(2)}, u32[]{:S(2)}) collective-permute-start(bf16[512,512]{1,0:T(8,128)(2,1)} %bitcast.23), channel_id=1, source_target_pairs={{0,4},{4,8},{8,12},{12,14},{14,10},{10,6},{6,2},{2,0},{1,5},{5,9},... | collective-permute-start | bytes 1572872 | tf_op jit(solution)/shard_map/ppermute | solution.py:269
  15.3 57.1 %collective-permute-start.4 = (bf16[6,640,128]{2,1,0:T(8,128)(2,1)}, bf16[6,640,128]{2,1,0:T(8,128)(2,1)}, u32[]{:S(2)}, u32[]{:S(2)}) collective-permute-start(bf16[6,640,128]{2,1,0:T(8,128)(2,1)} %pad_maximum_fusion.4), channel_id=1, source_target_pairs={{1,17},{16,0},{3,19},{18,2},{5,21},{20,4},{7,23},{22,6},{9,25},{24... | collective-permute-start | bytes 2949128 | tf_op jit(solution)/shard_map/ppermute | solution.py:53
  16.6 57.1 %collective-permute-start.3 = (bf16[4,640]{1,0:T(4,128)(2,1)S(1)}, bf16[4,640]{1,0:T(4,128)(2,1)S(1)}, u32[]{:S(2)}, u32[]{:S(2)}) collective-permute-start(bf16[4,640]{1,0:T(4,128)(2,1)S(1)} %pad_maximum_fusion.6), channel_id=1, source_target_pairs={{0,1},{1,0},{2,3},{3,2},{4,5},{5,4},{6,7},{7,6},{8,9},{9,8},{10,11... | collective-permute-start | bytes 15368 | tf_op jit(solution)/shard_map/ppermute | solution.py:24
  18.2 70.7 %collective-permute-start.9 = (bf16[512,512]{1,0:T(8,128)(2,1)}, bf16[512,512]{1,0:T(8,128)(2,1)S(1)}, u32[]{:S(2)}, u32[]{:S(2)}) collective-permute-start(bf16[512,512]{1,0:T(8,128)(2,1)} %bitcast.22), channel_id=1, source_target_pairs={{0,4},{4,8},{8,12},{12,14},{14,10},{10,6},{6,2},{2,0},{1,5},{5,9},... | collective-permute-start | bytes 1572872 | tf_op jit(solution)/shard_map/ppermute | solution.py:264
  72.4 4.0 %collective-permute-start.5 = (bf16[6,640,128]{2,1,0:T(8,128)(2,1)}, bf16[6,640,128]{2,1,0:T(8,128)(2,1)S(1)}, u32[]{:S(2)}, u32[]{:S(2)}) collective-permute-start(bf16[6,640,128]{2,1,0:T(8,128)(2,1)} %collective-permute-done.4), channel_id=1, source_target_pairs={{0,1},{17,16},{2,3},{19,18},{4,5},{21,20},{6,7},{23,22},{8,9},{25,... | collective-permute-start | bytes 2949128 | tf_op jit(solution)/shard_map/ppermute | solution.py:56
  73.9 16.4 %collective-permute-start.2 = (bf16[6,640,128]{2,1,0:T(8,128)(2,1)}, bf16[6,640,128]{2,1,0:T(8,128)(2,1)}, u32[]{:S(2)}, u32[]{:S(2)}) collective-permute-start(bf16[6,640,128]{2,1,0:T(8,128)(2,1)} %pad_maximum_fusion.4), channel_id=1, source_target_pairs={{0,1},{17,16},{2,3},{19,18},{4,5},{21,20},{6,7},{23,22},{8,9},{25,... | collective-permute-start | bytes 2949128 | tf_op jit(solution)/shard_map/ppermute | solution.py:55
  77.7 10.4 %copy-start.10 = (bf16[640]{0:T(1024)(128)(2,1)S(1)}, bf16[640]{0:T(1024)(128)(2,1)}, u32[]{:S(2)}) copy-start(bf16[640]{0:T(1024)(128)(2,1)} %param.19) | copy-start | bytes 3844
  86.3 17.1 %collective-permute-start.6 = (bf16[4,640,128]{2,1,0:T(8,128)(2,1)S(1)}, bf16[4,640,128]{2,1,0:T(8,128)(2,1)}, u32[]{:S(2)}, u32[]{:S(2)}) collective-permute-start(bf16[4,640,128]{2,1,0:T(8,128)(2,1)S(1)} %norm_conv.3), channel_id=1, source_target_pairs={{0,16},{16,0},{1,17},{17,1},{2,18},{18,2},{3,19},{19,3},{4,20},{20... | collective-permute-start | bytes 1966088 | tf_op jit(solution)/shard_map/ppermute | solution.py:24
  88.3 17.4 %collective-permute-start.20 = (bf16[512,512]{1,0:T(8,128)(2,1)}, bf16[512,512]{1,0:T(8,128)(2,1)S(1)}, u32[]{:S(2)}, u32[]{:S(2)}) collective-permute-start(bf16[512,512]{1,0:T(8,128)(2,1)} %bitcast.22), channel_id=1, source_target_pairs={{4,0},{8,4},{12,8},{14,12},{10,14},{6,10},{2,6},{0,2},{5,1},{9,5},... | collective-permute-start | bytes 1572872 | tf_op jit(solution)/shard_map/ppermute | solution.py:270
  88.9 18.8 %collective-permute-start.10 = (bf16[512,512]{1,0:T(8,128)(2,1)S(1)}, bf16[512,512]{1,0:T(8,128)(2,1)}, u32[]{:S(2)}, u32[]{:S(2)}) collective-permute-start(bf16[512,512]{1,0:T(8,128)(2,1)S(1)} %collective-permute-done.9.refs_3_), channel_id=1, source_target_pairs={{0,4},{4,8},{8,12},{12,14},{14,10},{10,6},{6,2},{2,0},{1,5},{5,9},... | collective-permute-start | bytes 1572872 | tf_op jit(solution)/shard_map/ppermute | solution.py:264
  90.4 24.0 %collective-permute-start.14 = (bf16[512,512]{1,0:T(8,128)(2,1)S(1)}, bf16[512,512]{1,0:T(8,128)(2,1)}, u32[]{:S(2)}, u32[]{:S(2)}) collective-permute-start(bf16[512,512]{1,0:T(8,128)(2,1)S(1)} %collective-permute-done.13.refs_6_), channel_id=1, source_target_pairs={{4,0},{8,4},{12,8},{14,12},{10,14},{6,10},{2,6},{0,2},{5,1},{9,5},... | collective-permute-start | bytes 1572872 | tf_op jit(solution)/shard_map/ppermute | solution.py:265
  92.2 11.2 %copy-start.3 = (bf16[1,4,640,128]{3,2,1,0:T(8,128)(2,1)S(1)}, bf16[1,4,640,128]{3,2,1,0:T(8,128)(2,1)}, u32[]{:S(2)}) copy-start(bf16[1,4,640,128]{3,2,1,0:T(8,128)(2,1)} %param.12) | copy-start | bytes 1966084
  104.8 34.0 %copy-start.4 = (bf16[4,640,128]{2,1,0:T(8,128)(2,1)}, bf16[4,640,128]{2,1,0:T(8,128)(2,1)S(1)}, u32[]{:S(2)}) copy-start(bf16[4,640,128]{2,1,0:T(8,128)(2,1)S(1)} %add_convert_fusion) | copy-start | bytes 1966084
  104.8 32.0 %collective-permute-start.8 = (bf16[4,640,128]{2,1,0:T(8,128)(2,1)S(1)}, bf16[4,640,128]{2,1,0:T(8,128)(2,1)}, u32[]{:S(2)}, u32[]{:S(2)}) collective-permute-start(bf16[4,640,128]{2,1,0:T(8,128)(2,1)S(1)} %add_convert_fusion), channel_id=1, source_target_pairs={{0,1},{1,0},{2,3},{3,2},{4,5},{5,4},{6,7},{7,6},{8,9},{9,8},{10,11... | collective-permute-start | bytes 1966088 | tf_op jit(solution)/shard_map/ppermute | solution.py:24
  105.6 24.9 %collective-permute-start.18 = (bf16[512,512]{1,0:T(8,128)(2,1)S(1)}, bf16[512,512]{1,0:T(8,128)(2,1)}, u32[]{:S(2)}, u32[]{:S(2)}) collective-permute-start(bf16[512,512]{1,0:T(8,128)(2,1)S(1)} %collective-permute-done.17.refs_4_), channel_id=1, source_target_pairs={{0,4},{4,8},{8,12},{12,14},{14,10},{10,6},{6,2},{2,0},{1,5},{5,9},... | collective-permute-start | bytes 1572872 | tf_op jit(solution)/shard_map/ppermute | solution.py:269
  105.7 25.0 %collective-permute-start.21 = (bf16[512,512]{1,0:T(8,128)(2,1)S(1)}, bf16[512,512]{1,0:T(8,128)(2,1)}, u32[]{:S(2)}, u32[]{:S(2)}) collective-permute-start(bf16[512,512]{1,0:T(8,128)(2,1)S(1)} %collective-permute-done.20.refs_5_), channel_id=1, source_target_pairs={{4,0},{8,4},{12,8},{14,12},{10,14},{6,10},{2,6},{0,2},{5,1},{9,5},... | collective-permute-start | bytes 1572872 | tf_op jit(solution)/shard_map/ppermute | solution.py:270
  107.7 24.6 %collective-permute-start.11 = (bf16[512,512]{1,0:T(8,128)(2,1)}, bf16[512,512]{1,0:T(8,128)(2,1)}, u32[]{:S(2)}, u32[]{:S(2)}) collective-permute-start(bf16[512,512]{1,0:T(8,128)(2,1)} %collective-permute-done.10.refs_1_), channel_id=1, source_target_pairs={{0,4},{4,8},{8,12},{12,14},{14,10},{10,6},{6,2},{2,0},{1,5},{5,9},... | collective-permute-start | bytes 1572872 | tf_op jit(solution)/shard_map/ppermute | solution.py:264
  114.3 22.5 %collective-permute-start.15 = (bf16[512,512]{1,0:T(8,128)(2,1)}, bf16[512,512]{1,0:T(8,128)(2,1)}, u32[]{:S(2)}, u32[]{:S(2)}) collective-permute-start(bf16[512,512]{1,0:T(8,128)(2,1)} %collective-permute-done.14.refs_4_), channel_id=1, source_target_pairs={{4,0},{8,4},{12,8},{14,12},{10,14},{6,10},{2,6},{0,2},{5,1},{9,5},... | collective-permute-start | bytes 1572872 | tf_op jit(solution)/shard_map/ppermute | solution.py:265
  130.6 69.2 %collective-permute-start.7 = (bf16[512,640]{1,0:T(8,128)(2,1)}, bf16[512,640]{1,0:T(8,128)(2,1)}, u32[]{:S(2)}, u32[]{:S(2)}) collective-permute-start(bf16[512,640]{1,0:T(8,128)(2,1)} %bitcast.95), channel_id=1, source_target_pairs={{0,1},{1,0},{2,3},{3,2},{4,5},{5,4},{6,7},{7,6},{8,9},{9,8},{10,11... | collective-permute-start | bytes 1966088 | tf_op jit(solution)/shard_map/ppermute | solution.py:24
  130.7 48.3 %collective-permute-start.19 = (bf16[512,512]{1,0:T(8,128)(2,1)}, bf16[512,512]{1,0:T(8,128)(2,1)}, u32[]{:S(2)}, u32[]{:S(2)}) collective-permute-start(bf16[512,512]{1,0:T(8,128)(2,1)} %collective-permute-done.18.refs_2_), channel_id=1, source_target_pairs={{0,4},{4,8},{8,12},{12,14},{14,10},{10,6},{6,2},{2,0},{1,5},{5,9},... | collective-permute-start | bytes 1572872 | tf_op jit(solution)/shard_map/ppermute | solution.py:269
  132.3 46.7 %collective-permute-start.22 = (bf16[512,512]{1,0:T(8,128)(2,1)}, bf16[512,512]{1,0:T(8,128)(2,1)}, u32[]{:S(2)}, u32[]{:S(2)}) collective-permute-start(bf16[512,512]{1,0:T(8,128)(2,1)} %collective-permute-done.21.refs_3_), channel_id=1, source_target_pairs={{4,0},{8,4},{12,8},{14,12},{10,14},{6,10},{2,6},{0,2},{5,1},{9,5},... | collective-permute-start | bytes 1572872 | tf_op jit(solution)/shard_map/ppermute | solution.py:270
  136.8 55.2 %collective-permute-start.12 = (bf16[512,512]{1,0:T(8,128)(2,1)}, bf16[512,512]{1,0:T(8,128)(2,1)}, u32[]{:S(2)}, u32[]{:S(2)}) collective-permute-start(bf16[512,512]{1,0:T(8,128)(2,1)} %collective-permute-done.11.refs_1_), channel_id=1, source_target_pairs={{0,4},{4,8},{8,12},{12,14},{14,10},{10,6},{6,2},{2,0},{1,5},{5,9},... | collective-permute-start | bytes 1572872 | tf_op jit(solution)/shard_map/ppermute | solution.py:264
  136.8 55.2 %collective-permute-start.16 = (bf16[512,512]{1,0:T(8,128)(2,1)}, bf16[512,512]{1,0:T(8,128)(2,1)}, u32[]{:S(2)}, u32[]{:S(2)}) collective-permute-start(bf16[512,512]{1,0:T(8,128)(2,1)} %collective-permute-done.15.refs_4_), channel_id=1, source_target_pairs={{4,0},{8,4},{12,8},{14,12},{10,14},{6,10},{2,6},{0,2},{5,1},{9,5},... | collective-permute-start | bytes 1572872 | tf_op jit(solution)/shard_map/ppermute | solution.py:265
  192.0 7.8 %copy-start.6 = (bf16[512,1,640]{2,0,1:T(8,128)(2,1)S(1)}, bf16[512,1,640]{2,0,1:T(8,128)(2,1)}, u32[]{:S(2)}) copy-start(bf16[512,1,640]{2,0,1:T(8,128)(2,1)} %copy.44) | copy-start | bytes 1966084
  199.5 12.2 %collective-permute-start.23 = (bf16[512,512]{1,0:T(8,128)(2,1)S(1)}, bf16[512,512]{1,0:T(8,128)(2,1)}, u32[]{:S(2)}, u32[]{:S(2)}) collective-permute-start(bf16[512,512]{1,0:T(8,128)(2,1)S(1)} %attend.7), channel_id=1, source_target_pairs={{0,1},{1,0},{2,3},{3,2},{4,5},{5,4},{6,7},{7,6},{8,9},{9,8},{10,11... | collective-permute-start | bytes 1572872 | tf_op jit(solution)/shard_map/ppermute | solution.py:24
  205.7 3.8 %copy-start.5 = (bf16[4,640,128]{2,1,0:T(8,128)(2,1)S(1)}, bf16[4,640,128]{2,1,0:T(8,128)(2,1)}, u32[]{:S(2)}) copy-start(bf16[4,640,128]{2,1,0:T(8,128)(2,1)} %copy-done.4) | copy-start | bytes 1966084
  213.0 1.0 copy-start.8
  213.9 10.0 %copy-start.7 = (bf16[1024,320,1]{0,2,1:T(2,128)(2,1)S(1)}, bf16[1024,320,1]{0,2,1:T(2,128)(2,1)}, u32[]{:S(2)}) copy-start(bf16[1024,320,1]{0,2,1:T(2,128)(2,1)} %get-tuple-element.31) | copy-start | bytes 1966084
  213.9 10.0 %copy-start.9 = (bf16[4,320,1,128]{3,2,1,0:T(2,128)(2,1)S(1)}, bf16[4,320,1,128]{3,2,1,0:T(2,128)(2,1)}, u32[]{:S(2)}) copy-start(bf16[4,320,1,128]{3,2,1,0:T(2,128)(2,1)} %get-tuple-element.43) | copy-start | bytes 983044
  213.9 10.0 %collective-permute-start.24 = (bf16[4,320,128]{2,1,0:T(8,128)(2,1)S(1)}, bf16[4,320,128]{2,1,0:T(8,128)(2,1)}, u32[]{:S(2)}, u32[]{:S(2)}) collective-permute-start(bf16[4,320,128]{2,1,0:T(8,128)(2,1)S(1)} %fusion.10), channel_id=1, source_target_pairs={{0,16},{16,0},{1,17},{17,1},{2,18},{18,2},{3,19},{19,3},{4,20},{20... | collective-permute-start | bytes 983048 | tf_op jit(solution)/shard_map/ppermute | solution.py:24
  223.9 2.7 %copy-start.1 = (bf16[320,640]{1,0:T(8,128)(2,1)S(1)}, bf16[320,640]{1,0:T(8,128)(2,1)}, u32[]{:S(2)}) copy-start(bf16[320,640]{1,0:T(8,128)(2,1)} %param.15) | copy-start | bytes 1228804

commit v2 on v1

v2 whole, which is shorter than its diff:
```python
import functools
import math

import jax
import jax.numpy as jnp
from jax import lax
from jax.experimental import pallas as pl
from jax.experimental.pallas import tpu as pltpu
from jax.sharding import PartitionSpec as P

D = 1280
HD = 64
GROUPS = 32
TEMB = 320
LANES = 128

epsilon = 1e-05
guidance = 5.0
SCORE_SCALE = 1.0 / math.sqrt(HD)
VMEM_LIMIT = 50 * 1024 * 1024


def swapped(array, axis):
    return lax.ppermute(array, axis, [(i, i ^ 1) for i in range(lax.axis_size(axis))])


def ring_pairs(count):
    order = list(range(0, count, 2)) + list(range(count - 1, 0, -2))
    forward = [(order[i], order[(i + 1) % count]) for i in range(count)]
    backward = [(j, i) for i, j in forward]
    return forward, backward


def gather_tp(array, axis):
    if lax.axis_size("tp") != 2:
        return lax.all_gather(array, "tp", axis=axis, tiled=True)
    other = swapped(array, "tp")
    first = lax.axis_index("tp") == 0
    return jnp.concatenate(
        [jnp.where(first, array, other), jnp.where(first, other, array)], axis=axis
    )


def summed(array, axes):
    for axis in axes:
        count = lax.axis_size(axis)
        if count & (count - 1):
            array = lax.psum(array, axis)
            continue
        distance = 1
        while distance < count:
            pairs = [(i, i ^ distance) for i in range(count)]
            array = array + lax.ppermute(array, axis, pairs)
            distance *= 2
    return array


def halves_of_inputs(own):
    cfg = lax.axis_index("cfg")
    if lax.axis_size("tp") != 2:
        full = lax.all_gather(own, "tp", axis=1, tiled=True)
        half = full.shape[1] // 2
        mine = lax.dynamic_slice_in_dim(full, cfg * half, half, 1)
        sent = lax.dynamic_slice_in_dim(full, (1 - cfg) * half, half, 1)
        return [mine], [swapped(sent, "cfg")]
    across = lax.ppermute(own, ("cfg", "tp"), [(1, 3), (2, 0)])
    pairs = [(0, 1), (3, 2)]
    own_side = lax.ppermute(own, ("cfg", "tp"), pairs)
    across_side = lax.ppermute(across, ("cfg", "tp"), pairs)
    return [own, own_side], [across, across_side]


def conv_kernel(choices, flags_ref, *refs):
    x_refs = refs[:choices]
    coef_ref, w_ref, out_ref, act_ref, acc_ref = refs[choices:]
    rows = out_ref.shape[0]
    step = pl.program_id(0)

    @pl.when(step == 0)
    def _():
        mean = coef_ref[:, 0:1]
        scale = coef_ref[:, 1:2]
        shift = coef_ref[:, 2:3]
        for r in range(rows + 2):
            x = x_refs[0][r]
            if choices == 2:
                x = jnp.where(flags_ref[2] == 1, x, x_refs[1][r])
            x = x.astype(jnp.float32)
            z = (x - mean) * scale + shift
            z = z * jax.nn.sigmoid(z)
            if r == 0:
                z = jnp.where(flags_ref[0] == 1, z, 0.0)
            if r == rows + 1:
                z = jnp.where(flags_ref[1] == 1, z, 0.0)
            act_ref[:, r * LANES : (r + 1) * LANES] = z.astype(jnp.bfloat16)

    def product(row_tap):
        return jnp.dot(
            w_ref[row_tap, 0],
            act_ref[:, row_tap * LANES : (row_tap + rows) * LANES],
            preferred_element_type=jnp.float32,
        )

    y = product(0) + product(1) + product(2)
    lane = lax.broadcasted_iota(jnp.int32, (y.shape[0], LANES), 1)

    @pl.when(step == 0)
    def _():
        for r in range(rows):
            part = pltpu.roll(y[:, r * LANES : (r + 1) * LANES], 1, axis=1)
            acc_ref[r] = jnp.where(lane == 0, 0.0, part)

    @pl.when(step == 1)
    def _():
        for r in range(rows):
            acc_ref[r] += y[:, r * LANES : (r + 1) * LANES]

    @pl.when(step == 2)
    def _():
        for r in range(rows):
            part = pltpu.roll(y[:, r * LANES : (r + 1) * LANES], LANES - 1, axis=1)
            total = acc_ref[r] + jnp.where(lane == LANES - 1, 0.0, part)
            out_ref[r] = total.astype(out_ref.dtype)


def conv_call(flags, xs, coef, conv_w, out_dtype):
    x = xs[0]
    rows = x.shape[0] - 2
    outs, ins = conv_w.shape[2:]
    return pl.pallas_call(
        functools.partial(conv_kernel, len(xs)),
        grid=(3,),
        in_specs=[
            pl.BlockSpec(memory_space=pltpu.SMEM),
            *[pl.BlockSpec(x.shape, lambda i: (0, 0, 0))] * len(xs),
            pl.BlockSpec(coef.shape, lambda i: (0, 0)),
            pl.BlockSpec((3, 1, outs, ins), lambda i: (0, i, 0, 0)),
        ],
        out_specs=pl.BlockSpec((rows, outs, LANES), lambda i: (0, 0, 0)),
        out_shape=jax.ShapeDtypeStruct((rows, outs, LANES), out_dtype),
        scratch_shapes=[
            pltpu.VMEM((ins, (rows + 2) * LANES), jnp.bfloat16),
            pltpu.VMEM((rows, outs, LANES), jnp.float32),
        ],
        compiler_params=pltpu.CompilerParams(vmem_limit_bytes=VMEM_LIMIT),
        cost_estimate=pl.CostEstimate(
            flops=2 * 9 * outs * ins * rows * LANES,
            bytes_accessed=2 * 9 * outs * ins,
            transcendentals=ins * rows * LANES,
        ),
        name="norm_conv",
    )(flags, *xs, coef, conv_w)


def project_kernel(parts, order_ref, *refs):
    part_refs = refs[:parts]
    own_ref, gain_ref, bias_ref, w_ref, q_ref, kv_ref, split_ref, normed_ref = refs[parts:]
    rows, channels, _ = part_refs[0].shape
    total = parts * channels
    step = pl.program_id(0)

    @pl.when(step == 0)
    def _():
        for r in range(rows):
            x = [ref[r].astype(jnp.float32) for ref in part_refs]
            mean = sum(jnp.sum(a, axis=0, keepdims=True) for a in x) / total
            var = sum(jnp.sum(a * a, axis=0, keepdims=True) for a in x) / total - mean * mean
            inverse = lax.rsqrt(var + epsilon)
            for j in range(parts):
                at = pl.ds(pl.multiple_of(order_ref[j] * channels, LANES), channels)
                z = (x[j] - mean) * inverse * gain_ref[at, :] + bias_ref[at, :]
                normed_ref[r * LANES : (r + 1) * LANES, at] = z.astype(jnp.bfloat16).T
        own_channels = own_ref.shape[1]
        half = own_channels // 2
        shape = (own_channels, own_channels)
        to = lax.broadcasted_iota(jnp.int32, shape, 0)
        source = lax.broadcasted_iota(jnp.int32, shape, 1)
        wanted = jnp.where(to < half, 2 * to, 2 * (to - half) + 1)
        chosen = (source == wanted).astype(jnp.bfloat16)
        for r in range(rows):
            y = jnp.dot(chosen, own_ref[r], preferred_element_type=jnp.float32)
            y = y.astype(jnp.bfloat16)
            split_ref[0, r] = y[:half]
            split_ref[1, r] = y[half:]

    y = jnp.dot(normed_ref[...], w_ref[0], preferred_element_type=jnp.float32)
    y = y.astype(jnp.bfloat16)

    @pl.when(step == 0)
    def _():
        q_ref[...] = y * SCORE_SCALE

    @pl.when(step > 0)
    def _():
        kv_ref[0] = y


def project_call(order, parts, own, gain, bias, w):
    rows, channels, _ = parts[0].shape
    positions = rows * LANES
    _, depth, features = w.shape
    half = own.shape[1] // 2
    whole = lambda shape: pl.BlockSpec(shape, lambda i: (0,) * len(shape))
    return pl.pallas_call(
        functools.partial(project_kernel, len(parts)),
        grid=(3,),
        in_specs=[
            pl.BlockSpec(memory_space=pltpu.SMEM),
            *[whole(part.shape) for part in parts],
            whole(own.shape),
            whole(gain.shape),
            whole(bias.shape),
            pl.BlockSpec((1, depth, features), lambda i: (i, 0, 0)),
        ],
        out_specs=(
            whole((positions, features)),
            pl.BlockSpec((1, positions, features), lambda i: (jnp.maximum(i - 1, 0), 0, 0)),
            whole((2, rows, half, LANES)),
        ),
        out_shape=(
            jax.ShapeDtypeStruct((positions, features), jnp.bfloat16),
            jax.ShapeDtypeStruct((2, positions, features), jnp.bfloat16),
            jax.ShapeDtypeStruct((2, rows, half, LANES), jnp.bfloat16),
        ),
        scratch_shapes=[pltpu.VMEM((positions, depth), jnp.bfloat16)],
        compiler_params=pltpu.CompilerParams(vmem_limit_bytes=VMEM_LIMIT),
        cost_estimate=pl.CostEstimate(
            flops=6 * positions * depth * features,
            bytes_accessed=6 * depth * features,
            transcendentals=0,
        ),
        name="norm_project",
    )(order, *parts, own, gain, bias, w)


def attention_kernel(blocks, carried, final, *refs):
    q_ref = refs[0]
    kv_refs = refs[1 : 1 + 2 * blocks]
    at = 1 + 2 * blocks
    if carried:
        m_in, acc_in = refs[at : at + 2]
        at += 2
    if final:
        w_ref = refs[at]
        at += 1
        out_refs = refs[at:-1]
        joined_ref = refs[-1]
    else:
        m_out, acc_out = refs[at:]
    positions = q_ref.shape[0]
    tile = min(256, positions)
    starts = range(0, positions, tile)
    lanes = lambda array, low: (lax.broadcasted_iota(jnp.int32, array.shape, 1) < HD) == low

    def scores(item):
        start, head, block = item
        q = q_ref[start : start + tile, :]
        q = jnp.where(lanes(q, head == 0), q, jnp.zeros_like(q))
        return lax.dot_general(
            q,
            kv_refs[2 * block][0],
            (((1,), (1,)), ((), ())),
            preferred_element_type=jnp.float32,
        )

    items = [(start, head, block) for start in starts for block in range(blocks) for head in (0, 1)]
    state = {}
    upcoming = scores(items[0])
    for number, item in enumerate(items):
        s = upcoming
        if number + 1 < len(items):
            upcoming = scores(items[number + 1])
        start, head, block = item
        rows = slice(start, start + tile)
        if block == 0 and carried:
            peak, acc = m_in[0, head, rows, :], acc_in[0, head, rows, :]
        elif block == 0:
            peak = acc = None
        else:
            peak, acc = state[start, head]
        v = kv_refs[2 * block + 1][0]
        v = jnp.where(lanes(v, head == 0), v, jnp.ones_like(v))
        top = jnp.broadcast_to(jnp.max(s, axis=1, keepdims=True), (tile, LANES))
        new_peak = top if peak is None else jnp.maximum(peak, top)
        wide = jnp.concatenate([new_peak] * (s.shape[1] // LANES), axis=1)
        p = jnp.exp(s - wide).astype(jnp.bfloat16)
        term = jnp.dot(p, v, preferred_element_type=jnp.float32)
        acc = term if acc is None else acc * jnp.exp(peak - new_peak) + term
        state[start, head] = new_peak, acc
        if block < blocks - 1:
            continue
        if not final:
            m_out[0, head, rows, :] = new_peak
            acc_out[0, head, rows, :] = acc
        elif head == 1:
            parts = [state[start, h][1] for h in (0, 1)]
            parts = [a / pltpu.roll(a, HD, axis=1) for a in parts]
            pair = jnp.where(lanes(acc, True), parts[0], parts[1]).astype(jnp.bfloat16)
            joined_ref[pl.program_id(0), rows, :] = pair

    if final:
        tiles, _, _ = joined_ref.shape

        @pl.when(pl.program_id(0) == tiles - 1)
        def _():
            joined = jnp.concatenate([joined_ref[i] for i in range(tiles)], axis=1)
            for j in range(w_ref.shape[0]):
                y = lax.dot_general(
                    w_ref[j],
                    joined,
                    (((1,), (1,)), ((), ())),
                    preferred_element_type=jnp.float32,
                )
                out = out_refs[j] if len(out_refs) > 1 else out_refs[0].at[j]
                half = w_ref.shape[1] // 2
                for parity in range(2):
                    for r in range(positions // LANES):
                        out[parity, r] = y[
                            parity * half : (parity + 1) * half, r * LANES : (r + 1) * LANES
                        ].astype(out.dtype)


def attention_call(q, pairs, state, w=None, own_apart=False):
    positions, features = q.shape
    tiles = features // LANES
    final = w is not None
    carry = pl.BlockSpec((1, 2, positions, LANES), lambda i: (i, 0, 0, 0))
    carry_shape = jax.ShapeDtypeStruct((tiles, 2, positions, LANES), jnp.float32)
    operands = [q]
    specs = [pl.BlockSpec((positions, LANES), lambda i: (0, i))]
    for pair in pairs:
        for array, place in pair:
            operands.append(array)
            specs.append(
                pl.BlockSpec((1, positions, LANES), functools.partial(lambda p, i: (p, 0, i), place))
            )
    if state is not None:
        operands += list(state)
        specs += [carry, carry]
    scratch = []
    if final:
        operands.append(w)
        specs.append(pl.BlockSpec(w.shape, lambda i: (0, 0, 0)))
        shape = (2, positions // LANES, w.shape[1] // 2, LANES)
        if own_apart:
            out_shape = (
                jax.ShapeDtypeStruct(shape, jnp.bfloat16),
                jax.ShapeDtypeStruct(shape, jnp.float32),
            )
        else:
            out_shape = (jax.ShapeDtypeStruct((w.shape[0],) + shape, jnp.bfloat16),)
        out_specs = tuple(
            pl.BlockSpec(o.shape, functools.partial(lambda n, i: (0,) * n, len(o.shape)))
            for o in out_shape
        )
        scratch = [pltpu.VMEM((tiles, positions, LANES), jnp.bfloat16)]
    else:
        out_shape = (carry_shape, carry_shape)
        out_specs = (carry, carry)
    keys = positions * len(pairs)
    return pl.pallas_call(
        functools.partial(attention_kernel, len(pairs), state is not None, final),
        grid=(tiles,),
        in_specs=specs,
        out_specs=out_specs,
        out_shape=out_shape,
        scratch_shapes=scratch,
        compiler_params=pltpu.CompilerParams(vmem_limit_bytes=VMEM_LIMIT),
        cost_estimate=pl.CostEstimate(
            flops=16 * positions * keys * features,
            bytes_accessed=4 * keys * features,
            transcendentals=positions * keys * features // HD,
        ),
        name="attend",
    )(*operands)


def per_device(
    latent,
    stale_kv,
    timestep,
    w_time,
    gn_gain,
    gn_bias,
    conv_w,
    conv_b,
    ln_gain,
    ln_bias,
    w_qkv,
    w_out,
):
    latent_rows = latent[0]
    rows_count = lax.axis_size("rows")
    tp_count = lax.axis_size("tp")
    span_rows, local_channels, grid_width = latent_rows.shape
    positions = span_rows * grid_width
    group_width = D // GROUPS
    local_groups = local_channels // group_width
    my_block = lax.axis_index("rows")
    cfg = lax.axis_index("cfg")
    tp = lax.axis_index("tp")

    up_pairs = [(i, i + 1) for i in range(rows_count - 1)]
    down_pairs = [(i + 1, i) for i in range(rows_count - 1)]
    before = lax.ppermute(latent_rows[span_rows - 1 :], "rows", up_pairs)
    after = lax.ppermute(latent_rows[:1], "rows", down_pairs)
    rimmed = jnp.concatenate([before, latent_rows, after], axis=0)
    x_mine, x_other = halves_of_inputs(rimmed)

    forward, backward = ring_pairs(rows_count)
    pair = stale_kv[0].reshape(2, positions, -1)
    ahead = behind = pair
    hops = []
    for hop in range(1, rows_count // 2):
        ahead = lax.ppermute(ahead, "rows", forward)
        behind = lax.ppermute(behind, "rows", backward)
        hops.append([((ahead, 0), (ahead, 1)), ((behind, 0), (behind, 1))])
    far_k = lax.ppermute(ahead[:1], "rows", forward)
    far_v = lax.ppermute(behind[1:], "rows", backward)
    hops.append([((far_k, 0), (far_v, 0))])

    latent32 = latent_rows.astype(jnp.float32)
    values32 = latent32.reshape(span_rows, local_groups, group_width, grid_width)
    sums = jnp.stack(
        [jnp.sum(values32, axis=(0, 2, 3)), jnp.sum(values32 * values32, axis=(0, 2, 3))]
    )
    table = jnp.zeros((2, 2, GROUPS), jnp.float32)
    table = lax.dynamic_update_slice(table, sums[None], (cfg, 0, tp * local_groups))
    table = summed(table.reshape(1, -1), ("tp", "cfg", "rows")).reshape(2, 2, GROUPS)
    vectors = gather_tp(jnp.stack([gn_gain, gn_bias, ln_gain, ln_bias]), 1).astype(jnp.float32)

    amount = span_rows * rows_count * grid_width * group_width
    table = lax.dynamic_slice_in_dim(table, cfg * (GROUPS // 2), GROUPS // 2, 2)
    group_mean = table[:, 0] / amount
    variance = table[:, 1] / amount - group_mean * group_mean
    inverse = lax.rsqrt(variance + epsilon)
    half = D // 2
    gain_half = lax.dynamic_slice_in_dim(vectors[0], cfg * half, half)
    bias_half = lax.dynamic_slice_in_dim(vectors[1], cfg * half, half)
    mean_c = jnp.repeat(group_mean, group_width, axis=1)
    scale_c = jnp.repeat(inverse, group_width, axis=1) * gain_half[None]
    coef = jnp.stack(
        [mean_c, scale_c, jnp.broadcast_to(bias_half[None], mean_c.shape)], axis=2
    )
    coef_mine = lax.dynamic_index_in_dim(coef, cfg, 0, keepdims=False)
    coef_other = lax.dynamic_index_in_dim(coef, 1 - cfg, 0, keepdims=False)
    flags = jnp.stack([my_block > 0, my_block < rows_count - 1, tp == cfg]).astype(jnp.int32)

    local_features = w_qkv.shape[2]
    w_project = w_qkv.transpose(1, 0, 2)
    w_back = w_out.T.reshape(tp_count, local_channels // 2, 2, local_features)
    w_back = w_back.transpose(0, 2, 1, 3).reshape(tp_count, local_channels, local_features)
    if tp_count == 2:
        w_back = jnp.where(tp == 0, w_back[::-1], w_back)
    conv_w, coef_other, w_project, w_back = lax.optimization_barrier(
        (conv_w, coef_other, w_project, w_back)
    )

    conv_sent = conv_call(flags, x_other, coef_other, conv_w, jnp.bfloat16)
    conv_received = swapped(conv_sent, "cfg")
    conv_own = conv_call(flags, x_mine, coef_mine, conv_w, jnp.float32)

    half_width = TEMB // 2
    frequencies = jnp.exp(
        -math.log(10000.0) * jnp.arange(half_width, dtype=jnp.float32) / half_width
    )
    angles = timestep.astype(jnp.float32)[0] * frequencies
    embedding = jnp.concatenate([jnp.cos(angles), jnp.sin(angles)])
    time_bias = jnp.dot(
        jax.nn.silu(embedding)[None, :], w_time.astype(jnp.float32), precision=lax.Precision.HIGHEST
    )[0]
    bias = conv_b.astype(jnp.float32) + time_bias
    resid = (
        latent32 + (conv_own + conv_received.astype(jnp.float32) + bias[None, :, None])
    ).astype(jnp.bfloat16)

    if tp_count == 2:
        parts = [resid, swapped(resid, "tp")]
        order = jnp.stack([tp, 1 - tp]).astype(jnp.int32)
    else:
        parts = [lax.all_gather(resid, "tp", axis=1, tiled=True)]
        order = jnp.zeros((1,), jnp.int32)
    queries, fresh, resid_split = project_call(
        order, parts, resid, vectors[2][:, None], vectors[3][:, None], w_project
    )
    fresh_kv = fresh.reshape(1, 2, span_rows, grid_width, local_features)

    state = attention_call(queries, [((fresh, 0), (fresh, 1))] + hops[0] + hops[1], None)
    for group in hops[2:-1]:
        state = attention_call(queries, group, state)
    if tp_count == 2:
        sent, kept_terms = attention_call(queries, hops[-1], state, w_back, True)
        terms = kept_terms + swapped(sent, "tp").astype(jnp.float32)
    else:
        (sent,) = attention_call(queries, hops[-1], state, w_back)
        terms = lax.psum_scatter(sent, "tp", scatter_dimension=0).astype(jnp.float32)

    def branch_out(parity):
        term = lax.dynamic_index_in_dim(terms, parity, 0, keepdims=False)
        base = lax.dynamic_index_in_dim(resid_split, parity, 0, keepdims=False)
        return (base.astype(jnp.float32) + term).astype(jnp.bfloat16)

    other_branch = swapped(branch_out(1 - cfg), "cfg")
    kept = branch_out(cfg)
    is_cond = cfg == 0
    cond_out = jnp.where(is_cond, kept, other_branch).astype(jnp.float32)
    uncond_out = jnp.where(is_cond, other_branch, kept).astype(jnp.float32)
    guided = (uncond_out + guidance * (cond_out - uncond_out)).astype(jnp.bfloat16)
    return (guided[:, :, None, :], fresh_kv)


def solution(mesh):
    in_specs = (
        P("cfg", "rows", "tp", None),
        P("cfg", None, "rows", None, "tp"),
        P(),
        P(None, "tp"),
        P("tp"),
        P("tp"),
        P(None, None, "tp", "cfg"),
        P("tp"),
        P("tp"),
        P("tp"),
        P(None, None, "tp"),
        P("tp", None),
    )
    out_specs = (P("rows", "tp", "cfg", None), P("cfg", None, "rows", None, "tp"))
    return jax.shard_map(
        per_device, mesh=mesh, in_specs=in_specs, out_specs=out_specs, check_vma=False
    )
```

time: 228 us -> 165 us (0.72)
  blocking collectives: 47.5 us -> 0 us
  waiting for transfers between devices: 22.3 us -> 53.3 us
  local copies, waits for them, and re-layouts: 33.6 us -> 12.9 us
  Pallas kernels: 67.2 us -> 57.4 us
  matrix products: 8.3 us -> 0.29 us
  other arithmetic: 12.7 us -> 6.07 us
    psum x1 -> x0, blocking collectives: 47.5 us -> none  [per_device(): table = lax.psum(table, ('cfg', 'rows', 'tp'))]
    pallas_call x4 -> x3, Pallas kernels: 50 us -> 32.1 us  [attention_call(): pl.pallas_call(functools.partial(attention_kernel, len(pairs), state is n...]
    ppermute x14 -> x13, waiting for transfers between devices: 10.7 us -> 27.1 us  [the longest x3 19 us: per_device(): ahead = lax.ppermute(ahead, 'rows', forward)]
    ppermute x1, waiting for transfers between devices: 0.01 us -> 14.1 us  [per_device(): before = lax.ppermute(latent_rows[span_rows - 1:], 'rows', up_pairs)]
    dynamic_slice x6 -> x1, local copies, waits for them, and re-layouts: 12.8 us -> 0.03 us  [per_device(): bias_half = lax.dynamic_slice_in_dim(vectors[1], cfg * half, half)]
    pallas_call x2 -> x3, Pallas kernels: 17.2 us -> 25.4 us  [the longest x2 18 us: conv_call(): pl.pallas_call(functools.partial(conv_kernel, len(xs)), grid=(3,), in_spe...]
    dot_general x3 -> x0, matrix products: 8 us -> none  [the longest x1 4.74 us: per_device(): jnp.einsum('rdw,df->rwf', normed, w_qkv.reshape(D, 3 * local_features), p...]
    unnamed x32 -> x28, local copies, waits for them, and re-layouts: 9.15 us -> 3.21 us
  transfers between devices with their start and end apart: 25 -> 23, of which waited for: 5 -> 11; matrix products, arithmetic and copies ran while one was open for 21% -> 9% of each run, Pallas kernels for 30% -> 31%
where the time goes in v2:
time: 165 us; the launch traced here: 164 us
  Pallas kernels  57.4 us (35%)
  waiting for transfers between devices  53.3 us (32%)
  starting transfers between devices  32.1 us (19%)
  local copies, waits for them, and re-layouts  12.9 us (8%)
  other arithmetic  6.07 us (4%)
  between operations  1.77 us (1%)
    pallas_call x3, Pallas kernels, attention_call(): pl.pallas_call(functools.partial(attention_kernel, len(pairs), state is n...  32.1 us
    ppermute x3, waiting for transfers between devices, per_device(): ahead = lax.ppermute(ahead, 'rows', forward)  19 us
    pallas_call x2, Pallas kernels, conv_call(): pl.pallas_call(functools.partial(conv_kernel, len(xs)), grid=(3,), in_spe...  18 us
    ppermute x1, waiting for transfers between devices, per_device(): before = lax.ppermute(latent_rows[span_rows - 1:], 'rows', up_pairs)  14.1 us
    ppermute x5, waiting for transfers between devices, swapped(): lax.ppermute(array, axis, [(i, i ^ 1) for i in range(lax.axis_size(axis))])  10.3 us
    ppermute x5, waiting for transfers between devices, summed(): array = array + lax.ppermute(array, axis, pairs)  7.94 us
    pallas_call x1, Pallas kernels, project_call(): pl.pallas_call(functools.partial(project_kernel, len(parts)), grid=(3,),...  7.39 us
    ppermute x5, starting transfers between devices, summed(): array = array + lax.ppermute(array, axis, pairs)  5.93 us
  transfers between devices with their start and end apart: 23, of which 11 were waited for; matrix products, arithmetic and copies ran while one was open for 9% of the time, Pallas kernels for 31%

profile of v2, /device:TPU:0, one launch (start us, length us, event | category | flops | bytes accessed | tf_op | source)
XLA Modules:
  0.0 163.9 jit_solution(16902176978176067708)
XLA Ops:
  0.7 3.1 %collective-permute-start.13 = (bf16[2,512,512]{2,1,0:T(8,128)(2,1)}, bf16[2,512,512]{2,1,0:T(8,128)(2,1)S(1)}, u32[]{:S(2)}, u32[]{:S(2)}) collective-permute-start(bf16[2,512,512]{2,1,0:T(8,128)(2,1)} %bitcast.55), channel_id=1, source_target_pairs={{0,4},{4,8},{8,12},{12,14},{14,10},{10,6},{6,2},{2,0},{1,5},{5,9},... | collective-permute-start | bytes 3145736 | tf_op jit(solution)/shard_map/ppermute | solution.py:415
  3.7 1.3 convert_reduce_fusion
  5.1 0.1 reduce_sum.24
  5.2 0.1 reduce_sum.36
  5.3 0.1 reduce_sum.25
  5.4 0.1 reduce_sum.37
  5.5 0.1 dynamic_update_slice.3
  5.7 0.1 reshape.94
  5.8 1.0 slice_bitcast_fusion.1
  6.8 3.9 %collective-permute-start = (bf16[1,640,128]{2,1,0:T(8,128)(2,1)S(1)}, bf16[1,640,128]{2,1,0:T(8,128)(2,1)S(1)}, u32[]{:S(2)}, u32[]{:S(2)}) collective-permute-start(bf16[1,640,128]{2,1,0:T(8,128)(2,1)S(1)} %get-tuple-element.36), channel_id=1, source_target_pairs={{0,2},{2,4},{4,6},{6,8},{8,10},{10,12},{12,14},{1,3},{3,5},{5,7},{... | collective-permute-start | bytes 491528 | tf_op jit(solution)/shard_map/ppermute | solution.py:405
  10.6 1.3 collective-permute-start.1
  12.0 1.5 copy.25
  13.5 3.1 %reshape.97 = bf16[2,320,2,512]{3,2,1,0:T(2,128)(2,1)S(1)} reshape(bf16[1280,512]{1,0:T(8,128)(2,1)} %copy.25) | data formatting | bytes 2621440 | tf_op jit(solution)/shard_map/reshape | solution.py:451
  16.6 0.2 copy.26
  16.8 1.4 reverse_select_fusion.refs_5_
  19.0 0.3 collective-permute-start.8
  19.3 14.1 %collective-permute-done = bf16[1,640,128]{2,1,0:T(8,128)(2,1)S(1)} collective-permute-done((bf16[1,640,128]{2,1,0:T(8,128)(2,1)S(1)}, bf16[1,640,128]{2,1,0:T(8,128)(2,1)S(1)}, u32[]{:S(2)}, u32[]{:S(2)}) %collective-permute-start) | collective-permute-done | bytes 163872 | tf_op jit(solution)/shard_map/ppermute | solution.py:405
  33.4 1.7 %collective-permute-start.4 = (f32[1,128]{1,0:T(1,128)S(1)}, f32[1,128]{1,0:T(1,128)S(1)}, u32[]{:S(2)}, u32[]{:S(2)}) collective-permute-start(f32[1,128]{1,0:T(1,128)S(1)} %add.85), channel_id=1, source_target_pairs={{0,16},{16,0},{1,17},{17,1},{2,18},{18,2},{3,19},{19,3},{4,20},{20... | collective-permute-start | bytes 1544 | tf_op jit(solution)/shard_map/ppermute | solution.py:53
  35.1 0.1 pad_maximum_fusion.refs_0_
  35.2 1.3 collective-permute-start.9
  36.6 0.4 collective-permute-done.4
  37.0 2.5 %collective-permute-start.5 = (f32[1,128]{1,0:T(1,128)S(1)}, f32[1,128]{1,0:T(1,128)S(1)}, u32[]{:S(2)}, u32[]{:S(2)}) collective-permute-start(f32[1,128]{1,0:T(1,128)S(1)} %add.86), channel_id=1, source_target_pairs={{0,2},{2,0},{4,6},{6,4},{8,10},{10,8},{12,14},{14,12},{1,3},{3,1},... | collective-permute-start | bytes 1544 | tf_op jit(solution)/shard_map/ppermute | solution.py:53
  39.4 0.1 divide_multiply_fusion
  39.5 1.4 collective-permute-done.5
  41.0 3.5 %collective-permute-done.6 = f32[1,128]{1,0:T(1,128)S(1)} collective-permute-done((f32[1,128]{1,0:T(1,128)S(1)}, f32[1,128]{1,0:T(1,128)S(1)}, u32[]{:S(2)}, u32[]{:S(2)}) %collective-permute-start.6) | collective-permute-done | bytes 544 | tf_op jit(solution)/shard_map/ppermute | solution.py:53
  44.5 1.8 %collective-permute-start.7 = (f32[1,128]{1,0:T(1,128)S(1)}, f32[1,128]{1,0:T(1,128)S(1)}, u32[]{:S(2)}, u32[]{:S(2)}) collective-permute-start(f32[1,128]{1,0:T(1,128)S(1)} %add.88), channel_id=1, source_target_pairs={{0,8},{2,10},{4,12},{6,14},{8,0},{10,2},{12,4},{14,6},{1,9},{3,11}... | collective-permute-start | bytes 1544 | tf_op jit(solution)/shard_map/ppermute | solution.py:53
  46.3 2.6 %collective-permute-done.7 = f32[1,128]{1,0:T(1,128)S(1)} collective-permute-done((f32[1,128]{1,0:T(1,128)S(1)}, f32[1,128]{1,0:T(1,128)S(1)}, u32[]{:S(2)}, u32[]{:S(2)}) %collective-permute-start.7) | collective-permute-done | bytes 544 | tf_op jit(solution)/shard_map/ppermute | solution.py:53
  49.0 0.1 reshape.95
  49.1 0.1 fusion.7
  49.2 0.1 reshape.96
  49.4 0.1 stack_reshape.3
  49.5 1.8 %collective-permute-done.9.refs_0_ = bf16[6,640,128]{2,1,0:T(8,128)(2,1)} collective-permute-done((bf16[6,640,128]{2,1,0:T(8,128)(2,1)S(1)}, bf16[6,640,128]{2,1,0:T(8,128)(2,1)}, u32[]{:S(2)}, u32[]{:S(2)}) %collective-permute-start.9) | collective-permute-done | bytes 983072 | tf_op jit(solution)/shard_map/ppermute | solution.py:66
  51.3 2.2 %collective-permute-start.10 = (bf16[6,640,128]{2,1,0:T(8,128)(2,1)}, bf16[6,640,128]{2,1,0:T(8,128)(2,1)}, u32[]{:S(2)}, u32[]{:S(2)}) collective-permute-start(bf16[6,640,128]{2,1,0:T(8,128)(2,1)} %collective-permute-done.9.refs_0_), channel_id=1, source_target_pairs={{0,1},{17,16},{2,3},{19,18},{4,5},{21,20},{6,7},{23,22},{8,9},{25,... | collective-permute-start | bytes 2949128 | tf_op jit(solution)/shard_map/ppermute | solution.py:69
  53.6 2.3 %collective-permute-start.2 = (bf16[6,640,128]{2,1,0:T(8,128)(2,1)S(1)}, bf16[6,640,128]{2,1,0:T(8,128)(2,1)}, u32[]{:S(2)}, u32[]{:S(2)}) collective-permute-start(bf16[6,640,128]{2,1,0:T(8,128)(2,1)S(1)} %pad_maximum_fusion.refs_0_), channel_id=1, source_target_pairs={{0,1},{17,16},{2,3},{19,18},{4,5},{21,20},{6,7},{23,22},{8,9},{25,... | collective-permute-start | bytes 2949128 | tf_op jit(solution)/shard_map/ppermute | solution.py:68
  55.9 2.5 %collective-permute-start.18 = (bf16[2,512,512]{2,1,0:T(8,128)(2,1)}, bf16[2,512,512]{2,1,0:T(8,128)(2,1)}, u32[]{:S(2)}, u32[]{:S(2)}) collective-permute-start(bf16[2,512,512]{2,1,0:T(8,128)(2,1)} %collective-permute-done.17.refs_5_.refs_6_), channel_id=1, source_target_pairs={{4,0},{8,4},{12,8},{14,12},{10,14},{6,10},{2,6},{0,2},{5,1},{9,5},... | collective-permute-start | bytes 3145736 | tf_op jit(solution)/shard_map/ppermute | solution.py:416
  58.5 0.2 copy.24
  58.7 9.1 %norm_conv.3 = bf16[4,640,128]{2,1,0:T(8,128)(2,1)S(1)} custom-call(s32[3]{0:T(128)S(1)} %add_convert_fusion.3.flags_ref, bf16[6,640,128]{2,1,0:T(8,128)(2,1)} %collective-permute-done.9.refs_0_, bf16[6,640,128]{2,1,0:T(8,128)(2,1)} %collective-permute-done.10.refs_1_, f32[640,3]{1,0:T(8,128)S(1)} %bitcast.43, bf16[3,3,640,640]{3,2,1,0:T(8,128)(2,1)} %refs_3_.1), custom_call_target="tpu_custom_call" | custom-call | flops 3774873600 | bytes 7372800 | tf_op jit(solution)/shard_map/norm_conv/pallas_call | solution.py:130
  67.9 0.3 convolution_reduce_fusion
  68.2 0.2 copy.23
  68.4 9.7 %collective-permute-done.14.refs_7_.refs_8_ = bf16[2,512,512]{2,1,0:T(8,128)(2,1)} collective-permute-done((bf16[2,512,512]{2,1,0:T(8,128)(2,1)S(1)}, bf16[2,512,512]{2,1,0:T(8,128)(2,1)}, u32[]{:S(2)}, u32[]{:S(2)}) %collective-permute-start.14) | collective-permute-done | bytes 1048608 | tf_op jit(solution)/shard_map/ppermute | solution.py:415
  78.1 0.9 collective-permute-start.15
  79.0 0.1 collective-permute-done.18.refs_9_.refs_10_
  79.1 1.0 collective-permute-start.19
  80.1 8.9 %norm_conv.2 = f32[4,640,128]{2,1,0:T(8,128)S(1)} custom-call(s32[3]{0:T(128)S(1)} %add_convert_fusion.3.flags_ref, bf16[6,640,128]{2,1,0:T(8,128)(2,1)S(1)} %pad_maximum_fusion.refs_0_, bf16[6,640,128]{2,1,0:T(8,128)(2,1)} %collective-permute-done.2.refs_1_, f32[640,3]{1,0:T(8,128)S(1)} %bitcast.42, bf16[3,3,640,640]{3,2,1,0:T(8,128)(2,1)} %refs_3_.1), custom_call_target="tpu_custom_call" | custom-call | flops 3774873600 | bytes 7372800 | tf_op jit(solution)/shard_map/norm_conv/pallas_call | solution.py:130
  89.0 1.4 add_convert_fusion.refs_0_.refs_2_
  90.6 0.3 copy.27.refs_3_
  90.8 0.3 copy.28.refs_4_
  91.1 9.3 %collective-permute-done.15.refs_1_.refs_2_ = bf16[2,512,512]{2,1,0:T(8,128)(2,1)} collective-permute-done((bf16[2,512,512]{2,1,0:T(8,128)(2,1)}, bf16[2,512,512]{2,1,0:T(8,128)(2,1)}, u32[]{:S(2)}, u32[]{:S(2)}) %collective-permute-start.15) | collective-permute-done | bytes 1048608 | tf_op jit(solution)/shard_map/ppermute | solution.py:415
  100.4 1.1 slice.52
  101.5 1.1 collective-permute-start.16
  102.5 1.1 slice.53
  103.6 1.3 collective-permute-start.20
  104.9 0.8 copy-done.3
  105.7 1.1 copy-done.4
  106.8 7.4 %norm_project.1 = (bf16[512,512]{1,0:T(8,128)(2,1)S(1)}, bf16[2,512,512]{2,1,0:T(8,128)(2,1)}, bf16[2,4,320,128]{3,2,1,0:T(8,128)(2,1)S(1)}) custom-call(s32[2]{0:T(128)S(1)} %pad_add_fusion.order_ref, bf16[4,640,128]{2,1,0:T(8,128)(2,1)S(1)} %add_convert_fusion.refs_0_.refs_2_, bf16[4,640,128]{2,1,0:T(8,128)(2,1)S(1)} %copy-done.4, ...), custom_call_target="tpu_custom_call" | custom-call | flops 2013265920 | bytes 3932160 | tf_op jit(solution)/shard_map/norm_project/pallas_call | solution.py:204
  114.2 1.2 copy-done.5
  115.4 16.0 %attend.3 = (f32[4,2,512,128]{3,2,1,0:T(8,128)}, f32[4,2,512,128]{3,2,1,0:T(8,128)}) custom-call(bf16[512,512]{1,0:T(8,128)(2,1)S(1)} %get-tuple-element.19.refs_0_, bf16[2,512,512]{2,1,0:T(8,128)(2,1)S(1)} %copy-done.5, bf16[2,512,512]{2,1,0:T(8,128)(2,1)S(1)} %copy-done.5, bf16[2,512,512]{2,1,0:T(8,128)(2,1)S(1)} %copy-done.2, ...), custom_call_target="tpu_custom_call" | custom-call | flops 10737418240 | bytes 5242880 | tf_op jit(solution)/shard_map/attend/pallas_call | solution.py:361
  131.4 8.9 %attend.4 = (f32[4,2,512,128]{3,2,1,0:T(8,128)}, f32[4,2,512,128]{3,2,1,0:T(8,128)}) custom-call(bf16[512,512]{1,0:T(8,128)(2,1)S(1)} %get-tuple-element.19.refs_0_, bf16[2,512,512]{2,1,0:T(8,128)(2,1)} %collective-permute-done.15.refs_1_.refs_2_, bf16[2,512,512]{2,1,0:T(8,128)(2,1)} %collective-permute-done.15.refs_1_.refs_2_, ...), custom_call_target="tpu_custom_call" | custom-call | flops 4294967296 | bytes 2097152 | tf_op jit(solution)/shard_map/attend/pallas_call | solution.py:361
  140.3 7.2 %attend.5 = (bf16[2,4,320,128]{3,2,1,0:T(8,128)(2,1)S(1)}, f32[2,4,320,128]{3,2,1,0:T(8,128)S(1)}) custom-call(bf16[512,512]{1,0:T(8,128)(2,1)S(1)} %get-tuple-element.19.refs_0_, bf16[1,512,512]{2,1,0:T(8,128)(2,1)S(1)} %collective-permute-done.16.refs_1_, bf16[1,512,512]{2,1,0:T(8,128)(2,1)S(1)} %collective-permute-done.20.refs_2_, ...), custom_call_target="tpu_custom_call" | custom-call | flops 2147483648 | bytes 1048576 | tf_op jit(solution)/shard_map/attend/pallas_call | solution.py:361
  147.6 2.1 %collective-permute-done.21 = bf16[2,4,320,128]{3,2,1,0:T(8,128)(2,1)S(1)} collective-permute-done((bf16[2,4,320,128]{3,2,1,0:T(8,128)(2,1)S(1)}, bf16[2,4,320,128]{3,2,1,0:T(8,128)(2,1)S(1)}, u32[]{:S(2)}, u32[]{:S(2)}) %collective-permute-start.21) | collective-permute-done | bytes 655392 | tf_op jit(solution)/shard_map/ppermute | solution.py:24
  149.7 0.1 convert_add_fusion
  149.9 4.9 %collective-permute-start.22 = (bf16[4,320,128]{2,1,0:T(8,128)(2,1)S(1)}, bf16[4,320,128]{2,1,0:T(8,128)(2,1)S(1)}, u32[]{:S(2)}, u32[]{:S(2)}) collective-permute-start(bf16[4,320,128]{2,1,0:T(8,128)(2,1)S(1)} %fusion.3), channel_id=1, source_target_pairs={{0,16},{16,0},{1,17},{17,1},{2,18},{18,2},{3,19},{19,3},{4,20},{20... | collective-permute-start | bytes 983048 | tf_op jit(solution)/shard_map/ppermute | solution.py:24
  154.8 8.2 %collective-permute-done.22 = bf16[4,320,128]{2,1,0:T(8,128)(2,1)S(1)} collective-permute-done((bf16[4,320,128]{2,1,0:T(8,128)(2,1)S(1)}, bf16[4,320,128]{2,1,0:T(8,128)(2,1)S(1)}, u32[]{:S(2)}, u32[]{:S(2)}) %collective-permute-start.22) | collective-permute-done | bytes 327712 | tf_op jit(solution)/shard_map/ppermute | solution.py:24
  163.0 0.9 fusion.5
  (73 shorter events, 1.0 us)
Async XLA Ops:
  0.6 67.2 %copy-start = (bf16[320,640]{1,0:T(8,128)(2,1)S(1)}, bf16[320,640]{1,0:T(8,128)(2,1)}, u32[]{:S(2)}) copy-start(bf16[320,640]{1,0:T(8,128)(2,1)} %param.15) | copy-start | bytes 1228804
  0.6 11.3 %copy-start.8 = (bf16[512,1280]{1,0:T(8,128)(2,1)S(1)}, bf16[512,1280]{1,0:T(8,128)(2,1)}, u32[]{:S(2)}) copy-start(bf16[512,1280]{1,0:T(8,128)(2,1)} %param.23) | copy-start | bytes 3932164
  0.7 55.2 %collective-permute-start.13 = (bf16[2,512,512]{2,1,0:T(8,128)(2,1)}, bf16[2,512,512]{2,1,0:T(8,128)(2,1)S(1)}, u32[]{:S(2)}, u32[]{:S(2)}) collective-permute-start(bf16[2,512,512]{2,1,0:T(8,128)(2,1)} %bitcast.55), channel_id=1, source_target_pairs={{0,4},{4,8},{8,12},{12,14},{14,10},{10,6},{6,2},{2,0},{1,5},{5,9},... | collective-permute-start | bytes 3145736 | tf_op jit(solution)/shard_map/ppermute | solution.py:415
  3.7 52.1 %collective-permute-start.17 = (bf16[2,512,512]{2,1,0:T(8,128)(2,1)}, bf16[2,512,512]{2,1,0:T(8,128)(2,1)}, u32[]{:S(2)}, u32[]{:S(2)}) collective-permute-start(bf16[2,512,512]{2,1,0:T(8,128)(2,1)} %bitcast.56), channel_id=1, source_target_pairs={{4,0},{8,4},{12,8},{14,12},{10,14},{6,10},{2,6},{0,2},{5,1},{9,5},... | collective-permute-start | bytes 3145736 | tf_op jit(solution)/shard_map/ppermute | solution.py:416
  5.8 13.2 %collective-permute-start.3 = (f32[1,128]{1,0:T(1,128)S(1)}, f32[1,128]{1,0:T(1,128)S(1)}, u32[]{:S(2)}, u32[]{:S(2)}) collective-permute-start(f32[1,128]{1,0:T(1,128)S(1)} %reshape.94), channel_id=1, source_target_pairs={{0,1},{1,0},{2,3},{3,2},{4,5},{5,4},{6,7},{7,6},{8,9},{9,8},{10,11... | collective-permute-start | bytes 1544 | tf_op jit(solution)/shard_map/ppermute | solution.py:53
  6.8 26.6 %collective-permute-start = (bf16[1,640,128]{2,1,0:T(8,128)(2,1)S(1)}, bf16[1,640,128]{2,1,0:T(8,128)(2,1)S(1)}, u32[]{:S(2)}, u32[]{:S(2)}) collective-permute-start(bf16[1,640,128]{2,1,0:T(8,128)(2,1)S(1)} %get-tuple-element.36), channel_id=1, source_target_pairs={{0,2},{2,4},{4,6},{6,8},{8,10},{10,12},{12,14},{1,3},{3,5},{5,7},{... | collective-permute-start | bytes 491528 | tf_op jit(solution)/shard_map/ppermute | solution.py:405
  10.6 24.4 %collective-permute-start.1 = (bf16[1,640,128]{2,1,0:T(8,128)(2,1)S(1)}, bf16[1,640,128]{2,1,0:T(8,128)(2,1)S(1)}, u32[]{:S(2)}, u32[]{:S(2)}) collective-permute-start(bf16[1,640,128]{2,1,0:T(8,128)(2,1)S(1)} %get-tuple-element.37), channel_id=1, source_target_pairs={{2,0},{4,2},{6,4},{8,6},{10,8},{12,10},{14,12},{3,1},{5,3},{7,5},{... | collective-permute-start | bytes 491528 | tf_op jit(solution)/shard_map/ppermute | solution.py:406
  16.8 1.5 copy-start.10
  16.8 1.4 copy-start.11
  16.8 1.5 copy-start.12
  16.8 1.5 copy-start.13
  16.8 18.2 %copy-start.6 = (bf16[1,4,640,128]{3,2,1,0:T(8,128)(2,1)S(1)}, bf16[1,4,640,128]{3,2,1,0:T(8,128)(2,1)}, u32[]{:S(2)}) copy-start(bf16[1,4,640,128]{3,2,1,0:T(8,128)(2,1)} %param.12) | copy-start | bytes 1966084
  19.0 30.5 %collective-permute-start.8 = (bf16[4,640]{1,0:T(4,128)(2,1)S(1)}, bf16[4,640]{1,0:T(4,128)(2,1)S(1)}, u32[]{:S(2)}, u32[]{:S(2)}) collective-permute-start(bf16[4,640]{1,0:T(4,128)(2,1)S(1)} %pad_maximum_fusion.2), channel_id=1, source_target_pairs={{0,1},{1,0},{2,3},{3,2},{4,5},{5,4},{6,7},{7,6},{8,9},{9,8},{10,11... | collective-permute-start | bytes 15368 | tf_op jit(solution)/shard_map/ppermute | solution.py:24
  33.4 3.5 %collective-permute-start.4 = (f32[1,128]{1,0:T(1,128)S(1)}, f32[1,128]{1,0:T(1,128)S(1)}, u32[]{:S(2)}, u32[]{:S(2)}) collective-permute-start(f32[1,128]{1,0:T(1,128)S(1)} %add.85), channel_id=1, source_target_pairs={{0,16},{16,0},{1,17},{17,1},{2,18},{18,2},{3,19},{19,3},{4,20},{20... | collective-permute-start | bytes 1544 | tf_op jit(solution)/shard_map/ppermute | solution.py:53
  35.2 16.1 %collective-permute-start.9 = (bf16[6,640,128]{2,1,0:T(8,128)(2,1)S(1)}, bf16[6,640,128]{2,1,0:T(8,128)(2,1)}, u32[]{:S(2)}, u32[]{:S(2)}) collective-permute-start(bf16[6,640,128]{2,1,0:T(8,128)(2,1)S(1)} %pad_maximum_fusion.refs_0_), channel_id=1, source_target_pairs={{1,17},{16,0},{3,19},{18,2},{5,21},{20,4},{7,23},{22,6},{9,25},{24... | collective-permute-start | bytes 2949128 | tf_op jit(solution)/shard_map/ppermute | solution.py:66
  37.0 4.0 %collective-permute-start.5 = (f32[1,128]{1,0:T(1,128)S(1)}, f32[1,128]{1,0:T(1,128)S(1)}, u32[]{:S(2)}, u32[]{:S(2)}) collective-permute-start(f32[1,128]{1,0:T(1,128)S(1)} %add.86), channel_id=1, source_target_pairs={{0,2},{2,0},{4,6},{6,4},{8,10},{10,8},{12,14},{14,12},{1,3},{3,1},... | collective-permute-start | bytes 1544 | tf_op jit(solution)/shard_map/ppermute | solution.py:53
  41.0 3.5 %collective-permute-start.6 = (f32[1,128]{1,0:T(1,128)S(1)}, f32[1,128]{1,0:T(1,128)S(1)}, u32[]{:S(2)}, u32[]{:S(2)}) collective-permute-start(f32[1,128]{1,0:T(1,128)S(1)} %add.87), channel_id=1, source_target_pairs={{0,4},{2,6},{4,0},{6,2},{8,12},{10,14},{12,8},{14,10},{1,5},{3,7},... | collective-permute-start | bytes 1544 | tf_op jit(solution)/shard_map/ppermute | solution.py:53
  44.5 4.4 %collective-permute-start.7 = (f32[1,128]{1,0:T(1,128)S(1)}, f32[1,128]{1,0:T(1,128)S(1)}, u32[]{:S(2)}, u32[]{:S(2)}) collective-permute-start(f32[1,128]{1,0:T(1,128)S(1)} %add.88), channel_id=1, source_target_pairs={{0,8},{2,10},{4,12},{6,14},{8,0},{10,2},{12,4},{14,6},{1,9},{3,11}... | collective-permute-start | bytes 1544 | tf_op jit(solution)/shard_map/ppermute | solution.py:53
  51.3 7.3 %collective-permute-start.10 = (bf16[6,640,128]{2,1,0:T(8,128)(2,1)}, bf16[6,640,128]{2,1,0:T(8,128)(2,1)}, u32[]{:S(2)}, u32[]{:S(2)}) collective-permute-start(bf16[6,640,128]{2,1,0:T(8,128)(2,1)} %collective-permute-done.9.refs_0_), channel_id=1, source_target_pairs={{0,1},{17,16},{2,3},{19,18},{4,5},{21,20},{6,7},{23,22},{8,9},{25,... | collective-permute-start | bytes 2949128 | tf_op jit(solution)/shard_map/ppermute | solution.py:69
  53.6 26.5 %collective-permute-start.2 = (bf16[6,640,128]{2,1,0:T(8,128)(2,1)S(1)}, bf16[6,640,128]{2,1,0:T(8,128)(2,1)}, u32[]{:S(2)}, u32[]{:S(2)}) collective-permute-start(bf16[6,640,128]{2,1,0:T(8,128)(2,1)S(1)} %pad_maximum_fusion.refs_0_), channel_id=1, source_target_pairs={{0,1},{17,16},{2,3},{19,18},{4,5},{21,20},{6,7},{23,22},{8,9},{25,... | collective-permute-start | bytes 2949128 | tf_op jit(solution)/shard_map/ppermute | solution.py:68
  55.9 11.9 %copy-start.1 = (bf16[2,512,512]{2,1,0:T(8,128)(2,1)}, bf16[2,512,512]{2,1,0:T(8,128)(2,1)S(1)}, u32[]{:S(2)}) copy-start(bf16[2,512,512]{2,1,0:T(8,128)(2,1)S(1)} %collective-permute-done.13.refs_3_.refs_4_) | copy-start | bytes 3145732
  55.9 22.2 %collective-permute-start.14 = (bf16[2,512,512]{2,1,0:T(8,128)(2,1)S(1)}, bf16[2,512,512]{2,1,0:T(8,128)(2,1)}, u32[]{:S(2)}, u32[]{:S(2)}) collective-permute-start(bf16[2,512,512]{2,1,0:T(8,128)(2,1)S(1)} %collective-permute-done.13.refs_3_.refs_4_), channel_id=1, source_target_pairs={{0,4},{4,8},{8,12},{12,14},{14,10},{10,6},{6,2},{2,0},{1,5},{5,9},... | collective-permute-start | bytes 3145736 | tf_op jit(solution)/shard_map/ppermute | solution.py:415
  55.9 23.3 %collective-permute-start.18 = (bf16[2,512,512]{2,1,0:T(8,128)(2,1)}, bf16[2,512,512]{2,1,0:T(8,128)(2,1)}, u32[]{:S(2)}, u32[]{:S(2)}) collective-permute-start(bf16[2,512,512]{2,1,0:T(8,128)(2,1)} %collective-permute-done.17.refs_5_.refs_6_), channel_id=1, source_target_pairs={{4,0},{8,4},{12,8},{14,12},{10,14},{6,10},{2,6},{0,2},{5,1},{9,5},... | collective-permute-start | bytes 3145736 | tf_op jit(solution)/shard_map/ppermute | solution.py:416
  58.6 9.6 %copy-start.9 = (bf16[640]{0:T(1024)(128)(2,1)S(1)}, bf16[640]{0:T(1024)(128)(2,1)}, u32[]{:S(2)}) copy-start(bf16[640]{0:T(1024)(128)(2,1)} %param.19) | copy-start | bytes 3844
  67.8 21.2 %collective-permute-start.11 = (bf16[4,640,128]{2,1,0:T(8,128)(2,1)S(1)}, bf16[4,640,128]{2,1,0:T(8,128)(2,1)}, u32[]{:S(2)}, u32[]{:S(2)}) collective-permute-start(bf16[4,640,128]{2,1,0:T(8,128)(2,1)S(1)} %norm_conv.3), channel_id=1, source_target_pairs={{0,16},{16,0},{1,17},{17,1},{2,18},{18,2},{3,19},{19,3},{4,20},{20... | collective-permute-start | bytes 1966088 | tf_op jit(solution)/shard_map/ppermute | solution.py:24
  78.1 22.3 %collective-permute-start.15 = (bf16[2,512,512]{2,1,0:T(8,128)(2,1)}, bf16[2,512,512]{2,1,0:T(8,128)(2,1)}, u32[]{:S(2)}, u32[]{:S(2)}) collective-permute-start(bf16[2,512,512]{2,1,0:T(8,128)(2,1)} %collective-permute-done.14.refs_7_.refs_8_), channel_id=1, source_target_pairs={{0,4},{4,8},{8,12},{12,14},{14,10},{10,6},{6,2},{2,0},{1,5},{5,9},... | collective-permute-start | bytes 3145736 | tf_op jit(solution)/shard_map/ppermute | solution.py:415
  79.1 23.4 %collective-permute-start.19 = (bf16[2,512,512]{2,1,0:T(8,128)(2,1)}, bf16[2,512,512]{2,1,0:T(8,128)(2,1)}, u32[]{:S(2)}, u32[]{:S(2)}) collective-permute-start(bf16[2,512,512]{2,1,0:T(8,128)(2,1)} %collective-permute-done.18.refs_9_.refs_10_), channel_id=1, source_target_pairs={{4,0},{8,4},{12,8},{14,12},{10,14},{6,10},{2,6},{0,2},{5,1},{9,5},... | collective-permute-start | bytes 3145736 | tf_op jit(solution)/shard_map/ppermute | solution.py:416
  80.1 8.9 %copy-start.7 = (bf16[1,4,640,128]{3,2,1,0:T(8,128)(2,1)S(1)}, bf16[1,4,640,128]{3,2,1,0:T(8,128)(2,1)}, u32[]{:S(2)}) copy-start(bf16[1,4,640,128]{3,2,1,0:T(8,128)(2,1)} %param.12) | copy-start | bytes 1966084
  90.4 14.5 %collective-permute-start.12 = (bf16[4,640,128]{2,1,0:T(8,128)(2,1)S(1)}, bf16[4,640,128]{2,1,0:T(8,128)(2,1)S(1)}, u32[]{:S(2)}, u32[]{:S(2)}) collective-permute-start(bf16[4,640,128]{2,1,0:T(8,128)(2,1)S(1)} %add_convert_fusion.refs_0_.refs_2_), channel_id=1, source_target_pairs={{0,1},{1,0},{2,3},{3,2},{4,5},{5,4},{6,7},{7,6},{8,9},{9,8},{10,11... | collective-permute-start | bytes 1966088 | tf_op jit(solution)/shard_map/ppermute | solution.py:24
  101.5 38.8 %collective-permute-start.16 = (bf16[1,512,512]{2,1,0:T(8,128)(2,1)S(1)}, bf16[1,512,512]{2,1,0:T(8,128)(2,1)S(1)}, u32[]{:S(2)}, u32[]{:S(2)}) collective-permute-start(bf16[1,512,512]{2,1,0:T(8,128)(2,1)S(1)} %slice.52), channel_id=1, source_target_pairs={{0,4},{4,8},{8,12},{12,14},{14,10},{10,6},{6,2},{2,0},{1,5},{5,9},... | collective-permute-start | bytes 1572872 | tf_op jit(solution)/shard_map/ppermute | solution.py:418
  103.6 10.6 %copy-start.2 = (bf16[2,512,512]{2,1,0:T(8,128)(2,1)S(1)}, bf16[2,512,512]{2,1,0:T(8,128)(2,1)}, u32[]{:S(2)}) copy-start(bf16[2,512,512]{2,1,0:T(8,128)(2,1)} %copy-done.1) | copy-start | bytes 3145732
  103.6 36.7 %collective-permute-start.20 = (bf16[1,512,512]{2,1,0:T(8,128)(2,1)S(1)}, bf16[1,512,512]{2,1,0:T(8,128)(2,1)S(1)}, u32[]{:S(2)}, u32[]{:S(2)}) collective-permute-start(bf16[1,512,512]{2,1,0:T(8,128)(2,1)S(1)} %slice.53), channel_id=1, source_target_pairs={{4,0},{8,4},{12,8},{14,12},{10,14},{6,10},{2,6},{0,2},{5,1},{9,5},... | collective-permute-start | bytes 1572872 | tf_op jit(solution)/shard_map/ppermute | solution.py:419
  104.9 0.8 copy-start.3
  105.7 1.1 copy-start.4
  114.2 1.2 copy-start.5
  147.5 2.2 %collective-permute-start.21 = (bf16[2,4,320,128]{3,2,1,0:T(8,128)(2,1)S(1)}, bf16[2,4,320,128]{3,2,1,0:T(8,128)(2,1)S(1)}, u32[]{:S(2)}, u32[]{:S(2)}) collective-permute-start(bf16[2,4,320,128]{3,2,1,0:T(8,128)(2,1)S(1)} %get-tuple-element.27), channel_id=1, source_target_pairs={{0,1},{1,0},{2,3},{3,2},{4,5},{5,4},{6,7},{7,6},{8,9},{9,8},{10,11... | collective-permute-start | bytes 1966088 | tf_op jit(solution)/shard_map/ppermute | solution.py:24
  149.9 13.1 %collective-permute-start.22 = (bf16[4,320,128]{2,1,0:T(8,128)(2,1)S(1)}, bf16[4,320,128]{2,1,0:T(8,128)(2,1)S(1)}, u32[]{:S(2)}, u32[]{:S(2)}) collective-permute-start(bf16[4,320,128]{2,1,0:T(8,128)(2,1)S(1)} %fusion.3), channel_id=1, source_target_pairs={{0,16},{16,0},{1,17},{17,1},{2,18},{18,2},{3,19},{19,3},{4,20},{20... | collective-permute-start | bytes 983048 | tf_op jit(solution)/shard_map/ppermute | solution.py:24

commit v3 on v2

--- a/solution.py
+++ b/solution.py
@@ -17,7 +17,8 @@
 epsilon = 1e-05
 guidance = 5.0
 SCORE_SCALE = 1.0 / math.sqrt(HD)
-VMEM_LIMIT = 50 * 1024 * 1024
+VMEM_LIMIT = 32 * 1024 * 1024
+COST_DIVISOR = 2
 
 
 def swapped(array, axis):
@@ -42,17 +43,9 @@
 
 
 def summed(array, axes):
-    for axis in axes:
-        count = lax.axis_size(axis)
-        if count & (count - 1):
-            array = lax.psum(array, axis)
-            continue
-        distance = 1
-        while distance < count:
-            pairs = [(i, i ^ distance) for i in range(count)]
-            array = array + lax.ppermute(array, axis, pairs)
-            distance *= 2
-    return array
+    count = lax.axis_size(axes)
+    spread = jnp.broadcast_to(array[None], (count,) + array.shape)
+    return jnp.sum(lax.all_to_all(spread, axes, 0, 0, tiled=True), axis=0)
 
 
 def halves_of_inputs(own):
@@ -70,91 +63,125 @@
     return [own, own_side], [across, across_side]
 
 
-def conv_kernel(choices, flags_ref, *refs):
+def conv_kernel(choices, amount, flags_ref, sums_ref, *refs):
     x_refs = refs[:choices]
-    coef_ref, w_ref, out_ref, act_ref, acc_ref = refs[choices:]
+    affine_ref, w_hbm, out_ref, w_ref, act_ref, sems = refs[choices:]
     rows = out_ref.shape[0]
-    step = pl.program_id(0)
-
-    @pl.when(step == 0)
-    def _():
-        mean = coef_ref[:, 0:1]
-        scale = coef_ref[:, 1:2]
-        shift = coef_ref[:, 2:3]
-        for r in range(rows + 2):
-            x = x_refs[0][r]
-            if choices == 2:
-                x = jnp.where(flags_ref[2] == 1, x, x_refs[1][r])
-            x = x.astype(jnp.float32)
-            z = (x - mean) * scale + shift
-            z = z * jax.nn.sigmoid(z)
-            if r == 0:
-                z = jnp.where(flags_ref[0] == 1, z, 0.0)
-            if r == rows + 1:
-                z = jnp.where(flags_ref[1] == 1, z, 0.0)
-            act_ref[:, r * LANES : (r + 1) * LANES] = z.astype(jnp.bfloat16)
-
-    def product(row_tap):
-        return jnp.dot(
-            w_ref[row_tap, 0],
-            act_ref[:, row_tap * LANES : (row_tap + rows) * LANES],
-            preferred_element_type=jnp.float32,
+    ins = affine_ref.shape[0]
+    copies = {}
+    for b in (1, 0, 2):
+        for a in range(3):
+            copies[a, b] = pltpu.make_async_copy(
+                w_hbm.at[a, b], w_ref.at[b, :, a * ins : (a + 1) * ins], sems.at[a, b]
+            )
+            copies[a, b].start()
+
+    groups = ins // (D // GROUPS)
+    base = flags_ref[3]
+
+    def column(offset):
+        return jnp.concatenate(
+            [jnp.full((D // GROUPS, 1), sums_ref[base + offset + g], jnp.float32) for g in range(groups)],
+            axis=0,
         )
 
-    y = product(0) + product(1) + product(2)
-    lane = lax.broadcasted_iota(jnp.int32, (y.shape[0], LANES), 1)
-
-    @pl.when(step == 0)
-    def _():
-        for r in range(rows):
-            part = pltpu.roll(y[:, r * LANES : (r + 1) * LANES], 1, axis=1)
-            acc_ref[r] = jnp.where(lane == 0, 0.0, part)
-
-    @pl.when(step == 1)
-    def _():
-        for r in range(rows):
-            acc_ref[r] += y[:, r * LANES : (r + 1) * LANES]
-
-    @pl.when(step == 2)
-    def _():
-        for r in range(rows):
-            part = pltpu.roll(y[:, r * LANES : (r + 1) * LANES], LANES - 1, axis=1)
-            total = acc_ref[r] + jnp.where(lane == LANES - 1, 0.0, part)
-            out_ref[r] = total.astype(out_ref.dtype)
-
-
-def conv_call(flags, xs, coef, conv_w, out_dtype):
+    mean = column(0) / amount
+    variance = column(GROUPS) / amount - mean * mean
+    scale = lax.rsqrt(variance + epsilon) * affine_ref[:, 0:1]
+    shift = affine_ref[:, 1:2]
+    for r in range(rows + 2):
+        x = x_refs[0][r]
+        if choices == 2:
+            x = jnp.where(flags_ref[2] == 1, x, x_refs[1][r])
+        z = (x.astype(jnp.float32) - mean) * scale + shift
+        z = z * jax.nn.sigmoid(z)
+        if r == 0:
+            z = jnp.where(flags_ref[0] == 1, z, 0.0)
+        if r == rows + 1:
+            z = jnp.where(flags_ref[1] == 1, z, 0.0)
+        z = z.astype(jnp.bfloat16)
+        for a in range(3):
+            if 0 <= r - a < rows:
+                act_ref[a * ins : (a + 1) * ins, (r - a) * LANES : (r - a + 1) * LANES] = z
+
+    width = min(2, rows)
+    lane = lax.broadcasted_iota(jnp.int32, (out_ref.shape[1], LANES), 1)
+    for start in range(0, rows, width):
+        cols = slice(start * LANES, (start + width) * LANES)
+        total = [0.0] * width
+        for b in (1, 0, 2):
+            if start == 0:
+                for a in range(3):
+                    copies[a, b].wait()
+            y = jnp.dot(w_ref[b], act_ref[:, cols], preferred_element_type=jnp.float32)
+            for r in range(width):
+                part = y[:, r * LANES : (r + 1) * LANES]
+                if b == 0:
+                    part = jnp.where(lane == 0, 0.0, pltpu.roll(part, 1, axis=1))
+                if b == 2:
+                    part = jnp.where(lane == LANES - 1, 0.0, pltpu.roll(part, LANES - 1, axis=1))
+                total[r] = total[r] + part
+        for r in range(width):
+            out_ref[start + r] = total[r].astype(out_ref.dtype)
+
+
+def conv_call(flags, sums, amount, xs, affine, conv_w, out_dtype):
     x = xs[0]
     rows = x.shape[0] - 2
     outs, ins = conv_w.shape[2:]
     return pl.pallas_call(
-        functools.partial(conv_kernel, len(xs)),
-        grid=(3,),
+        functools.partial(conv_kernel, len(xs), amount),
         in_specs=[
             pl.BlockSpec(memory_space=pltpu.SMEM),
-            *[pl.BlockSpec(x.shape, lambda i: (0, 0, 0))] * len(xs),
-            pl.BlockSpec(coef.shape, lambda i: (0, 0)),
-            pl.BlockSpec((3, 1, outs, ins), lambda i: (0, i, 0, 0)),
+            pl.BlockSpec(memory_space=pltpu.SMEM),
+            *[pl.BlockSpec(memory_space=pltpu.VMEM)] * (len(xs) + 1),
+            pl.BlockSpec(memory_space=pl.ANY),
         ],
-        out_specs=pl.BlockSpec((rows, outs, LANES), lambda i: (0, 0, 0)),
+        out_specs=pl.BlockSpec(memory_space=pltpu.VMEM),
         out_shape=jax.ShapeDtypeStruct((rows, outs, LANES), out_dtype),
         scratch_shapes=[
-            pltpu.VMEM((ins, (rows + 2) * LANES), jnp.bfloat16),
-            pltpu.VMEM((rows, outs, LANES), jnp.float32),
+            pltpu.VMEM((3, outs, 3 * ins), jnp.bfloat16),
+            pltpu.VMEM((3 * ins, rows * LANES), jnp.bfloat16),
+            pltpu.SemaphoreType.DMA((3, 3)),
         ],
         compiler_params=pltpu.CompilerParams(vmem_limit_bytes=VMEM_LIMIT),
         cost_estimate=pl.CostEstimate(
-            flops=2 * 9 * outs * ins * rows * LANES,
-            bytes_accessed=2 * 9 * outs * ins,
-            transcendentals=ins * rows * LANES,
+            flops=2 * 9 * outs * ins * rows * LANES // COST_DIVISOR,
+            bytes_accessed=2 * 9 * outs * ins // COST_DIVISOR,
+            transcendentals=0,
         ),
         name="norm_conv",
-    )(flags, *xs, coef, conv_w)
+    )(flags, sums, *xs, affine, conv_w)
+
+
+def split_kernel(own_ref, split_ref):
+    rows, channels, _ = own_ref.shape
+    half = channels // 2
+    to = lax.broadcasted_iota(jnp.int32, (channels, channels), 0)
+    source = lax.broadcasted_iota(jnp.int32, (channels, channels), 1)
+    wanted = jnp.where(to < half, 2 * to, 2 * (to - half) + 1)
+    chosen = (source == wanted).astype(jnp.bfloat16)
+    for r in range(rows):
+        y = jnp.dot(chosen, own_ref[r], preferred_element_type=jnp.float32).astype(jnp.bfloat16)
+        split_ref[0, r] = y[:half]
+        split_ref[1, r] = y[half:]
+
+
+def split_call(own):
+    rows, channels, _ = own.shape
+    return pl.pallas_call(
+        split_kernel,
+        in_specs=[pl.BlockSpec(memory_space=pltpu.VMEM)],
+        out_specs=pl.BlockSpec(memory_space=pltpu.VMEM),
+        out_shape=jax.ShapeDtypeStruct((2, rows, channels // 2, LANES), jnp.bfloat16),
+        compiler_params=pltpu.CompilerParams(vmem_limit_bytes=VMEM_LIMIT),
+        name="parity_split",
+    )(own)
 
 
 def project_kernel(parts, order_ref, *refs):
     part_refs = refs[:parts]
-    own_ref, gain_ref, bias_ref, w_ref, q_ref, kv_ref, split_ref, normed_ref = refs[parts:]
+    affine_ref, w_ref, q_ref, kv_ref, normed_ref = refs[parts:]
     rows, channels, _ = part_refs[0].shape
     total = parts * channels
     step = pl.program_id(0)
@@ -168,20 +195,8 @@
             inverse = lax.rsqrt(var + epsilon)
             for j in range(parts):
                 at = pl.ds(pl.multiple_of(order_ref[j] * channels, LANES), channels)
-                z = (x[j] - mean) * inverse * gain_ref[at, :] + bias_ref[at, :]
+                z = (x[j] - mean) * inverse * affine_ref[at, 0:1] + affine_ref[at, 1:2]
                 normed_ref[r * LANES : (r + 1) * LANES, at] = z.astype(jnp.bfloat16).T
-        own_channels = own_ref.shape[1]
-        half = own_channels // 2
-        shape = (own_channels, own_channels)
-        to = lax.broadcasted_iota(jnp.int32, shape, 0)
-        source = lax.broadcasted_iota(jnp.int32, shape, 1)
-        wanted = jnp.where(to < half, 2 * to, 2 * (to - half) + 1)
-        chosen = (source == wanted).astype(jnp.bfloat16)
-        for r in range(rows):
-            y = jnp.dot(chosen, own_ref[r], preferred_element_type=jnp.float32)
-            y = y.astype(jnp.bfloat16)
-            split_ref[0, r] = y[:half]
-            split_ref[1, r] = y[half:]
 
     y = jnp.dot(normed_ref[...], w_ref[0], preferred_element_type=jnp.float32)
     y = y.astype(jnp.bfloat16)
@@ -195,11 +210,10 @@
         kv_ref[0] = y
 
 
-def project_call(order, parts, own, gain, bias, w):
+def project_call(order, parts, affine, w):
     rows, channels, _ = parts[0].shape
     positions = rows * LANES
     _, depth, features = w.shape
-    half = own.shape[1] // 2
     whole = lambda shape: pl.BlockSpec(shape, lambda i: (0,) * len(shape))
     return pl.pallas_call(
         functools.partial(project_kernel, len(parts)),
@@ -207,30 +221,26 @@
         in_specs=[
             pl.BlockSpec(memory_space=pltpu.SMEM),
             *[whole(part.shape) for part in parts],
-            whole(own.shape),
-            whole(gain.shape),
-            whole(bias.shape),
+            whole(affine.shape),
             pl.BlockSpec((1, depth, features), lambda i: (i, 0, 0)),
         ],
         out_specs=(
             whole((positions, features)),
             pl.BlockSpec((1, positions, features), lambda i: (jnp.maximum(i - 1, 0), 0, 0)),
-            whole((2, rows, half, LANES)),
         ),
         out_shape=(
             jax.ShapeDtypeStruct((positions, features), jnp.bfloat16),
             jax.ShapeDtypeStruct((2, positions, features), jnp.bfloat16),
-            jax.ShapeDtypeStruct((2, rows, half, LANES), jnp.bfloat16),
         ),
         scratch_shapes=[pltpu.VMEM((positions, depth), jnp.bfloat16)],
         compiler_params=pltpu.CompilerParams(vmem_limit_bytes=VMEM_LIMIT),
         cost_estimate=pl.CostEstimate(
-            flops=6 * positions * depth * features,
-            bytes_accessed=6 * depth * features,
+            flops=6 * positions * depth * features // COST_DIVISOR,
+            bytes_accessed=6 * depth * features // COST_DIVISOR,
             transcendentals=0,
         ),
         name="norm_project",
-    )(order, *parts, own, gain, bias, w)
+    )(order, *parts, affine, w)
 
 
 def attention_kernel(blocks, carried, final, *refs):
@@ -367,9 +377,9 @@
         scratch_shapes=scratch,
         compiler_params=pltpu.CompilerParams(vmem_limit_bytes=VMEM_LIMIT),
         cost_estimate=pl.CostEstimate(
-            flops=16 * positions * keys * features,
-            bytes_accessed=4 * keys * features,
-            transcendentals=positions * keys * features // HD,
+            flops=16 * positions * keys * features // COST_DIVISOR,
+            bytes_accessed=4 * keys * features // COST_DIVISOR,
+            transcendentals=0,
         ),
         name="attend",
     )(*operands)
@@ -400,25 +410,6 @@
     cfg = lax.axis_index("cfg")
     tp = lax.axis_index("tp")
 
-    up_pairs = [(i, i + 1) for i in range(rows_count - 1)]
-    down_pairs = [(i + 1, i) for i in range(rows_count - 1)]
-    before = lax.ppermute(latent_rows[span_rows - 1 :], "rows", up_pairs)
-    after = lax.ppermute(latent_rows[:1], "rows", down_pairs)
-    rimmed = jnp.concatenate([before, latent_rows, after], axis=0)
-    x_mine, x_other = halves_of_inputs(rimmed)
-
-    forward, backward = ring_pairs(rows_count)
-    pair = stale_kv[0].reshape(2, positions, -1)
-    ahead = behind = pair
-    hops = []
-    for hop in range(1, rows_count // 2):
-        ahead = lax.ppermute(ahead, "rows", forward)
-        behind = lax.ppermute(behind, "rows", backward)
-        hops.append([((ahead, 0), (ahead, 1)), ((behind, 0), (behind, 1))])
-    far_k = lax.ppermute(ahead[:1], "rows", forward)
-    far_v = lax.ppermute(behind[1:], "rows", backward)
-    hops.append([((far_k, 0), (far_v, 0))])
-
     latent32 = latent_rows.astype(jnp.float32)
     values32 = latent32.reshape(span_rows, local_groups, group_width, grid_width)
     sums = jnp.stack(
@@ -426,25 +417,46 @@
     )
     table = jnp.zeros((2, 2, GROUPS), jnp.float32)
     table = lax.dynamic_update_slice(table, sums[None], (cfg, 0, tp * local_groups))
-    table = summed(table.reshape(1, -1), ("tp", "cfg", "rows")).reshape(2, 2, GROUPS)
+    table = summed(table.reshape(-1), ("cfg", "rows", "tp"))
+
+    up_pairs = [(i, i + 1) for i in range(rows_count - 1)]
+    down_pairs = [(i + 1, i) for i in range(rows_count - 1)]
+    before = lax.ppermute(latent_rows[span_rows - 1 :], "rows", up_pairs)
+    after = lax.ppermute(latent_rows[:1], "rows", down_pairs)
+    pair = stale_kv[0].reshape(2, positions, -1)
+    pair, table, before, after = lax.optimization_barrier((pair, table, before, after))
+    rimmed = jnp.concatenate([before, latent_rows, after], axis=0)
+    x_mine, x_other = halves_of_inputs(rimmed)
+
+    forward, backward = ring_pairs(rows_count)
+    hops = [(pair, pair)]
+
+    def next_hop(*after):
+        ahead, behind = hops[-1]
+        if len(hops) == rows_count // 2:
+            ahead, behind = ahead[:1], behind[1:]
+        ahead, behind, *_ = lax.optimization_barrier((ahead, behind) + after)
+        hops.append(
+            (lax.ppermute(ahead, "rows", forward), lax.ppermute(behind, "rows", backward))
+        )
+
+    def blocks_of(hop):
+        ahead, behind = hops[hop]
+        if hop == rows_count // 2:
+            return [((ahead, 0), (behind, 0))]
+        return [((ahead, 0), (ahead, 1)), ((behind, 0), (behind, 1))]
+
+    next_hop()
+
     vectors = gather_tp(jnp.stack([gn_gain, gn_bias, ln_gain, ln_bias]), 1).astype(jnp.float32)
-
     amount = span_rows * rows_count * grid_width * group_width
-    table = lax.dynamic_slice_in_dim(table, cfg * (GROUPS // 2), GROUPS // 2, 2)
-    group_mean = table[:, 0] / amount
-    variance = table[:, 1] / amount - group_mean * group_mean
-    inverse = lax.rsqrt(variance + epsilon)
     half = D // 2
-    gain_half = lax.dynamic_slice_in_dim(vectors[0], cfg * half, half)
-    bias_half = lax.dynamic_slice_in_dim(vectors[1], cfg * half, half)
-    mean_c = jnp.repeat(group_mean, group_width, axis=1)
-    scale_c = jnp.repeat(inverse, group_width, axis=1) * gain_half[None]
-    coef = jnp.stack(
-        [mean_c, scale_c, jnp.broadcast_to(bias_half[None], mean_c.shape)], axis=2
-    )
-    coef_mine = lax.dynamic_index_in_dim(coef, cfg, 0, keepdims=False)
-    coef_other = lax.dynamic_index_in_dim(coef, 1 - cfg, 0, keepdims=False)
+    gn_affine = lax.dynamic_slice_in_dim(vectors[:2], cfg * half, half, 1).T
+    ln_affine = vectors[2:].T
     flags = jnp.stack([my_block > 0, my_block < rows_count - 1, tp == cfg]).astype(jnp.int32)
+    place = cfg * (GROUPS // 2)
+    flags_mine = jnp.append(flags, cfg * 2 * GROUPS + place)
+    flags_other = jnp.append(flags, (1 - cfg) * 2 * GROUPS + place)
 
     local_features = w_qkv.shape[2]
     w_project = w_qkv.transpose(1, 0, 2)
@@ -452,13 +464,13 @@
     w_back = w_back.transpose(0, 2, 1, 3).reshape(tp_count, local_channels, local_features)
     if tp_count == 2:
         w_back = jnp.where(tp == 0, w_back[::-1], w_back)
-    conv_w, coef_other, w_project, w_back = lax.optimization_barrier(
-        (conv_w, coef_other, w_project, w_back)
-    )
-
-    conv_sent = conv_call(flags, x_other, coef_other, conv_w, jnp.bfloat16)
+    gn_affine, w_back = lax.optimization_barrier((gn_affine, w_back))
+
+    conv_sent = conv_call(flags_other, table, amount, x_other, gn_affine, conv_w, jnp.bfloat16)
     conv_received = swapped(conv_sent, "cfg")
-    conv_own = conv_call(flags, x_mine, coef_mine, conv_w, jnp.float32)
+    flags_mine, *_ = lax.optimization_barrier((flags_mine,) + hops[1])
+    next_hop(conv_sent)
+    conv_own = conv_call(flags_mine, table, amount, x_mine, gn_affine, conv_w, jnp.float32)
 
     half_width = TEMB // 2
     frequencies = jnp.exp(
@@ -480,19 +492,24 @@
     else:
         parts = [lax.all_gather(resid, "tp", axis=1, tiled=True)]
         order = jnp.zeros((1,), jnp.int32)
-    queries, fresh, resid_split = project_call(
-        order, parts, resid, vectors[2][:, None], vectors[3][:, None], w_project
-    )
+    queries, fresh = project_call(order, parts, ln_affine, w_project)
+    resid_split = split_call(resid)
     fresh_kv = fresh.reshape(1, 2, span_rows, grid_width, local_features)
 
-    state = attention_call(queries, [((fresh, 0), (fresh, 1))] + hops[0] + hops[1], None)
-    for group in hops[2:-1]:
+    last = rows_count // 2
+    state = attention_call(queries, [((fresh, 0), (fresh, 1))], None)
+    next_hop(state[0])
+    group = blocks_of(1) + blocks_of(2)
+    for hop in range(3, last + 1):
         state = attention_call(queries, group, state)
+        if hop < last:
+            next_hop(state[0])
+        group = blocks_of(hop)
     if tp_count == 2:
-        sent, kept_terms = attention_call(queries, hops[-1], state, w_back, True)
+        sent, kept_terms = attention_call(queries, group, state, w_back, True)
         terms = kept_terms + swapped(sent, "tp").astype(jnp.float32)
     else:
-        (sent,) = attention_call(queries, hops[-1], state, w_back)
+        (sent,) = attention_call(queries, group, state, w_back)
         terms = lax.psum_scatter(sent, "tp", scatter_dimension=0).astype(jnp.float32)
 
     def branch_out(parity):

time: 165 us -> 170 us (1.030)
  waiting for transfers between devices: 53.3 us -> 37.6 us
  blocking collectives: 0 us -> 13.2 us
  local copies, waits for them, and re-layouts: 12.9 us -> 18.4 us
  other arithmetic: 6.07 us -> 8.19 us
  Pallas kernels: 57.4 us -> 55.6 us
    ppermute x1, waiting for transfers between devices: 14.1 us -> 0.01 us  [per_device(): before = lax.ppermute(latent_rows[span_rows - 1:], 'rows', up_pairs)]
    all_to_all x0 -> x1, blocking collectives: none -> 13.2 us  [summed(): return jnp.sum(lax.all_to_all(spread, axes, 0, 0, tiled=True), axis=0)]
    unnamed x28 -> x29, local copies, waits for them, and re-layouts: 3.21 us -> 10.8 us
    ppermute x13 -> x8, starting transfers between devices: 15.7 us -> 8.21 us  [the longest x4 5.93 us: next_hop(): lax.ppermute(behind, 'rows', backward)]
    ppermute x5, starting transfers between devices: 5.39 us -> 12.8 us  [swapped(): lax.ppermute(array, axis, [(i, i ^ 1) for i in range(lax.axis_size(axis))])]
    ppermute x13 -> x8, waiting for transfers between devices: 27.1 us -> 20.2 us  [the longest x4 19.1 us: next_hop(): lax.ppermute(ahead, 'rows', forward)]
    ppermute x1, waiting for transfers between devices: 1.77 us -> 6.08 us  [halves_of_inputs(): across = lax.ppermute(own, ('cfg', 'tp'), [(1, 3), (2, 0)])]
    pallas_call x3 -> x4, Pallas kernels: 32.1 us -> 29.8 us  [attention_call(): pl.pallas_call(functools.partial(attention_kernel, len(pairs), state is n...]
  transfers between devices with their start and end apart: 23 -> 18, of which waited for: 11 -> 12; matrix products, arithmetic and copies ran while one was open for 9% -> 6% of each run, Pallas kernels for 31% -> 29%
where the time goes in v3:
time: 170 us; the launch traced here: 169 us
  Pallas kernels  55.6 us (33%)
  waiting for transfers between devices  37.6 us (22%)
  starting transfers between devices  33.7 us (20%)
  local copies, waits for them, and re-layouts  18.4 us (11%)
  blocking collectives  13.2 us (8%)
  other arithmetic  8.19 us (5%)
  between operations  1.7 us (1%)
    pallas_call x4, Pallas kernels, attention_call(): pl.pallas_call(functools.partial(attention_kernel, len(pairs), state is n...  29.8 us
    ppermute x4, waiting for transfers between devices, next_hop(): lax.ppermute(ahead, 'rows', forward)  19.1 us
    pallas_call x2, Pallas kernels, conv_call(): pl.pallas_call(functools.partial(conv_kernel, len(xs), amount), in_specs=...  18 us
    all_to_all x1, blocking collectives, summed(): return jnp.sum(lax.all_to_all(spread, axes, 0, 0, tiled=True), axis=0)  13.2 us
    ppermute x5, starting transfers between devices, swapped(): lax.ppermute(array, axis, [(i, i ^ 1) for i in range(lax.axis_size(axis))])  12.8 us
    ppermute x5, waiting for transfers between devices, swapped(): lax.ppermute(array, axis, [(i, i ^ 1) for i in range(lax.axis_size(axis))])  11.3 us
    unnamed x29, local copies, waits for them, and re-layouts  10.8 us
    pallas_call x1, Pallas kernels, project_call(): pl.pallas_call(functools.partial(project_kernel, len(parts)), grid=(3,),...  6.75 us
  transfers between devices with their start and end apart: 18, of which 12 were waited for; matrix products, arithmetic and copies ran while one was open for 6% of the time, Pallas kernels for 29%

profile of v3, /device:TPU:0, one launch (start us, length us, event | category | flops | bytes accessed | tf_op | source)
XLA Modules:
  0.0 168.7 jit_solution(13361548877535216645)
XLA Ops:
  0.7 1.1 slice_bitcast_fusion
  1.8 1.3 collective-permute-start.1
  3.1 5.6 %collective-permute-start = (bf16[1,640,128]{2,1,0:T(8,128)(2,1)S(1)}, bf16[1,640,128]{2,1,0:T(8,128)(2,1)S(1)}, u32[]{:S(2)}, u32[]{:S(2)}) collective-permute-start(bf16[1,640,128]{2,1,0:T(8,128)(2,1)S(1)} %get-tuple-element.65), channel_id=1, source_target_pairs={{0,2},{2,4},{4,6},{6,8},{8,10},{10,12},{12,14},{1,3},{3,5},{5,7},{... | collective-permute-start | bytes 491528 | tf_op jit(solution)/shard_map/ppermute | solution.py:424
  8.7 1.3 convert_reduce_fusion
  10.1 0.1 reduce_sum.32
  10.2 0.1 reduce_sum.45
  10.3 0.1 reduce_sum.36
  10.4 0.1 reduce_sum.46
  10.5 0.1 dynamic_update_slice.3
  10.7 0.1 broadcast_in_dim.20
  10.8 13.2 %all_to_all.6 = f32[32,1,128]{2,1,0:T(1,128)S(1)} all-to-all(f32[32,1,128]{2,1,0:T(1,128)S(1)} %broadcast_in_dim.21), channel_id=1, replica_groups=mesh['cfg'=2,'rows'=8,'tp'=2] {'cfg','rows','tp'}, dimensions={0} | all-to-all | bytes 32768 | tf_op jit(solution)/shard_map/all_to_all | solution.py:48
  24.0 0.1 pad_maximum_fusion.refs_0_
  24.2 1.3 collective-permute-start.6
  25.6 1.7 %collective-permute-start.5 = (bf16[4,640]{1,0:T(4,128)(2,1)S(1)}, bf16[4,640]{1,0:T(4,128)(2,1)S(1)}, u32[]{:S(2)}, u32[]{:S(2)}) collective-permute-start(bf16[4,640]{1,0:T(4,128)(2,1)S(1)} %pad_maximum_fusion.1), channel_id=1, source_target_pairs={{0,1},{1,0},{2,3},{3,2},{4,5},{5,4},{6,7},{7,6},{8,9},{9,8},{10,11... | collective-permute-start | bytes 15368 | tf_op jit(solution)/shard_map/ppermute | solution.py:25
  27.3 2.5 %copy.35 = bf16[1280,512]{1,0:T(8,128)(2,1)} copy(bf16[1280,512]{0,1:T(8,128)(2,1)} %bitcast.47) | data formatting | bytes 2621440 | tf_op jit(solution)/shard_map/transpose | solution.py:463
  29.8 3.1 %reshape.51 = bf16[2,320,2,512]{3,2,1,0:T(2,128)(2,1)S(1)} reshape(bf16[1280,512]{1,0:T(8,128)(2,1)} %copy.35) | data formatting | bytes 2621440 | tf_op jit(solution)/shard_map/reshape | solution.py:463
  32.9 0.2 copy.36
  33.1 0.1 add_convert_fusion.3
  33.2 0.3 reverse_select_fusion.refs_5_
  33.4 0.1 pad_add_fusion.1
  34.2 6.1 %collective-permute-done.6.refs_0_ = bf16[6,640,128]{2,1,0:T(8,128)(2,1)} collective-permute-done((bf16[6,640,128]{2,1,0:T(8,128)(2,1)S(1)}, bf16[6,640,128]{2,1,0:T(8,128)(2,1)}, u32[]{:S(2)}, u32[]{:S(2)}) %collective-permute-start.6) | collective-permute-done | bytes 983072 | tf_op jit(solution)/shard_map/ppermute | solution.py:59
  40.3 2.2 %collective-permute-start.7 = (bf16[6,640,128]{2,1,0:T(8,128)(2,1)}, bf16[6,640,128]{2,1,0:T(8,128)(2,1)}, u32[]{:S(2)}, u32[]{:S(2)}) collective-permute-start(bf16[6,640,128]{2,1,0:T(8,128)(2,1)} %collective-permute-done.6.refs_0_), channel_id=1, source_target_pairs={{0,1},{17,16},{2,3},{19,18},{4,5},{21,20},{6,7},{23,22},{8,9},{25,... | collective-permute-start | bytes 2949128 | tf_op jit(solution)/shard_map/ppermute | solution.py:62
  42.5 2.3 %collective-permute-start.4 = (bf16[6,640,128]{2,1,0:T(8,128)(2,1)S(1)}, bf16[6,640,128]{2,1,0:T(8,128)(2,1)}, u32[]{:S(2)}, u32[]{:S(2)}) collective-permute-start(bf16[6,640,128]{2,1,0:T(8,128)(2,1)S(1)} %pad_maximum_fusion.refs_0_), channel_id=1, source_target_pairs={{0,1},{17,16},{2,3},{19,18},{4,5},{21,20},{6,7},{23,22},{8,9},{25,... | collective-permute-start | bytes 2949128 | tf_op jit(solution)/shard_map/ppermute | solution.py:61
  44.8 0.5 collective-permute-start.2
  45.3 1.5 collective-permute-start.3
  46.9 0.2 copy.39
  47.1 3.1 %copy-done.1 = bf16[3,3,640,640]{3,2,1,0:T(8,128)(2,1)S(1)} copy-done((bf16[3,3,640,640]{3,2,1,0:T(8,128)(2,1)S(1)}, bf16[3,3,640,640]{3,2,1,0:T(8,128)(2,1)}, u32[]{:S(2)}) %copy-start.1) | copy-done | bytes 7372824
  50.1 9.1 %norm_conv.3 = bf16[4,640,128]{2,1,0:T(8,128)(2,1)S(1)} custom-call(s32[4]{0:T(128)S(1)} %get-tuple-element.70.flags_ref, f32[128]{0:T(128)S(1)} %reduce_sum.47.sums_ref, bf16[6,640,128]{2,1,0:T(8,128)(2,1)} %collective-permute-done.6.refs_0_, bf16[6,640,128]{2,1,0:T(8,128)(2,1)} %collective-permute-done.7.refs_1_, f32[640,2]{1,0:T(8,128)S(1)} %bitcast.40, ...), custom_call_target="tpu_custom_call" | custom-call | flops 1887436800 | bytes 3686400 | tf_op jit(solution)/shard_map/norm_conv/pallas_call | solution.py:132
  59.4 0.1 divide_multiply_fusion
  59.5 0.3 convolution_reduce_fusion
  59.9 5.4 %collective-permute-done.2.refs_1_.refs_2_ = bf16[2,512,512]{2,1,0:T(8,128)(2,1)} collective-permute-done((bf16[2,512,512]{2,1,0:T(8,128)(2,1)}, bf16[2,512,512]{2,1,0:T(8,128)(2,1)}, u32[]{:S(2)}, u32[]{:S(2)}) %collective-permute-start.2) | collective-permute-done | bytes 1048608 | tf_op jit(solution)/shard_map/ppermute | solution.py:440
  65.3 0.3 collective-permute-done.3.refs_3_.refs_4_
  65.6 3.1 %copy-done.2 = bf16[3,3,640,640]{3,2,1,0:T(8,128)(2,1)S(1)} copy-done((bf16[3,3,640,640]{3,2,1,0:T(8,128)(2,1)S(1)}, bf16[3,3,640,640]{3,2,1,0:T(8,128)(2,1)}, u32[]{:S(2)}) %copy-start.2) | copy-done | bytes 7372824
  68.7 8.9 %norm_conv.2 = f32[4,640,128]{2,1,0:T(8,128)S(1)} custom-call(s32[4]{0:T(128)S(1)} %get-tuple-element.30.flags_ref, f32[128]{0:T(128)S(1)} %reduce_sum.47.sums_ref, bf16[6,640,128]{2,1,0:T(8,128)(2,1)S(1)} %pad_maximum_fusion.refs_0_, bf16[6,640,128]{2,1,0:T(8,128)(2,1)} %collective-permute-done.4.refs_1_, f32[640,2]{1,0:T(8,128)S(1)} %bitcast.41, ...), custom_call_target="tpu_custom_call" | custom-call | flops 1887436800 | bytes 3686400 | tf_op jit(solution)/shard_map/norm_conv/pallas_call | solution.py:132
  77.6 0.6 collective-permute-start.10
  78.2 1.5 collective-permute-start.11
  79.7 0.3 add_convert_fusion.own_ref.refs_0_
  80.2 0.3 copy.37
  80.4 1.9 %collective-permute-done.9.refs_1_ = bf16[4,640,128]{2,1,0:T(8,128)(2,1)} collective-permute-done((bf16[4,640,128]{2,1,0:T(8,128)(2,1)S(1)}, bf16[4,640,128]{2,1,0:T(8,128)(2,1)}, u32[]{:S(2)}, u32[]{:S(2)}) %collective-permute-start.9) | collective-permute-done | bytes 655392 | tf_op jit(solution)/shard_map/ppermute | solution.py:25
  82.3 2.1 %copy-done.3 = bf16[1280,3,512]{2,0,1:T(8,128)(2,1)S(1)} copy-done((bf16[1280,3,512]{2,0,1:T(8,128)(2,1)S(1)}, bf16[1280,3,512]{2,0,1:T(8,128)(2,1)}, u32[]{:S(2)}) %copy-start.3) | copy-done | bytes 3932184
  84.4 6.7 %norm_project.1 = (bf16[512,512]{1,0:T(8,128)(2,1)S(1)}, bf16[2,512,512]{2,1,0:T(8,128)(2,1)}) custom-call(s32[2]{0:T(128)S(1)} %pad_add_fusion.2.order_ref, bf16[4,640,128]{2,1,0:T(8,128)(2,1)S(1)} %add_convert_fusion.own_ref.refs_0_, bf16[4,640,128]{2,1,0:T(8,128)(2,1)} %collective-permute-done.9.refs_1_, f32[1280,2]{1,0:T(8,128)S(1)} %bitcast.42, ...), custom_call_target="tpu_custom_call" | custom-call | flops 1006632960 | bytes 1966080 | tf_op jit(solution)/shard_map/norm_project/pallas_call | solution.py:218
  91.2 1.2 copy-done.6
  92.4 4.0 %attend.4 = (f32[4,2,512,128]{3,2,1,0:T(8,128)S(1)}, f32[4,2,512,128]{3,2,1,0:T(8,128)S(1)}) custom-call(bf16[512,512]{1,0:T(8,128)(2,1)S(1)} %get-tuple-element.35.refs_0_, bf16[2,512,512]{2,1,0:T(8,128)(2,1)S(1)} %copy-done.6, bf16[2,512,512]{2,1,0:T(8,128)(2,1)S(1)} %copy-done.6), custom_call_target="tpu_custom_call" | custom-call | flops 1073741824 | bytes 524288 | tf_op jit(solution)/shard_map/attend/pallas_call | solution.py:371
  96.4 0.6 collective-permute-done.10.refs_5_.refs_6_
  97.0 0.3 collective-permute-done.11.refs_7_.refs_8_
  97.3 0.6 collective-permute-start.12
  97.9 1.5 collective-permute-start.13
  99.4 12.6 %attend.5 = (f32[4,2,512,128]{3,2,1,0:T(8,128)S(1)}, f32[4,2,512,128]{3,2,1,0:T(8,128)S(1)}) custom-call(bf16[512,512]{1,0:T(8,128)(2,1)S(1)} %get-tuple-element.35.refs_0_, bf16[2,512,512]{2,1,0:T(8,128)(2,1)} %collective-permute-done.2.refs_1_.refs_2_, bf16[2,512,512]{2,1,0:T(8,128)(2,1)} %collective-permute-done.2.refs_1_.refs_2_, ...), custom_call_target="tpu_custom_call" | custom-call | flops 4294967296 | bytes 2097152 | tf_op jit(solution)/shard_map/attend/pallas_call | solution.py:371
  112.0 9.9 %collective-permute-done.12.refs_1_.refs_2_ = bf16[2,512,512]{2,1,0:T(8,128)(2,1)S(1)} collective-permute-done((bf16[2,512,512]{2,1,0:T(8,128)(2,1)}, bf16[2,512,512]{2,1,0:T(8,128)(2,1)S(1)}, u32[]{:S(2)}, u32[]{:S(2)}) %collective-permute-start.12) | collective-permute-done | bytes 1048608 | tf_op jit(solution)/shard_map/ppermute | solution.py:440
  122.0 0.2 collective-permute-done.13.refs_3_.refs_4_
  122.2 0.6 collective-permute-start.14
  122.8 1.5 collective-permute-start.15
  124.3 6.9 %attend.6 = (f32[4,2,512,128]{3,2,1,0:T(8,128)S(1)}, f32[4,2,512,128]{3,2,1,0:T(8,128)S(1)}) custom-call(bf16[512,512]{1,0:T(8,128)(2,1)S(1)} %get-tuple-element.35.refs_0_, bf16[2,512,512]{2,1,0:T(8,128)(2,1)S(1)} %collective-permute-done.12.refs_1_.refs_2_, bf16[2,512,512]{2,1,0:T(8,128)(2,1)S(1)} %collective-permute-done.12.refs_1_.refs_2_, ...), custom_call_target="tpu_custom_call" | custom-call | flops 2147483648 | bytes 1048576 | tf_op jit(solution)/shard_map/attend/pallas_call | solution.py:371
  131.1 3.1 %collective-permute-done.14.refs_1_ = bf16[1,512,512]{2,1,0:T(8,128)(2,1)S(1)} collective-permute-done((bf16[1,512,512]{2,1,0:T(8,128)(2,1)S(1)}, bf16[1,512,512]{2,1,0:T(8,128)(2,1)S(1)}, u32[]{:S(2)}, u32[]{:S(2)}) %collective-permute-start.14) | collective-permute-done | bytes 524320 | tf_op jit(solution)/shard_map/ppermute | solution.py:440
  134.3 0.3 collective-permute-done.15.refs_2_
  134.6 6.3 %attend.7 = (bf16[2,4,320,128]{3,2,1,0:T(8,128)(2,1)}, f32[2,4,320,128]{3,2,1,0:T(8,128)S(1)}) custom-call(bf16[512,512]{1,0:T(8,128)(2,1)S(1)} %get-tuple-element.35.refs_0_, bf16[1,512,512]{2,1,0:T(8,128)(2,1)S(1)} %collective-permute-done.14.refs_1_, bf16[1,512,512]{2,1,0:T(8,128)(2,1)S(1)} %collective-permute-done.15.refs_2_, ...), custom_call_target="tpu_custom_call" | custom-call | flops 1073741824 | bytes 524288 | tf_op jit(solution)/shard_map/attend/pallas_call | solution.py:371
  140.9 1.1 copy-done.4
  141.9 1.0 parity_split.1
  143.0 1.4 collective-permute-done.16
  144.4 2.3 %convert_add_fusion = f32[2,4,320,128]{3,2,1,0:T(8,128)} fusion(f32[2,4,320,128]{3,2,1,0:T(8,128)S(1)} %copy-done.5, bf16[2,4,320,128]{3,2,1,0:T(8,128)(2,1)} %collective-permute-done.16), kind=kLoop, calls=%fused_computation.4 | loop fusion | flops 655360 | bytes 3276800 | tf_op jit(solution)/shard_map/add | solution.py:510
  146.6 1.2 fusion.3
  147.8 10.9 %collective-permute-start.17 = (bf16[4,320,128]{2,1,0:T(8,128)(2,1)S(1)}, bf16[4,320,128]{2,1,0:T(8,128)(2,1)S(1)}, u32[]{:S(2)}, u32[]{:S(2)}) collective-permute-start(bf16[4,320,128]{2,1,0:T(8,128)(2,1)S(1)} %fusion.3), channel_id=1, source_target_pairs={{0,16},{16,0},{1,17},{17,1},{2,18},{18,2},{3,19},{19,3},{4,20},{20... | collective-permute-start | bytes 983048 | tf_op jit(solution)/shard_map/ppermute | solution.py:25
  158.7 8.0 %collective-permute-done.17 = bf16[4,320,128]{2,1,0:T(8,128)(2,1)S(1)} collective-permute-done((bf16[4,320,128]{2,1,0:T(8,128)(2,1)S(1)}, bf16[4,320,128]{2,1,0:T(8,128)(2,1)S(1)}, u32[]{:S(2)}, u32[]{:S(2)}) %collective-permute-start.17) | collective-permute-done | bytes 327712 | tf_op jit(solution)/shard_map/ppermute | solution.py:25
  166.7 2.0 %fusion.5 = bf16[4,320,1,128]{3,1,2,0:T(8,128)(2,1)} fusion(bf16[4,320,128]{2,1,0:T(8,128)(2,1)S(1)} %collective-permute-done.17, f32[2,4,320,128]{3,2,1,0:T(8,128)} %convert_add_fusion, s32[]{:T(128)S(6)} %select_n.50, bf16[2,4,320,128]{3,2,1,0:T(8,128)(2,1)S(1)} %parity_split.1, pred[]{:T(512)S(6)} %eq.10), kind=kLoop, calls=%fused_computation.16 | loop fusion | flops 1802240 | bytes 1638405
  (51 shorter events, 0.6 us)
Async XLA Ops:
  0.6 58.9 %copy-start = (bf16[320,640]{1,0:T(8,128)(2,1)S(1)}, bf16[320,640]{1,0:T(8,128)(2,1)}, u32[]{:S(2)}) copy-start(bf16[320,640]{1,0:T(8,128)(2,1)} %param.15) | copy-start | bytes 1228804
  0.6 23.4 %copy-start.7 = (bf16[1,4,640,128]{3,2,1,0:T(8,128)(2,1)S(1)}, bf16[1,4,640,128]{3,2,1,0:T(8,128)(2,1)}, u32[]{:S(2)}) copy-start(bf16[1,4,640,128]{3,2,1,0:T(8,128)(2,1)} %param.12) | copy-start | bytes 1966084
  1.8 22.2 %collective-permute-start.1 = (bf16[1,640,128]{2,1,0:T(8,128)(2,1)S(1)}, bf16[1,640,128]{2,1,0:T(8,128)(2,1)S(1)}, u32[]{:S(2)}, u32[]{:S(2)}) collective-permute-start(bf16[1,640,128]{2,1,0:T(8,128)(2,1)S(1)} %get-tuple-element.64), channel_id=1, source_target_pairs={{2,0},{4,2},{6,4},{8,6},{10,8},{12,10},{14,12},{3,1},{5,3},{7,5},{... | collective-permute-start | bytes 491528 | tf_op jit(solution)/shard_map/ppermute | solution.py:425
  3.1 22.4 %copy-start.10 = (bf16[640]{0:T(1024)(128)(2,1)S(1)}, bf16[640]{0:T(1024)(128)(2,1)}, u32[]{:S(2)}) copy-start(bf16[640]{0:T(1024)(128)(2,1)} %param.16) | copy-start | bytes 3844
  3.1 22.4 %copy-start.11 = (bf16[640]{0:T(1024)(128)(2,1)S(1)}, bf16[640]{0:T(1024)(128)(2,1)}, u32[]{:S(2)}) copy-start(bf16[640]{0:T(1024)(128)(2,1)} %param.17) | copy-start | bytes 3844
  3.1 22.4 %copy-start.12 = (bf16[640]{0:T(1024)(128)(2,1)S(1)}, bf16[640]{0:T(1024)(128)(2,1)}, u32[]{:S(2)}) copy-start(bf16[640]{0:T(1024)(128)(2,1)} %param.20) | copy-start | bytes 3844
  3.1 22.4 %copy-start.13 = (bf16[640]{0:T(1024)(128)(2,1)S(1)}, bf16[640]{0:T(1024)(128)(2,1)}, u32[]{:S(2)}) copy-start(bf16[640]{0:T(1024)(128)(2,1)} %param.21) | copy-start | bytes 3844
  3.1 20.9 %collective-permute-start = (bf16[1,640,128]{2,1,0:T(8,128)(2,1)S(1)}, bf16[1,640,128]{2,1,0:T(8,128)(2,1)S(1)}, u32[]{:S(2)}, u32[]{:S(2)}) collective-permute-start(bf16[1,640,128]{2,1,0:T(8,128)(2,1)S(1)} %get-tuple-element.65), channel_id=1, source_target_pairs={{0,2},{2,4},{4,6},{6,8},{8,10},{10,12},{12,14},{1,3},{3,5},{5,7},{... | collective-permute-start | bytes 491528 | tf_op jit(solution)/shard_map/ppermute | solution.py:424
  24.2 16.1 %collective-permute-start.6 = (bf16[6,640,128]{2,1,0:T(8,128)(2,1)S(1)}, bf16[6,640,128]{2,1,0:T(8,128)(2,1)}, u32[]{:S(2)}, u32[]{:S(2)}) collective-permute-start(bf16[6,640,128]{2,1,0:T(8,128)(2,1)S(1)} %pad_maximum_fusion.refs_0_), channel_id=1, source_target_pairs={{1,17},{16,0},{3,19},{18,2},{5,21},{20,4},{7,23},{22,6},{9,25},{24... | collective-permute-start | bytes 2949128 | tf_op jit(solution)/shard_map/ppermute | solution.py:59
  25.6 16.9 %collective-permute-start.5 = (bf16[4,640]{1,0:T(4,128)(2,1)S(1)}, bf16[4,640]{1,0:T(4,128)(2,1)S(1)}, u32[]{:S(2)}, u32[]{:S(2)}) collective-permute-start(bf16[4,640]{1,0:T(4,128)(2,1)S(1)} %pad_maximum_fusion.1), channel_id=1, source_target_pairs={{0,1},{1,0},{2,3},{3,2},{4,5},{5,4},{6,7},{7,6},{8,9},{9,8},{10,11... | collective-permute-start | bytes 15368 | tf_op jit(solution)/shard_map/ppermute | solution.py:25
  40.3 6.8 %collective-permute-start.7 = (bf16[6,640,128]{2,1,0:T(8,128)(2,1)}, bf16[6,640,128]{2,1,0:T(8,128)(2,1)}, u32[]{:S(2)}, u32[]{:S(2)}) collective-permute-start(bf16[6,640,128]{2,1,0:T(8,128)(2,1)} %collective-permute-done.6.refs_0_), channel_id=1, source_target_pairs={{0,1},{17,16},{2,3},{19,18},{4,5},{21,20},{6,7},{23,22},{8,9},{25,... | collective-permute-start | bytes 2949128 | tf_op jit(solution)/shard_map/ppermute | solution.py:62
  42.5 23.1 %collective-permute-start.4 = (bf16[6,640,128]{2,1,0:T(8,128)(2,1)S(1)}, bf16[6,640,128]{2,1,0:T(8,128)(2,1)}, u32[]{:S(2)}, u32[]{:S(2)}) collective-permute-start(bf16[6,640,128]{2,1,0:T(8,128)(2,1)S(1)} %pad_maximum_fusion.refs_0_), channel_id=1, source_target_pairs={{0,1},{17,16},{2,3},{19,18},{4,5},{21,20},{6,7},{23,22},{8,9},{25,... | collective-permute-start | bytes 2949128 | tf_op jit(solution)/shard_map/ppermute | solution.py:61
  44.8 20.5 %collective-permute-start.2 = (bf16[2,512,512]{2,1,0:T(8,128)(2,1)}, bf16[2,512,512]{2,1,0:T(8,128)(2,1)}, u32[]{:S(2)}, u32[]{:S(2)}) collective-permute-start(bf16[2,512,512]{2,1,0:T(8,128)(2,1)} %bitcast.51), channel_id=1, source_target_pairs={{0,4},{4,8},{8,12},{12,14},{14,10},{10,6},{6,2},{2,0},{1,5},{5,9},... | collective-permute-start | bytes 3145736 | tf_op jit(solution)/shard_map/ppermute | solution.py:440
  45.3 20.3 %collective-permute-start.3 = (bf16[2,512,512]{2,1,0:T(8,128)(2,1)}, bf16[2,512,512]{2,1,0:T(8,128)(2,1)}, u32[]{:S(2)}, u32[]{:S(2)}) collective-permute-start(bf16[2,512,512]{2,1,0:T(8,128)(2,1)} %bitcast.52), channel_id=1, source_target_pairs={{4,0},{8,4},{12,8},{14,12},{10,14},{6,10},{2,6},{0,2},{5,1},{9,5},... | collective-permute-start | bytes 3145736 | tf_op jit(solution)/shard_map/ppermute | solution.py:440
  47.0 3.1 %copy-start.1 = (bf16[3,3,640,640]{3,2,1,0:T(8,128)(2,1)S(1)}, bf16[3,3,640,640]{3,2,1,0:T(8,128)(2,1)}, u32[]{:S(2)}) copy-start(bf16[3,3,640,640]{3,2,1,0:T(8,128)(2,1)} %refs_3_.3) | copy-start | bytes 22118404
  50.1 9.7 %copy-start.9 = (bf16[640]{0:T(1024)(128)(2,1)S(1)}, bf16[640]{0:T(1024)(128)(2,1)}, u32[]{:S(2)}) copy-start(bf16[640]{0:T(1024)(128)(2,1)} %param.19) | copy-start | bytes 3844
  59.3 20.4 %collective-permute-start.8 = (bf16[4,640,128]{2,1,0:T(8,128)(2,1)S(1)}, bf16[4,640,128]{2,1,0:T(8,128)(2,1)S(1)}, u32[]{:S(2)}, u32[]{:S(2)}) collective-permute-start(bf16[4,640,128]{2,1,0:T(8,128)(2,1)S(1)} %norm_conv.3), channel_id=1, source_target_pairs={{0,16},{16,0},{1,17},{17,1},{2,18},{18,2},{3,19},{19,3},{4,20},{20... | collective-permute-start | bytes 1966088 | tf_op jit(solution)/shard_map/ppermute | solution.py:25
  65.6 3.1 %copy-start.2 = (bf16[3,3,640,640]{3,2,1,0:T(8,128)(2,1)S(1)}, bf16[3,3,640,640]{3,2,1,0:T(8,128)(2,1)}, u32[]{:S(2)}) copy-start(bf16[3,3,640,640]{3,2,1,0:T(8,128)(2,1)} %refs_3_.3) | copy-start | bytes 22118404
  68.7 11.0 %copy-start.8 = (bf16[1,4,640,128]{3,2,1,0:T(8,128)(2,1)S(1)}, bf16[1,4,640,128]{3,2,1,0:T(8,128)(2,1)}, u32[]{:S(2)}) copy-start(bf16[1,4,640,128]{3,2,1,0:T(8,128)(2,1)} %param.12) | copy-start | bytes 1966084
  77.6 19.4 %collective-permute-start.10 = (bf16[2,512,512]{2,1,0:T(8,128)(2,1)}, bf16[2,512,512]{2,1,0:T(8,128)(2,1)}, u32[]{:S(2)}, u32[]{:S(2)}) collective-permute-start(bf16[2,512,512]{2,1,0:T(8,128)(2,1)} %collective-permute-done.2.refs_1_.refs_2_), channel_id=1, source_target_pairs={{0,4},{4,8},{8,12},{12,14},{14,10},{10,6},{6,2},{2,0},{1,5},{5,9},... | collective-permute-start | bytes 3145736 | tf_op jit(solution)/shard_map/ppermute | solution.py:440
  78.2 19.2 %collective-permute-start.11 = (bf16[2,512,512]{2,1,0:T(8,128)(2,1)}, bf16[2,512,512]{2,1,0:T(8,128)(2,1)}, u32[]{:S(2)}, u32[]{:S(2)}) collective-permute-start(bf16[2,512,512]{2,1,0:T(8,128)(2,1)} %collective-permute-done.3.refs_3_.refs_4_), channel_id=1, source_target_pairs={{4,0},{8,4},{12,8},{14,12},{10,14},{6,10},{2,6},{0,2},{5,1},{9,5},... | collective-permute-start | bytes 3145736 | tf_op jit(solution)/shard_map/ppermute | solution.py:440
  80.0 2.3 %collective-permute-start.9 = (bf16[4,640,128]{2,1,0:T(8,128)(2,1)S(1)}, bf16[4,640,128]{2,1,0:T(8,128)(2,1)}, u32[]{:S(2)}, u32[]{:S(2)}) collective-permute-start(bf16[4,640,128]{2,1,0:T(8,128)(2,1)S(1)} %add_convert_fusion.own_ref.refs_0_), channel_id=1, source_target_pairs={{0,1},{1,0},{2,3},{3,2},{4,5},{5,4},{6,7},{7,6},{8,9},{9,8},{10,11... | collective-permute-start | bytes 1966088 | tf_op jit(solution)/shard_map/ppermute | solution.py:25
  82.3 2.1 %copy-start.3 = (bf16[1280,3,512]{2,0,1:T(8,128)(2,1)S(1)}, bf16[1280,3,512]{2,0,1:T(8,128)(2,1)}, u32[]{:S(2)}) copy-start(bf16[1280,3,512]{2,0,1:T(8,128)(2,1)} %param.22) | copy-start | bytes 11796484
  91.2 1.2 copy-start.6
  97.3 24.6 %collective-permute-start.12 = (bf16[2,512,512]{2,1,0:T(8,128)(2,1)}, bf16[2,512,512]{2,1,0:T(8,128)(2,1)S(1)}, u32[]{:S(2)}, u32[]{:S(2)}) collective-permute-start(bf16[2,512,512]{2,1,0:T(8,128)(2,1)} %collective-permute-done.10.refs_5_.refs_6_), channel_id=1, source_target_pairs={{0,4},{4,8},{8,12},{12,14},{14,10},{10,6},{6,2},{2,0},{1,5},{5,9},... | collective-permute-start | bytes 3145736 | tf_op jit(solution)/shard_map/ppermute | solution.py:440
  97.9 24.3 %collective-permute-start.13 = (bf16[2,512,512]{2,1,0:T(8,128)(2,1)}, bf16[2,512,512]{2,1,0:T(8,128)(2,1)S(1)}, u32[]{:S(2)}, u32[]{:S(2)}) collective-permute-start(bf16[2,512,512]{2,1,0:T(8,128)(2,1)} %collective-permute-done.11.refs_7_.refs_8_), channel_id=1, source_target_pairs={{4,0},{8,4},{12,8},{14,12},{10,14},{6,10},{2,6},{0,2},{5,1},{9,5},... | collective-permute-start | bytes 3145736 | tf_op jit(solution)/shard_map/ppermute | solution.py:440
  122.2 12.1 %collective-permute-start.14 = (bf16[1,512,512]{2,1,0:T(8,128)(2,1)S(1)}, bf16[1,512,512]{2,1,0:T(8,128)(2,1)S(1)}, u32[]{:S(2)}, u32[]{:S(2)}) collective-permute-start(bf16[1,512,512]{2,1,0:T(8,128)(2,1)S(1)} %slice.34), channel_id=1, source_target_pairs={{0,4},{4,8},{8,12},{12,14},{14,10},{10,6},{6,2},{2,0},{1,5},{5,9},... | collective-permute-start | bytes 1572872 | tf_op jit(solution)/shard_map/ppermute | solution.py:440
  122.8 11.8 %collective-permute-start.15 = (bf16[1,512,512]{2,1,0:T(8,128)(2,1)S(1)}, bf16[1,512,512]{2,1,0:T(8,128)(2,1)S(1)}, u32[]{:S(2)}, u32[]{:S(2)}) collective-permute-start(bf16[1,512,512]{2,1,0:T(8,128)(2,1)S(1)} %slice.35), channel_id=1, source_target_pairs={{4,0},{8,4},{12,8},{14,12},{10,14},{6,10},{2,6},{0,2},{5,1},{9,5},... | collective-permute-start | bytes 1572872 | tf_op jit(solution)/shard_map/ppermute | solution.py:440
  140.9 1.1 copy-start.4
  141.9 2.4 %copy-start.5 = (f32[2,4,320,128]{3,2,1,0:T(8,128)S(1)}, f32[2,4,320,128]{3,2,1,0:T(8,128)}, u32[]{:S(2)}) copy-start(f32[2,4,320,128]{3,2,1,0:T(8,128)} %copy-done.4) | copy-start | bytes 3932164
  141.9 2.4 %collective-permute-start.16 = (bf16[2,4,320,128]{3,2,1,0:T(8,128)(2,1)}, bf16[2,4,320,128]{3,2,1,0:T(8,128)(2,1)}, u32[]{:S(2)}, u32[]{:S(2)}) collective-permute-start(bf16[2,4,320,128]{3,2,1,0:T(8,128)(2,1)} %get-tuple-element.51), channel_id=1, source_target_pairs={{0,1},{1,0},{2,3},{3,2},{4,5},{5,4},{6,7},{7,6},{8,9},{9,8},{10,11... | collective-permute-start | bytes 1966088 | tf_op jit(solution)/shard_map/ppermute | solution.py:25
  147.8 18.9 %collective-permute-start.17 = (bf16[4,320,128]{2,1,0:T(8,128)(2,1)S(1)}, bf16[4,320,128]{2,1,0:T(8,128)(2,1)S(1)}, u32[]{:S(2)}, u32[]{:S(2)}) collective-permute-start(bf16[4,320,128]{2,1,0:T(8,128)(2,1)S(1)} %fusion.3), channel_id=1, source_target_pairs={{0,16},{16,0},{1,17},{17,1},{2,18},{18,2},{3,19},{19,3},{4,20},{20... | collective-permute-start | bytes 983048 | tf_op jit(solution)/shard_map/ppermute | solution.py:25

commit v4 on v3

--- a/solution.py
+++ b/solution.py
@@ -18,7 +18,11 @@
 guidance = 5.0
 SCORE_SCALE = 1.0 / math.sqrt(HD)
 VMEM_LIMIT = 32 * 1024 * 1024
-COST_DIVISOR = 2
+COST_SHARE = 0.02
+
+
+def cost(work):
+    return pl.CostEstimate(flops=int(work * 1e6 * COST_SHARE), bytes_accessed=1000, transcendentals=0)
 
 
 def swapped(array, axis):
@@ -48,7 +52,11 @@
     return jnp.sum(lax.all_to_all(spread, axes, 0, 0, tiled=True), axis=0)
 
 
-def halves_of_inputs(own):
+def need(array, others):
+    return lax.optimization_barrier((array,) + tuple(others))[0]
+
+
+def halves_of_inputs(own, others):
     cfg = lax.axis_index("cfg")
     if lax.axis_size("tp") != 2:
         full = lax.all_gather(own, "tp", axis=1, tiled=True)
@@ -58,8 +66,8 @@
         return [mine], [swapped(sent, "cfg")]
     across = lax.ppermute(own, ("cfg", "tp"), [(1, 3), (2, 0)])
     pairs = [(0, 1), (3, 2)]
-    own_side = lax.ppermute(own, ("cfg", "tp"), pairs)
-    across_side = lax.ppermute(across, ("cfg", "tp"), pairs)
+    own_side = lax.ppermute(need(own, others), ("cfg", "tp"), pairs)
+    across_side = lax.ppermute(need(across, others), ("cfg", "tp"), pairs)
     return [own, own_side], [across, across_side]
 
 
@@ -135,7 +143,7 @@
             pl.BlockSpec(memory_space=pltpu.SMEM),
             pl.BlockSpec(memory_space=pltpu.SMEM),
             *[pl.BlockSpec(memory_space=pltpu.VMEM)] * (len(xs) + 1),
-            pl.BlockSpec(memory_space=pl.ANY),
+            pl.BlockSpec(memory_space=pltpu.HBM),
         ],
         out_specs=pl.BlockSpec(memory_space=pltpu.VMEM),
         out_shape=jax.ShapeDtypeStruct((rows, outs, LANES), out_dtype),
@@ -145,11 +153,7 @@
             pltpu.SemaphoreType.DMA((3, 3)),
         ],
         compiler_params=pltpu.CompilerParams(vmem_limit_bytes=VMEM_LIMIT),
-        cost_estimate=pl.CostEstimate(
-            flops=2 * 9 * outs * ins * rows * LANES // COST_DIVISOR,
-            bytes_accessed=2 * 9 * outs * ins // COST_DIVISOR,
-            transcendentals=0,
-        ),
+        cost_estimate=cost(9000),
         name="norm_conv",
     )(flags, sums, *xs, affine, conv_w)
 
@@ -175,72 +179,89 @@
         out_specs=pl.BlockSpec(memory_space=pltpu.VMEM),
         out_shape=jax.ShapeDtypeStruct((2, rows, channels // 2, LANES), jnp.bfloat16),
         compiler_params=pltpu.CompilerParams(vmem_limit_bytes=VMEM_LIMIT),
+        cost_estimate=cost(1000),
         name="parity_split",
     )(own)
 
 
 def project_kernel(parts, order_ref, *refs):
     part_refs = refs[:parts]
-    affine_ref, w_ref, q_ref, kv_ref, normed_ref = refs[parts:]
+    affine_ref, w_hbm, q_ref, kv_ref, w_ref, normed_ref, sems = refs[parts:]
     rows, channels, _ = part_refs[0].shape
     total = parts * channels
-    step = pl.program_id(0)
-
-    @pl.when(step == 0)
-    def _():
-        for r in range(rows):
-            x = [ref[r].astype(jnp.float32) for ref in part_refs]
-            mean = sum(jnp.sum(a, axis=0, keepdims=True) for a in x) / total
-            var = sum(jnp.sum(a * a, axis=0, keepdims=True) for a in x) / total - mean * mean
-            inverse = lax.rsqrt(var + epsilon)
-            for j in range(parts):
-                at = pl.ds(pl.multiple_of(order_ref[j] * channels, LANES), channels)
-                z = (x[j] - mean) * inverse * affine_ref[at, 0:1] + affine_ref[at, 1:2]
-                normed_ref[r * LANES : (r + 1) * LANES, at] = z.astype(jnp.bfloat16).T
-
-    y = jnp.dot(normed_ref[...], w_ref[0], preferred_element_type=jnp.float32)
-    y = y.astype(jnp.bfloat16)
-
-    @pl.when(step == 0)
-    def _():
-        q_ref[...] = y * SCORE_SCALE
-
-    @pl.when(step > 0)
-    def _():
-        kv_ref[0] = y
+    copies = [pltpu.make_async_copy(w_hbm.at[i], w_ref.at[i], sems.at[i]) for i in range(3)]
+    for copy in copies:
+        copy.start()
+    for r in range(rows):
+        x = [ref[r].astype(jnp.float32) for ref in part_refs]
+        mean = sum(jnp.sum(a, axis=0, keepdims=True) for a in x) / total
+        var = sum(jnp.sum(a * a, axis=0, keepdims=True) for a in x) / total - mean * mean
+        inverse = lax.rsqrt(var + epsilon)
+        for j in range(parts):
+            at = pl.ds(pl.multiple_of(order_ref[j] * channels, LANES), channels)
+            z = (x[j] - mean) * inverse * affine_ref[at, 0:1] + affine_ref[at, 1:2]
+            normed_ref[r * LANES : (r + 1) * LANES, at] = z.astype(jnp.bfloat16).T
+    for i in range(3):
+        copies[i].wait()
+        y = jnp.dot(normed_ref[...], w_ref[i], preferred_element_type=jnp.float32)
+        y = y.astype(jnp.bfloat16)
+        if i == 0:
+            q_ref[...] = y * SCORE_SCALE
+        else:
+            kv_ref[i - 1] = y
 
 
 def project_call(order, parts, affine, w):
-    rows, channels, _ = parts[0].shape
+    rows = parts[0].shape[0]
     positions = rows * LANES
     _, depth, features = w.shape
-    whole = lambda shape: pl.BlockSpec(shape, lambda i: (0,) * len(shape))
+    vmem = pl.BlockSpec(memory_space=pltpu.VMEM)
     return pl.pallas_call(
         functools.partial(project_kernel, len(parts)),
-        grid=(3,),
         in_specs=[
             pl.BlockSpec(memory_space=pltpu.SMEM),
-            *[whole(part.shape) for part in parts],
-            whole(affine.shape),
-            pl.BlockSpec((1, depth, features), lambda i: (i, 0, 0)),
+            *[vmem] * (len(parts) + 1),
+            pl.BlockSpec(memory_space=pltpu.HBM),
         ],
-        out_specs=(
-            whole((positions, features)),
-            pl.BlockSpec((1, positions, features), lambda i: (jnp.maximum(i - 1, 0), 0, 0)),
-        ),
+        out_specs=(vmem, vmem),
         out_shape=(
             jax.ShapeDtypeStruct((positions, features), jnp.bfloat16),
             jax.ShapeDtypeStruct((2, positions, features), jnp.bfloat16),
         ),
-        scratch_shapes=[pltpu.VMEM((positions, depth), jnp.bfloat16)],
+        scratch_shapes=[
+            pltpu.VMEM((3, depth, features), jnp.bfloat16),
+            pltpu.VMEM((positions, depth), jnp.bfloat16),
+            pltpu.SemaphoreType.DMA((3,)),
+        ],
         compiler_params=pltpu.CompilerParams(vmem_limit_bytes=VMEM_LIMIT),
-        cost_estimate=pl.CostEstimate(
-            flops=6 * positions * depth * features // COST_DIVISOR,
-            bytes_accessed=6 * depth * features // COST_DIVISOR,
-            transcendentals=0,
-        ),
+        cost_estimate=cost(6500),
         name="norm_project",
     )(order, *parts, affine, w)
+
+
+def branch_kernel(parity_ref, resid_ref, *refs):
+    total = resid_ref[0].astype(jnp.float32)
+    for ref in refs[:-1]:
+        total = total + ref[0].astype(jnp.float32)
+    refs[-1][...] = total.astype(jnp.bfloat16)
+
+
+def branch_call(parity, resid_split, terms):
+    shape = resid_split.shape
+    block = pl.BlockSpec((1,) + shape[1:], lambda i, parity: (parity[0], 0, 0, 0))
+    return pl.pallas_call(
+        branch_kernel,
+        grid_spec=pltpu.PrefetchScalarGridSpec(
+            num_scalar_prefetch=1,
+            grid=(1,),
+            in_specs=[block] * (1 + len(terms)),
+            out_specs=pl.BlockSpec(shape[1:], lambda i, parity: (0, 0, 0)),
+        ),
+        out_shape=jax.ShapeDtypeStruct(shape[1:], jnp.bfloat16),
+        compiler_params=pltpu.CompilerParams(vmem_limit_bytes=VMEM_LIMIT),
+        cost_estimate=cost(1000),
+        name="branch_out",
+    )(parity.astype(jnp.int32).reshape(1), resid_split, *terms)
 
 
 def attention_kernel(blocks, carried, final, *refs):
@@ -376,11 +397,7 @@
         out_shape=out_shape,
         scratch_shapes=scratch,
         compiler_params=pltpu.CompilerParams(vmem_limit_bytes=VMEM_LIMIT),
-        cost_estimate=pl.CostEstimate(
-            flops=16 * positions * keys * features // COST_DIVISOR,
-            bytes_accessed=4 * keys * features // COST_DIVISOR,
-            transcendentals=0,
-        ),
+        cost_estimate=cost(1000 + 3200 * len(pairs)),
         name="attend",
     )(*operands)
 
@@ -423,30 +440,34 @@
     down_pairs = [(i + 1, i) for i in range(rows_count - 1)]
     before = lax.ppermute(latent_rows[span_rows - 1 :], "rows", up_pairs)
     after = lax.ppermute(latent_rows[:1], "rows", down_pairs)
-    pair = stale_kv[0].reshape(2, positions, -1)
-    pair, table, before, after = lax.optimization_barrier((pair, table, before, after))
     rimmed = jnp.concatenate([before, latent_rows, after], axis=0)
-    x_mine, x_other = halves_of_inputs(rimmed)
 
     forward, backward = ring_pairs(rows_count)
-    hops = [(pair, pair)]
-
-    def next_hop(*after):
-        ahead, behind = hops[-1]
-        if len(hops) == rows_count // 2:
-            ahead, behind = ahead[:1], behind[1:]
-        ahead, behind, *_ = lax.optimization_barrier((ahead, behind) + after)
-        hops.append(
-            (lax.ppermute(ahead, "rows", forward), lax.ppermute(behind, "rows", backward))
-        )
+    last = rows_count // 2
+    stale = stale_kv[0].reshape(2, 1, positions, -1)
+    hops = [[(stale[which], stale[which])] for which in range(2)]
+
+    def next_hop(which, *after):
+        ahead, behind = hops[which][-1]
+        if after:
+            ahead, behind, *_ = lax.optimization_barrier((ahead, behind) + after)
+        final = len(hops[which]) == last
+        if not (final and which == 1):
+            ahead = lax.ppermute(ahead, "rows", forward)
+        if not (final and which == 0):
+            behind = lax.ppermute(behind, "rows", backward)
+        hops[which].append((ahead, behind))
 
     def blocks_of(hop):
-        ahead, behind = hops[hop]
-        if hop == rows_count // 2:
-            return [((ahead, 0), (behind, 0))]
-        return [((ahead, 0), (ahead, 1)), ((behind, 0), (behind, 1))]
-
-    next_hop()
+        keys, values = hops[0][hop], hops[1][hop]
+        if hop == last:
+            return [((keys[0], 0), (values[1], 0))]
+        return [((keys[0], 0), (values[0], 0)), ((keys[1], 0), (values[1], 0))]
+
+    next_hop(0)
+    x_mine, x_other = halves_of_inputs(rimmed, hops[0][1])
+    next_hop(1, table)
+    next_hop(0, table)
 
     vectors = gather_tp(jnp.stack([gn_gain, gn_bias, ln_gain, ln_bias]), 1).astype(jnp.float32)
     amount = span_rows * rows_count * grid_width * group_width
@@ -468,8 +489,8 @@
 
     conv_sent = conv_call(flags_other, table, amount, x_other, gn_affine, conv_w, jnp.bfloat16)
     conv_received = swapped(conv_sent, "cfg")
-    flags_mine, *_ = lax.optimization_barrier((flags_mine,) + hops[1])
-    next_hop(conv_sent)
+    next_hop(1, conv_sent)
+    flags_mine = need(flags_mine, hops[1][1] + hops[0][2])
     conv_own = conv_call(flags_mine, table, amount, x_mine, gn_affine, conv_w, jnp.float32)
 
     half_width = TEMB // 2
@@ -486,39 +507,38 @@
         latent32 + (conv_own + conv_received.astype(jnp.float32) + bias[None, :, None])
     ).astype(jnp.bfloat16)
 
+    next_hop(0, conv_sent)
     if tp_count == 2:
         parts = [resid, swapped(resid, "tp")]
         order = jnp.stack([tp, 1 - tp]).astype(jnp.int32)
     else:
         parts = [lax.all_gather(resid, "tp", axis=1, tiled=True)]
         order = jnp.zeros((1,), jnp.int32)
+    next_hop(1, resid)
+    order = need(order, hops[1][2])
     queries, fresh = project_call(order, parts, ln_affine, w_project)
+    while len(hops[0]) <= last:
+        next_hop(0, queries)
     resid_split = split_call(resid)
     fresh_kv = fresh.reshape(1, 2, span_rows, grid_width, local_features)
 
-    last = rows_count // 2
+    queries = need(queries, hops[0][3])
     state = attention_call(queries, [((fresh, 0), (fresh, 1))], None)
-    next_hop(state[0])
-    group = blocks_of(1) + blocks_of(2)
-    for hop in range(3, last + 1):
-        state = attention_call(queries, group, state)
-        if hop < last:
-            next_hop(state[0])
-        group = blocks_of(hop)
+    while len(hops[1]) <= last:
+        next_hop(1, state[0])
+    for hop in range(1, last):
+        if hop == 2:
+            queries = need(queries, hops[1][3])
+        state = attention_call(queries, blocks_of(hop), state)
     if tp_count == 2:
-        sent, kept_terms = attention_call(queries, group, state, w_back, True)
-        terms = kept_terms + swapped(sent, "tp").astype(jnp.float32)
+        sent, kept_terms = attention_call(queries, blocks_of(last), state, w_back, True)
+        terms = (kept_terms, swapped(sent, "tp"))
     else:
-        (sent,) = attention_call(queries, group, state, w_back)
-        terms = lax.psum_scatter(sent, "tp", scatter_dimension=0).astype(jnp.float32)
-
-    def branch_out(parity):
-        term = lax.dynamic_index_in_dim(terms, parity, 0, keepdims=False)
-        base = lax.dynamic_index_in_dim(resid_split, parity, 0, keepdims=False)
-        return (base.astype(jnp.float32) + term).astype(jnp.bfloat16)
-
-    other_branch = swapped(branch_out(1 - cfg), "cfg")
-    kept = branch_out(cfg)
+        (sent,) = attention_call(queries, blocks_of(last), state, w_back)
+        terms = (lax.psum_scatter(sent, "tp", scatter_dimension=0),)
+
+    other_branch = swapped(branch_call(1 - cfg, resid_split, terms), "cfg")
+    kept = branch_call(cfg, resid_split, terms)
     is_cond = cfg == 0
     cond_out = jnp.where(is_cond, kept, other_branch).astype(jnp.float32)
     uncond_out = jnp.where(is_cond, other_branch, kept).astype(jnp.float32)

time: 170 us -> 161 us (0.947)
  blocking collectives: 13.2 us -> 0 us
  waiting for transfers between devices: 37.6 us -> 30.9 us
  starting transfers between devices: 33.7 us -> 39.6 us
  local copies, waits for them, and re-layouts: 18.4 us -> 23.4 us
  Pallas kernels: 55.6 us -> 58.5 us
  other arithmetic: 8.19 us -> 6.02 us
    all_to_all x1 -> x0, blocking collectives: 13.2 us -> none  [summed(): return jnp.sum(lax.all_to_all(spread, axes, 0, 0, tiled=True), axis=0)]
    ppermute x10 -> x16, starting transfers between devices: 12.7 us -> 21.9 us  [the longest x7 12.4 us: next_hop(): ahead = lax.ppermute(ahead, 'rows', forward)]
    ppermute x5, starting transfers between devices: 12.8 us -> 4.91 us  [swapped(): lax.ppermute(array, axis, [(i, i ^ 1) for i in range(lax.axis_size(axis))])]
    ppermute x1, waiting for transfers between devices: 6.08 us -> 0.01 us  [halves_of_inputs(): across = lax.ppermute(own, ('cfg', 'tp'), [(1, 3), (2, 0)])]
    all_to_all x0 -> x1, starting transfers between devices: none -> 5.15 us  [summed(): return jnp.sum(lax.all_to_all(spread, axes, 0, 0, tiled=True), axis=0)]
    ppermute x1, waiting for transfers between devices: 0.01 us -> 4.12 us  [per_device(): after = lax.ppermute(latent_rows[:1], 'rows', down_pairs)]
    ppermute x5, waiting for transfers between devices: 11.3 us -> 7.67 us  [swapped(): lax.ppermute(array, axis, [(i, i ^ 1) for i in range(lax.axis_size(axis))])]
    ppermute x10 -> x16, waiting for transfers between devices: 20.2 us -> 17 us  [the longest x7 11.6 us: next_hop(): behind = lax.ppermute(behind, 'rows', backward)]
  transfers between devices with their start and end apart: 18 -> 25, of which waited for: 12 -> 9; matrix products, arithmetic and copies ran while one was open for 6% -> 9% of each run, Pallas kernels for 29% -> 33%
where the time goes in v4:
time: 161 us; the launch traced here: 160 us
  Pallas kernels  58.5 us (36%)
  starting transfers between devices  39.6 us (25%)
  waiting for transfers between devices  30.9 us (19%)
  local copies, waits for them, and re-layouts  23.4 us (15%)
  other arithmetic  6.02 us (4%)
  between operations  1.8 us (1%)
    pallas_call x5, Pallas kernels, attention_call(): pl.pallas_call(functools.partial(attention_kernel, len(pairs), state is n...  32.2 us
    pallas_call x2, Pallas kernels, conv_call(): pl.pallas_call(functools.partial(conv_kernel, len(xs), amount), in_specs=...  18.1 us
    ppermute x7, starting transfers between devices, next_hop(): ahead = lax.ppermute(ahead, 'rows', forward)  12.4 us
    unnamed x39, local copies, waits for them, and re-layouts  11.7 us
    ppermute x7, waiting for transfers between devices, next_hop(): behind = lax.ppermute(behind, 'rows', backward)  11.6 us
    ppermute x5, waiting for transfers between devices, swapped(): lax.ppermute(array, axis, [(i, i ^ 1) for i in range(lax.axis_size(axis))])  7.67 us
    pallas_call x1, Pallas kernels, project_call(): pl.pallas_call(functools.partial(project_kernel, len(parts)), in_specs=[p...  6.99 us
    ppermute x7, waiting for transfers between devices, next_hop(): ahead = lax.ppermute(ahead, 'rows', forward)  5.41 us
  transfers between devices with their start and end apart: 25, of which 9 were waited for; matrix products, arithmetic and copies ran while one was open for 9% of the time, Pallas kernels for 33%

profile of v4, /device:TPU:0, one launch (start us, length us, event | category | flops | bytes accessed | tf_op | source)
XLA Modules:
  0.0 160.5 jit_solution(8042143437238596044)
XLA Ops:
  0.7 1.1 slice_bitcast_fusion.1
  1.8 4.9 %collective-permute-start.6 = (bf16[1,640,128]{2,1,0:T(8,128)(2,1)S(1)}, bf16[1,640,128]{2,1,0:T(8,128)(2,1)S(1)}, u32[]{:S(2)}, u32[]{:S(2)}) collective-permute-start(bf16[1,640,128]{2,1,0:T(8,128)(2,1)S(1)} %get-tuple-element.80), channel_id=1, source_target_pairs={{0,2},{2,4},{4,6},{6,8},{8,10},{10,12},{12,14},{1,3},{3,5},{5,7},{... | collective-permute-start | bytes 491528 | tf_op jit(solution)/shard_map/ppermute | solution.py:441
  6.6 1.3 collective-permute-start.7
  7.9 2.1 %collective-permute-done.6 = bf16[1,640,128]{2,1,0:T(8,128)(2,1)S(1)} collective-permute-done((bf16[1,640,128]{2,1,0:T(8,128)(2,1)S(1)}, bf16[1,640,128]{2,1,0:T(8,128)(2,1)S(1)}, u32[]{:S(2)}, u32[]{:S(2)}) %collective-permute-start.6) | collective-permute-done | bytes 163872 | tf_op jit(solution)/shard_map/ppermute | solution.py:441
  10.1 4.1 %collective-permute-done.7 = bf16[1,640,128]{2,1,0:T(8,128)(2,1)S(1)} collective-permute-done((bf16[1,640,128]{2,1,0:T(8,128)(2,1)S(1)}, bf16[1,640,128]{2,1,0:T(8,128)(2,1)S(1)}, u32[]{:S(2)}, u32[]{:S(2)}) %collective-permute-start.7) | collective-permute-done | bytes 163872 | tf_op jit(solution)/shard_map/ppermute | solution.py:442
  14.2 1.2 pad_maximum_fusion.refs_0_
  15.5 1.4 collective-permute-start.10
  16.9 1.1 fusion.6
  18.0 2.9 %collective-permute-start.2 = (bf16[1,512,512]{2,1,0:T(8,128)(2,1)}, bf16[1,512,512]{2,1,0:T(8,128)(2,1)}, u32[]{:S(2)}, u32[]{:S(2)}) collective-permute-start(bf16[1,512,512]{2,1,0:T(8,128)(2,1)} %bitcast.11), channel_id=1, source_target_pairs={{0,4},{4,8},{8,12},{12,14},{14,10},{10,6},{6,2},{2,0},{1,5},{5,9},... | collective-permute-start | bytes 1572872 | tf_op jit(solution)/shard_map/ppermute | solution.py:456
  21.0 2.6 %collective-permute-start.9 = (bf16[4,640]{1,0:T(4,128)(2,1)S(1)}, bf16[4,640]{1,0:T(4,128)(2,1)S(1)}, u32[]{:S(2)}, u32[]{:S(2)}) collective-permute-start(bf16[4,640]{1,0:T(4,128)(2,1)S(1)} %pad_maximum_fusion.1), channel_id=1, source_target_pairs={{0,1},{1,0},{2,3},{3,2},{4,5},{5,4},{6,7},{7,6},{8,9},{9,8},{10,11... | collective-permute-start | bytes 15368 | tf_op jit(solution)/shard_map/ppermute | solution.py:29
  23.5 0.3 convert_reduce_fusion
  24.0 0.1 reduce_sum.36
  24.1 0.1 reduce_sum.46
  24.2 0.1 dynamic_update_slice.3
  24.5 0.6 broadcast_in_dim.21
  25.1 5.1 %all-to-all-start = ((f32[32,1,128]{2,1,0:T(1,128)}), f32[32,1,128]{2,1,0:T(1,128)S(1)}, u32[]{:S(2)}, u32[]{:S(2)}) async-start(f32[32,1,128]{2,1,0:T(1,128)} %broadcast_in_dim.21), calls=%async_computation | async-start | bytes 32768 | tf_op jit(solution)/shard_map/all_to_all | solution.py:52
  30.3 2.4 %copy.35 = bf16[1280,512]{1,0:T(8,128)(2,1)} copy(bf16[1280,512]{0,1:T(8,128)(2,1)} %bitcast.44) | data formatting | bytes 2621440 | tf_op jit(solution)/shard_map/transpose | solution.py:484
  32.7 3.1 %reshape.56 = bf16[2,320,2,512]{3,2,1,0:T(2,128)(2,1)S(1)} reshape(bf16[1280,512]{1,0:T(8,128)(2,1)} %copy.35) | data formatting | bytes 2621440 | tf_op jit(solution)/shard_map/reshape | solution.py:484
  35.8 1.3 copy.36
  37.1 2.1 %reverse_select_fusion.refs_5_ = bf16[2,640,512]{2,1,0:T(8,128)(2,1)S(1)} fusion(bf16[2,640,512]{2,1,0:T(8,128)(2,1)} %bitcast.42, pred[]{:T(512)S(6)} %eq.12), kind=kLoop, calls=%fused_computation | loop fusion | flops 655360 | bytes 2621441 | tf_op jit(solution)/shard_map/jit(_where)/select_n | solution.py:487
  39.3 3.1 %collective-permute-start.11 = (bf16[6,640,128]{2,1,0:T(8,128)(2,1)}, bf16[6,640,128]{2,1,0:T(8,128)(2,1)}, u32[]{:S(2)}, u32[]{:S(2)}) collective-permute-start(bf16[6,640,128]{2,1,0:T(8,128)(2,1)} %collective-permute-done.10.refs_0_), channel_id=1, source_target_pairs={{0,1},{17,16},{2,3},{19,18},{4,5},{21,20},{6,7},{23,22},{8,9},{25,... | collective-permute-start | bytes 2949128 | tf_op jit(solution)/shard_map/ppermute | solution.py:70
  42.5 1.7 %collective-permute-start = (bf16[1,512,512]{2,1,0:T(8,128)(2,1)}, bf16[1,512,512]{2,1,0:T(8,128)(2,1)}, u32[]{:S(2)}, u32[]{:S(2)}) collective-permute-start(bf16[1,512,512]{2,1,0:T(8,128)(2,1)} %bitcast.45), channel_id=1, source_target_pairs={{0,4},{4,8},{8,12},{12,14},{14,10},{10,6},{6,2},{2,0},{1,5},{5,9},... | collective-permute-start | bytes 1572872 | tf_op jit(solution)/shard_map/ppermute | solution.py:456
  44.3 2.3 %collective-permute-start.8 = (bf16[6,640,128]{2,1,0:T(8,128)(2,1)S(1)}, bf16[6,640,128]{2,1,0:T(8,128)(2,1)}, u32[]{:S(2)}, u32[]{:S(2)}) collective-permute-start(bf16[6,640,128]{2,1,0:T(8,128)(2,1)S(1)} %pad_maximum_fusion.refs_0_), channel_id=1, source_target_pairs={{0,1},{17,16},{2,3},{19,18},{4,5},{21,20},{6,7},{23,22},{8,9},{25,... | collective-permute-start | bytes 2949128 | tf_op jit(solution)/shard_map/ppermute | solution.py:69
  46.5 0.6 fusion.7
  47.1 0.4 collective-permute-start.1
  47.5 1.7 %collective-permute-start.4 = (bf16[1,512,512]{2,1,0:T(8,128)(2,1)}, bf16[1,512,512]{2,1,0:T(8,128)(2,1)}, u32[]{:S(2)}, u32[]{:S(2)}) collective-permute-start(bf16[1,512,512]{2,1,0:T(8,128)(2,1)} %collective-permute-done.2.refs_1_), channel_id=1, source_target_pairs={{0,4},{4,8},{8,12},{12,14},{14,10},{10,6},{6,2},{2,0},{1,5},{5,9},... | collective-permute-start | bytes 1572872 | tf_op jit(solution)/shard_map/ppermute | solution.py:456
  49.2 0.2 copy.39
  49.4 3.1 %copy-done.1 = bf16[3,3,640,640]{3,2,1,0:T(8,128)(2,1)S(1)} copy-done((bf16[3,3,640,640]{3,2,1,0:T(8,128)(2,1)S(1)}, bf16[3,3,640,640]{3,2,1,0:T(8,128)(2,1)}, u32[]{:S(2)}) %copy-start.1) | copy-done | bytes 7372824
  52.5 9.2 %norm_conv.3 = bf16[4,640,128]{2,1,0:T(8,128)(2,1)S(1)} custom-call(s32[4]{0:T(128)S(1)} %get-tuple-element.86.flags_ref, f32[128]{0:T(128)S(1)} %reduce_sum.47.sums_ref, bf16[6,640,128]{2,1,0:T(8,128)(2,1)} %collective-permute-done.10.refs_0_, bf16[6,640,128]{2,1,0:T(8,128)(2,1)} %collective-permute-done.11.refs_1_, f32[640,2]{1,0:T(8,128)S(1)} %bitcast.38, ...), custom_call_target="tpu_custom_call" | custom-call | flops 180000000 | bytes 1000 | tf_op jit(solution)/shard_map/norm_conv/pallas_call | solution.py:140
  62.4 0.4 collective-permute-start.5
  62.9 0.3 convolution_reduce_fusion
  63.3 1.7 %collective-permute-start.13 = (bf16[1,512,512]{2,1,0:T(8,128)(2,1)}, bf16[1,512,512]{2,1,0:T(8,128)(2,1)}, u32[]{:S(2)}, u32[]{:S(2)}) collective-permute-start(bf16[1,512,512]{2,1,0:T(8,128)(2,1)} %collective-permute-done.refs_2_), channel_id=1, source_target_pairs={{0,4},{4,8},{8,12},{12,14},{14,10},{10,6},{6,2},{2,0},{1,5},{5,9},... | collective-permute-start | bytes 1572872 | tf_op jit(solution)/shard_map/ppermute | solution.py:456
  65.0 1.4 collective-permute-done.4.refs_1_
  66.4 1.7 %collective-permute-start.14 = (bf16[1,512,512]{2,1,0:T(8,128)(2,1)}, bf16[1,512,512]{2,1,0:T(8,128)(2,1)}, u32[]{:S(2)}, u32[]{:S(2)}) collective-permute-start(bf16[1,512,512]{2,1,0:T(8,128)(2,1)} %collective-permute-done.1.refs_4_), channel_id=1, source_target_pairs={{4,0},{8,4},{12,8},{14,12},{10,14},{6,10},{2,6},{0,2},{5,1},{9,5},... | collective-permute-start | bytes 1572872 | tf_op jit(solution)/shard_map/ppermute | solution.py:458
  68.1 9.3 %collective-permute-done.5.refs_3_ = bf16[1,512,512]{2,1,0:T(8,128)(2,1)} collective-permute-done((bf16[1,512,512]{2,1,0:T(8,128)(2,1)S(1)}, bf16[1,512,512]{2,1,0:T(8,128)(2,1)}, u32[]{:S(2)}, u32[]{:S(2)}) %collective-permute-start.5) | collective-permute-done | bytes 524320 | tf_op jit(solution)/shard_map/ppermute | solution.py:458
  77.3 3.1 %copy-done.2 = bf16[3,3,640,640]{3,2,1,0:T(8,128)(2,1)S(1)} copy-done((bf16[3,3,640,640]{3,2,1,0:T(8,128)(2,1)S(1)}, bf16[3,3,640,640]{3,2,1,0:T(8,128)(2,1)}, u32[]{:S(2)}) %copy-start.2) | copy-done | bytes 7372824
  80.4 8.9 %norm_conv.2 = f32[4,640,128]{2,1,0:T(8,128)S(1)} custom-call(s32[4]{0:T(128)S(1)} %get-tuple-element.38.flags_ref, f32[128]{0:T(128)S(1)} %reduce_sum.47.sums_ref, bf16[6,640,128]{2,1,0:T(8,128)(2,1)S(1)} %pad_maximum_fusion.refs_0_, bf16[6,640,128]{2,1,0:T(8,128)(2,1)} %collective-permute-done.8.refs_1_, f32[640,2]{1,0:T(8,128)S(1)} %bitcast.39, ...), custom_call_target="tpu_custom_call" | custom-call | flops 180000000 | bytes 1000 | tf_op jit(solution)/shard_map/norm_conv/pallas_call | solution.py:140
  89.4 0.3 add_convert_fusion.own_ref.refs_0_
  89.8 1.5 collective-permute-start.16
  91.3 0.5 collective-permute-start.17
  91.9 1.5 collective-permute-start.18
  93.4 0.5 collective-permute-start.19
  93.9 0.7 pad_add_fusion.2.order_ref
  94.6 0.9 copy.37
  95.5 2.1 %copy-done.6 = bf16[1280,3,512]{2,0,1:T(8,128)(2,1)S(1)} copy-done((bf16[1280,3,512]{2,0,1:T(8,128)(2,1)S(1)}, bf16[1280,3,512]{2,0,1:T(8,128)(2,1)}, u32[]{:S(2)}) %copy-start.6) | copy-done | bytes 3932184
  97.6 0.7 copy-done.10
  98.3 7.0 %norm_project.1 = (bf16[512,512]{1,0:T(8,128)(2,1)S(1)}, bf16[2,512,512]{2,1,0:T(8,128)(2,1)}) custom-call(s32[2]{0:T(128)S(1)} %copy-done.10, bf16[4,640,128]{2,1,0:T(8,128)(2,1)S(1)} %add_convert_fusion.own_ref.refs_0_, bf16[4,640,128]{2,1,0:T(8,128)(2,1)} %collective-permute-done.15.refs_1_, f32[1280,2]{1,0:T(8,128)S(1)} %bitcast.40, ...), custom_call_target="tpu_custom_call" | custom-call | flops 130000000 | bytes 1000 | tf_op jit(solution)/shard_map/norm_project/pallas_call | solution.py:219
  105.3 1.1 collective-permute-done.17.refs_3_
  106.4 1.2 copy-done.5
  107.6 4.0 %attend.5 = (f32[4,2,512,128]{3,2,1,0:T(8,128)S(1)}, f32[4,2,512,128]{3,2,1,0:T(8,128)S(1)}) custom-call(bf16[512,512]{1,0:T(8,128)(2,1)S(1)} %get-tuple-element.51.refs_0_, bf16[2,512,512]{2,1,0:T(8,128)(2,1)S(1)} %copy-done.5, bf16[2,512,512]{2,1,0:T(8,128)(2,1)S(1)} %copy-done.5), custom_call_target="tpu_custom_call" | custom-call | flops 84000000 | bytes 1000 | tf_op jit(solution)/shard_map/attend/pallas_call | solution.py:392
  111.7 4.0 %collective-permute-done.18.refs_2_ = bf16[1,512,512]{2,1,0:T(8,128)(2,1)} collective-permute-done((bf16[1,512,512]{2,1,0:T(8,128)(2,1)}, bf16[1,512,512]{2,1,0:T(8,128)(2,1)}, u32[]{:S(2)}, u32[]{:S(2)}) %collective-permute-start.18) | collective-permute-done | bytes 524320 | tf_op jit(solution)/shard_map/ppermute | solution.py:456
  115.7 1.2 collective-permute-done.19.refs_4_
  116.9 0.5 collective-permute-start.21
  117.4 1.5 collective-permute-start.20
  118.9 7.5 %attend.6 = (f32[4,2,512,128]{3,2,1,0:T(8,128)S(1)}, f32[4,2,512,128]{3,2,1,0:T(8,128)S(1)}) custom-call(bf16[512,512]{1,0:T(8,128)(2,1)S(1)} %get-tuple-element.51.refs_0_, bf16[1,512,512]{2,1,0:T(8,128)(2,1)} %collective-permute-done.2.refs_1_, bf16[1,512,512]{2,1,0:T(8,128)(2,1)} %collective-permute-done.refs_2_, bf16[1,512,512]{2,1,0:T(8,128)(2,1)S(1)} %copy-done.9, ...), custom_call_target="tpu_custom_call" | custom-call | flops 148000000 | bytes 1000 | tf_op jit(solution)/shard_map/attend/pallas_call | solution.py:392
  126.5 7.6 %attend.7 = (f32[4,2,512,128]{3,2,1,0:T(8,128)S(1)}, f32[4,2,512,128]{3,2,1,0:T(8,128)S(1)}) custom-call(bf16[512,512]{1,0:T(8,128)(2,1)S(1)} %get-tuple-element.51.refs_0_, bf16[1,512,512]{2,1,0:T(8,128)(2,1)} %collective-permute-done.4.refs_1_, bf16[1,512,512]{2,1,0:T(8,128)(2,1)} %collective-permute-done.13.refs_2_, ...), custom_call_target="tpu_custom_call" | custom-call | flops 148000000 | bytes 1000 | tf_op jit(solution)/shard_map/attend/pallas_call | solution.py:392
  134.1 7.6 %attend.8 = (f32[4,2,512,128]{3,2,1,0:T(8,128)S(1)}, f32[4,2,512,128]{3,2,1,0:T(8,128)S(1)}) custom-call(bf16[512,512]{1,0:T(8,128)(2,1)S(1)} %get-tuple-element.51.refs_0_, bf16[1,512,512]{2,1,0:T(8,128)(2,1)S(1)} %collective-permute-done.16.refs_1_, bf16[1,512,512]{2,1,0:T(8,128)(2,1)} %collective-permute-done.18.refs_2_, ...), custom_call_target="tpu_custom_call" | custom-call | flops 148000000 | bytes 1000 | tf_op jit(solution)/shard_map/attend/pallas_call | solution.py:392
  141.7 5.4 %attend.9 = (bf16[2,4,320,128]{3,2,1,0:T(8,128)(2,1)S(1)}, f32[2,4,320,128]{3,2,1,0:T(8,128)S(1)}) custom-call(bf16[512,512]{1,0:T(8,128)(2,1)S(1)} %get-tuple-element.51.refs_0_, bf16[1,512,512]{2,1,0:T(8,128)(2,1)S(1)} %collective-permute-done.20.refs_1_, bf16[1,512,512]{2,1,0:T(8,128)(2,1)S(1)} %collective-permute-done.21.refs_2_, ...), custom_call_target="tpu_custom_call" | custom-call | flops 84000000 | bytes 1000 | tf_op jit(solution)/shard_map/attend/pallas_call | solution.py:392
  147.3 1.0 parity_split.1.resid_ref
  148.3 1.1 collective-permute-done.22.refs_1_
  149.5 2.1 %collective-permute-start.23 = (bf16[4,320,128]{2,1,0:T(8,128)(2,1)S(1)}, bf16[4,320,128]{2,1,0:T(8,128)(2,1)S(1)}, u32[]{:S(2)}, u32[]{:S(2)}) collective-permute-start(bf16[4,320,128]{2,1,0:T(8,128)(2,1)S(1)} %branch_out.2), channel_id=1, source_target_pairs={{0,16},{16,0},{1,17},{17,1},{2,18},{18,2},{3,19},{19,3},{4,20},{20... | collective-permute-start | bytes 983048 | tf_op jit(solution)/shard_map/ppermute | solution.py:29
  151.6 1.3 copy-done.4
  153.0 6.6 %collective-permute-done.23 = bf16[4,320,128]{2,1,0:T(8,128)(2,1)S(1)} collective-permute-done((bf16[4,320,128]{2,1,0:T(8,128)(2,1)S(1)}, bf16[4,320,128]{2,1,0:T(8,128)(2,1)S(1)}, u32[]{:S(2)}, u32[]{:S(2)}) %collective-permute-start.23) | collective-permute-done | bytes 327712 | tf_op jit(solution)/shard_map/ppermute | solution.py:29
  159.6 0.9 fusion.3
  (74 shorter events, 1.2 us)
Async XLA Ops:
  0.6 62.3 %copy-start = (bf16[320,640]{1,0:T(8,128)(2,1)S(1)}, bf16[320,640]{1,0:T(8,128)(2,1)}, u32[]{:S(2)}) copy-start(bf16[320,640]{1,0:T(8,128)(2,1)} %param.15) | copy-start | bytes 1228804
  0.6 16.3 %copy-start.13 = (bf16[1,2,4,128,512]{4,3,2,1,0:T(8,128)(2,1)S(1)}, bf16[1,2,4,128,512]{4,3,2,1,0:T(8,128)(2,1)}, u32[]{:S(2)}) copy-start(bf16[1,2,4,128,512]{4,3,2,1,0:T(8,128)(2,1)} %param.13) | copy-start | bytes 3145732
  1.8 8.3 %collective-permute-start.6 = (bf16[1,640,128]{2,1,0:T(8,128)(2,1)S(1)}, bf16[1,640,128]{2,1,0:T(8,128)(2,1)S(1)}, u32[]{:S(2)}, u32[]{:S(2)}) collective-permute-start(bf16[1,640,128]{2,1,0:T(8,128)(2,1)S(1)} %get-tuple-element.80), channel_id=1, source_target_pairs={{0,2},{2,4},{4,6},{6,8},{8,10},{10,12},{12,14},{1,3},{3,5},{5,7},{... | collective-permute-start | bytes 491528 | tf_op jit(solution)/shard_map/ppermute | solution.py:441
  6.6 7.6 %collective-permute-start.7 = (bf16[1,640,128]{2,1,0:T(8,128)(2,1)S(1)}, bf16[1,640,128]{2,1,0:T(8,128)(2,1)S(1)}, u32[]{:S(2)}, u32[]{:S(2)}) collective-permute-start(bf16[1,640,128]{2,1,0:T(8,128)(2,1)S(1)} %get-tuple-element.81), channel_id=1, source_target_pairs={{2,0},{4,2},{6,4},{8,6},{10,8},{12,10},{14,12},{3,1},{5,3},{7,5},{... | collective-permute-start | bytes 491528 | tf_op jit(solution)/shard_map/ppermute | solution.py:442
  15.4 5.5 %copy-start.15 = (bf16[640]{0:T(1024)(128)(2,1)S(1)}, bf16[640]{0:T(1024)(128)(2,1)}, u32[]{:S(2)}) copy-start(bf16[640]{0:T(1024)(128)(2,1)} %param.16) | copy-start | bytes 3844
  15.4 5.5 %copy-start.16 = (bf16[640]{0:T(1024)(128)(2,1)S(1)}, bf16[640]{0:T(1024)(128)(2,1)}, u32[]{:S(2)}) copy-start(bf16[640]{0:T(1024)(128)(2,1)} %param.17) | copy-start | bytes 3844
  15.4 5.5 %copy-start.17 = (bf16[640]{0:T(1024)(128)(2,1)S(1)}, bf16[640]{0:T(1024)(128)(2,1)}, u32[]{:S(2)}) copy-start(bf16[640]{0:T(1024)(128)(2,1)} %param.20) | copy-start | bytes 3844
  15.4 5.5 %copy-start.18 = (bf16[640]{0:T(1024)(128)(2,1)S(1)}, bf16[640]{0:T(1024)(128)(2,1)}, u32[]{:S(2)}) copy-start(bf16[640]{0:T(1024)(128)(2,1)} %param.21) | copy-start | bytes 3844
  15.5 8.1 %copy-start.11 = (bf16[1,4,640,128]{3,2,1,0:T(8,128)(2,1)S(1)}, bf16[1,4,640,128]{3,2,1,0:T(8,128)(2,1)}, u32[]{:S(2)}) copy-start(bf16[1,4,640,128]{3,2,1,0:T(8,128)(2,1)} %param.12) | copy-start | bytes 1966084
  15.5 23.8 %collective-permute-start.10 = (bf16[6,640,128]{2,1,0:T(8,128)(2,1)S(1)}, bf16[6,640,128]{2,1,0:T(8,128)(2,1)}, u32[]{:S(2)}, u32[]{:S(2)}) collective-permute-start(bf16[6,640,128]{2,1,0:T(8,128)(2,1)S(1)} %pad_maximum_fusion.refs_0_), channel_id=1, source_target_pairs={{1,17},{16,0},{3,19},{18,2},{5,21},{20,4},{7,23},{22,6},{9,25},{24... | collective-permute-start | bytes 2949128 | tf_op jit(solution)/shard_map/ppermute | solution.py:67
  18.0 21.3 %collective-permute-start.2 = (bf16[1,512,512]{2,1,0:T(8,128)(2,1)}, bf16[1,512,512]{2,1,0:T(8,128)(2,1)}, u32[]{:S(2)}, u32[]{:S(2)}) collective-permute-start(bf16[1,512,512]{2,1,0:T(8,128)(2,1)} %bitcast.11), channel_id=1, source_target_pairs={{0,4},{4,8},{8,12},{12,14},{14,10},{10,6},{6,2},{2,0},{1,5},{5,9},... | collective-permute-start | bytes 1572872 | tf_op jit(solution)/shard_map/ppermute | solution.py:456
  20.9 18.4 %collective-permute-start.3 = (bf16[1,512,512]{2,1,0:T(8,128)(2,1)}, bf16[1,512,512]{2,1,0:T(8,128)(2,1)S(1)}, u32[]{:S(2)}, u32[]{:S(2)}) collective-permute-start(bf16[1,512,512]{2,1,0:T(8,128)(2,1)} %bitcast.11), channel_id=1, source_target_pairs={{4,0},{8,4},{12,8},{14,12},{10,14},{6,10},{2,6},{0,2},{5,1},{9,5},... | collective-permute-start | bytes 1572872 | tf_op jit(solution)/shard_map/ppermute | solution.py:458
  21.0 21.5 %collective-permute-start.9 = (bf16[4,640]{1,0:T(4,128)(2,1)S(1)}, bf16[4,640]{1,0:T(4,128)(2,1)S(1)}, u32[]{:S(2)}, u32[]{:S(2)}) collective-permute-start(bf16[4,640]{1,0:T(4,128)(2,1)S(1)} %pad_maximum_fusion.1), channel_id=1, source_target_pairs={{0,1},{1,0},{2,3},{3,2},{4,5},{5,4},{6,7},{7,6},{8,9},{9,8},{10,11... | collective-permute-start | bytes 15368 | tf_op jit(solution)/shard_map/ppermute | solution.py:29
  25.1 17.4 %all-to-all-start = ((f32[32,1,128]{2,1,0:T(1,128)}), f32[32,1,128]{2,1,0:T(1,128)S(1)}, u32[]{:S(2)}, u32[]{:S(2)}) async-start(f32[32,1,128]{2,1,0:T(1,128)} %broadcast_in_dim.21), calls=%async_computation | async-start | bytes 32768 | tf_op jit(solution)/shard_map/all_to_all | solution.py:52
  39.3 9.9 %copy-start.7 = (bf16[1,512,512]{2,1,0:T(8,128)(2,1)}, bf16[1,512,512]{2,1,0:T(8,128)(2,1)S(1)}, u32[]{:S(2)}) copy-start(bf16[1,512,512]{2,1,0:T(8,128)(2,1)S(1)} %collective-permute-done.3.refs_3_) | copy-start | bytes 1572868
  39.3 10.0 %collective-permute-start.11 = (bf16[6,640,128]{2,1,0:T(8,128)(2,1)}, bf16[6,640,128]{2,1,0:T(8,128)(2,1)}, u32[]{:S(2)}, u32[]{:S(2)}) collective-permute-start(bf16[6,640,128]{2,1,0:T(8,128)(2,1)} %collective-permute-done.10.refs_0_), channel_id=1, source_target_pairs={{0,1},{17,16},{2,3},{19,18},{4,5},{21,20},{6,7},{23,22},{8,9},{25,... | collective-permute-start | bytes 2949128 | tf_op jit(solution)/shard_map/ppermute | solution.py:70
  42.5 19.8 %collective-permute-start = (bf16[1,512,512]{2,1,0:T(8,128)(2,1)}, bf16[1,512,512]{2,1,0:T(8,128)(2,1)}, u32[]{:S(2)}, u32[]{:S(2)}) collective-permute-start(bf16[1,512,512]{2,1,0:T(8,128)(2,1)} %bitcast.45), channel_id=1, source_target_pairs={{0,4},{4,8},{8,12},{12,14},{14,10},{10,6},{6,2},{2,0},{1,5},{5,9},... | collective-permute-start | bytes 1572872 | tf_op jit(solution)/shard_map/ppermute | solution.py:456
  44.3 33.1 %collective-permute-start.8 = (bf16[6,640,128]{2,1,0:T(8,128)(2,1)S(1)}, bf16[6,640,128]{2,1,0:T(8,128)(2,1)}, u32[]{:S(2)}, u32[]{:S(2)}) collective-permute-start(bf16[6,640,128]{2,1,0:T(8,128)(2,1)S(1)} %pad_maximum_fusion.refs_0_), channel_id=1, source_target_pairs={{0,1},{17,16},{2,3},{19,18},{4,5},{21,20},{6,7},{23,22},{8,9},{25,... | collective-permute-start | bytes 2949128 | tf_op jit(solution)/shard_map/ppermute | solution.py:69
  47.1 16.1 %collective-permute-start.1 = (bf16[1,512,512]{2,1,0:T(8,128)(2,1)}, bf16[1,512,512]{2,1,0:T(8,128)(2,1)}, u32[]{:S(2)}, u32[]{:S(2)}) collective-permute-start(bf16[1,512,512]{2,1,0:T(8,128)(2,1)} %bitcast.46), channel_id=1, source_target_pairs={{4,0},{8,4},{12,8},{14,12},{10,14},{6,10},{2,6},{0,2},{5,1},{9,5},... | collective-permute-start | bytes 1572872 | tf_op jit(solution)/shard_map/ppermute | solution.py:458
  47.5 18.9 %collective-permute-start.4 = (bf16[1,512,512]{2,1,0:T(8,128)(2,1)}, bf16[1,512,512]{2,1,0:T(8,128)(2,1)}, u32[]{:S(2)}, u32[]{:S(2)}) collective-permute-start(bf16[1,512,512]{2,1,0:T(8,128)(2,1)} %collective-permute-done.2.refs_1_), channel_id=1, source_target_pairs={{0,4},{4,8},{8,12},{12,14},{14,10},{10,6},{6,2},{2,0},{1,5},{5,9},... | collective-permute-start | bytes 1572872 | tf_op jit(solution)/shard_map/ppermute | solution.py:456
  49.4 3.1 %copy-start.1 = (bf16[3,3,640,640]{3,2,1,0:T(8,128)(2,1)S(1)}, bf16[3,3,640,640]{3,2,1,0:T(8,128)(2,1)}, u32[]{:S(2)}) copy-start(bf16[3,3,640,640]{3,2,1,0:T(8,128)(2,1)} %refs_3_.3) | copy-start | bytes 22118404
  52.4 9.9 %copy-start.8 = (bf16[1,512,512]{2,1,0:T(8,128)(2,1)S(1)}, bf16[1,512,512]{2,1,0:T(8,128)(2,1)}, u32[]{:S(2)}) copy-start(bf16[1,512,512]{2,1,0:T(8,128)(2,1)} %copy-done.7) | copy-start | bytes 1572868
  52.5 15.6 %copy-start.14 = (bf16[640]{0:T(1024)(128)(2,1)S(1)}, bf16[640]{0:T(1024)(128)(2,1)}, u32[]{:S(2)}) copy-start(bf16[640]{0:T(1024)(128)(2,1)} %param.19) | copy-start | bytes 3844
  61.6 27.7 %collective-permute-start.12 = (bf16[4,640,128]{2,1,0:T(8,128)(2,1)S(1)}, bf16[4,640,128]{2,1,0:T(8,128)(2,1)S(1)}, u32[]{:S(2)}, u32[]{:S(2)}) collective-permute-start(bf16[4,640,128]{2,1,0:T(8,128)(2,1)S(1)} %norm_conv.3), channel_id=1, source_target_pairs={{0,16},{16,0},{1,17},{17,1},{2,18},{18,2},{3,19},{19,3},{4,20},{20... | collective-permute-start | bytes 1966088 | tf_op jit(solution)/shard_map/ppermute | solution.py:29
  62.4 15.0 %collective-permute-start.5 = (bf16[1,512,512]{2,1,0:T(8,128)(2,1)S(1)}, bf16[1,512,512]{2,1,0:T(8,128)(2,1)}, u32[]{:S(2)}, u32[]{:S(2)}) collective-permute-start(bf16[1,512,512]{2,1,0:T(8,128)(2,1)S(1)} %copy-done.8), channel_id=1, source_target_pairs={{4,0},{8,4},{12,8},{14,12},{10,14},{6,10},{2,6},{0,2},{5,1},{9,5},... | collective-permute-start | bytes 1572872 | tf_op jit(solution)/shard_map/ppermute | solution.py:458
  63.3 28.6 %collective-permute-start.13 = (bf16[1,512,512]{2,1,0:T(8,128)(2,1)}, bf16[1,512,512]{2,1,0:T(8,128)(2,1)}, u32[]{:S(2)}, u32[]{:S(2)}) collective-permute-start(bf16[1,512,512]{2,1,0:T(8,128)(2,1)} %collective-permute-done.refs_2_), channel_id=1, source_target_pairs={{0,4},{4,8},{8,12},{12,14},{14,10},{10,6},{6,2},{2,0},{1,5},{5,9},... | collective-permute-start | bytes 1572872 | tf_op jit(solution)/shard_map/ppermute | solution.py:456
  66.4 25.5 %collective-permute-start.14 = (bf16[1,512,512]{2,1,0:T(8,128)(2,1)}, bf16[1,512,512]{2,1,0:T(8,128)(2,1)}, u32[]{:S(2)}, u32[]{:S(2)}) collective-permute-start(bf16[1,512,512]{2,1,0:T(8,128)(2,1)} %collective-permute-done.1.refs_4_), channel_id=1, source_target_pairs={{4,0},{8,4},{12,8},{14,12},{10,14},{6,10},{2,6},{0,2},{5,1},{9,5},... | collective-permute-start | bytes 1572872 | tf_op jit(solution)/shard_map/ppermute | solution.py:458
  77.3 3.1 %copy-start.2 = (bf16[3,3,640,640]{3,2,1,0:T(8,128)(2,1)S(1)}, bf16[3,3,640,640]{3,2,1,0:T(8,128)(2,1)}, u32[]{:S(2)}) copy-start(bf16[3,3,640,640]{3,2,1,0:T(8,128)(2,1)} %refs_3_.3) | copy-start | bytes 22118404
  80.4 8.9 %copy-start.12 = (bf16[1,4,640,128]{3,2,1,0:T(8,128)(2,1)S(1)}, bf16[1,4,640,128]{3,2,1,0:T(8,128)(2,1)}, u32[]{:S(2)}) copy-start(bf16[1,4,640,128]{3,2,1,0:T(8,128)(2,1)} %param.12) | copy-start | bytes 1966084
  89.7 5.8 %collective-permute-start.15 = (bf16[4,640,128]{2,1,0:T(8,128)(2,1)S(1)}, bf16[4,640,128]{2,1,0:T(8,128)(2,1)}, u32[]{:S(2)}, u32[]{:S(2)}) collective-permute-start(bf16[4,640,128]{2,1,0:T(8,128)(2,1)S(1)} %add_convert_fusion.own_ref.refs_0_), channel_id=1, source_target_pairs={{0,1},{1,0},{2,3},{3,2},{4,5},{5,4},{6,7},{7,6},{8,9},{9,8},{10,11... | collective-permute-start | bytes 1966088 | tf_op jit(solution)/shard_map/ppermute | solution.py:29
  89.8 15.5 %collective-permute-start.16 = (bf16[1,512,512]{2,1,0:T(8,128)(2,1)}, bf16[1,512,512]{2,1,0:T(8,128)(2,1)S(1)}, u32[]{:S(2)}, u32[]{:S(2)}) collective-permute-start(bf16[1,512,512]{2,1,0:T(8,128)(2,1)} %collective-permute-done.4.refs_1_), channel_id=1, source_target_pairs={{0,4},{4,8},{8,12},{12,14},{14,10},{10,6},{6,2},{2,0},{1,5},{5,9},... | collective-permute-start | bytes 1572872 | tf_op jit(solution)/shard_map/ppermute | solution.py:456
  91.3 15.1 %collective-permute-start.17 = (bf16[1,512,512]{2,1,0:T(8,128)(2,1)}, bf16[1,512,512]{2,1,0:T(8,128)(2,1)}, u32[]{:S(2)}, u32[]{:S(2)}) collective-permute-start(bf16[1,512,512]{2,1,0:T(8,128)(2,1)} %collective-permute-done.5.refs_3_), channel_id=1, source_target_pairs={{4,0},{8,4},{12,8},{14,12},{10,14},{6,10},{2,6},{0,2},{5,1},{9,5},... | collective-permute-start | bytes 1572872 | tf_op jit(solution)/shard_map/ppermute | solution.py:458
  91.9 23.8 %collective-permute-start.18 = (bf16[1,512,512]{2,1,0:T(8,128)(2,1)}, bf16[1,512,512]{2,1,0:T(8,128)(2,1)}, u32[]{:S(2)}, u32[]{:S(2)}) collective-permute-start(bf16[1,512,512]{2,1,0:T(8,128)(2,1)} %collective-permute-done.13.refs_2_), channel_id=1, source_target_pairs={{0,4},{4,8},{8,12},{12,14},{14,10},{10,6},{6,2},{2,0},{1,5},{5,9},... | collective-permute-start | bytes 1572872 | tf_op jit(solution)/shard_map/ppermute | solution.py:456
  93.4 23.5 %collective-permute-start.19 = (bf16[1,512,512]{2,1,0:T(8,128)(2,1)}, bf16[1,512,512]{2,1,0:T(8,128)(2,1)}, u32[]{:S(2)}, u32[]{:S(2)}) collective-permute-start(bf16[1,512,512]{2,1,0:T(8,128)(2,1)} %collective-permute-done.14.refs_4_), channel_id=1, source_target_pairs={{4,0},{8,4},{12,8},{14,12},{10,14},{6,10},{2,6},{0,2},{5,1},{9,5},... | collective-permute-start | bytes 1572872 | tf_op jit(solution)/shard_map/ppermute | solution.py:458
  95.5 2.1 %copy-start.6 = (bf16[1280,3,512]{2,0,1:T(8,128)(2,1)S(1)}, bf16[1280,3,512]{2,0,1:T(8,128)(2,1)}, u32[]{:S(2)}) copy-start(bf16[1280,3,512]{2,0,1:T(8,128)(2,1)} %param.22) | copy-start | bytes 11796484
  97.6 0.7 copy-start.10
  106.4 1.2 copy-start.5
  107.6 11.3 %copy-start.9 = (bf16[1,512,512]{2,1,0:T(8,128)(2,1)S(1)}, bf16[1,512,512]{2,1,0:T(8,128)(2,1)}, u32[]{:S(2)}) copy-start(bf16[1,512,512]{2,1,0:T(8,128)(2,1)} %copy-done.7) | copy-start | bytes 1572868
  116.9 24.8 %collective-permute-start.21 = (bf16[1,512,512]{2,1,0:T(8,128)(2,1)}, bf16[1,512,512]{2,1,0:T(8,128)(2,1)S(1)}, u32[]{:S(2)}, u32[]{:S(2)}) collective-permute-start(bf16[1,512,512]{2,1,0:T(8,128)(2,1)} %collective-permute-done.19.refs_4_), channel_id=1, source_target_pairs={{4,0},{8,4},{12,8},{14,12},{10,14},{6,10},{2,6},{0,2},{5,1},{9,5},... | collective-permute-start | bytes 1572872 | tf_op jit(solution)/shard_map/ppermute | solution.py:458
  117.4 24.3 %collective-permute-start.20 = (bf16[1,512,512]{2,1,0:T(8,128)(2,1)S(1)}, bf16[1,512,512]{2,1,0:T(8,128)(2,1)S(1)}, u32[]{:S(2)}, u32[]{:S(2)}) collective-permute-start(bf16[1,512,512]{2,1,0:T(8,128)(2,1)S(1)} %collective-permute-done.16.refs_1_), channel_id=1, source_target_pairs={{0,4},{4,8},{8,12},{12,14},{14,10},{10,6},{6,2},{2,0},{1,5},{5,9},... | collective-permute-start | bytes 1572872 | tf_op jit(solution)/shard_map/ppermute | solution.py:456
  147.2 2.3 %copy-start.3 = (f32[2,4,320,128]{3,2,1,0:T(8,128)}, f32[2,4,320,128]{3,2,1,0:T(8,128)S(1)}, u32[]{:S(2)}) copy-start(f32[2,4,320,128]{3,2,1,0:T(8,128)S(1)} %get-tuple-element.64.refs_0_) | copy-start | bytes 3932164
  147.2 2.2 %collective-permute-start.22 = (bf16[2,4,320,128]{3,2,1,0:T(8,128)(2,1)S(1)}, bf16[2,4,320,128]{3,2,1,0:T(8,128)(2,1)S(1)}, u32[]{:S(2)}, u32[]{:S(2)}) collective-permute-start(bf16[2,4,320,128]{3,2,1,0:T(8,128)(2,1)S(1)} %get-tuple-element.65), channel_id=1, source_target_pairs={{0,1},{1,0},{2,3},{3,2},{4,5},{5,4},{6,7},{7,6},{8,9},{9,8},{10,11... | collective-permute-start | bytes 1966088 | tf_op jit(solution)/shard_map/ppermute | solution.py:29
  149.5 10.1 %collective-permute-start.23 = (bf16[4,320,128]{2,1,0:T(8,128)(2,1)S(1)}, bf16[4,320,128]{2,1,0:T(8,128)(2,1)S(1)}, u32[]{:S(2)}, u32[]{:S(2)}) collective-permute-start(bf16[4,320,128]{2,1,0:T(8,128)(2,1)S(1)} %branch_out.2), channel_id=1, source_target_pairs={{0,16},{16,0},{1,17},{17,1},{2,18},{18,2},{3,19},{19,3},{4,20},{20... | collective-permute-start | bytes 983048 | tf_op jit(solution)/shard_map/ppermute | solution.py:29
  151.6 1.3 copy-start.4

commit v5 on v4

--- a/solution.py
+++ b/solution.py
@@ -17,7 +17,8 @@
 epsilon = 1e-05
 guidance = 5.0
 SCORE_SCALE = 1.0 / math.sqrt(HD)
-VMEM_LIMIT = 32 * 1024 * 1024
+MIB = 1024 * 1024
+VMEM_LIMIT = 32 * MIB
 COST_SHARE = 0.02
 
 
@@ -56,7 +57,7 @@
     return lax.optimization_barrier((array,) + tuple(others))[0]
 
 
-def halves_of_inputs(own, others):
+def halves_of_inputs(own):
     cfg = lax.axis_index("cfg")
     if lax.axis_size("tp") != 2:
         full = lax.all_gather(own, "tp", axis=1, tiled=True)
@@ -66,8 +67,8 @@
         return [mine], [swapped(sent, "cfg")]
     across = lax.ppermute(own, ("cfg", "tp"), [(1, 3), (2, 0)])
     pairs = [(0, 1), (3, 2)]
-    own_side = lax.ppermute(need(own, others), ("cfg", "tp"), pairs)
-    across_side = lax.ppermute(need(across, others), ("cfg", "tp"), pairs)
+    own_side = lax.ppermute(own, ("cfg", "tp"), pairs)
+    across_side = lax.ppermute(across, ("cfg", "tp"), pairs)
     return [own, own_side], [across, across_side]
 
 
@@ -152,19 +153,24 @@
             pltpu.VMEM((3 * ins, rows * LANES), jnp.bfloat16),
             pltpu.SemaphoreType.DMA((3, 3)),
         ],
-        compiler_params=pltpu.CompilerParams(vmem_limit_bytes=VMEM_LIMIT),
+        compiler_params=pltpu.CompilerParams(vmem_limit_bytes=57 * MIB),
         cost_estimate=cost(9000),
         name="norm_conv",
     )(flags, sums, *xs, affine, conv_w)
 
 
-def split_kernel(own_ref, split_ref):
-    rows, channels, _ = own_ref.shape
+def parity_matrix(channels):
     half = channels // 2
     to = lax.broadcasted_iota(jnp.int32, (channels, channels), 0)
     source = lax.broadcasted_iota(jnp.int32, (channels, channels), 1)
     wanted = jnp.where(to < half, 2 * to, 2 * (to - half) + 1)
-    chosen = (source == wanted).astype(jnp.bfloat16)
+    return (source == wanted).astype(jnp.bfloat16)
+
+
+def split_kernel(own_ref, split_ref):
+    rows, channels, _ = own_ref.shape
+    half = channels // 2
+    chosen = parity_matrix(channels)
     for r in range(rows):
         y = jnp.dot(chosen, own_ref[r], preferred_element_type=jnp.float32).astype(jnp.bfloat16)
         split_ref[0, r] = y[:half]
@@ -182,6 +188,35 @@
         cost_estimate=cost(1000),
         name="parity_split",
     )(own)
+
+
+def arrange_kernel(flip_ref, w_ref, out_ref):
+    count, channels, _ = out_ref.shape
+    chosen = parity_matrix(channels)
+    for i in range(count):
+        y = lax.dot_general(
+            chosen,
+            w_ref[:, i * channels : (i + 1) * channels],
+            (((1,), (1,)), ((), ())),
+            preferred_element_type=jnp.float32,
+        )
+        out_ref[jnp.where(flip_ref[0] == 1, count - 1 - i, i)] = y.astype(jnp.bfloat16)
+
+
+def arrange_call(flip, w_out, count):
+    features, channels = w_out.shape
+    return pl.pallas_call(
+        arrange_kernel,
+        in_specs=[
+            pl.BlockSpec(memory_space=pltpu.SMEM),
+            pl.BlockSpec(memory_space=pltpu.VMEM),
+        ],
+        out_specs=pl.BlockSpec(memory_space=pltpu.VMEM),
+        out_shape=jax.ShapeDtypeStruct((count, channels // count, features), jnp.bfloat16),
+        compiler_params=pltpu.CompilerParams(vmem_limit_bytes=VMEM_LIMIT),
+        cost_estimate=cost(2000),
+        name="arrange",
+    )(flip.astype(jnp.int32).reshape(1), w_out)
 
 
 def project_kernel(parts, order_ref, *refs):
@@ -233,7 +268,7 @@
             pltpu.VMEM((positions, depth), jnp.bfloat16),
             pltpu.SemaphoreType.DMA((3,)),
         ],
-        compiler_params=pltpu.CompilerParams(vmem_limit_bytes=VMEM_LIMIT),
+        compiler_params=pltpu.CompilerParams(vmem_limit_bytes=60 * MIB),
         cost_estimate=cost(6500),
         name="norm_project",
     )(order, *parts, affine, w)
@@ -442,32 +477,30 @@
     after = lax.ppermute(latent_rows[:1], "rows", down_pairs)
     rimmed = jnp.concatenate([before, latent_rows, after], axis=0)
 
+    x_mine, x_other = halves_of_inputs(rimmed)
+
     forward, backward = ring_pairs(rows_count)
     last = rows_count // 2
-    stale = stale_kv[0].reshape(2, 1, positions, -1)
-    hops = [[(stale[which], stale[which])] for which in range(2)]
-
-    def next_hop(which, *after):
-        ahead, behind = hops[which][-1]
+    pair = stale_kv[0].reshape(2, positions, -1)
+    hops = [(pair, pair)]
+
+    def next_hop(*after):
+        ahead, behind = hops[-1]
+        if len(hops) == last:
+            ahead, behind = ahead[:1], behind[1:]
         if after:
             ahead, behind, *_ = lax.optimization_barrier((ahead, behind) + after)
-        final = len(hops[which]) == last
-        if not (final and which == 1):
-            ahead = lax.ppermute(ahead, "rows", forward)
-        if not (final and which == 0):
-            behind = lax.ppermute(behind, "rows", backward)
-        hops[which].append((ahead, behind))
+        hops.append(
+            (lax.ppermute(ahead, "rows", forward), lax.ppermute(behind, "rows", backward))
+        )
 
     def blocks_of(hop):
-        keys, values = hops[0][hop], hops[1][hop]
+        ahead, behind = hops[hop]
         if hop == last:
-            return [((keys[0], 0), (values[1], 0))]
-        return [((keys[0], 0), (values[0], 0)), ((keys[1], 0), (values[1], 0))]
-
-    next_hop(0)
-    x_mine, x_other = halves_of_inputs(rimmed, hops[0][1])
-    next_hop(1, table)
-    next_hop(0, table)
+            return [((ahead, 0), (behind, 0))]
+        return [((ahead, 0), (ahead, 1)), ((behind, 0), (behind, 1))]
+
+    next_hop()
 
     vectors = gather_tp(jnp.stack([gn_gain, gn_bias, ln_gain, ln_bias]), 1).astype(jnp.float32)
     amount = span_rows * rows_count * grid_width * group_width
@@ -481,16 +514,14 @@
 
     local_features = w_qkv.shape[2]
     w_project = w_qkv.transpose(1, 0, 2)
-    w_back = w_out.T.reshape(tp_count, local_channels // 2, 2, local_features)
-    w_back = w_back.transpose(0, 2, 1, 3).reshape(tp_count, local_channels, local_features)
-    if tp_count == 2:
-        w_back = jnp.where(tp == 0, w_back[::-1], w_back)
+    flip = jnp.logical_and(tp_count == 2, tp == 0)
+    w_back = arrange_call(flip, w_out, tp_count)
     gn_affine, w_back = lax.optimization_barrier((gn_affine, w_back))
 
+    flags_other = need(flags_other, hops[1])
     conv_sent = conv_call(flags_other, table, amount, x_other, gn_affine, conv_w, jnp.bfloat16)
     conv_received = swapped(conv_sent, "cfg")
-    next_hop(1, conv_sent)
-    flags_mine = need(flags_mine, hops[1][1] + hops[0][2])
+    next_hop()
     conv_own = conv_call(flags_mine, table, amount, x_mine, gn_affine, conv_w, jnp.float32)
 
     half_width = TEMB // 2
@@ -507,34 +538,29 @@
         latent32 + (conv_own + conv_received.astype(jnp.float32) + bias[None, :, None])
     ).astype(jnp.bfloat16)
 
-    next_hop(0, conv_sent)
     if tp_count == 2:
-        parts = [resid, swapped(resid, "tp")]
+        parts = [resid, need(swapped(resid, "tp"), hops[2])]
         order = jnp.stack([tp, 1 - tp]).astype(jnp.int32)
     else:
         parts = [lax.all_gather(resid, "tp", axis=1, tiled=True)]
         order = jnp.zeros((1,), jnp.int32)
-    next_hop(1, resid)
-    order = need(order, hops[1][2])
+    next_hop(resid)
     queries, fresh = project_call(order, parts, ln_affine, w_project)
-    while len(hops[0]) <= last:
-        next_hop(0, queries)
     resid_split = split_call(resid)
     fresh_kv = fresh.reshape(1, 2, span_rows, grid_width, local_features)
 
-    queries = need(queries, hops[0][3])
-    state = attention_call(queries, [((fresh, 0), (fresh, 1))], None)
-    while len(hops[1]) <= last:
-        next_hop(1, state[0])
-    for hop in range(1, last):
-        if hop == 2:
-            queries = need(queries, hops[1][3])
-        state = attention_call(queries, blocks_of(hop), state)
+    group = [((fresh, 0), (fresh, 1))] + blocks_of(1)
+    state = None
+    for hop in range(2, last + 1):
+        state = attention_call(queries, group, state)
+        while len(hops) <= last:
+            next_hop(state[0])
+        group = blocks_of(hop)
     if tp_count == 2:
-        sent, kept_terms = attention_call(queries, blocks_of(last), state, w_back, True)
+        sent, kept_terms = attention_call(queries, group, state, w_back, True)
         terms = (kept_terms, swapped(sent, "tp"))
     else:
-        (sent,) = attention_call(queries, blocks_of(last), state, w_back)
+        (sent,) = attention_call(queries, group, state, w_back)
         terms = (lax.psum_scatter(sent, "tp", scatter_dimension=0),)
 
     other_branch = swapped(branch_call(1 - cfg, resid_split, terms), "cfg")

time: 161 us -> 142 us (0.88)
  local copies, waits for them, and re-layouts: 23.4 us -> 12.3 us
  starting transfers between devices: 39.6 us -> 31.9 us
  waiting for transfers between devices: 30.9 us -> 26 us
  Pallas kernels: 58.5 us -> 60.9 us
  other arithmetic: 6.02 us -> 8.15 us
    ppermute x16 -> x10, waiting for transfers between devices: 17 us -> 5.27 us  [the longest x4 4.98 us: next_hop(): lax.ppermute(ahead, 'rows', forward)]
    ppermute x16 -> x10, starting transfers between devices: 21.9 us -> 13.8 us  [the longest x4 5.9 us: next_hop(): lax.ppermute(ahead, 'rows', forward)]
    ppermute x5, waiting for transfers between devices: 7.67 us -> 12.6 us  [swapped(): lax.ppermute(array, axis, [(i, i ^ 1) for i in range(lax.axis_size(axis))])]
    transpose x2 -> x0, local copies, waits for them, and re-layouts: 3.7 us -> none  [the longest x1 2.43 us: per_device(): w_back = w_out.T.reshape(tp_count, local_channels // 2, 2, local_features)]
    reshape x1 -> x0, local copies, waits for them, and re-layouts: 3.09 us -> none  [per_device(): w_back = w_out.T.reshape(tp_count, local_channels // 2, 2, local_features)]
    pallas_call x5 -> x4, Pallas kernels: 32.2 us -> 29.2 us  [attention_call(): pl.pallas_call(functools.partial(attention_kernel, len(pairs), state is n...]
    pallas_call x2, Pallas kernels: 18.1 us -> 21 us  [conv_call(): pl.pallas_call(functools.partial(conv_kernel, len(xs), amount), in_specs=...]
    unnamed x39 -> x41, local copies, waits for them, and re-layouts: 11.7 us -> 9.01 us
  transfers between devices with their start and end apart: 25 -> 19, of which waited for: 9 -> 9; matrix products, arithmetic and copies ran while one was open for 9% -> 5% of each run, Pallas kernels for 33% -> 39%
where the time goes in v5:
time: 142 us; the launch traced here: 141 us
  Pallas kernels  60.9 us (43%)
  starting transfers between devices  31.9 us (22%)
  waiting for transfers between devices  26 us (18%)
  local copies, waits for them, and re-layouts  12.3 us (9%)
  other arithmetic  8.15 us (6%)
  between operations  1.79 us (1%)
    pallas_call x4, Pallas kernels, attention_call(): pl.pallas_call(functools.partial(attention_kernel, len(pairs), state is n...  29.2 us
    pallas_call x2, Pallas kernels, conv_call(): pl.pallas_call(functools.partial(conv_kernel, len(xs), amount), in_specs=...  21 us
    ppermute x5, waiting for transfers between devices, swapped(): lax.ppermute(array, axis, [(i, i ^ 1) for i in range(lax.axis_size(axis))])  12.6 us
    unnamed x41, local copies, waits for them, and re-layouts  9.01 us
    pallas_call x1, Pallas kernels, project_call(): pl.pallas_call(functools.partial(project_kernel, len(parts)), in_specs=[p...  8.31 us
    ppermute x4, starting transfers between devices, next_hop(): lax.ppermute(ahead, 'rows', forward)  5.9 us
    ppermute x5, starting transfers between devices, swapped(): lax.ppermute(array, axis, [(i, i ^ 1) for i in range(lax.axis_size(axis))])  5.5 us
    all_to_all x1, starting transfers between devices, summed(): return jnp.sum(lax.all_to_all(spread, axes, 0, 0, tiled=True), axis=0)  5.15 us
  transfers between devices with their start and end apart: 19, of which 9 were waited for; matrix products, arithmetic and copies ran while one was open for 5% of the time, Pallas kernels for 39%

profile of v5, /device:TPU:0, one launch (start us, length us, event | category | flops | bytes accessed | tf_op | source)
XLA Modules:
  0.0 141.4 jit_solution(12447028974784778296)
XLA Ops:
  0.7 1.1 slice_bitcast_fusion.1
  1.8 4.9 %collective-permute-start = (bf16[1,640,128]{2,1,0:T(8,128)(2,1)S(1)}, bf16[1,640,128]{2,1,0:T(8,128)(2,1)S(1)}, u32[]{:S(2)}, u32[]{:S(2)}) collective-permute-start(bf16[1,640,128]{2,1,0:T(8,128)(2,1)S(1)} %get-tuple-element.50), channel_id=1, source_target_pairs={{0,2},{2,4},{4,6},{6,8},{8,10},{10,12},{12,14},{1,3},{3,5},{5,7},{... | collective-permute-start | bytes 491528 | tf_op jit(solution)/shard_map/ppermute | solution.py:476
  6.7 1.3 collective-permute-start.1
  8.0 2.1 %collective-permute-done = bf16[1,640,128]{2,1,0:T(8,128)(2,1)S(1)} collective-permute-done((bf16[1,640,128]{2,1,0:T(8,128)(2,1)S(1)}, bf16[1,640,128]{2,1,0:T(8,128)(2,1)S(1)}, u32[]{:S(2)}, u32[]{:S(2)}) %collective-permute-start) | collective-permute-done | bytes 163872 | tf_op jit(solution)/shard_map/ppermute | solution.py:476
  10.1 4.1 %collective-permute-done.1 = bf16[1,640,128]{2,1,0:T(8,128)(2,1)S(1)} collective-permute-done((bf16[1,640,128]{2,1,0:T(8,128)(2,1)S(1)}, bf16[1,640,128]{2,1,0:T(8,128)(2,1)S(1)}, u32[]{:S(2)}, u32[]{:S(2)}) %collective-permute-start.1) | collective-permute-done | bytes 163872 | tf_op jit(solution)/shard_map/ppermute | solution.py:477
  14.2 2.1 %pad_maximum_fusion.refs_0_ = bf16[6,640,128]{2,1,0:T(8,128)(2,1)} fusion(bf16[1,640,128]{2,1,0:T(8,128)(2,1)S(1)} %collective-permute-done.1, bf16[4,640,128]{2,1,0:T(8,128)(2,1)} %bitcast.34, bf16[1,640,128]{2,1,0:T(8,128)(2,1)S(1)} %collective-permute-done), kind=kLoop, calls=%fused_computation.5 | loop fusion | flops 983040 | bytes 1966080 | tf_op jit(solution)/shard_map/concatenate | solution.py:478
  16.4 1.3 collective-permute-start.6
  17.6 2.9 %collective-permute-start.4 = (bf16[2,512,512]{2,1,0:T(8,128)(2,1)}, bf16[2,512,512]{2,1,0:T(8,128)(2,1)S(1)}, u32[]{:S(2)}, u32[]{:S(2)}) collective-permute-start(bf16[2,512,512]{2,1,0:T(8,128)(2,1)} %bitcast.15), channel_id=1, source_target_pairs={{0,4},{4,8},{8,12},{12,14},{14,10},{10,6},{6,2},{2,0},{1,5},{5,9},... | collective-permute-start | bytes 3145736 | tf_op jit(solution)/shard_map/ppermute | solution.py:494
  20.7 2.5 %collective-permute-start.3 = (bf16[4,640]{1,0:T(4,128)(2,1)S(1)}, bf16[4,640]{1,0:T(4,128)(2,1)S(1)}, u32[]{:S(2)}, u32[]{:S(2)}) collective-permute-start(bf16[4,640]{1,0:T(4,128)(2,1)S(1)} %pad_maximum_fusion.1), channel_id=1, source_target_pairs={{0,1},{1,0},{2,3},{3,2},{4,5},{5,4},{6,7},{7,6},{8,9},{9,8},{10,11... | collective-permute-start | bytes 15368 | tf_op jit(solution)/shard_map/ppermute | solution.py:30
  23.2 0.3 convert_reduce_fusion
  23.5 0.1 reduce_sum.32
  23.5 0.1 reduce_sum.45
  23.6 0.1 reduce_sum.36
  23.7 0.1 reduce_sum.46
  23.9 0.1 dynamic_update_slice.3
  24.0 0.1 broadcast_in_dim.20
  24.1 0.6 broadcast_in_dim.21
  24.7 5.1 %all-to-all-start = ((f32[32,1,128]{2,1,0:T(1,128)}), f32[32,1,128]{2,1,0:T(1,128)S(1)}, u32[]{:S(2)}, u32[]{:S(2)}) async-start(f32[32,1,128]{2,1,0:T(1,128)} %broadcast_in_dim.21), calls=%async_computation | async-start | bytes 32768 | tf_op jit(solution)/shard_map/all_to_all | solution.py:53
  29.9 0.1 add_convert_fusion.1
  30.0 0.6 pad_add_fusion.1
  30.6 1.3 copy-done.11
  31.9 1.2 arrange.1.refs_5_
  33.1 1.1 copy-done.4
  34.2 3.1 %collective-permute-start.7 = (bf16[6,640,128]{2,1,0:T(8,128)(2,1)}, bf16[6,640,128]{2,1,0:T(8,128)(2,1)}, u32[]{:S(2)}, u32[]{:S(2)}) collective-permute-start(bf16[6,640,128]{2,1,0:T(8,128)(2,1)} %collective-permute-done.6.refs_0_), channel_id=1, source_target_pairs={{0,1},{17,16},{2,3},{19,18},{4,5},{21,20},{6,7},{23,22},{8,9},{25,... | collective-permute-start | bytes 2949128 | tf_op jit(solution)/shard_map/ppermute | solution.py:71
  37.3 1.4 collective-permute-start.2
  38.7 5.0 %collective-permute-done.4.refs_3_.refs_4_ = bf16[2,512,512]{2,1,0:T(8,128)(2,1)S(1)} collective-permute-done((bf16[2,512,512]{2,1,0:T(8,128)(2,1)}, bf16[2,512,512]{2,1,0:T(8,128)(2,1)S(1)}, u32[]{:S(2)}, u32[]{:S(2)}) %collective-permute-start.4) | collective-permute-done | bytes 1048608 | tf_op jit(solution)/shard_map/ppermute | solution.py:494
  43.7 1.3 collective-permute-start.10
  45.0 0.3 collective-permute-done.5.refs_5_.refs_6_
  45.2 1.0 collective-permute-start.11
  46.3 0.9 copy.30
  47.2 1.9 %all-to-all-done = f32[32,1,128]{2,1,0:T(1,128)S(1)} async-done(((f32[32,1,128]{2,1,0:T(1,128)}), f32[32,1,128]{2,1,0:T(1,128)S(1)}, u32[]{:S(2)}, u32[]{:S(2)}) %all-to-all-start) | async-done | bytes 16416 | tf_op jit(solution)/shard_map/all_to_all | solution.py:53
  49.1 0.5 reduce_sum.47.sums_ref
  49.6 10.4 %norm_conv.3 = bf16[4,640,128]{2,1,0:T(8,128)(2,1)} custom-call(s32[4]{0:T(128)} %get-tuple-element.21.flags_ref, f32[128]{0:T(128)} %reduce_sum.47.sums_ref, bf16[6,640,128]{2,1,0:T(8,128)(2,1)} %collective-permute-done.6.refs_0_, bf16[6,640,128]{2,1,0:T(8,128)(2,1)} %collective-permute-done.7.refs_1_, f32[640,2]{1,0:T(8,128)} %bitcast.36, ...), custom_call_target="tpu_custom_call" | custom-call | flops 180000000 | bytes 1000 | tf_op jit(solution)/shard_map/norm_conv/pallas_call | solution.py:141
  60.0 1.5 %collective-permute-start.8 = (bf16[4,640,128]{2,1,0:T(8,128)(2,1)}, bf16[4,640,128]{2,1,0:T(8,128)(2,1)S(1)}, u32[]{:S(2)}, u32[]{:S(2)}) collective-permute-start(bf16[4,640,128]{2,1,0:T(8,128)(2,1)} %norm_conv.3), channel_id=1, source_target_pairs={{0,16},{16,0},{1,17},{17,1},{2,18},{18,2},{3,19},{19,3},{4,20},{20... | collective-permute-start | bytes 1966088 | tf_op jit(solution)/shard_map/ppermute | solution.py:30
  62.3 0.1 divide_multiply_fusion
  62.4 0.3 convolution_reduce_fusion
  62.7 0.9 copy-done.14
  63.7 10.6 %norm_conv.2 = f32[4,640,128]{2,1,0:T(8,128)} custom-call(s32[4]{0:T(128)} %get-tuple-element.57.flags_ref, f32[128]{0:T(128)} %reduce_sum.47.sums_ref, bf16[6,640,128]{2,1,0:T(8,128)(2,1)} %pad_maximum_fusion.refs_0_, bf16[6,640,128]{2,1,0:T(8,128)(2,1)} %copy-done.14, f32[640,2]{1,0:T(8,128)} %bitcast.37, bf16[3,3,640,640]{3,2,1,0:T(8,128)(2,1)} %refs_3_.3), custom_call_target="tpu_custom_call" | custom-call | flops 180000000 | bytes 1000 | tf_op jit(solution)/shard_map/norm_conv/pallas_call | solution.py:141
  74.3 2.6 %collective-permute-done.8 = bf16[4,640,128]{2,1,0:T(8,128)(2,1)S(1)} collective-permute-done((bf16[4,640,128]{2,1,0:T(8,128)(2,1)}, bf16[4,640,128]{2,1,0:T(8,128)(2,1)S(1)}, u32[]{:S(2)}, u32[]{:S(2)}) %collective-permute-start.8) | collective-permute-done | bytes 655392 | tf_op jit(solution)/shard_map/ppermute | solution.py:30
  76.9 1.6 %add_convert_fusion.own_ref.refs_0_ = bf16[4,640,128]{2,1,0:T(8,128)(2,1)S(1)} fusion(f32[4,640,128]{2,1,0:T(8,128)} %norm_conv.2, bf16[4,640,128]{2,1,0:T(8,128)(2,1)S(1)} %collective-permute-done.8, f32[640]{0:T(1024)S(1)} %convert_add_fusion.1, bf16[1,4,640,128]{3,2,1,0:T(8,128)(2,1)S(1)} %copy-done.13), kind=kLoop, calls=%fused_computation.3 | loop fusion | flops 1966080 | bytes 3279360 | tf_op jit(solution)/shard_map/convert_element_type | solution.py:539
  78.5 0.9 collective-permute-start.12
  79.4 1.2 collective-permute-start.13
  80.6 0.7 pad_add_fusion.2.order_ref
  81.3 1.1 copy.28
  82.4 0.5 collective-permute-done.9.refs_1_
  82.8 8.3 %norm_project.1 = (bf16[512,512]{1,0:T(8,128)(2,1)}, bf16[2,512,512]{2,1,0:T(8,128)(2,1)}) custom-call(s32[2]{0:T(128)} %pad_add_fusion.2.order_ref, bf16[4,640,128]{2,1,0:T(8,128)(2,1)} %copy-done.2, bf16[4,640,128]{2,1,0:T(8,128)(2,1)} %collective-permute-done.9.refs_1_, f32[1280,2]{1,0:T(8,128)} %bitcast.38, bf16[3,1280,512]{2,1,0:T(8,128)(2,1)} %bitcast.35), custom_call_target="tpu_custom_call" | custom-call | flops 130000000 | bytes 1000 | tf_op jit(solution)/shard_map/norm_project/pallas_call | solution.py:254
  91.2 1.0 copy-done.1
  92.2 1.2 copy-done.7
  93.4 1.2 copy-done.9
  94.7 1.2 copy-done.10
  95.9 9.3 %attend.4 = (f32[4,2,512,128]{3,2,1,0:T(8,128)S(1)}, f32[4,2,512,128]{3,2,1,0:T(8,128)S(1)}) custom-call(bf16[512,512]{1,0:T(8,128)(2,1)S(1)} %copy-done.1, bf16[2,512,512]{2,1,0:T(8,128)(2,1)S(1)} %copy-done.10, bf16[2,512,512]{2,1,0:T(8,128)(2,1)S(1)} %copy-done.10, bf16[2,512,512]{2,1,0:T(8,128)(2,1)S(1)} %copy-done.7, ...), custom_call_target="tpu_custom_call" | custom-call | flops 212000000 | bytes 1000 | tf_op jit(solution)/shard_map/attend/pallas_call | solution.py:427
  105.3 0.9 collective-permute-start.14
  106.2 1.2 collective-permute-start.15
  107.4 7.6 %attend.5 = (f32[4,2,512,128]{3,2,1,0:T(8,128)S(1)}, f32[4,2,512,128]{3,2,1,0:T(8,128)S(1)}) custom-call(bf16[512,512]{1,0:T(8,128)(2,1)S(1)} %copy-done.1, bf16[2,512,512]{2,1,0:T(8,128)(2,1)} %collective-permute-done.10.refs_1_.refs_2_, bf16[2,512,512]{2,1,0:T(8,128)(2,1)} %collective-permute-done.10.refs_1_.refs_2_, ...), custom_call_target="tpu_custom_call" | custom-call | flops 148000000 | bytes 1000 | tf_op jit(solution)/shard_map/attend/pallas_call | solution.py:427
  115.0 6.9 %attend.6 = (f32[4,2,512,128]{3,2,1,0:T(8,128)S(1)}, f32[4,2,512,128]{3,2,1,0:T(8,128)S(1)}) custom-call(bf16[512,512]{1,0:T(8,128)(2,1)S(1)} %copy-done.1, bf16[2,512,512]{2,1,0:T(8,128)(2,1)S(1)} %collective-permute-done.12.refs_1_.refs_2_, bf16[2,512,512]{2,1,0:T(8,128)(2,1)S(1)} %collective-permute-done.12.refs_1_.refs_2_, ...), custom_call_target="tpu_custom_call" | custom-call | flops 148000000 | bytes 1000 | tf_op jit(solution)/shard_map/attend/pallas_call | solution.py:427
  121.9 5.5 %attend.7 = (bf16[2,4,320,128]{3,2,1,0:T(8,128)(2,1)S(1)}, f32[2,4,320,128]{3,2,1,0:T(8,128)S(1)}) custom-call(bf16[512,512]{1,0:T(8,128)(2,1)S(1)} %copy-done.1, bf16[1,512,512]{2,1,0:T(8,128)(2,1)S(1)} %collective-permute-done.14.refs_1_, bf16[1,512,512]{2,1,0:T(8,128)(2,1)S(1)} %collective-permute-done.15.refs_2_, ...), custom_call_target="tpu_custom_call" | custom-call | flops 84000000 | bytes 1000 | tf_op jit(solution)/shard_map/attend/pallas_call | solution.py:427
  127.3 0.1 collective-permute-start.16
  127.4 1.0 parity_split.1.resid_ref
  128.4 1.1 collective-permute-done.16.refs_1_
  129.5 0.1 branch_out.2
  129.6 1.4 collective-permute-start.17
  131.0 0.1 branch_out.3
  131.1 8.4 %collective-permute-done.17 = bf16[4,320,128]{2,1,0:T(8,128)(2,1)} collective-permute-done((bf16[4,320,128]{2,1,0:T(8,128)(2,1)S(1)}, bf16[4,320,128]{2,1,0:T(8,128)(2,1)}, u32[]{:S(2)}, u32[]{:S(2)}) %collective-permute-start.17) | collective-permute-done | bytes 327712 | tf_op jit(solution)/shard_map/ppermute | solution.py:30
  139.5 1.9 %fusion.3 = bf16[4,320,1,128]{3,1,2,0:T(8,128)(2,1)} fusion(bf16[4,320,128]{2,1,0:T(8,128)(2,1)S(1)} %branch_out.3, bf16[4,320,128]{2,1,0:T(8,128)(2,1)} %collective-permute-done.17, pred[]{:T(512)S(6)} %eq.10), kind=kLoop, calls=%fused_computation.10 | loop fusion | flops 1310720 | bytes 983041
  (61 shorter events, 0.3 us)
Async XLA Ops:
  0.6 61.7 %copy-start = (bf16[320,640]{1,0:T(8,128)(2,1)S(1)}, bf16[320,640]{1,0:T(8,128)(2,1)}, u32[]{:S(2)}) copy-start(bf16[320,640]{1,0:T(8,128)(2,1)} %param.15) | copy-start | bytes 1228804
  0.6 22.5 %copy-start.12 = (bf16[1,4,640,128]{3,2,1,0:T(8,128)(2,1)S(1)}, bf16[1,4,640,128]{3,2,1,0:T(8,128)(2,1)}, u32[]{:S(2)}) copy-start(bf16[1,4,640,128]{3,2,1,0:T(8,128)(2,1)} %param.12) | copy-start | bytes 1966084
  0.7 19.9 %copy-start.16 = (bf16[640]{0:T(1024)(128)(2,1)S(1)}, bf16[640]{0:T(1024)(128)(2,1)}, u32[]{:S(2)}) copy-start(bf16[640]{0:T(1024)(128)(2,1)} %param.16) | copy-start | bytes 3844
  0.7 19.9 %copy-start.17 = (bf16[640]{0:T(1024)(128)(2,1)S(1)}, bf16[640]{0:T(1024)(128)(2,1)}, u32[]{:S(2)}) copy-start(bf16[640]{0:T(1024)(128)(2,1)} %param.17) | copy-start | bytes 3844
  0.7 19.9 %copy-start.18 = (bf16[640]{0:T(1024)(128)(2,1)S(1)}, bf16[640]{0:T(1024)(128)(2,1)}, u32[]{:S(2)}) copy-start(bf16[640]{0:T(1024)(128)(2,1)} %param.20) | copy-start | bytes 3844
  0.7 19.9 %copy-start.19 = (bf16[640]{0:T(1024)(128)(2,1)S(1)}, bf16[640]{0:T(1024)(128)(2,1)}, u32[]{:S(2)}) copy-start(bf16[640]{0:T(1024)(128)(2,1)} %param.21) | copy-start | bytes 3844
  1.8 8.3 %collective-permute-start = (bf16[1,640,128]{2,1,0:T(8,128)(2,1)S(1)}, bf16[1,640,128]{2,1,0:T(8,128)(2,1)S(1)}, u32[]{:S(2)}, u32[]{:S(2)}) collective-permute-start(bf16[1,640,128]{2,1,0:T(8,128)(2,1)S(1)} %get-tuple-element.50), channel_id=1, source_target_pairs={{0,2},{2,4},{4,6},{6,8},{8,10},{10,12},{12,14},{1,3},{3,5},{5,7},{... | collective-permute-start | bytes 491528 | tf_op jit(solution)/shard_map/ppermute | solution.py:476
  6.7 7.6 %collective-permute-start.1 = (bf16[1,640,128]{2,1,0:T(8,128)(2,1)S(1)}, bf16[1,640,128]{2,1,0:T(8,128)(2,1)S(1)}, u32[]{:S(2)}, u32[]{:S(2)}) collective-permute-start(bf16[1,640,128]{2,1,0:T(8,128)(2,1)S(1)} %get-tuple-element.51), channel_id=1, source_target_pairs={{2,0},{4,2},{6,4},{8,6},{10,8},{12,10},{14,12},{3,1},{5,3},{7,5},{... | collective-permute-start | bytes 491528 | tf_op jit(solution)/shard_map/ppermute | solution.py:477
  16.4 17.8 %collective-permute-start.6 = (bf16[6,640,128]{2,1,0:T(8,128)(2,1)}, bf16[6,640,128]{2,1,0:T(8,128)(2,1)}, u32[]{:S(2)}, u32[]{:S(2)}) collective-permute-start(bf16[6,640,128]{2,1,0:T(8,128)(2,1)} %pad_maximum_fusion.refs_0_), channel_id=1, source_target_pairs={{1,17},{16,0},{3,19},{18,2},{5,21},{20,4},{7,23},{22,6},{9,25},{24... | collective-permute-start | bytes 2949128 | tf_op jit(solution)/shard_map/ppermute | solution.py:68
  17.6 26.1 %collective-permute-start.4 = (bf16[2,512,512]{2,1,0:T(8,128)(2,1)}, bf16[2,512,512]{2,1,0:T(8,128)(2,1)S(1)}, u32[]{:S(2)}, u32[]{:S(2)}) collective-permute-start(bf16[2,512,512]{2,1,0:T(8,128)(2,1)} %bitcast.15), channel_id=1, source_target_pairs={{0,4},{4,8},{8,12},{12,14},{14,10},{10,6},{6,2},{2,0},{1,5},{5,9},... | collective-permute-start | bytes 3145736 | tf_op jit(solution)/shard_map/ppermute | solution.py:494
  20.6 24.7 %collective-permute-start.5 = (bf16[2,512,512]{2,1,0:T(8,128)(2,1)}, bf16[2,512,512]{2,1,0:T(8,128)(2,1)S(1)}, u32[]{:S(2)}, u32[]{:S(2)}) collective-permute-start(bf16[2,512,512]{2,1,0:T(8,128)(2,1)} %bitcast.15), channel_id=1, source_target_pairs={{4,0},{8,4},{12,8},{14,12},{10,14},{6,10},{2,6},{0,2},{5,1},{9,5},... | collective-permute-start | bytes 3145736 | tf_op jit(solution)/shard_map/ppermute | solution.py:494
  20.7 16.6 %collective-permute-start.3 = (bf16[4,640]{1,0:T(4,128)(2,1)S(1)}, bf16[4,640]{1,0:T(4,128)(2,1)S(1)}, u32[]{:S(2)}, u32[]{:S(2)}) collective-permute-start(bf16[4,640]{1,0:T(4,128)(2,1)S(1)} %pad_maximum_fusion.1), channel_id=1, source_target_pairs={{0,1},{1,0},{2,3},{3,2},{4,5},{5,4},{6,7},{7,6},{8,9},{9,8},{10,11... | collective-permute-start | bytes 15368 | tf_op jit(solution)/shard_map/ppermute | solution.py:30
  24.7 24.4 %all-to-all-start = ((f32[32,1,128]{2,1,0:T(1,128)}), f32[32,1,128]{2,1,0:T(1,128)S(1)}, u32[]{:S(2)}, u32[]{:S(2)}) async-start(f32[32,1,128]{2,1,0:T(1,128)} %broadcast_in_dim.21), calls=%async_computation | async-start | bytes 32768 | tf_op jit(solution)/shard_map/all_to_all | solution.py:53
  30.6 1.3 copy-start.11
  33.1 1.1 copy-start.4
  34.2 15.4 %collective-permute-start.7 = (bf16[6,640,128]{2,1,0:T(8,128)(2,1)}, bf16[6,640,128]{2,1,0:T(8,128)(2,1)}, u32[]{:S(2)}, u32[]{:S(2)}) collective-permute-start(bf16[6,640,128]{2,1,0:T(8,128)(2,1)} %collective-permute-done.6.refs_0_), channel_id=1, source_target_pairs={{0,1},{17,16},{2,3},{19,18},{4,5},{21,20},{6,7},{23,22},{8,9},{25,... | collective-permute-start | bytes 2949128 | tf_op jit(solution)/shard_map/ppermute | solution.py:71
  37.3 25.3 %collective-permute-start.2 = (bf16[6,640,128]{2,1,0:T(8,128)(2,1)}, bf16[6,640,128]{2,1,0:T(8,128)(2,1)S(1)}, u32[]{:S(2)}, u32[]{:S(2)}) collective-permute-start(bf16[6,640,128]{2,1,0:T(8,128)(2,1)} %pad_maximum_fusion.refs_0_), channel_id=1, source_target_pairs={{0,1},{17,16},{2,3},{19,18},{4,5},{21,20},{6,7},{23,22},{8,9},{25,... | collective-permute-start | bytes 2949128 | tf_op jit(solution)/shard_map/ppermute | solution.py:70
  43.7 16.3 %copy-start.6 = (bf16[2,512,512]{2,1,0:T(8,128)(2,1)}, bf16[2,512,512]{2,1,0:T(8,128)(2,1)S(1)}, u32[]{:S(2)}) copy-start(bf16[2,512,512]{2,1,0:T(8,128)(2,1)S(1)} %collective-permute-done.4.refs_3_.refs_4_) | copy-start | bytes 3145732
  43.7 34.8 %collective-permute-start.10 = (bf16[2,512,512]{2,1,0:T(8,128)(2,1)S(1)}, bf16[2,512,512]{2,1,0:T(8,128)(2,1)}, u32[]{:S(2)}, u32[]{:S(2)}) collective-permute-start(bf16[2,512,512]{2,1,0:T(8,128)(2,1)S(1)} %collective-permute-done.4.refs_3_.refs_4_), channel_id=1, source_target_pairs={{0,4},{4,8},{8,12},{12,14},{14,10},{10,6},{6,2},{2,0},{1,5},{5,9},... | collective-permute-start | bytes 3145736 | tf_op jit(solution)/shard_map/ppermute | solution.py:494
  45.2 14.8 %copy-start.8 = (bf16[2,512,512]{2,1,0:T(8,128)(2,1)}, bf16[2,512,512]{2,1,0:T(8,128)(2,1)S(1)}, u32[]{:S(2)}) copy-start(bf16[2,512,512]{2,1,0:T(8,128)(2,1)S(1)} %collective-permute-done.5.refs_5_.refs_6_) | copy-start | bytes 3145732
  45.2 33.3 %collective-permute-start.11 = (bf16[2,512,512]{2,1,0:T(8,128)(2,1)S(1)}, bf16[2,512,512]{2,1,0:T(8,128)(2,1)}, u32[]{:S(2)}, u32[]{:S(2)}) collective-permute-start(bf16[2,512,512]{2,1,0:T(8,128)(2,1)S(1)} %collective-permute-done.5.refs_5_.refs_6_), channel_id=1, source_target_pairs={{4,0},{8,4},{12,8},{14,12},{10,14},{6,10},{2,6},{0,2},{5,1},{9,5},... | collective-permute-start | bytes 3145736 | tf_op jit(solution)/shard_map/ppermute | solution.py:494
  49.6 13.1 %copy-start.15 = (bf16[640]{0:T(1024)(128)(2,1)S(1)}, bf16[640]{0:T(1024)(128)(2,1)}, u32[]{:S(2)}) copy-start(bf16[640]{0:T(1024)(128)(2,1)} %param.19) | copy-start | bytes 3844
  60.0 16.8 %collective-permute-start.8 = (bf16[4,640,128]{2,1,0:T(8,128)(2,1)}, bf16[4,640,128]{2,1,0:T(8,128)(2,1)S(1)}, u32[]{:S(2)}, u32[]{:S(2)}) collective-permute-start(bf16[4,640,128]{2,1,0:T(8,128)(2,1)} %norm_conv.3), channel_id=1, source_target_pairs={{0,16},{16,0},{1,17},{17,1},{2,18},{18,2},{3,19},{19,3},{4,20},{20... | collective-permute-start | bytes 1966088 | tf_op jit(solution)/shard_map/ppermute | solution.py:30
  62.7 1.0 copy-start.14
  63.6 13.2 %copy-start.13 = (bf16[1,4,640,128]{3,2,1,0:T(8,128)(2,1)S(1)}, bf16[1,4,640,128]{3,2,1,0:T(8,128)(2,1)}, u32[]{:S(2)}) copy-start(bf16[1,4,640,128]{3,2,1,0:T(8,128)(2,1)} %param.12) | copy-start | bytes 1966084
  78.5 4.3 %copy-start.2 = (bf16[4,640,128]{2,1,0:T(8,128)(2,1)}, bf16[4,640,128]{2,1,0:T(8,128)(2,1)S(1)}, u32[]{:S(2)}) copy-start(bf16[4,640,128]{2,1,0:T(8,128)(2,1)S(1)} %add_convert_fusion.own_ref.refs_0_) | copy-start | bytes 1966084
  78.5 26.6 %collective-permute-start.12 = (bf16[2,512,512]{2,1,0:T(8,128)(2,1)}, bf16[2,512,512]{2,1,0:T(8,128)(2,1)S(1)}, u32[]{:S(2)}, u32[]{:S(2)}) collective-permute-start(bf16[2,512,512]{2,1,0:T(8,128)(2,1)} %collective-permute-done.10.refs_1_.refs_2_), channel_id=1, source_target_pairs={{0,4},{4,8},{8,12},{12,14},{14,10},{10,6},{6,2},{2,0},{1,5},{5,9},... | collective-permute-start | bytes 3145736 | tf_op jit(solution)/shard_map/ppermute | solution.py:494
  79.4 25.8 %collective-permute-start.13 = (bf16[2,512,512]{2,1,0:T(8,128)(2,1)}, bf16[2,512,512]{2,1,0:T(8,128)(2,1)S(1)}, u32[]{:S(2)}, u32[]{:S(2)}) collective-permute-start(bf16[2,512,512]{2,1,0:T(8,128)(2,1)} %collective-permute-done.11.refs_3_.refs_4_), channel_id=1, source_target_pairs={{4,0},{8,4},{12,8},{14,12},{10,14},{6,10},{2,6},{0,2},{5,1},{9,5},... | collective-permute-start | bytes 3145736 | tf_op jit(solution)/shard_map/ppermute | solution.py:494
  80.6 2.2 %collective-permute-start.9 = (bf16[4,640,128]{2,1,0:T(8,128)(2,1)S(1)}, bf16[4,640,128]{2,1,0:T(8,128)(2,1)}, u32[]{:S(2)}, u32[]{:S(2)}) collective-permute-start(bf16[4,640,128]{2,1,0:T(8,128)(2,1)S(1)} %add_convert_fusion.own_ref.refs_0_), channel_id=1, source_target_pairs={{0,1},{1,0},{2,3},{3,2},{4,5},{5,4},{6,7},{7,6},{8,9},{9,8},{10,11... | collective-permute-start | bytes 1966088 | tf_op jit(solution)/shard_map/ppermute | solution.py:30
  91.2 1.0 copy-start.1
  92.2 1.2 copy-start.7
  93.4 1.2 copy-start.9
  94.7 1.2 copy-start.10
  105.3 16.5 %collective-permute-start.14 = (bf16[1,512,512]{2,1,0:T(8,128)(2,1)S(1)}, bf16[1,512,512]{2,1,0:T(8,128)(2,1)S(1)}, u32[]{:S(2)}, u32[]{:S(2)}) collective-permute-start(bf16[1,512,512]{2,1,0:T(8,128)(2,1)S(1)} %slice.34), channel_id=1, source_target_pairs={{0,4},{4,8},{8,12},{12,14},{14,10},{10,6},{6,2},{2,0},{1,5},{5,9},... | collective-permute-start | bytes 1572872 | tf_op jit(solution)/shard_map/ppermute | solution.py:494
  106.2 15.7 %collective-permute-start.15 = (bf16[1,512,512]{2,1,0:T(8,128)(2,1)S(1)}, bf16[1,512,512]{2,1,0:T(8,128)(2,1)S(1)}, u32[]{:S(2)}, u32[]{:S(2)}) collective-permute-start(bf16[1,512,512]{2,1,0:T(8,128)(2,1)S(1)} %slice.35), channel_id=1, source_target_pairs={{4,0},{8,4},{12,8},{14,12},{10,14},{6,10},{2,6},{0,2},{5,1},{9,5},... | collective-permute-start | bytes 1572872 | tf_op jit(solution)/shard_map/ppermute | solution.py:494
  114.9 6.9 %copy-start.5 = (bf16[2,640,512]{2,1,0:T(8,128)(2,1)S(1)}, bf16[2,640,512]{2,1,0:T(8,128)(2,1)}, u32[]{:S(2)}) copy-start(bf16[2,640,512]{2,1,0:T(8,128)(2,1)} %copy-done.4) | copy-start | bytes 3932164
  121.9 5.6 %copy-start.3 = (bf16[4,640,128]{2,1,0:T(8,128)(2,1)S(1)}, bf16[4,640,128]{2,1,0:T(8,128)(2,1)}, u32[]{:S(2)}) copy-start(bf16[4,640,128]{2,1,0:T(8,128)(2,1)} %copy-done.2) | copy-start | bytes 1966084
  127.3 2.2 %collective-permute-start.16 = (bf16[2,4,320,128]{3,2,1,0:T(8,128)(2,1)S(1)}, bf16[2,4,320,128]{3,2,1,0:T(8,128)(2,1)S(1)}, u32[]{:S(2)}, u32[]{:S(2)}) collective-permute-start(bf16[2,4,320,128]{3,2,1,0:T(8,128)(2,1)S(1)} %get-tuple-element.37), channel_id=1, source_target_pairs={{0,1},{1,0},{2,3},{3,2},{4,5},{5,4},{6,7},{7,6},{8,9},{9,8},{10,11... | collective-permute-start | bytes 1966088 | tf_op jit(solution)/shard_map/ppermute | solution.py:30
  129.6 9.9 %collective-permute-start.17 = (bf16[4,320,128]{2,1,0:T(8,128)(2,1)S(1)}, bf16[4,320,128]{2,1,0:T(8,128)(2,1)}, u32[]{:S(2)}, u32[]{:S(2)}) collective-permute-start(bf16[4,320,128]{2,1,0:T(8,128)(2,1)S(1)} %branch_out.2), channel_id=1, source_target_pairs={{0,16},{16,0},{1,17},{17,1},{2,18},{18,2},{3,19},{19,3},{4,20},{20... | collective-permute-start | bytes 983048 | tf_op jit(solution)/shard_map/ppermute | solution.py:30

commit v6 on v5

--- a/solution.py
+++ b/solution.py
@@ -54,10 +54,10 @@
 
 
 def need(array, others):
-    return lax.optimization_barrier((array,) + tuple(others))[0]
-
-
-def halves_of_inputs(own):
+    return lax.optimization_barrier((array,) + tuple(others))[0] if others else array
+
+
+def halves_of_inputs(own, others=()):
     cfg = lax.axis_index("cfg")
     if lax.axis_size("tp") != 2:
         full = lax.all_gather(own, "tp", axis=1, tiled=True)
@@ -68,13 +68,14 @@
     across = lax.ppermute(own, ("cfg", "tp"), [(1, 3), (2, 0)])
     pairs = [(0, 1), (3, 2)]
     own_side = lax.ppermute(own, ("cfg", "tp"), pairs)
-    across_side = lax.ppermute(across, ("cfg", "tp"), pairs)
+    across_side = lax.ppermute(need(across, others), ("cfg", "tp"), pairs)
     return [own, own_side], [across, across_side]
 
 
 def conv_kernel(choices, amount, flags_ref, sums_ref, *refs):
     x_refs = refs[:choices]
-    affine_ref, w_hbm, out_ref, w_ref, act_ref, sems = refs[choices:]
+    edge_refs = refs[choices : 2 * choices]
+    affine_ref, w_hbm, out_ref, w_ref, act_ref, sems = refs[2 * choices :]
     rows = out_ref.shape[0]
     ins = affine_ref.shape[0]
     copies = {}
@@ -99,11 +100,13 @@
     scale = lax.rsqrt(variance + epsilon) * affine_ref[:, 0:1]
     shift = affine_ref[:, 1:2]
     for r in range(rows + 2):
-        x = x_refs[0][r]
-        if choices == 2:
-            x = jnp.where(flags_ref[2] == 1, x, x_refs[1][r])
-        z = (x.astype(jnp.float32) - mean) * scale + shift
-        z = z * jax.nn.sigmoid(z)
+        if 0 < r <= rows:
+            x = [ref[r - 1] for ref in x_refs]
+        else:
+            x = [ref[0 if r == 0 else 1] for ref in edge_refs]
+        x = x[0] if choices == 1 else jnp.where(flags_ref[2] == 1, x[0], x[1])
+        z = ((x.astype(jnp.float32) - mean) * scale + shift) * 0.5
+        z = z + z * jnp.tanh(z)
         if r == 0:
             z = jnp.where(flags_ref[0] == 1, z, 0.0)
         if r == rows + 1:
@@ -134,16 +137,15 @@
             out_ref[start + r] = total[r].astype(out_ref.dtype)
 
 
-def conv_call(flags, sums, amount, xs, affine, conv_w, out_dtype):
-    x = xs[0]
-    rows = x.shape[0] - 2
+def conv_call(flags, sums, amount, xs, edges, affine, conv_w, out_dtype):
+    rows = xs[0].shape[0]
     outs, ins = conv_w.shape[2:]
     return pl.pallas_call(
         functools.partial(conv_kernel, len(xs), amount),
         in_specs=[
             pl.BlockSpec(memory_space=pltpu.SMEM),
             pl.BlockSpec(memory_space=pltpu.SMEM),
-            *[pl.BlockSpec(memory_space=pltpu.VMEM)] * (len(xs) + 1),
+            *[pl.BlockSpec(memory_space=pltpu.VMEM)] * (2 * len(xs) + 1),
             pl.BlockSpec(memory_space=pltpu.HBM),
         ],
         out_specs=pl.BlockSpec(memory_space=pltpu.VMEM),
@@ -156,7 +158,7 @@
         compiler_params=pltpu.CompilerParams(vmem_limit_bytes=57 * MIB),
         cost_estimate=cost(9000),
         name="norm_conv",
-    )(flags, sums, *xs, affine, conv_w)
+    )(flags, sums, *xs, *edges, affine, conv_w)
 
 
 def parity_matrix(channels):
@@ -268,7 +270,7 @@
             pltpu.VMEM((positions, depth), jnp.bfloat16),
             pltpu.SemaphoreType.DMA((3,)),
         ],
-        compiler_params=pltpu.CompilerParams(vmem_limit_bytes=60 * MIB),
+        compiler_params=pltpu.CompilerParams(vmem_limit_bytes=55 * MIB),
         cost_estimate=cost(6500),
         name="norm_project",
     )(order, *parts, affine, w)
@@ -475,9 +477,8 @@
     down_pairs = [(i + 1, i) for i in range(rows_count - 1)]
     before = lax.ppermute(latent_rows[span_rows - 1 :], "rows", up_pairs)
     after = lax.ppermute(latent_rows[:1], "rows", down_pairs)
-    rimmed = jnp.concatenate([before, latent_rows, after], axis=0)
-
-    x_mine, x_other = halves_of_inputs(rimmed)
+    x_mine, x_other = halves_of_inputs(latent_rows, (table,))
+    edges_mine, edges_other = halves_of_inputs(jnp.concatenate([before, after], axis=0))
 
     forward, backward = ring_pairs(rows_count)
     last = rows_count // 2
@@ -500,7 +501,7 @@
             return [((ahead, 0), (behind, 0))]
         return [((ahead, 0), (ahead, 1)), ((behind, 0), (behind, 1))]
 
-    next_hop()
+    next_hop(table)
 
     vectors = gather_tp(jnp.stack([gn_gain, gn_bias, ln_gain, ln_bias]), 1).astype(jnp.float32)
     amount = span_rows * rows_count * grid_width * group_width
@@ -518,11 +519,10 @@
     w_back = arrange_call(flip, w_out, tp_count)
     gn_affine, w_back = lax.optimization_barrier((gn_affine, w_back))
 
-    flags_other = need(flags_other, hops[1])
-    conv_sent = conv_call(flags_other, table, amount, x_other, gn_affine, conv_w, jnp.bfloat16)
+    conv_sent = conv_call(flags_other, table, amount, x_other, edges_other, gn_affine, conv_w, jnp.bfloat16)
     conv_received = swapped(conv_sent, "cfg")
-    next_hop()
-    conv_own = conv_call(flags_mine, table, amount, x_mine, gn_affine, conv_w, jnp.float32)
+    next_hop(conv_sent)
+    conv_own = conv_call(flags_mine, table, amount, x_mine, edges_mine, gn_affine, conv_w, jnp.float32)
 
     half_width = TEMB // 2
     frequencies = jnp.exp(

time: 142 us -> 144 us (1.014)
  starting transfers between devices: 31.9 us -> 35.9 us
  waiting for transfers between devices: 26 us -> 22.8 us
  local copies, waits for them, and re-layouts: 12.3 us -> 13.9 us
    ppermute x5, starting transfers between devices: 5.5 us -> 0.73 us  [swapped(): lax.ppermute(array, axis, [(i, i ^ 1) for i in range(lax.axis_size(axis))])]
    ppermute x1, waiting for transfers between devices: 4.12 us -> 0.01 us  [per_device(): after = lax.ppermute(latent_rows[:1], 'rows', down_pairs)]
    ppermute x4, waiting for transfers between devices: 0.29 us -> 3.84 us  [next_hop(): lax.ppermute(behind, 'rows', backward)]
    ppermute x1 -> x2, starting transfers between devices: 3.11 us -> 6.65 us  [halves_of_inputs(): across_side = lax.ppermute(need(across, others), ('cfg', 'tp'), pairs)]
    ppermute x1 -> x2, waiting for transfers between devices: 0.01 us -> 3.15 us  [halves_of_inputs(): across = lax.ppermute(own, ('cfg', 'tp'), [(1, 3), (2, 0)])]
    ppermute x1 -> x2, starting transfers between devices: 1.35 us -> 4.26 us  [halves_of_inputs(): own_side = lax.ppermute(own, ('cfg', 'tp'), pairs)]
    another operation x4, local copies, waits for them, and re-layouts: 0.02 us -> 2.86 us  [per_device(): jnp.stack([gn_gain, gn_bias, ln_gain, ln_bias])]
    unnamed x41 -> x40, local copies, waits for them, and re-layouts: 9.01 us -> 6.19 us
  transfers between devices with their start and end apart: 19 -> 22, of which waited for: 9 -> 9; matrix products, arithmetic and copies ran while one was open for 5% -> 8% of each run, Pallas kernels for 39% -> 39%
where the time goes in v6:
time: 144 us; the launch traced here: 143 us
  Pallas kernels  61.1 us (42%)
  starting transfers between devices  35.9 us (25%)
  waiting for transfers between devices  22.8 us (16%)
  local copies, waits for them, and re-layouts  13.9 us (10%)
  other arithmetic  7.06 us (5%)
  between operations  1.8 us (1%)
    pallas_call x4, Pallas kernels, attention_call(): pl.pallas_call(functools.partial(attention_kernel, len(pairs), state is n...  29.2 us
    pallas_call x2, Pallas kernels, conv_call(): pl.pallas_call(functools.partial(conv_kernel, len(xs), amount), in_specs=...  21 us
    ppermute x5, waiting for transfers between devices, swapped(): lax.ppermute(array, axis, [(i, i ^ 1) for i in range(lax.axis_size(axis))])  11.3 us
    pallas_call x1, Pallas kernels, project_call(): pl.pallas_call(functools.partial(project_kernel, len(parts)), in_specs=[p...  8.46 us
    ppermute x4, starting transfers between devices, next_hop(): lax.ppermute(ahead, 'rows', forward)  7.13 us
    all_to_all x1, starting transfers between devices, summed(): return jnp.sum(lax.all_to_all(spread, axes, 0, 0, tiled=True), axis=0)  7.06 us
    ppermute x2, starting transfers between devices, halves_of_inputs(): across_side = lax.ppermute(need(across, others), ('cfg', 'tp'), pairs)  6.65 us
    unnamed x40, local copies, waits for them, and re-layouts  6.19 us
  transfers between devices with their start and end apart: 22, of which 9 were waited for; matrix products, arithmetic and copies ran while one was open for 8% of the time, Pallas kernels for 39%

profile of v6, /device:TPU:0, one launch (start us, length us, event | category | flops | bytes accessed | tf_op | source)
XLA Modules:
  0.0 142.9 jit_solution(6977436446758970528)
XLA Ops:
  0.7 0.8 stack.52
  1.5 0.7 stack.53
  2.2 0.7 stack.54
  2.8 0.7 stack.55
  3.5 0.5 collective-permute-start.4
  4.1 1.3 convert_reduce_fusion
  5.6 0.1 reduce_sum.36
  5.7 0.1 reduce_sum.46
  5.8 0.1 dynamic_update_slice.3
  6.0 0.1 broadcast_in_dim.20
  6.1 0.6 broadcast_in_dim.21
  6.7 7.1 %all-to-all-start = ((f32[32,1,128]{2,1,0:T(1,128)}), f32[32,1,128]{2,1,0:T(1,128)S(1)}, u32[]{:S(2)}, u32[]{:S(2)}) async-start(f32[32,1,128]{2,1,0:T(1,128)} %broadcast_in_dim.21), calls=%async_computation | async-start | bytes 32768 | tf_op jit(solution)/shard_map/all_to_all | solution.py:53
  13.8 1.3 collective-permute-start.5
  15.1 1.7 %slice_bitcast_fusion = (bf16[1,640,128]{2,1,0:T(8,128)(2,1)}, bf16[1,640,128]{2,1,0:T(8,128)(2,1)S(1)}) fusion(bf16[1,4,640,128]{3,2,1,0:T(8,128)(2,1)} %param.12), kind=kLoop, calls=%fused_computation.10 | loop fusion | bytes 655360 | tf_op jit(solution)/shard_map/slice | solution.py:479
  16.8 4.3 %collective-permute-start.1 = (bf16[1,640,128]{2,1,0:T(8,128)(2,1)S(1)}, bf16[1,640,128]{2,1,0:T(8,128)(2,1)}, u32[]{:S(2)}, u32[]{:S(2)}) collective-permute-start(bf16[1,640,128]{2,1,0:T(8,128)(2,1)S(1)} %get-tuple-element.59), channel_id=1, source_target_pairs={{0,2},{2,4},{4,6},{6,8},{8,10},{10,12},{12,14},{1,3},{3,5},{5,7},{... | collective-permute-start | bytes 491528 | tf_op jit(solution)/shard_map/ppermute | solution.py:478
  21.1 1.3 collective-permute-start.2
  22.5 0.6 pad_add_fusion.1
  23.1 1.2 arrange.1.refs_5_
  24.3 1.1 copy-done.4
  25.4 0.6 reduce_sum.47.sums_ref
  25.9 2.9 %collective-permute-start.11 = (bf16[2,512,512]{2,1,0:T(8,128)(2,1)}, bf16[2,512,512]{2,1,0:T(8,128)(2,1)S(1)}, u32[]{:S(2)}, u32[]{:S(2)}) collective-permute-start(bf16[2,512,512]{2,1,0:T(8,128)(2,1)} %bitcast.44), channel_id=1, source_target_pairs={{0,4},{4,8},{8,12},{12,14},{14,10},{10,6},{6,2},{2,0},{1,5},{5,9},... | collective-permute-start | bytes 3145736 | tf_op jit(solution)/shard_map/ppermute | solution.py:495
  28.8 0.9 constant_dynamic-update-slice_fusion.1
  29.7 0.9 constant_dynamic-update-slice_fusion.refs_2_
  30.7 1.3 collective-permute-start.7
  32.1 4.6 %collective-permute-start.6 = (bf16[4,640,128]{2,1,0:T(8,128)(2,1)S(1)}, bf16[4,640,128]{2,1,0:T(8,128)(2,1)}, u32[]{:S(2)}, u32[]{:S(2)}) collective-permute-start(bf16[4,640,128]{2,1,0:T(8,128)(2,1)S(1)} %collective-permute-done.5.refs_0_), channel_id=1, source_target_pairs={{0,1},{17,16},{2,3},{19,18},{4,5},{21,20},{6,7},{23,22},{8,9},{25,... | collective-permute-start | bytes 1966088 | tf_op jit(solution)/shard_map/ppermute | solution.py:71
  36.7 3.1 %collective-permute-done.7.refs_2_ = bf16[2,640,128]{2,1,0:T(8,128)(2,1)} collective-permute-done((bf16[2,640,128]{2,1,0:T(8,128)(2,1)S(1)}, bf16[2,640,128]{2,1,0:T(8,128)(2,1)}, u32[]{:S(2)}, u32[]{:S(2)}) %collective-permute-start.7) | collective-permute-done | bytes 327712 | tf_op jit(solution)/shard_map/ppermute | solution.py:68
  39.8 2.0 %collective-permute-start.8 = (bf16[2,640,128]{2,1,0:T(8,128)(2,1)}, bf16[2,640,128]{2,1,0:T(8,128)(2,1)}, u32[]{:S(2)}, u32[]{:S(2)}) collective-permute-start(bf16[2,640,128]{2,1,0:T(8,128)(2,1)} %collective-permute-done.7.refs_2_), channel_id=1, source_target_pairs={{0,1},{17,16},{2,3},{19,18},{4,5},{21,20},{6,7},{23,22},{8,9},{25,... | collective-permute-start | bytes 983048 | tf_op jit(solution)/shard_map/ppermute | solution.py:71
  41.9 0.9 copy.30
  42.9 10.4 %norm_conv.3 = bf16[4,640,128]{2,1,0:T(8,128)(2,1)} custom-call(s32[4]{0:T(128)} %get-tuple-element.64.flags_ref, f32[128]{0:T(128)} %reduce_sum.47.sums_ref, bf16[4,640,128]{2,1,0:T(8,128)(2,1)} %copy-done.16, bf16[4,640,128]{2,1,0:T(8,128)(2,1)} %collective-permute-done.6.refs_1_, bf16[2,640,128]{2,1,0:T(8,128)(2,1)} %collective-permute-done.7.refs_2_, ...), custom_call_target="tpu_custom_call" | custom-call | flops 180000000 | bytes 1000 | tf_op jit(solution)/shard_map/norm_conv/pallas_call | solution.py:143
  53.3 1.6 %collective-permute-done.12.refs_5_.refs_6_ = bf16[2,512,512]{2,1,0:T(8,128)(2,1)S(1)} collective-permute-done((bf16[2,512,512]{2,1,0:T(8,128)(2,1)}, bf16[2,512,512]{2,1,0:T(8,128)(2,1)S(1)}, u32[]{:S(2)}, u32[]{:S(2)}) %collective-permute-start.12) | collective-permute-done | bytes 1048608 | tf_op jit(solution)/shard_map/ppermute | solution.py:495
  54.9 1.5 %collective-permute-start.13 = (bf16[2,512,512]{2,1,0:T(8,128)(2,1)S(1)}, bf16[2,512,512]{2,1,0:T(8,128)(2,1)}, u32[]{:S(2)}, u32[]{:S(2)}) collective-permute-start(bf16[2,512,512]{2,1,0:T(8,128)(2,1)S(1)} %collective-permute-done.11.refs_3_.refs_4_), channel_id=1, source_target_pairs={{0,4},{4,8},{8,12},{12,14},{14,10},{10,6},{6,2},{2,0},{1,5},{5,9},... | collective-permute-start | bytes 3145736 | tf_op jit(solution)/shard_map/ppermute | solution.py:495
  56.3 0.6 collective-permute-start.14
  56.9 1.5 %collective-permute-start = (bf16[4,640,128]{2,1,0:T(8,128)(2,1)S(1)}, bf16[4,640,128]{2,1,0:T(8,128)(2,1)S(1)}, u32[]{:S(2)}, u32[]{:S(2)}) collective-permute-start(bf16[4,640,128]{2,1,0:T(8,128)(2,1)S(1)} %bitcast.36), channel_id=1, source_target_pairs={{0,1},{17,16},{2,3},{19,18},{4,5},{21,20},{6,7},{23,22},{8,9},{25,... | collective-permute-start | bytes 1966088 | tf_op jit(solution)/shard_map/ppermute | solution.py:70
  59.2 0.1 divide_multiply_fusion
  59.3 2.8 %collective-permute-start.3 = (bf16[2,640,128]{2,1,0:T(8,128)(2,1)S(1)}, bf16[2,640,128]{2,1,0:T(8,128)(2,1)S(1)}, u32[]{:S(2)}, u32[]{:S(2)}) collective-permute-start(bf16[2,640,128]{2,1,0:T(8,128)(2,1)S(1)} %constant_dynamic-update-slice_fusion.refs_2_), channel_id=1, source_target_pairs={{0,1},{17,16},{2,3},{19,18},{4,5},{21,20},{6,7},{23,22},{8,9},{25,... | collective-permute-start | bytes 983048 | tf_op jit(solution)/shard_map/ppermute | solution.py:70
  62.0 0.3 convolution_reduce_fusion
  62.4 0.7 collective-permute-done.3.refs_3_
  63.1 0.7 copy-done.17
  63.8 0.2 copy-done.15
  64.0 10.6 %norm_conv.2 = f32[4,640,128]{2,1,0:T(8,128)} custom-call(s32[4]{0:T(128)} %get-tuple-element.65.flags_ref, f32[128]{0:T(128)} %reduce_sum.47.sums_ref, bf16[4,640,128]{2,1,0:T(8,128)(2,1)} %bitcast.35, bf16[4,640,128]{2,1,0:T(8,128)(2,1)} %copy-done.15, bf16[2,640,128]{2,1,0:T(8,128)(2,1)} %copy-done.14, bf16[2,640,128]{2,1,0:T(8,128)(2,1)} %copy-done.17, ...), custom_call_target="tpu_custom_call" | custom-call | flops 180000000 | bytes 1000 | tf_op jit(solution)/shard_map/norm_conv/pallas_call | solution.py:143
  74.7 1.6 %add_convert_fusion.own_ref.refs_0_ = bf16[4,640,128]{2,1,0:T(8,128)(2,1)S(1)} fusion(f32[4,640,128]{2,1,0:T(8,128)} %norm_conv.2, bf16[4,640,128]{2,1,0:T(8,128)(2,1)S(1)} %collective-permute-done.9, f32[640]{0:T(1024)S(1)} %convert_add_fusion.1, bf16[1,4,640,128]{3,2,1,0:T(8,128)(2,1)S(1)} %copy-done.13), kind=kLoop, calls=%fused_computation.3 | loop fusion | flops 1966080 | bytes 3279360 | tf_op jit(solution)/shard_map/convert_element_type | solution.py:539
  76.3 3.8 %collective-permute-done.13.refs_1_.refs_2_ = bf16[2,512,512]{2,1,0:T(8,128)(2,1)} collective-permute-done((bf16[2,512,512]{2,1,0:T(8,128)(2,1)S(1)}, bf16[2,512,512]{2,1,0:T(8,128)(2,1)}, u32[]{:S(2)}, u32[]{:S(2)}) %collective-permute-start.13) | collective-permute-done | bytes 1048608 | tf_op jit(solution)/shard_map/ppermute | solution.py:495
  80.1 1.2 collective-permute-done.14.refs_3_.refs_4_
  81.3 1.5 %collective-permute-start.15 = (bf16[2,512,512]{2,1,0:T(8,128)(2,1)}, bf16[2,512,512]{2,1,0:T(8,128)(2,1)S(1)}, u32[]{:S(2)}, u32[]{:S(2)}) collective-permute-start(bf16[2,512,512]{2,1,0:T(8,128)(2,1)} %collective-permute-done.13.refs_1_.refs_2_), channel_id=1, source_target_pairs={{0,4},{4,8},{8,12},{12,14},{14,10},{10,6},{6,2},{2,0},{1,5},{5,9},... | collective-permute-start | bytes 3145736 | tf_op jit(solution)/shard_map/ppermute | solution.py:495
  82.8 0.5 collective-permute-start.16
  83.4 0.6 pad_add_fusion.2.order_ref
  83.9 1.1 copy.28
  85.0 0.5 collective-permute-done.10.refs_1_
  85.6 8.5 %norm_project.1 = (bf16[512,512]{1,0:T(8,128)(2,1)}, bf16[2,512,512]{2,1,0:T(8,128)(2,1)}) custom-call(s32[2]{0:T(128)} %pad_add_fusion.2.order_ref, bf16[4,640,128]{2,1,0:T(8,128)(2,1)} %copy-done.2, bf16[4,640,128]{2,1,0:T(8,128)(2,1)} %collective-permute-done.10.refs_1_, f32[1280,2]{1,0:T(8,128)} %bitcast.40, bf16[3,1280,512]{2,1,0:T(8,128)(2,1)} %bitcast.37), custom_call_target="tpu_custom_call" | custom-call | flops 130000000 | bytes 1000 | tf_op jit(solution)/shard_map/norm_project/pallas_call | solution.py:256
  94.1 1.0 copy-done.1
  95.1 1.2 copy-done.10
  96.3 9.3 %attend.4 = (f32[4,2,512,128]{3,2,1,0:T(8,128)S(1)}, f32[4,2,512,128]{3,2,1,0:T(8,128)S(1)}) custom-call(bf16[512,512]{1,0:T(8,128)(2,1)S(1)} %copy-done.1, bf16[2,512,512]{2,1,0:T(8,128)(2,1)S(1)} %copy-done.10, bf16[2,512,512]{2,1,0:T(8,128)(2,1)S(1)} %copy-done.10, bf16[2,512,512]{2,1,0:T(8,128)(2,1)S(1)} %copy-done.7, ...), custom_call_target="tpu_custom_call" | custom-call | flops 212000000 | bytes 1000 | tf_op jit(solution)/shard_map/attend/pallas_call | solution.py:429
  105.7 1.1 collective-permute-done.16.refs_3_.refs_4_
  106.8 1.3 collective-permute-start.17
  108.1 0.8 collective-permute-start.18
  108.9 7.6 %attend.5 = (f32[4,2,512,128]{3,2,1,0:T(8,128)S(1)}, f32[4,2,512,128]{3,2,1,0:T(8,128)S(1)}) custom-call(bf16[512,512]{1,0:T(8,128)(2,1)S(1)} %copy-done.1, bf16[2,512,512]{2,1,0:T(8,128)(2,1)} %collective-permute-done.13.refs_1_.refs_2_, bf16[2,512,512]{2,1,0:T(8,128)(2,1)} %collective-permute-done.13.refs_1_.refs_2_, ...), custom_call_target="tpu_custom_call" | custom-call | flops 148000000 | bytes 1000 | tf_op jit(solution)/shard_map/attend/pallas_call | solution.py:429
  116.5 6.9 %attend.6 = (f32[4,2,512,128]{3,2,1,0:T(8,128)S(1)}, f32[4,2,512,128]{3,2,1,0:T(8,128)S(1)}) custom-call(bf16[512,512]{1,0:T(8,128)(2,1)S(1)} %copy-done.1, bf16[2,512,512]{2,1,0:T(8,128)(2,1)S(1)} %collective-permute-done.15.refs_1_.refs_2_, bf16[2,512,512]{2,1,0:T(8,128)(2,1)S(1)} %collective-permute-done.15.refs_1_.refs_2_, ...), custom_call_target="tpu_custom_call" | custom-call | flops 148000000 | bytes 1000 | tf_op jit(solution)/shard_map/attend/pallas_call | solution.py:429
  123.4 5.5 %attend.7 = (bf16[2,4,320,128]{3,2,1,0:T(8,128)(2,1)S(1)}, f32[2,4,320,128]{3,2,1,0:T(8,128)S(1)}) custom-call(bf16[512,512]{1,0:T(8,128)(2,1)S(1)} %copy-done.1, bf16[1,512,512]{2,1,0:T(8,128)(2,1)S(1)} %collective-permute-done.17.refs_1_, bf16[1,512,512]{2,1,0:T(8,128)(2,1)S(1)} %collective-permute-done.18.refs_2_, ...), custom_call_target="tpu_custom_call" | custom-call | flops 84000000 | bytes 1000 | tf_op jit(solution)/shard_map/attend/pallas_call | solution.py:429
  129.0 1.0 parity_split.1.resid_ref
  130.0 1.1 collective-permute-done.19.refs_1_
  131.0 0.1 branch_out.2
  131.2 0.1 branch_out.3
  131.3 9.7 %collective-permute-done.20 = bf16[4,320,128]{2,1,0:T(8,128)(2,1)} collective-permute-done((bf16[4,320,128]{2,1,0:T(8,128)(2,1)S(1)}, bf16[4,320,128]{2,1,0:T(8,128)(2,1)}, u32[]{:S(2)}, u32[]{:S(2)}) %collective-permute-start.20) | collective-permute-done | bytes 327712 | tf_op jit(solution)/shard_map/ppermute | solution.py:30
  141.1 1.9 %fusion.3 = bf16[4,320,1,128]{3,1,2,0:T(8,128)(2,1)} fusion(bf16[4,320,128]{2,1,0:T(8,128)(2,1)S(1)} %branch_out.3, bf16[4,320,128]{2,1,0:T(8,128)(2,1)} %collective-permute-done.20, pred[]{:T(512)S(6)} %eq.10), kind=kLoop, calls=%fused_computation.9 | loop fusion | flops 1310720 | bytes 983041
  (66 shorter events, 0.8 us)
Async XLA Ops:
  0.6 61.4 %copy-start = (bf16[320,640]{1,0:T(8,128)(2,1)S(1)}, bf16[320,640]{1,0:T(8,128)(2,1)}, u32[]{:S(2)}) copy-start(bf16[320,640]{1,0:T(8,128)(2,1)} %param.15) | copy-start | bytes 1228804
  0.6 22.4 %copy-start.11 = (bf16[512,1280]{1,0:T(8,128)(2,1)S(1)}, bf16[512,1280]{1,0:T(8,128)(2,1)}, u32[]{:S(2)}) copy-start(bf16[512,1280]{1,0:T(8,128)(2,1)} %w_ref.1) | copy-start | bytes 3932164
  3.5 28.5 %collective-permute-start.4 = (bf16[4,640]{1,0:T(4,128)(2,1)S(1)}, bf16[4,640]{1,0:T(4,128)(2,1)S(1)}, u32[]{:S(2)}, u32[]{:S(2)}) collective-permute-start(bf16[4,640]{1,0:T(4,128)(2,1)S(1)} %pad_maximum_fusion), channel_id=1, source_target_pairs={{0,1},{1,0},{2,3},{3,2},{4,5},{5,4},{6,7},{7,6},{8,9},{9,8},{10,11... | collective-permute-start | bytes 15368 | tf_op jit(solution)/shard_map/ppermute | solution.py:30
  6.7 18.7 %all-to-all-start = ((f32[32,1,128]{2,1,0:T(1,128)}), f32[32,1,128]{2,1,0:T(1,128)S(1)}, u32[]{:S(2)}, u32[]{:S(2)}) async-start(f32[32,1,128]{2,1,0:T(1,128)} %broadcast_in_dim.21), calls=%async_computation | async-start | bytes 32768 | tf_op jit(solution)/shard_map/all_to_all | solution.py:53
  13.8 18.3 %collective-permute-start.5 = (bf16[4,640,128]{2,1,0:T(8,128)(2,1)}, bf16[4,640,128]{2,1,0:T(8,128)(2,1)S(1)}, u32[]{:S(2)}, u32[]{:S(2)}) collective-permute-start(bf16[4,640,128]{2,1,0:T(8,128)(2,1)} %bitcast.34), channel_id=1, source_target_pairs={{1,17},{16,0},{3,19},{18,2},{5,21},{20,4},{7,23},{22,6},{9,25},{24... | collective-permute-start | bytes 1966088 | tf_op jit(solution)/shard_map/ppermute | solution.py:68
  16.8 12.0 %collective-permute-start.1 = (bf16[1,640,128]{2,1,0:T(8,128)(2,1)S(1)}, bf16[1,640,128]{2,1,0:T(8,128)(2,1)}, u32[]{:S(2)}, u32[]{:S(2)}) collective-permute-start(bf16[1,640,128]{2,1,0:T(8,128)(2,1)S(1)} %get-tuple-element.59), channel_id=1, source_target_pairs={{0,2},{2,4},{4,6},{6,8},{8,10},{10,12},{12,14},{1,3},{3,5},{5,7},{... | collective-permute-start | bytes 491528 | tf_op jit(solution)/shard_map/ppermute | solution.py:478
  21.1 8.6 %collective-permute-start.2 = (bf16[1,640,128]{2,1,0:T(8,128)(2,1)}, bf16[1,640,128]{2,1,0:T(8,128)(2,1)}, u32[]{:S(2)}, u32[]{:S(2)}) collective-permute-start(bf16[1,640,128]{2,1,0:T(8,128)(2,1)} %get-tuple-element.58), channel_id=1, source_target_pairs={{2,0},{4,2},{6,4},{8,6},{10,8},{12,10},{14,12},{3,1},{5,3},{7,5},{... | collective-permute-start | bytes 491528 | tf_op jit(solution)/shard_map/ppermute | solution.py:479
  24.3 1.1 copy-start.4
  25.9 27.4 %collective-permute-start.11 = (bf16[2,512,512]{2,1,0:T(8,128)(2,1)}, bf16[2,512,512]{2,1,0:T(8,128)(2,1)S(1)}, u32[]{:S(2)}, u32[]{:S(2)}) collective-permute-start(bf16[2,512,512]{2,1,0:T(8,128)(2,1)} %bitcast.44), channel_id=1, source_target_pairs={{0,4},{4,8},{8,12},{12,14},{14,10},{10,6},{6,2},{2,0},{1,5},{5,9},... | collective-permute-start | bytes 3145736 | tf_op jit(solution)/shard_map/ppermute | solution.py:495
  28.8 26.1 %collective-permute-start.12 = (bf16[2,512,512]{2,1,0:T(8,128)(2,1)}, bf16[2,512,512]{2,1,0:T(8,128)(2,1)S(1)}, u32[]{:S(2)}, u32[]{:S(2)}) collective-permute-start(bf16[2,512,512]{2,1,0:T(8,128)(2,1)} %bitcast.45), channel_id=1, source_target_pairs={{4,0},{8,4},{12,8},{14,12},{10,14},{6,10},{2,6},{0,2},{5,1},{9,5},... | collective-permute-start | bytes 3145736 | tf_op jit(solution)/shard_map/ppermute | solution.py:495
  30.7 28.6 %copy-start.14 = (bf16[2,640,128]{2,1,0:T(8,128)(2,1)}, bf16[2,640,128]{2,1,0:T(8,128)(2,1)S(1)}, u32[]{:S(2)}) copy-start(bf16[2,640,128]{2,1,0:T(8,128)(2,1)S(1)} %constant_dynamic-update-slice_fusion.refs_2_) | copy-start | bytes 983044
  30.7 9.1 %collective-permute-start.7 = (bf16[2,640,128]{2,1,0:T(8,128)(2,1)S(1)}, bf16[2,640,128]{2,1,0:T(8,128)(2,1)}, u32[]{:S(2)}, u32[]{:S(2)}) collective-permute-start(bf16[2,640,128]{2,1,0:T(8,128)(2,1)S(1)} %constant_dynamic-update-slice_fusion.refs_2_), channel_id=1, source_target_pairs={{1,17},{16,0},{3,19},{18,2},{5,21},{20,4},{7,23},{22,6},{9,25},{24... | collective-permute-start | bytes 983048 | tf_op jit(solution)/shard_map/ppermute | solution.py:68
  32.0 10.8 %copy-start.16 = (bf16[4,640,128]{2,1,0:T(8,128)(2,1)}, bf16[4,640,128]{2,1,0:T(8,128)(2,1)S(1)}, u32[]{:S(2)}) copy-start(bf16[4,640,128]{2,1,0:T(8,128)(2,1)S(1)} %collective-permute-done.5.refs_0_) | copy-start | bytes 1966084
  32.1 10.8 %collective-permute-start.6 = (bf16[4,640,128]{2,1,0:T(8,128)(2,1)S(1)}, bf16[4,640,128]{2,1,0:T(8,128)(2,1)}, u32[]{:S(2)}, u32[]{:S(2)}) collective-permute-start(bf16[4,640,128]{2,1,0:T(8,128)(2,1)S(1)} %collective-permute-done.5.refs_0_), channel_id=1, source_target_pairs={{0,1},{17,16},{2,3},{19,18},{4,5},{21,20},{6,7},{23,22},{8,9},{25,... | collective-permute-start | bytes 1966088 | tf_op jit(solution)/shard_map/ppermute | solution.py:71
  39.8 3.0 %collective-permute-start.8 = (bf16[2,640,128]{2,1,0:T(8,128)(2,1)}, bf16[2,640,128]{2,1,0:T(8,128)(2,1)}, u32[]{:S(2)}, u32[]{:S(2)}) collective-permute-start(bf16[2,640,128]{2,1,0:T(8,128)(2,1)} %collective-permute-done.7.refs_2_), channel_id=1, source_target_pairs={{0,1},{17,16},{2,3},{19,18},{4,5},{21,20},{6,7},{23,22},{8,9},{25,... | collective-permute-start | bytes 983048 | tf_op jit(solution)/shard_map/ppermute | solution.py:71
  42.8 14.1 %copy-start.12 = (bf16[1,4,640,128]{3,2,1,0:T(8,128)(2,1)S(1)}, bf16[1,4,640,128]{3,2,1,0:T(8,128)(2,1)}, u32[]{:S(2)}) copy-start(bf16[1,4,640,128]{3,2,1,0:T(8,128)(2,1)} %param.12) | copy-start | bytes 1966084
  42.8 19.5 %copy-start.18 = (bf16[640]{0:T(1024)(128)(2,1)S(1)}, bf16[640]{0:T(1024)(128)(2,1)}, u32[]{:S(2)}) copy-start(bf16[640]{0:T(1024)(128)(2,1)} %param.19) | copy-start | bytes 3844
  53.3 21.4 %copy-start.6 = (bf16[2,512,512]{2,1,0:T(8,128)(2,1)}, bf16[2,512,512]{2,1,0:T(8,128)(2,1)S(1)}, u32[]{:S(2)}) copy-start(bf16[2,512,512]{2,1,0:T(8,128)(2,1)S(1)} %collective-permute-done.11.refs_3_.refs_4_) | copy-start | bytes 3145732
  54.9 19.8 %copy-start.8 = (bf16[2,512,512]{2,1,0:T(8,128)(2,1)}, bf16[2,512,512]{2,1,0:T(8,128)(2,1)S(1)}, u32[]{:S(2)}) copy-start(bf16[2,512,512]{2,1,0:T(8,128)(2,1)S(1)} %collective-permute-done.12.refs_5_.refs_6_) | copy-start | bytes 3145732
  54.9 25.3 %collective-permute-start.13 = (bf16[2,512,512]{2,1,0:T(8,128)(2,1)S(1)}, bf16[2,512,512]{2,1,0:T(8,128)(2,1)}, u32[]{:S(2)}, u32[]{:S(2)}) collective-permute-start(bf16[2,512,512]{2,1,0:T(8,128)(2,1)S(1)} %collective-permute-done.11.refs_3_.refs_4_), channel_id=1, source_target_pairs={{0,4},{4,8},{8,12},{12,14},{14,10},{10,6},{6,2},{2,0},{1,5},{5,9},... | collective-permute-start | bytes 3145736 | tf_op jit(solution)/shard_map/ppermute | solution.py:495
  56.3 25.0 %collective-permute-start.14 = (bf16[2,512,512]{2,1,0:T(8,128)(2,1)S(1)}, bf16[2,512,512]{2,1,0:T(8,128)(2,1)}, u32[]{:S(2)}, u32[]{:S(2)}) collective-permute-start(bf16[2,512,512]{2,1,0:T(8,128)(2,1)S(1)} %collective-permute-done.12.refs_5_.refs_6_), channel_id=1, source_target_pairs={{4,0},{8,4},{12,8},{14,12},{10,14},{6,10},{2,6},{0,2},{5,1},{9,5},... | collective-permute-start | bytes 3145736 | tf_op jit(solution)/shard_map/ppermute | solution.py:495
  56.9 6.2 %collective-permute-start = (bf16[4,640,128]{2,1,0:T(8,128)(2,1)S(1)}, bf16[4,640,128]{2,1,0:T(8,128)(2,1)S(1)}, u32[]{:S(2)}, u32[]{:S(2)}) collective-permute-start(bf16[4,640,128]{2,1,0:T(8,128)(2,1)S(1)} %bitcast.36), channel_id=1, source_target_pairs={{0,1},{17,16},{2,3},{19,18},{4,5},{21,20},{6,7},{23,22},{8,9},{25,... | collective-permute-start | bytes 1966088 | tf_op jit(solution)/shard_map/ppermute | solution.py:70
  58.4 16.3 %collective-permute-start.9 = (bf16[4,640,128]{2,1,0:T(8,128)(2,1)}, bf16[4,640,128]{2,1,0:T(8,128)(2,1)S(1)}, u32[]{:S(2)}, u32[]{:S(2)}) collective-permute-start(bf16[4,640,128]{2,1,0:T(8,128)(2,1)} %norm_conv.3), channel_id=1, source_target_pairs={{0,16},{16,0},{1,17},{17,1},{2,18},{18,2},{3,19},{19,3},{4,20},{20... | collective-permute-start | bytes 1966088 | tf_op jit(solution)/shard_map/ppermute | solution.py:30
  59.3 3.8 %collective-permute-start.3 = (bf16[2,640,128]{2,1,0:T(8,128)(2,1)S(1)}, bf16[2,640,128]{2,1,0:T(8,128)(2,1)S(1)}, u32[]{:S(2)}, u32[]{:S(2)}) collective-permute-start(bf16[2,640,128]{2,1,0:T(8,128)(2,1)S(1)} %constant_dynamic-update-slice_fusion.refs_2_), channel_id=1, source_target_pairs={{0,1},{17,16},{2,3},{19,18},{4,5},{21,20},{6,7},{23,22},{8,9},{25,... | collective-permute-start | bytes 983048 | tf_op jit(solution)/shard_map/ppermute | solution.py:70
  63.1 0.8 copy-start.17
  63.1 0.9 copy-start.15
  64.0 10.7 %copy-start.13 = (bf16[1,4,640,128]{3,2,1,0:T(8,128)(2,1)S(1)}, bf16[1,4,640,128]{3,2,1,0:T(8,128)(2,1)}, u32[]{:S(2)}) copy-start(bf16[1,4,640,128]{3,2,1,0:T(8,128)(2,1)} %param.12) | copy-start | bytes 1966084
  76.3 9.3 %copy-start.2 = (bf16[4,640,128]{2,1,0:T(8,128)(2,1)}, bf16[4,640,128]{2,1,0:T(8,128)(2,1)S(1)}, u32[]{:S(2)}) copy-start(bf16[4,640,128]{2,1,0:T(8,128)(2,1)S(1)} %add_convert_fusion.own_ref.refs_0_) | copy-start | bytes 1966084
  81.3 24.3 %collective-permute-start.15 = (bf16[2,512,512]{2,1,0:T(8,128)(2,1)}, bf16[2,512,512]{2,1,0:T(8,128)(2,1)S(1)}, u32[]{:S(2)}, u32[]{:S(2)}) collective-permute-start(bf16[2,512,512]{2,1,0:T(8,128)(2,1)} %collective-permute-done.13.refs_1_.refs_2_), channel_id=1, source_target_pairs={{0,4},{4,8},{8,12},{12,14},{14,10},{10,6},{6,2},{2,0},{1,5},{5,9},... | collective-permute-start | bytes 3145736 | tf_op jit(solution)/shard_map/ppermute | solution.py:495
  82.8 24.0 %collective-permute-start.16 = (bf16[2,512,512]{2,1,0:T(8,128)(2,1)}, bf16[2,512,512]{2,1,0:T(8,128)(2,1)S(1)}, u32[]{:S(2)}, u32[]{:S(2)}) collective-permute-start(bf16[2,512,512]{2,1,0:T(8,128)(2,1)} %collective-permute-done.14.refs_3_.refs_4_), channel_id=1, source_target_pairs={{4,0},{8,4},{12,8},{14,12},{10,14},{6,10},{2,6},{0,2},{5,1},{9,5},... | collective-permute-start | bytes 3145736 | tf_op jit(solution)/shard_map/ppermute | solution.py:495
  83.3 2.2 %collective-permute-start.10 = (bf16[4,640,128]{2,1,0:T(8,128)(2,1)S(1)}, bf16[4,640,128]{2,1,0:T(8,128)(2,1)}, u32[]{:S(2)}, u32[]{:S(2)}) collective-permute-start(bf16[4,640,128]{2,1,0:T(8,128)(2,1)S(1)} %add_convert_fusion.own_ref.refs_0_), channel_id=1, source_target_pairs={{0,1},{1,0},{2,3},{3,2},{4,5},{5,4},{6,7},{7,6},{8,9},{9,8},{10,11... | collective-permute-start | bytes 1966088 | tf_op jit(solution)/shard_map/ppermute | solution.py:30
  85.6 8.5 %copy-start.7 = (bf16[2,512,512]{2,1,0:T(8,128)(2,1)S(1)}, bf16[2,512,512]{2,1,0:T(8,128)(2,1)}, u32[]{:S(2)}) copy-start(bf16[2,512,512]{2,1,0:T(8,128)(2,1)} %copy-done.6) | copy-start | bytes 3145732
  85.6 8.5 %copy-start.9 = (bf16[2,512,512]{2,1,0:T(8,128)(2,1)S(1)}, bf16[2,512,512]{2,1,0:T(8,128)(2,1)}, u32[]{:S(2)}) copy-start(bf16[2,512,512]{2,1,0:T(8,128)(2,1)} %copy-done.8) | copy-start | bytes 3145732
  94.1 1.0 copy-start.1
  95.1 1.2 copy-start.10
  106.8 16.6 %collective-permute-start.17 = (bf16[1,512,512]{2,1,0:T(8,128)(2,1)S(1)}, bf16[1,512,512]{2,1,0:T(8,128)(2,1)S(1)}, u32[]{:S(2)}, u32[]{:S(2)}) collective-permute-start(bf16[1,512,512]{2,1,0:T(8,128)(2,1)S(1)} %slice.34), channel_id=1, source_target_pairs={{0,4},{4,8},{8,12},{12,14},{14,10},{10,6},{6,2},{2,0},{1,5},{5,9},... | collective-permute-start | bytes 1572872 | tf_op jit(solution)/shard_map/ppermute | solution.py:495
  108.1 15.3 %collective-permute-start.18 = (bf16[1,512,512]{2,1,0:T(8,128)(2,1)S(1)}, bf16[1,512,512]{2,1,0:T(8,128)(2,1)S(1)}, u32[]{:S(2)}, u32[]{:S(2)}) collective-permute-start(bf16[1,512,512]{2,1,0:T(8,128)(2,1)S(1)} %slice.35), channel_id=1, source_target_pairs={{4,0},{8,4},{12,8},{14,12},{10,14},{6,10},{2,6},{0,2},{5,1},{9,5},... | collective-permute-start | bytes 1572872 | tf_op jit(solution)/shard_map/ppermute | solution.py:495
  116.5 6.9 %copy-start.5 = (bf16[2,640,512]{2,1,0:T(8,128)(2,1)S(1)}, bf16[2,640,512]{2,1,0:T(8,128)(2,1)}, u32[]{:S(2)}) copy-start(bf16[2,640,512]{2,1,0:T(8,128)(2,1)} %copy-done.4) | copy-start | bytes 3932164
  123.4 5.6 %copy-start.3 = (bf16[4,640,128]{2,1,0:T(8,128)(2,1)S(1)}, bf16[4,640,128]{2,1,0:T(8,128)(2,1)}, u32[]{:S(2)}) copy-start(bf16[4,640,128]{2,1,0:T(8,128)(2,1)} %copy-done.2) | copy-start | bytes 1966084
  128.9 2.2 %collective-permute-start.19 = (bf16[2,4,320,128]{3,2,1,0:T(8,128)(2,1)S(1)}, bf16[2,4,320,128]{3,2,1,0:T(8,128)(2,1)S(1)}, u32[]{:S(2)}, u32[]{:S(2)}) collective-permute-start(bf16[2,4,320,128]{3,2,1,0:T(8,128)(2,1)S(1)} %get-tuple-element.45), channel_id=1, source_target_pairs={{0,1},{1,0},{2,3},{3,2},{4,5},{5,4},{6,7},{7,6},{8,9},{9,8},{10,11... | collective-permute-start | bytes 1966088 | tf_op jit(solution)/shard_map/ppermute | solution.py:30
  131.1 9.9 %collective-permute-start.20 = (bf16[4,320,128]{2,1,0:T(8,128)(2,1)S(1)}, bf16[4,320,128]{2,1,0:T(8,128)(2,1)}, u32[]{:S(2)}, u32[]{:S(2)}) collective-permute-start(bf16[4,320,128]{2,1,0:T(8,128)(2,1)S(1)} %branch_out.2), channel_id=1, source_target_pairs={{0,16},{16,0},{1,17},{17,1},{2,18},{18,2},{3,19},{19,3},{4,20},{20... | collective-permute-start | bytes 983048 | tf_op jit(solution)/shard_map/ppermute | solution.py:30

commit v7 on v6

--- a/solution.py
+++ b/solution.py
@@ -35,16 +35,6 @@
     forward = [(order[i], order[(i + 1) % count]) for i in range(count)]
     backward = [(j, i) for i, j in forward]
     return forward, backward
-
-
-def gather_tp(array, axis):
-    if lax.axis_size("tp") != 2:
-        return lax.all_gather(array, "tp", axis=axis, tiled=True)
-    other = swapped(array, "tp")
-    first = lax.axis_index("tp") == 0
-    return jnp.concatenate(
-        [jnp.where(first, array, other), jnp.where(first, other, array)], axis=axis
-    )
 
 
 def summed(array, axes):
@@ -477,8 +467,19 @@
     down_pairs = [(i + 1, i) for i in range(rows_count - 1)]
     before = lax.ppermute(latent_rows[span_rows - 1 :], "rows", up_pairs)
     after = lax.ppermute(latent_rows[:1], "rows", down_pairs)
-    x_mine, x_other = halves_of_inputs(latent_rows, (table,))
+    x_mine, x_other = halves_of_inputs(latent_rows)
     edges_mine, edges_other = halves_of_inputs(jnp.concatenate([before, after], axis=0))
+
+    joined = jnp.concatenate([gn_gain, gn_bias, ln_gain, ln_bias])
+    if tp_count == 2:
+        other = swapped(joined, "tp").reshape(4, 1, -1)
+        pieces = [joined.reshape(4, 1, -1), other]
+        vectors = jnp.where(
+            tp == 0, jnp.concatenate(pieces, axis=1), jnp.concatenate(pieces[::-1], axis=1)
+        ).reshape(4, -1)
+    else:
+        vectors = lax.all_gather(joined.reshape(4, -1), "tp", axis=1, tiled=True)
+    vectors = vectors.astype(jnp.float32)
 
     forward, backward = ring_pairs(rows_count)
     last = rows_count // 2
@@ -501,9 +502,8 @@
             return [((ahead, 0), (behind, 0))]
         return [((ahead, 0), (ahead, 1)), ((behind, 0), (behind, 1))]
 
-    next_hop(table)
-
-    vectors = gather_tp(jnp.stack([gn_gain, gn_bias, ln_gain, ln_bias]), 1).astype(jnp.float32)
+    next_hop(vectors)
+
     amount = span_rows * rows_count * grid_width * group_width
     half = D // 2
     gn_affine = lax.dynamic_slice_in_dim(vectors[:2], cfg * half, half, 1).T
@@ -517,11 +517,15 @@
     w_project = w_qkv.transpose(1, 0, 2)
     flip = jnp.logical_and(tp_count == 2, tp == 0)
     w_back = arrange_call(flip, w_out, tp_count)
-    gn_affine, w_back = lax.optimization_barrier((gn_affine, w_back))
+    order = jnp.stack([tp, 1 - tp]).astype(jnp.int32) if tp_count == 2 else jnp.zeros((1,), jnp.int32)
+    gn_affine, ln_affine, order, w_back = lax.optimization_barrier(
+        (gn_affine, ln_affine, order, w_back)
+    )
+    flags_other = need(flags_other, tuple(x_mine[1:] + edges_mine[1:]) + hops[1])
+    next_hop()
 
     conv_sent = conv_call(flags_other, table, amount, x_other, edges_other, gn_affine, conv_w, jnp.bfloat16)
     conv_received = swapped(conv_sent, "cfg")
-    next_hop(conv_sent)
     conv_own = conv_call(flags_mine, table, amount, x_mine, edges_mine, gn_affine, conv_w, jnp.float32)
 
     half_width = TEMB // 2
@@ -540,18 +544,16 @@
 
     if tp_count == 2:
         parts = [resid, need(swapped(resid, "tp"), hops[2])]
-        order = jnp.stack([tp, 1 - tp]).astype(jnp.int32)
     else:
         parts = [lax.all_gather(resid, "tp", axis=1, tiled=True)]
-        order = jnp.zeros((1,), jnp.int32)
     next_hop(resid)
     queries, fresh = project_call(order, parts, ln_affine, w_project)
     resid_split = split_call(resid)
     fresh_kv = fresh.reshape(1, 2, span_rows, grid_width, local_features)
 
-    group = [((fresh, 0), (fresh, 1))] + blocks_of(1)
+    group = [((fresh, 0), (fresh, 1))] + blocks_of(1) + blocks_of(2)
     state = None
-    for hop in range(2, last + 1):
+    for hop in range(3, last + 1):
         state = attention_call(queries, group, state)
         while len(hops) <= last:
             next_hop(state[0])

time: 144 us -> 145 us (level)
  starting transfers between devices: 35.9 us -> 40.6 us
  local copies, waits for them, and re-layouts: 13.9 us -> 12 us
  Pallas kernels: 61.1 us -> 59.2 us
    ppermute x5, starting transfers between devices: 0.73 us -> 5.11 us  [swapped(): lax.ppermute(array, axis, [(i, i ^ 1) for i in range(lax.axis_size(axis))])]
    ppermute x5, waiting for transfers between devices: 11.3 us -> 14.6 us  [swapped(): lax.ppermute(array, axis, [(i, i ^ 1) for i in range(lax.axis_size(axis))])]
    another operation x4 -> x0, local copies, waits for them, and re-layouts: 2.86 us -> none  [per_device(): jnp.stack([gn_gain, gn_bias, ln_gain, ln_bias])]
    ppermute x4, waiting for transfers between devices: 3.84 us -> 1.18 us  [next_hop(): lax.ppermute(behind, 'rows', backward)]
    pallas_call x4 -> x3, Pallas kernels: 29.2 us -> 27.4 us  [attention_call(): pl.pallas_call(functools.partial(attention_kernel, len(pairs), state is n...]
    transpose x0 -> x1, local copies, waits for them, and re-layouts: none -> 1.74 us  [per_device(): gn_affine = lax.dynamic_slice_in_dim(vectors[:2], cfg * half, half, 1).T]
    all_to_all x1, starting transfers between devices: 7.06 us -> 5.4 us  [summed(): return jnp.sum(lax.all_to_all(spread, axes, 0, 0, tiled=True), axis=0)]
    unnamed x40 -> x32, local copies, waits for them, and re-layouts: 6.19 us -> 5.17 us
  transfers between devices with their start and end apart: 22 -> 22, of which waited for: 9 -> 7; matrix products, arithmetic and copies ran while one was open for 8% -> 8% of each run, Pallas kernels for 39% -> 37%
where the time goes in v7:
time: 145 us; the launch traced here: 144 us
  Pallas kernels  59.2 us (41%)
  starting transfers between devices  40.6 us (28%)
  waiting for transfers between devices  23.4 us (16%)
  local copies, waits for them, and re-layouts  12 us (8%)
  other arithmetic  7.23 us (5%)
  between operations  1.74 us (1%)
    pallas_call x3, Pallas kernels, attention_call(): pl.pallas_call(functools.partial(attention_kernel, len(pairs), state is n...  27.4 us
    pallas_call x2, Pallas kernels, conv_call(): pl.pallas_call(functools.partial(conv_kernel, len(xs), amount), in_specs=...  21 us
    ppermute x5, waiting for transfers between devices, swapped(): lax.ppermute(array, axis, [(i, i ^ 1) for i in range(lax.axis_size(axis))])  14.6 us
    pallas_call x1, Pallas kernels, project_call(): pl.pallas_call(functools.partial(project_kernel, len(parts)), in_specs=[p...  8.31 us
    ppermute x4, starting transfers between devices, next_hop(): lax.ppermute(ahead, 'rows', forward)  8.13 us
    ppermute x2, starting transfers between devices, halves_of_inputs(): across_side = lax.ppermute(need(across, others), ('cfg', 'tp'), pairs)  6.74 us
    all_to_all x1, starting transfers between devices, summed(): return jnp.sum(lax.all_to_all(spread, axes, 0, 0, tiled=True), axis=0)  5.4 us
    unnamed x32, local copies, waits for them, and re-layouts  5.17 us
  transfers between devices with their start and end apart: 22, of which 7 were waited for; matrix products, arithmetic and copies ran while one was open for 8% of the time, Pallas kernels for 37%

profile of v7, /device:TPU:0, one launch (start us, length us, event | category | flops | bytes accessed | tf_op | source)
XLA Modules:
  0.0 144.5 jit_solution(14795783606347860407)
XLA Ops:
  0.6 0.0 copy-start
  0.7 1.1 slice_bitcast_fusion
  1.8 4.9 %collective-permute-start.1 = (bf16[1,640,128]{2,1,0:T(8,128)(2,1)S(1)}, bf16[1,640,128]{2,1,0:T(8,128)(2,1)S(1)}, u32[]{:S(2)}, u32[]{:S(2)}) collective-permute-start(bf16[1,640,128]{2,1,0:T(8,128)(2,1)S(1)} %get-tuple-element.53), channel_id=1, source_target_pairs={{0,2},{2,4},{4,6},{6,8},{8,10},{10,12},{12,14},{1,3},{3,5},{5,7},{... | collective-permute-start | bytes 491528 | tf_op jit(solution)/shard_map/ppermute | solution.py:468
  6.7 1.3 collective-permute-start.2
  8.0 3.7 %collective-permute-start.5 = (bf16[2,512,512]{2,1,0:T(8,128)(2,1)}, bf16[2,512,512]{2,1,0:T(8,128)(2,1)S(1)}, u32[]{:S(2)}, u32[]{:S(2)}) collective-permute-start(bf16[2,512,512]{2,1,0:T(8,128)(2,1)} %bitcast.47), channel_id=1, source_target_pairs={{0,4},{4,8},{8,12},{12,14},{14,10},{10,6},{6,2},{2,0},{1,5},{5,9},... | collective-permute-start | bytes 3145736 | tf_op jit(solution)/shard_map/ppermute | solution.py:496
  11.6 1.3 convert_reduce_fusion
  13.0 0.1 reduce_sum.32
  13.1 0.1 reduce_sum.45
  13.2 0.1 reduce_sum.36
  13.3 0.1 reduce_sum.46
  13.4 0.1 dynamic_update_slice.3
  13.6 0.1 broadcast_in_dim.20
  13.7 0.6 broadcast_in_dim.21
  14.3 5.4 %all-to-all-start = ((f32[32,1,128]{2,1,0:T(1,128)}), f32[32,1,128]{2,1,0:T(1,128)S(1)}, u32[]{:S(2)}, u32[]{:S(2)}) async-start(f32[32,1,128]{2,1,0:T(1,128)} %broadcast_in_dim.21), calls=%async_computation | async-start | bytes 32768 | tf_op jit(solution)/shard_map/all_to_all | solution.py:43
  19.7 1.3 collective-permute-start.7
  21.1 3.1 %collective-permute-start.4 = (bf16[2560]{0:T(1024)(128)(2,1)S(1)}, bf16[2560]{0:T(1024)(128)(2,1)S(1)}, u32[]{:S(2)}, u32[]{:S(2)}) collective-permute-start(bf16[2560]{0:T(1024)(128)(2,1)S(1)} %pad_maximum_fusion), channel_id=1, source_target_pairs={{0,1},{1,0},{2,3},{3,2},{4,5},{5,4},{6,7},{7,6},{8,9},{9,8},{10,11... | collective-permute-start | bytes 15368 | tf_op jit(solution)/shard_map/ppermute | solution.py:30
  24.2 0.7 constant_dynamic-update-slice_fusion.1
  24.9 0.7 constant_dynamic-update-slice_fusion.refs_2_
  25.6 2.7 %collective-permute-start.3 = (bf16[2,640,128]{2,1,0:T(8,128)(2,1)}, bf16[2,640,128]{2,1,0:T(8,128)(2,1)}, u32[]{:S(2)}, u32[]{:S(2)}) collective-permute-start(bf16[2,640,128]{2,1,0:T(8,128)(2,1)} %constant_dynamic-update-slice_fusion.refs_2_), channel_id=1, source_target_pairs={{0,1},{17,16},{2,3},{19,18},{4,5},{21,20},{6,7},{23,22},{8,9},{25,... | collective-permute-start | bytes 983048 | tf_op jit(solution)/shard_map/ppermute | solution.py:60
  28.3 0.1 add_convert_fusion.1
  28.3 0.6 pad_add_fusion.2
  29.0 1.3 copy-done.5
  30.3 1.2 arrange.1.refs_5_
  31.5 2.1 %collective-permute-start = (bf16[4,640,128]{2,1,0:T(8,128)(2,1)S(1)}, bf16[4,640,128]{2,1,0:T(8,128)(2,1)}, u32[]{:S(2)}, u32[]{:S(2)}) collective-permute-start(bf16[4,640,128]{2,1,0:T(8,128)(2,1)S(1)} %bitcast.40), channel_id=1, source_target_pairs={{0,1},{17,16},{2,3},{19,18},{4,5},{21,20},{6,7},{23,22},{8,9},{25,... | collective-permute-start | bytes 1966088 | tf_op jit(solution)/shard_map/ppermute | solution.py:60
  33.7 1.3 collective-permute-start.9
  35.0 4.7 %collective-permute-start.8 = (bf16[4,640,128]{2,1,0:T(8,128)(2,1)}, bf16[4,640,128]{2,1,0:T(8,128)(2,1)}, u32[]{:S(2)}, u32[]{:S(2)}) collective-permute-start(bf16[4,640,128]{2,1,0:T(8,128)(2,1)} %collective-permute-done.7.refs_0_), channel_id=1, source_target_pairs={{0,1},{17,16},{2,3},{19,18},{4,5},{21,20},{6,7},{23,22},{8,9},{25,... | collective-permute-start | bytes 1966088 | tf_op jit(solution)/shard_map/ppermute | solution.py:61
  39.7 0.7 pad_add_fusion.1.order_ref
  40.4 2.5 %collective-permute-done.9.refs_2_ = bf16[2,640,128]{2,1,0:T(8,128)(2,1)} collective-permute-done((bf16[2,640,128]{2,1,0:T(8,128)(2,1)}, bf16[2,640,128]{2,1,0:T(8,128)(2,1)}, u32[]{:S(2)}, u32[]{:S(2)}) %collective-permute-start.9) | collective-permute-done | bytes 327712 | tf_op jit(solution)/shard_map/ppermute | solution.py:58
  43.0 2.0 %collective-permute-start.10 = (bf16[2,640,128]{2,1,0:T(8,128)(2,1)}, bf16[2,640,128]{2,1,0:T(8,128)(2,1)}, u32[]{:S(2)}, u32[]{:S(2)}) collective-permute-start(bf16[2,640,128]{2,1,0:T(8,128)(2,1)} %collective-permute-done.9.refs_2_), channel_id=1, source_target_pairs={{0,1},{17,16},{2,3},{19,18},{4,5},{21,20},{6,7},{23,22},{8,9},{25,... | collective-permute-start | bytes 983048 | tf_op jit(solution)/shard_map/ppermute | solution.py:61
  45.0 1.1 copy.28
  46.1 1.5 %collective-permute-start.13 = (bf16[2,512,512]{2,1,0:T(8,128)(2,1)S(1)}, bf16[2,512,512]{2,1,0:T(8,128)(2,1)}, u32[]{:S(2)}, u32[]{:S(2)}) collective-permute-start(bf16[2,512,512]{2,1,0:T(8,128)(2,1)S(1)} %collective-permute-done.5.refs_3_.refs_4_), channel_id=1, source_target_pairs={{0,4},{4,8},{8,12},{12,14},{14,10},{10,6},{6,2},{2,0},{1,5},{5,9},... | collective-permute-start | bytes 3145736 | tf_op jit(solution)/shard_map/ppermute | solution.py:496
  47.6 0.6 collective-permute-start.14
  48.1 1.7 %dynamic-slice_bitcast_fusion.refs_4_ = f32[640,2]{1,0:T(8,128)} fusion(f32[2,1280]{0,1:T(8,128)} %bitcast.43, s32[]{:T(128)S(6)} %select_n.36), kind=kLoop, calls=%fused_computation.10 | loop fusion | bytes 10244 | tf_op jit(solution)/shard_map/transpose | solution.py:509
  49.9 1.1 copy.29
  51.0 0.6 reduce_sum.47.sums_ref
  51.6 10.3 %norm_conv.3 = bf16[4,640,128]{2,1,0:T(8,128)(2,1)} custom-call(s32[4]{0:T(128)} %get-tuple-element.25.flags_ref, f32[128]{0:T(128)} %reduce_sum.47.sums_ref, bf16[4,640,128]{2,1,0:T(8,128)(2,1)} %collective-permute-done.7.refs_0_, bf16[4,640,128]{2,1,0:T(8,128)(2,1)} %collective-permute-done.8.refs_1_, bf16[2,640,128]{2,1,0:T(8,128)(2,1)} %collective-permute-done.9.refs_2_, ...), custom_call_target="tpu_custom_call" | custom-call | flops 180000000 | bytes 1000 | tf_op jit(solution)/shard_map/norm_conv/pallas_call | solution.py:133
  62.0 0.1 collective-permute-start.11
  62.8 0.1 divide_multiply_fusion
  62.9 0.3 convolution_reduce_fusion
  63.2 10.6 %norm_conv.2 = f32[4,640,128]{2,1,0:T(8,128)} custom-call(s32[4]{0:T(128)} %get-tuple-element.57.flags_ref, f32[128]{0:T(128)} %reduce_sum.47.sums_ref, bf16[4,640,128]{2,1,0:T(8,128)(2,1)} %bitcast.38, bf16[4,640,128]{2,1,0:T(8,128)(2,1)} %collective-permute-done.refs_1_, bf16[2,640,128]{2,1,0:T(8,128)(2,1)} %constant_dynamic-update-slice_fusion.refs_2_, ...), custom_call_target="tpu_custom_call" | custom-call | flops 180000000 | bytes 1000 | tf_op jit(solution)/shard_map/norm_conv/pallas_call | solution.py:133
  73.9 3.4 %collective-permute-done.11 = bf16[4,640,128]{2,1,0:T(8,128)(2,1)S(1)} collective-permute-done((bf16[4,640,128]{2,1,0:T(8,128)(2,1)}, bf16[4,640,128]{2,1,0:T(8,128)(2,1)S(1)}, u32[]{:S(2)}, u32[]{:S(2)}) %collective-permute-start.11) | collective-permute-done | bytes 655392 | tf_op jit(solution)/shard_map/ppermute | solution.py:30
  77.3 1.6 %add_convert_fusion.own_ref.refs_0_ = bf16[4,640,128]{2,1,0:T(8,128)(2,1)S(1)} fusion(f32[4,640,128]{2,1,0:T(8,128)} %norm_conv.2, bf16[4,640,128]{2,1,0:T(8,128)(2,1)S(1)} %collective-permute-done.11, f32[640]{0:T(1024)S(1)} %convert_add_fusion.1, bf16[1,4,640,128]{3,2,1,0:T(8,128)(2,1)S(1)} %copy-done.7), kind=kLoop, calls=%fused_computation.3 | loop fusion | flops 1966080 | bytes 3279360 | tf_op jit(solution)/shard_map/convert_element_type | solution.py:543
  78.9 1.5 %collective-permute-start.15 = (bf16[2,512,512]{2,1,0:T(8,128)(2,1)}, bf16[2,512,512]{2,1,0:T(8,128)(2,1)S(1)}, u32[]{:S(2)}, u32[]{:S(2)}) collective-permute-start(bf16[2,512,512]{2,1,0:T(8,128)(2,1)} %collective-permute-done.13.refs_7_.refs_8_), channel_id=1, source_target_pairs={{0,4},{4,8},{8,12},{12,14},{14,10},{10,6},{6,2},{2,0},{1,5},{5,9},... | collective-permute-start | bytes 3145736 | tf_op jit(solution)/shard_map/ppermute | solution.py:496
  80.4 0.6 collective-permute-start.16
  81.0 2.1 %collective-permute-done.12.refs_1_ = bf16[4,640,128]{2,1,0:T(8,128)(2,1)S(1)} collective-permute-done((bf16[4,640,128]{2,1,0:T(8,128)(2,1)S(1)}, bf16[4,640,128]{2,1,0:T(8,128)(2,1)S(1)}, u32[]{:S(2)}, u32[]{:S(2)}) %collective-permute-start.12) | collective-permute-done | bytes 655392 | tf_op jit(solution)/shard_map/ppermute | solution.py:30
  83.1 0.8 copy-done.8
  83.9 8.3 %norm_project.1 = (bf16[512,512]{1,0:T(8,128)(2,1)}, bf16[2,512,512]{2,1,0:T(8,128)(2,1)}) custom-call(s32[2]{0:T(128)} %pad_add_fusion.1.order_ref, bf16[4,640,128]{2,1,0:T(8,128)(2,1)} %copy-done.1, bf16[4,640,128]{2,1,0:T(8,128)(2,1)} %copy-done.8, f32[1280,2]{1,0:T(8,128)} %bitcast.42, bf16[3,1280,512]{2,1,0:T(8,128)(2,1)} %bitcast.41), custom_call_target="tpu_custom_call" | custom-call | flops 130000000 | bytes 1000 | tf_op jit(solution)/shard_map/norm_project/pallas_call | solution.py:246
  92.3 1.0 copy-done.3
  93.3 1.2 copy-done.4
  94.5 15.2 %attend.3 = (f32[4,2,512,128]{3,2,1,0:T(8,128)S(1)}, f32[4,2,512,128]{3,2,1,0:T(8,128)S(1)}) custom-call(bf16[512,512]{1,0:T(8,128)(2,1)S(1)} %copy-done.3, bf16[2,512,512]{2,1,0:T(8,128)(2,1)S(1)} %copy-done.4, bf16[2,512,512]{2,1,0:T(8,128)(2,1)S(1)} %copy-done.4, bf16[2,512,512]{2,1,0:T(8,128)(2,1)S(1)} %collective-permute-done.5.refs_3_.refs_4_, ...), custom_call_target="tpu_custom_call" | custom-call | flops 340000000 | bytes 1000 | tf_op jit(solution)/shard_map/attend/pallas_call | solution.py:419
  109.8 1.5 %collective-permute-start.17 = (bf16[1,512,512]{2,1,0:T(8,128)(2,1)S(1)}, bf16[1,512,512]{2,1,0:T(8,128)(2,1)S(1)}, u32[]{:S(2)}, u32[]{:S(2)}) collective-permute-start(bf16[1,512,512]{2,1,0:T(8,128)(2,1)S(1)} %slice.42), channel_id=1, source_target_pairs={{0,4},{4,8},{8,12},{12,14},{14,10},{10,6},{6,2},{2,0},{1,5},{5,9},... | collective-permute-start | bytes 1572872 | tf_op jit(solution)/shard_map/ppermute | solution.py:496
  111.3 0.6 collective-permute-start.18
  111.9 6.8 %attend.4 = (f32[4,2,512,128]{3,2,1,0:T(8,128)S(1)}, f32[4,2,512,128]{3,2,1,0:T(8,128)S(1)}) custom-call(bf16[512,512]{1,0:T(8,128)(2,1)S(1)} %copy-done.3, bf16[2,512,512]{2,1,0:T(8,128)(2,1)S(1)} %collective-permute-done.15.refs_1_.refs_2_, bf16[2,512,512]{2,1,0:T(8,128)(2,1)S(1)} %collective-permute-done.15.refs_1_.refs_2_, ...), custom_call_target="tpu_custom_call" | custom-call | flops 148000000 | bytes 1000 | tf_op jit(solution)/shard_map/attend/pallas_call | solution.py:419
  118.7 5.1 %collective-permute-done.17.refs_1_ = bf16[1,512,512]{2,1,0:T(8,128)(2,1)S(1)} collective-permute-done((bf16[1,512,512]{2,1,0:T(8,128)(2,1)S(1)}, bf16[1,512,512]{2,1,0:T(8,128)(2,1)S(1)}, u32[]{:S(2)}, u32[]{:S(2)}) %collective-permute-start.17) | collective-permute-done | bytes 524320 | tf_op jit(solution)/shard_map/ppermute | solution.py:496
  123.8 1.2 collective-permute-done.18.refs_2_
  125.0 5.4 %attend.5 = (bf16[2,4,320,128]{3,2,1,0:T(8,128)(2,1)S(1)}, f32[2,4,320,128]{3,2,1,0:T(8,128)S(1)}) custom-call(bf16[512,512]{1,0:T(8,128)(2,1)S(1)} %copy-done.3, bf16[1,512,512]{2,1,0:T(8,128)(2,1)S(1)} %collective-permute-done.17.refs_1_, bf16[1,512,512]{2,1,0:T(8,128)(2,1)S(1)} %collective-permute-done.18.refs_2_, ...), custom_call_target="tpu_custom_call" | custom-call | flops 84000000 | bytes 1000 | tf_op jit(solution)/shard_map/attend/pallas_call | solution.py:419
  130.4 0.1 collective-permute-start.19
  130.5 1.0 parity_split.1.resid_ref
  131.5 1.1 collective-permute-done.19.refs_1_
  132.6 0.1 branch_out.2
  132.7 1.8 %collective-permute-start.20 = (bf16[4,320,128]{2,1,0:T(8,128)(2,1)S(1)}, bf16[4,320,128]{2,1,0:T(8,128)(2,1)}, u32[]{:S(2)}, u32[]{:S(2)}) collective-permute-start(bf16[4,320,128]{2,1,0:T(8,128)(2,1)S(1)} %branch_out.2), channel_id=1, source_target_pairs={{0,16},{16,0},{1,17},{17,1},{2,18},{18,2},{3,19},{19,3},{4,20},{20... | collective-permute-start | bytes 983048 | tf_op jit(solution)/shard_map/ppermute | solution.py:30
  134.5 0.1 branch_out.3
  134.6 8.0 %collective-permute-done.20 = bf16[4,320,128]{2,1,0:T(8,128)(2,1)} collective-permute-done((bf16[4,320,128]{2,1,0:T(8,128)(2,1)S(1)}, bf16[4,320,128]{2,1,0:T(8,128)(2,1)}, u32[]{:S(2)}, u32[]{:S(2)}) %collective-permute-start.20) | collective-permute-done | bytes 327712 | tf_op jit(solution)/shard_map/ppermute | solution.py:30
  142.6 1.9 %fusion.3 = bf16[4,320,1,128]{3,1,2,0:T(8,128)(2,1)} fusion(bf16[4,320,128]{2,1,0:T(8,128)(2,1)S(1)} %branch_out.3, bf16[4,320,128]{2,1,0:T(8,128)(2,1)} %collective-permute-done.20, pred[]{:T(512)S(6)} %eq.10), kind=kLoop, calls=%fused_computation.9 | loop fusion | flops 1310720 | bytes 983041
  (55 shorter events, 0.4 us)
Async XLA Ops:
  0.6 62.2 %copy-start = (bf16[320,640]{1,0:T(8,128)(2,1)S(1)}, bf16[320,640]{1,0:T(8,128)(2,1)}, u32[]{:S(2)}) copy-start(bf16[320,640]{1,0:T(8,128)(2,1)} %param.15) | copy-start | bytes 1228804
  0.6 19.0 %copy-start.6 = (bf16[1,4,640,128]{3,2,1,0:T(8,128)(2,1)S(1)}, bf16[1,4,640,128]{3,2,1,0:T(8,128)(2,1)}, u32[]{:S(2)}) copy-start(bf16[1,4,640,128]{3,2,1,0:T(8,128)(2,1)} %param.12) | copy-start | bytes 1966084
  0.7 20.3 %copy-start.9 = (bf16[640]{0:T(1024)(128)(2,1)S(1)}, bf16[640]{0:T(1024)(128)(2,1)}, u32[]{:S(2)}) copy-start(bf16[640]{0:T(1024)(128)(2,1)} %param.16) | copy-start | bytes 3844
  0.7 20.3 %copy-start.10 = (bf16[640]{0:T(1024)(128)(2,1)S(1)}, bf16[640]{0:T(1024)(128)(2,1)}, u32[]{:S(2)}) copy-start(bf16[640]{0:T(1024)(128)(2,1)} %param.17) | copy-start | bytes 3844
  0.7 20.3 %copy-start.11 = (bf16[640]{0:T(1024)(128)(2,1)S(1)}, bf16[640]{0:T(1024)(128)(2,1)}, u32[]{:S(2)}) copy-start(bf16[640]{0:T(1024)(128)(2,1)} %param.20) | copy-start | bytes 3844
  0.7 20.3 %copy-start.12 = (bf16[640]{0:T(1024)(128)(2,1)S(1)}, bf16[640]{0:T(1024)(128)(2,1)}, u32[]{:S(2)}) copy-start(bf16[640]{0:T(1024)(128)(2,1)} %param.21) | copy-start | bytes 3844
  1.8 19.3 %collective-permute-start.1 = (bf16[1,640,128]{2,1,0:T(8,128)(2,1)S(1)}, bf16[1,640,128]{2,1,0:T(8,128)(2,1)S(1)}, u32[]{:S(2)}, u32[]{:S(2)}) collective-permute-start(bf16[1,640,128]{2,1,0:T(8,128)(2,1)S(1)} %get-tuple-element.53), channel_id=1, source_target_pairs={{0,2},{2,4},{4,6},{6,8},{8,10},{10,12},{12,14},{1,3},{3,5},{5,7},{... | collective-permute-start | bytes 491528 | tf_op jit(solution)/shard_map/ppermute | solution.py:468
  6.7 18.3 %collective-permute-start.2 = (bf16[1,640,128]{2,1,0:T(8,128)(2,1)S(1)}, bf16[1,640,128]{2,1,0:T(8,128)(2,1)S(1)}, u32[]{:S(2)}, u32[]{:S(2)}) collective-permute-start(bf16[1,640,128]{2,1,0:T(8,128)(2,1)S(1)} %get-tuple-element.52), channel_id=1, source_target_pairs={{2,0},{4,2},{6,4},{8,6},{10,8},{12,10},{14,12},{3,1},{5,3},{7,5},{... | collective-permute-start | bytes 491528 | tf_op jit(solution)/shard_map/ppermute | solution.py:469
  8.0 38.2 %collective-permute-start.5 = (bf16[2,512,512]{2,1,0:T(8,128)(2,1)}, bf16[2,512,512]{2,1,0:T(8,128)(2,1)S(1)}, u32[]{:S(2)}, u32[]{:S(2)}) collective-permute-start(bf16[2,512,512]{2,1,0:T(8,128)(2,1)} %bitcast.47), channel_id=1, source_target_pairs={{0,4},{4,8},{8,12},{12,14},{14,10},{10,6},{6,2},{2,0},{1,5},{5,9},... | collective-permute-start | bytes 3145736 | tf_op jit(solution)/shard_map/ppermute | solution.py:496
  11.6 35.9 %collective-permute-start.6 = (bf16[2,512,512]{2,1,0:T(8,128)(2,1)}, bf16[2,512,512]{2,1,0:T(8,128)(2,1)}, u32[]{:S(2)}, u32[]{:S(2)}) collective-permute-start(bf16[2,512,512]{2,1,0:T(8,128)(2,1)} %bitcast.48), channel_id=1, source_target_pairs={{4,0},{8,4},{12,8},{14,12},{10,14},{6,10},{2,6},{0,2},{5,1},{9,5},... | collective-permute-start | bytes 3145736 | tf_op jit(solution)/shard_map/ppermute | solution.py:496
  14.3 36.8 %all-to-all-start = ((f32[32,1,128]{2,1,0:T(1,128)}), f32[32,1,128]{2,1,0:T(1,128)S(1)}, u32[]{:S(2)}, u32[]{:S(2)}) async-start(f32[32,1,128]{2,1,0:T(1,128)} %broadcast_in_dim.21), calls=%async_computation | async-start | bytes 32768 | tf_op jit(solution)/shard_map/all_to_all | solution.py:43
  19.7 15.3 %collective-permute-start.7 = (bf16[4,640,128]{2,1,0:T(8,128)(2,1)S(1)}, bf16[4,640,128]{2,1,0:T(8,128)(2,1)}, u32[]{:S(2)}, u32[]{:S(2)}) collective-permute-start(bf16[4,640,128]{2,1,0:T(8,128)(2,1)S(1)} %bitcast.39), channel_id=1, source_target_pairs={{1,17},{16,0},{3,19},{18,2},{5,21},{20,4},{7,23},{22,6},{9,25},{24... | collective-permute-start | bytes 1966088 | tf_op jit(solution)/shard_map/ppermute | solution.py:58
  21.1 10.4 %collective-permute-start.4 = (bf16[2560]{0:T(1024)(128)(2,1)S(1)}, bf16[2560]{0:T(1024)(128)(2,1)S(1)}, u32[]{:S(2)}, u32[]{:S(2)}) collective-permute-start(bf16[2560]{0:T(1024)(128)(2,1)S(1)} %pad_maximum_fusion), channel_id=1, source_target_pairs={{0,1},{1,0},{2,3},{3,2},{4,5},{5,4},{6,7},{7,6},{8,9},{9,8},{10,11... | collective-permute-start | bytes 15368 | tf_op jit(solution)/shard_map/ppermute | solution.py:30
  25.6 8.1 %collective-permute-start.3 = (bf16[2,640,128]{2,1,0:T(8,128)(2,1)}, bf16[2,640,128]{2,1,0:T(8,128)(2,1)}, u32[]{:S(2)}, u32[]{:S(2)}) collective-permute-start(bf16[2,640,128]{2,1,0:T(8,128)(2,1)} %constant_dynamic-update-slice_fusion.refs_2_), channel_id=1, source_target_pairs={{0,1},{17,16},{2,3},{19,18},{4,5},{21,20},{6,7},{23,22},{8,9},{25,... | collective-permute-start | bytes 983048 | tf_op jit(solution)/shard_map/ppermute | solution.py:60
  29.0 1.3 copy-start.5
  31.5 20.1 %collective-permute-start = (bf16[4,640,128]{2,1,0:T(8,128)(2,1)S(1)}, bf16[4,640,128]{2,1,0:T(8,128)(2,1)}, u32[]{:S(2)}, u32[]{:S(2)}) collective-permute-start(bf16[4,640,128]{2,1,0:T(8,128)(2,1)S(1)} %bitcast.40), channel_id=1, source_target_pairs={{0,1},{17,16},{2,3},{19,18},{4,5},{21,20},{6,7},{23,22},{8,9},{25,... | collective-permute-start | bytes 1966088 | tf_op jit(solution)/shard_map/ppermute | solution.py:60
  33.7 9.3 %collective-permute-start.9 = (bf16[2,640,128]{2,1,0:T(8,128)(2,1)}, bf16[2,640,128]{2,1,0:T(8,128)(2,1)}, u32[]{:S(2)}, u32[]{:S(2)}) collective-permute-start(bf16[2,640,128]{2,1,0:T(8,128)(2,1)} %constant_dynamic-update-slice_fusion.refs_2_), channel_id=1, source_target_pairs={{1,17},{16,0},{3,19},{18,2},{5,21},{20,4},{7,23},{22,6},{9,25},{24... | collective-permute-start | bytes 983048 | tf_op jit(solution)/shard_map/ppermute | solution.py:58
  35.0 16.6 %collective-permute-start.8 = (bf16[4,640,128]{2,1,0:T(8,128)(2,1)}, bf16[4,640,128]{2,1,0:T(8,128)(2,1)}, u32[]{:S(2)}, u32[]{:S(2)}) collective-permute-start(bf16[4,640,128]{2,1,0:T(8,128)(2,1)} %collective-permute-done.7.refs_0_), channel_id=1, source_target_pairs={{0,1},{17,16},{2,3},{19,18},{4,5},{21,20},{6,7},{23,22},{8,9},{25,... | collective-permute-start | bytes 1966088 | tf_op jit(solution)/shard_map/ppermute | solution.py:61
  43.0 8.6 %collective-permute-start.10 = (bf16[2,640,128]{2,1,0:T(8,128)(2,1)}, bf16[2,640,128]{2,1,0:T(8,128)(2,1)}, u32[]{:S(2)}, u32[]{:S(2)}) collective-permute-start(bf16[2,640,128]{2,1,0:T(8,128)(2,1)} %collective-permute-done.9.refs_2_), channel_id=1, source_target_pairs={{0,1},{17,16},{2,3},{19,18},{4,5},{21,20},{6,7},{23,22},{8,9},{25,... | collective-permute-start | bytes 983048 | tf_op jit(solution)/shard_map/ppermute | solution.py:61
  46.1 32.8 %collective-permute-start.13 = (bf16[2,512,512]{2,1,0:T(8,128)(2,1)S(1)}, bf16[2,512,512]{2,1,0:T(8,128)(2,1)}, u32[]{:S(2)}, u32[]{:S(2)}) collective-permute-start(bf16[2,512,512]{2,1,0:T(8,128)(2,1)S(1)} %collective-permute-done.5.refs_3_.refs_4_), channel_id=1, source_target_pairs={{0,4},{4,8},{8,12},{12,14},{14,10},{10,6},{6,2},{2,0},{1,5},{5,9},... | collective-permute-start | bytes 3145736 | tf_op jit(solution)/shard_map/ppermute | solution.py:496
  47.6 31.3 %collective-permute-start.14 = (bf16[2,512,512]{2,1,0:T(8,128)(2,1)}, bf16[2,512,512]{2,1,0:T(8,128)(2,1)}, u32[]{:S(2)}, u32[]{:S(2)}) collective-permute-start(bf16[2,512,512]{2,1,0:T(8,128)(2,1)} %collective-permute-done.6.refs_5_.refs_6_), channel_id=1, source_target_pairs={{4,0},{8,4},{12,8},{14,12},{10,14},{6,10},{2,6},{0,2},{5,1},{9,5},... | collective-permute-start | bytes 3145736 | tf_op jit(solution)/shard_map/ppermute | solution.py:496
  51.6 11.5 %copy-start.13 = (bf16[640]{0:T(1024)(128)(2,1)S(1)}, bf16[640]{0:T(1024)(128)(2,1)}, u32[]{:S(2)}) copy-start(bf16[640]{0:T(1024)(128)(2,1)} %param.19) | copy-start | bytes 3844
  62.0 15.3 %collective-permute-start.11 = (bf16[4,640,128]{2,1,0:T(8,128)(2,1)}, bf16[4,640,128]{2,1,0:T(8,128)(2,1)S(1)}, u32[]{:S(2)}, u32[]{:S(2)}) collective-permute-start(bf16[4,640,128]{2,1,0:T(8,128)(2,1)} %norm_conv.3), channel_id=1, source_target_pairs={{0,16},{16,0},{1,17},{17,1},{2,18},{18,2},{3,19},{19,3},{4,20},{20... | collective-permute-start | bytes 1966088 | tf_op jit(solution)/shard_map/ppermute | solution.py:30
  63.2 14.1 %copy-start.7 = (bf16[1,4,640,128]{3,2,1,0:T(8,128)(2,1)S(1)}, bf16[1,4,640,128]{3,2,1,0:T(8,128)(2,1)}, u32[]{:S(2)}) copy-start(bf16[1,4,640,128]{3,2,1,0:T(8,128)(2,1)} %param.12) | copy-start | bytes 1966084
  78.9 4.2 %copy-start.1 = (bf16[4,640,128]{2,1,0:T(8,128)(2,1)}, bf16[4,640,128]{2,1,0:T(8,128)(2,1)S(1)}, u32[]{:S(2)}) copy-start(bf16[4,640,128]{2,1,0:T(8,128)(2,1)S(1)} %add_convert_fusion.own_ref.refs_0_) | copy-start | bytes 1966084
  78.9 30.8 %collective-permute-start.15 = (bf16[2,512,512]{2,1,0:T(8,128)(2,1)}, bf16[2,512,512]{2,1,0:T(8,128)(2,1)S(1)}, u32[]{:S(2)}, u32[]{:S(2)}) collective-permute-start(bf16[2,512,512]{2,1,0:T(8,128)(2,1)} %collective-permute-done.13.refs_7_.refs_8_), channel_id=1, source_target_pairs={{0,4},{4,8},{8,12},{12,14},{14,10},{10,6},{6,2},{2,0},{1,5},{5,9},... | collective-permute-start | bytes 3145736 | tf_op jit(solution)/shard_map/ppermute | solution.py:496
  80.4 29.3 %collective-permute-start.16 = (bf16[2,512,512]{2,1,0:T(8,128)(2,1)}, bf16[2,512,512]{2,1,0:T(8,128)(2,1)S(1)}, u32[]{:S(2)}, u32[]{:S(2)}) collective-permute-start(bf16[2,512,512]{2,1,0:T(8,128)(2,1)} %collective-permute-done.14.refs_9_.refs_10_), channel_id=1, source_target_pairs={{4,0},{8,4},{12,8},{14,12},{10,14},{6,10},{2,6},{0,2},{5,1},{9,5},... | collective-permute-start | bytes 3145736 | tf_op jit(solution)/shard_map/ppermute | solution.py:496
  81.0 2.1 %collective-permute-start.12 = (bf16[4,640,128]{2,1,0:T(8,128)(2,1)S(1)}, bf16[4,640,128]{2,1,0:T(8,128)(2,1)S(1)}, u32[]{:S(2)}, u32[]{:S(2)}) collective-permute-start(bf16[4,640,128]{2,1,0:T(8,128)(2,1)S(1)} %add_convert_fusion.own_ref.refs_0_), channel_id=1, source_target_pairs={{0,1},{1,0},{2,3},{3,2},{4,5},{5,4},{6,7},{7,6},{8,9},{9,8},{10,11... | collective-permute-start | bytes 1966088 | tf_op jit(solution)/shard_map/ppermute | solution.py:30
  83.1 0.8 copy-start.8
  92.3 1.0 copy-start.3
  93.3 1.2 copy-start.4
  109.8 14.0 %collective-permute-start.17 = (bf16[1,512,512]{2,1,0:T(8,128)(2,1)S(1)}, bf16[1,512,512]{2,1,0:T(8,128)(2,1)S(1)}, u32[]{:S(2)}, u32[]{:S(2)}) collective-permute-start(bf16[1,512,512]{2,1,0:T(8,128)(2,1)S(1)} %slice.42), channel_id=1, source_target_pairs={{0,4},{4,8},{8,12},{12,14},{14,10},{10,6},{6,2},{2,0},{1,5},{5,9},... | collective-permute-start | bytes 1572872 | tf_op jit(solution)/shard_map/ppermute | solution.py:496
  111.3 13.7 %collective-permute-start.18 = (bf16[1,512,512]{2,1,0:T(8,128)(2,1)S(1)}, bf16[1,512,512]{2,1,0:T(8,128)(2,1)S(1)}, u32[]{:S(2)}, u32[]{:S(2)}) collective-permute-start(bf16[1,512,512]{2,1,0:T(8,128)(2,1)S(1)} %slice.43), channel_id=1, source_target_pairs={{4,0},{8,4},{12,8},{14,12},{10,14},{6,10},{2,6},{0,2},{5,1},{9,5},... | collective-permute-start | bytes 1572872 | tf_op jit(solution)/shard_map/ppermute | solution.py:496
  125.0 5.5 %copy-start.2 = (bf16[4,640,128]{2,1,0:T(8,128)(2,1)S(1)}, bf16[4,640,128]{2,1,0:T(8,128)(2,1)}, u32[]{:S(2)}) copy-start(bf16[4,640,128]{2,1,0:T(8,128)(2,1)} %copy-done.1) | copy-start | bytes 1966084
  130.4 2.2 %collective-permute-start.19 = (bf16[2,4,320,128]{3,2,1,0:T(8,128)(2,1)S(1)}, bf16[2,4,320,128]{3,2,1,0:T(8,128)(2,1)S(1)}, u32[]{:S(2)}, u32[]{:S(2)}) collective-permute-start(bf16[2,4,320,128]{3,2,1,0:T(8,128)(2,1)S(1)} %get-tuple-element.41), channel_id=1, source_target_pairs={{0,1},{1,0},{2,3},{3,2},{4,5},{5,4},{6,7},{7,6},{8,9},{9,8},{10,11... | collective-permute-start | bytes 1966088 | tf_op jit(solution)/shard_map/ppermute | solution.py:30
  132.7 9.9 %collective-permute-start.20 = (bf16[4,320,128]{2,1,0:T(8,128)(2,1)S(1)}, bf16[4,320,128]{2,1,0:T(8,128)(2,1)}, u32[]{:S(2)}, u32[]{:S(2)}) collective-permute-start(bf16[4,320,128]{2,1,0:T(8,128)(2,1)S(1)} %branch_out.2), channel_id=1, source_target_pairs={{0,16},{16,0},{1,17},{17,1},{2,18},{18,2},{3,19},{19,3},{4,20},{20... | collective-permute-start | bytes 983048 | tf_op jit(solution)/shard_map/ppermute | solution.py:30

commit v8 on v7

--- a/solution.py
+++ b/solution.py
@@ -47,27 +47,29 @@
     return lax.optimization_barrier((array,) + tuple(others))[0] if others else array
 
 
-def halves_of_inputs(own, others=()):
+def halves_of_inputs(own, gain, bias):
     cfg = lax.axis_index("cfg")
     if lax.axis_size("tp") != 2:
         full = lax.all_gather(own, "tp", axis=1, tiled=True)
         half = full.shape[1] // 2
+        vectors = lax.all_gather(jnp.stack([gain, bias]), "tp", axis=1, tiled=True)
+        vectors = lax.dynamic_slice_in_dim(vectors, cfg * half, half, 1)
+        rows = vector_rows(vectors[0], vectors[1])
         mine = lax.dynamic_slice_in_dim(full, cfg * half, half, 1)
         sent = lax.dynamic_slice_in_dim(full, (1 - cfg) * half, half, 1)
-        return [mine], [swapped(sent, "cfg")]
+        return [attached(mine, rows)], [attached(swapped(sent, "cfg"), rows)]
     across = lax.ppermute(own, ("cfg", "tp"), [(1, 3), (2, 0)])
     pairs = [(0, 1), (3, 2)]
     own_side = lax.ppermute(own, ("cfg", "tp"), pairs)
-    across_side = lax.ppermute(need(across, others), ("cfg", "tp"), pairs)
+    across_side = lax.ppermute(across, ("cfg", "tp"), pairs)
     return [own, own_side], [across, across_side]
 
 
 def conv_kernel(choices, amount, flags_ref, sums_ref, *refs):
     x_refs = refs[:choices]
-    edge_refs = refs[choices : 2 * choices]
-    affine_ref, w_hbm, out_ref, w_ref, act_ref, sems = refs[2 * choices :]
+    w_hbm, out_ref, w_ref, act_ref, sems = refs[choices:]
     rows = out_ref.shape[0]
-    ins = affine_ref.shape[0]
+    ins = w_hbm.shape[3]
     copies = {}
     for b in (1, 0, 2):
         for a in range(3):
@@ -87,14 +89,15 @@
 
     mean = column(0) / amount
     variance = column(GROUPS) / amount - mean * mean
-    scale = lax.rsqrt(variance + epsilon) * affine_ref[:, 0:1]
-    shift = affine_ref[:, 1:2]
+
+    def chosen(r, at):
+        x = [ref[r, at] for ref in x_refs]
+        return x[0] if choices == 1 else jnp.where(flags_ref[2] == 1, x[0], x[1])
+
+    gain, shift = columns_of(chosen(0, slice(ins, None)), ins)
+    scale = lax.rsqrt(variance + epsilon) * gain
     for r in range(rows + 2):
-        if 0 < r <= rows:
-            x = [ref[r - 1] for ref in x_refs]
-        else:
-            x = [ref[0 if r == 0 else 1] for ref in edge_refs]
-        x = x[0] if choices == 1 else jnp.where(flags_ref[2] == 1, x[0], x[1])
+        x = chosen(r, slice(0, ins))
         z = ((x.astype(jnp.float32) - mean) * scale + shift) * 0.5
         z = z + z * jnp.tanh(z)
         if r == 0:
@@ -127,15 +130,15 @@
             out_ref[start + r] = total[r].astype(out_ref.dtype)
 
 
-def conv_call(flags, sums, amount, xs, edges, affine, conv_w, out_dtype):
-    rows = xs[0].shape[0]
+def conv_call(flags, sums, amount, xs, conv_w, out_dtype):
+    rows = xs[0].shape[0] - 2
     outs, ins = conv_w.shape[2:]
     return pl.pallas_call(
         functools.partial(conv_kernel, len(xs), amount),
         in_specs=[
             pl.BlockSpec(memory_space=pltpu.SMEM),
             pl.BlockSpec(memory_space=pltpu.SMEM),
-            *[pl.BlockSpec(memory_space=pltpu.VMEM)] * (2 * len(xs) + 1),
+            *[pl.BlockSpec(memory_space=pltpu.VMEM)] * len(xs),
             pl.BlockSpec(memory_space=pltpu.HBM),
         ],
         out_specs=pl.BlockSpec(memory_space=pltpu.VMEM),
@@ -148,7 +151,59 @@
         compiler_params=pltpu.CompilerParams(vmem_limit_bytes=57 * MIB),
         cost_estimate=cost(9000),
         name="norm_conv",
-    )(flags, sums, *xs, *edges, affine, conv_w)
+    )(flags, sums, *xs, conv_w)
+
+
+def extra_rows(channels):
+    return -(-2 * channels // (16 * LANES)) * 16
+
+
+def vector_rows(gain, bias):
+    rows = jnp.concatenate([gain, bias]).reshape(-1, LANES)
+    return jnp.pad(rows, ((0, extra_rows(gain.shape[0]) - rows.shape[0]), (0, 0)))
+
+
+def columns_of(rows, channels):
+    turned = rows.astype(jnp.float32).T
+    count = channels // LANES
+    column = lambda at: jnp.concatenate([turned[:, at + j : at + j + 1] for j in range(count)], axis=0)
+    return column(0), column(count)
+
+
+def attached(array, rows):
+    shape = (array.shape[0],) + rows.shape
+    return jnp.concatenate([array, jnp.broadcast_to(rows[None], shape)], axis=1)
+
+
+def rim_kernel(before_ref, x_ref, after_ref, vector_ref, out_ref):
+    rows, channels, _ = x_ref.shape
+    out_ref[0, :channels] = before_ref[0]
+    out_ref[rows + 1, :channels] = after_ref[0]
+    for r in range(rows):
+        out_ref[r + 1, :channels] = x_ref[r]
+    for r in range(rows + 2):
+        out_ref[r, channels:] = vector_ref[...]
+
+
+def small_call(kernel, out_shape, name, *operands):
+    vmem = pl.BlockSpec(memory_space=pltpu.VMEM)
+    return pl.pallas_call(
+        kernel,
+        in_specs=[vmem] * len(operands),
+        out_specs=vmem,
+        out_shape=jax.ShapeDtypeStruct(out_shape, jnp.bfloat16),
+        compiler_params=pltpu.CompilerParams(vmem_limit_bytes=VMEM_LIMIT),
+        cost_estimate=cost(1000),
+        name=name,
+    )(*operands)
+
+
+def resid_kernel(own_ref, received_ref, x_ref, bias_ref, vector_ref, out_ref):
+    rows, channels, _ = x_ref.shape
+    for r in range(rows):
+        hidden = own_ref[r] + received_ref[r].astype(jnp.float32) + bias_ref[...]
+        out_ref[r, :channels] = (x_ref[r].astype(jnp.float32) + hidden).astype(jnp.bfloat16)
+        out_ref[r, channels:] = vector_ref[...]
 
 
 def parity_matrix(channels):
@@ -160,26 +215,13 @@
 
 
 def split_kernel(own_ref, split_ref):
-    rows, channels, _ = own_ref.shape
-    half = channels // 2
-    chosen = parity_matrix(channels)
+    _, rows, half, _ = split_ref.shape
+    chosen = parity_matrix(2 * half)
     for r in range(rows):
-        y = jnp.dot(chosen, own_ref[r], preferred_element_type=jnp.float32).astype(jnp.bfloat16)
+        y = jnp.dot(chosen, own_ref[r, : 2 * half], preferred_element_type=jnp.float32)
+        y = y.astype(jnp.bfloat16)
         split_ref[0, r] = y[:half]
         split_ref[1, r] = y[half:]
-
-
-def split_call(own):
-    rows, channels, _ = own.shape
-    return pl.pallas_call(
-        split_kernel,
-        in_specs=[pl.BlockSpec(memory_space=pltpu.VMEM)],
-        out_specs=pl.BlockSpec(memory_space=pltpu.VMEM),
-        out_shape=jax.ShapeDtypeStruct((2, rows, channels // 2, LANES), jnp.bfloat16),
-        compiler_params=pltpu.CompilerParams(vmem_limit_bytes=VMEM_LIMIT),
-        cost_estimate=cost(1000),
-        name="parity_split",
-    )(own)
 
 
 def arrange_kernel(flip_ref, w_ref, out_ref):
@@ -213,20 +255,22 @@
 
 def project_kernel(parts, order_ref, *refs):
     part_refs = refs[:parts]
-    affine_ref, w_hbm, q_ref, kv_ref, w_ref, normed_ref, sems = refs[parts:]
-    rows, channels, _ = part_refs[0].shape
+    w_hbm, q_ref, kv_ref, w_ref, normed_ref, sems = refs[parts:]
+    rows = part_refs[0].shape[0]
+    channels = w_hbm.shape[1] // parts
     total = parts * channels
     copies = [pltpu.make_async_copy(w_hbm.at[i], w_ref.at[i], sems.at[i]) for i in range(3)]
     for copy in copies:
         copy.start()
+    affine = [columns_of(ref[0, channels:], channels) for ref in part_refs]
     for r in range(rows):
-        x = [ref[r].astype(jnp.float32) for ref in part_refs]
+        x = [ref[r, :channels].astype(jnp.float32) for ref in part_refs]
         mean = sum(jnp.sum(a, axis=0, keepdims=True) for a in x) / total
         var = sum(jnp.sum(a * a, axis=0, keepdims=True) for a in x) / total - mean * mean
         inverse = lax.rsqrt(var + epsilon)
         for j in range(parts):
             at = pl.ds(pl.multiple_of(order_ref[j] * channels, LANES), channels)
-            z = (x[j] - mean) * inverse * affine_ref[at, 0:1] + affine_ref[at, 1:2]
+            z = (x[j] - mean) * inverse * affine[j][0] + affine[j][1]
             normed_ref[r * LANES : (r + 1) * LANES, at] = z.astype(jnp.bfloat16).T
     for i in range(3):
         copies[i].wait()
@@ -238,7 +282,7 @@
             kv_ref[i - 1] = y
 
 
-def project_call(order, parts, affine, w):
+def project_call(order, parts, w):
     rows = parts[0].shape[0]
     positions = rows * LANES
     _, depth, features = w.shape
@@ -247,7 +291,7 @@
         functools.partial(project_kernel, len(parts)),
         in_specs=[
             pl.BlockSpec(memory_space=pltpu.SMEM),
-            *[vmem] * (len(parts) + 1),
+            *[vmem] * len(parts),
             pl.BlockSpec(memory_space=pltpu.HBM),
         ],
         out_specs=(vmem, vmem),
@@ -263,7 +307,7 @@
         compiler_params=pltpu.CompilerParams(vmem_limit_bytes=55 * MIB),
         cost_estimate=cost(6500),
         name="norm_project",
-    )(order, *parts, affine, w)
+    )(order, *parts, w)
 
 
 def branch_kernel(parity_ref, resid_ref, *refs):
@@ -467,19 +511,15 @@
     down_pairs = [(i + 1, i) for i in range(rows_count - 1)]
     before = lax.ppermute(latent_rows[span_rows - 1 :], "rows", up_pairs)
     after = lax.ppermute(latent_rows[:1], "rows", down_pairs)
-    x_mine, x_other = halves_of_inputs(latent_rows)
-    edges_mine, edges_other = halves_of_inputs(jnp.concatenate([before, after], axis=0))
-
-    joined = jnp.concatenate([gn_gain, gn_bias, ln_gain, ln_bias])
     if tp_count == 2:
-        other = swapped(joined, "tp").reshape(4, 1, -1)
-        pieces = [joined.reshape(4, 1, -1), other]
-        vectors = jnp.where(
-            tp == 0, jnp.concatenate(pieces, axis=1), jnp.concatenate(pieces[::-1], axis=1)
-        ).reshape(4, -1)
+        shape = (span_rows + 2, local_channels + extra_rows(local_channels), grid_width)
+        rimmed = small_call(
+            rim_kernel, shape, "rim", before, latent_rows, after, vector_rows(gn_gain, gn_bias)
+        )
+        rimmed = need(rimmed, (table,))
     else:
-        vectors = lax.all_gather(joined.reshape(4, -1), "tp", axis=1, tiled=True)
-    vectors = vectors.astype(jnp.float32)
+        rimmed = jnp.concatenate([before, latent_rows, after], axis=0)
+    x_mine, x_other = halves_of_inputs(rimmed, gn_gain, gn_bias)
 
     forward, backward = ring_pairs(rows_count)
     last = rows_count // 2
@@ -502,12 +542,9 @@
             return [((ahead, 0), (behind, 0))]
         return [((ahead, 0), (ahead, 1)), ((behind, 0), (behind, 1))]
 
-    next_hop(vectors)
+    next_hop(table)
 
     amount = span_rows * rows_count * grid_width * group_width
-    half = D // 2
-    gn_affine = lax.dynamic_slice_in_dim(vectors[:2], cfg * half, half, 1).T
-    ln_affine = vectors[2:].T
     flags = jnp.stack([my_block > 0, my_block < rows_count - 1, tp == cfg]).astype(jnp.int32)
     place = cfg * (GROUPS // 2)
     flags_mine = jnp.append(flags, cfg * 2 * GROUPS + place)
@@ -518,15 +555,14 @@
     flip = jnp.logical_and(tp_count == 2, tp == 0)
     w_back = arrange_call(flip, w_out, tp_count)
     order = jnp.stack([tp, 1 - tp]).astype(jnp.int32) if tp_count == 2 else jnp.zeros((1,), jnp.int32)
-    gn_affine, ln_affine, order, w_back = lax.optimization_barrier(
-        (gn_affine, ln_affine, order, w_back)
+    flags_other, order, w_back, *_ = lax.optimization_barrier(
+        (flags_other, order, w_back) + tuple(x_mine[1:])
     )
-    flags_other = need(flags_other, tuple(x_mine[1:] + edges_mine[1:]) + hops[1])
-    next_hop()
-
-    conv_sent = conv_call(flags_other, table, amount, x_other, edges_other, gn_affine, conv_w, jnp.bfloat16)
+
+    conv_sent = conv_call(flags_other, table, amount, x_other, conv_w, jnp.bfloat16)
     conv_received = swapped(conv_sent, "cfg")
-    conv_own = conv_call(flags_mine, table, amount, x_mine, edges_mine, gn_affine, conv_w, jnp.float32)
+    next_hop(conv_sent)
+    conv_own = conv_call(flags_mine, table, amount, x_mine, conv_w, jnp.float32)
 
     half_width = TEMB // 2
     frequencies = jnp.exp(
@@ -538,17 +574,29 @@
         jax.nn.silu(embedding)[None, :], w_time.astype(jnp.float32), precision=lax.Precision.HIGHEST
     )[0]
     bias = conv_b.astype(jnp.float32) + time_bias
-    resid = (
-        latent32 + (conv_own + conv_received.astype(jnp.float32) + bias[None, :, None])
-    ).astype(jnp.bfloat16)
-
+    wide = tp_count == 2
+    rows = vector_rows(ln_gain, ln_bias) if wide else jnp.zeros((16, LANES), jnp.bfloat16)
+    resid = small_call(
+        resid_kernel,
+        (span_rows, local_channels + rows.shape[0], grid_width),
+        "residual",
+        conv_own,
+        conv_received,
+        latent_rows,
+        bias[:, None],
+        rows,
+    )
     if tp_count == 2:
         parts = [resid, need(swapped(resid, "tp"), hops[2])]
     else:
-        parts = [lax.all_gather(resid, "tp", axis=1, tiled=True)]
+        full = lax.all_gather(resid[:, :local_channels], "tp", axis=1, tiled=True)
+        vectors = lax.all_gather(jnp.stack([ln_gain, ln_bias]), "tp", axis=1, tiled=True)
+        parts = [attached(full, vector_rows(vectors[0], vectors[1]))]
     next_hop(resid)
-    queries, fresh = project_call(order, parts, ln_affine, w_project)
-    resid_split = split_call(resid)
+    queries, fresh = project_call(order, parts, w_project)
+    resid_split = small_call(
+        split_kernel, (2, span_rows, local_channels // 2, grid_width), "parity_split", resid
+    )
     fresh_kv = fresh.reshape(1, 2, span_rows, grid_width, local_features)
 
     group = [((fresh, 0), (fresh, 1))] + blocks_of(1) + blocks_of(2)

time: 145 us -> 147 us (1.014)
  waiting for transfers between devices: 23.4 us -> 41.7 us
  starting transfers between devices: 40.6 us -> 29.9 us
  local copies, waits for them, and re-layouts: 12 us -> 9.17 us
  Pallas kernels: 59.2 us -> 57.6 us
    ppermute x2 -> x1, waiting for transfers between devices: 2.55 us -> 9.01 us  [halves_of_inputs(): across = lax.ppermute(own, ('cfg', 'tp'), [(1, 3), (2, 0)])]
    all_to_all x1, waiting for transfers between devices: 0.01 us -> 6.36 us  [summed(): return jnp.sum(lax.all_to_all(spread, axes, 0, 0, tiled=True), axis=0)]
    ppermute x2 -> x1, starting transfers between devices: 6.74 us -> 2.25 us  [halves_of_inputs(): across_side = lax.ppermute(across, ('cfg', 'tp'), pairs)]
    ppermute x5 -> x4, starting transfers between devices: 5.11 us -> 0.95 us  [swapped(): lax.ppermute(array, axis, [(i, i ^ 1) for i in range(lax.axis_size(axis))])]
    ppermute x4, waiting for transfers between devices: 1.18 us -> 4.75 us  [next_hop(): lax.ppermute(behind, 'rows', backward)]
    ppermute x4, starting transfers between devices: 8.13 us -> 5.16 us  [next_hop(): lax.ppermute(ahead, 'rows', forward)]
    slice x3 -> x0, local copies, waits for them, and re-layouts: 2.25 us -> none  [the longest x2 1.14 us: per_device(): ln_affine = vectors[2:].T]
    pallas_call x1, Pallas kernels: 8.31 us -> 6.31 us  [project_call(): pl.pallas_call(functools.partial(project_kernel, len(parts)), in_specs=[p...]
  transfers between devices with their start and end apart: 22 -> 18, of which waited for: 7 -> 10; matrix products, arithmetic and copies ran while one was open for 8% -> 4% of each run, Pallas kernels for 37% -> 36%
where the time goes in v8:
time: 147 us; the launch traced here: 146 us
  Pallas kernels  57.6 us (39%)
  waiting for transfers between devices  41.7 us (28%)
  starting transfers between devices  29.9 us (20%)
  local copies, waits for them, and re-layouts  9.17 us (6%)
  other arithmetic  6.16 us (4%)
  between operations  1.65 us (1%)
    pallas_call x3, Pallas kernels, attention_call(): pl.pallas_call(functools.partial(attention_kernel, len(pairs), state is n...  27.4 us
    pallas_call x2, Pallas kernels, conv_call(): pl.pallas_call(functools.partial(conv_kernel, len(xs), amount), in_specs=...  21 us
    ppermute x4, waiting for transfers between devices, swapped(): lax.ppermute(array, axis, [(i, i ^ 1) for i in range(lax.axis_size(axis))])  15.9 us
    ppermute x1, waiting for transfers between devices, halves_of_inputs(): across = lax.ppermute(own, ('cfg', 'tp'), [(1, 3), (2, 0)])  9.01 us
    all_to_all x1, starting transfers between devices, summed(): return jnp.sum(lax.all_to_all(spread, axes, 0, 0, tiled=True), axis=0)  7 us
    unnamed x28, local copies, waits for them, and re-layouts  6.87 us
    all_to_all x1, waiting for transfers between devices, summed(): return jnp.sum(lax.all_to_all(spread, axes, 0, 0, tiled=True), axis=0)  6.36 us
    pallas_call x1, Pallas kernels, project_call(): pl.pallas_call(functools.partial(project_kernel, len(parts)), in_specs=[p...  6.31 us
  transfers between devices with their start and end apart: 18, of which 10 were waited for; matrix products, arithmetic and copies ran while one was open for 4% of the time, Pallas kernels for 36%

profile of v8, /device:TPU:0, one launch (start us, length us, event | category | flops | bytes accessed | tf_op | source)
XLA Modules:
  0.0 146.4 jit_solution(12876002958325404358)
XLA Ops:
  0.6 0.0 copy-start
  0.6 1.1 slice_bitcast_fusion
  1.7 4.9 %collective-permute-start = (bf16[1,640,128]{2,1,0:T(8,128)(2,1)S(1)}, bf16[1,640,128]{2,1,0:T(8,128)(2,1)S(1)}, u32[]{:S(2)}, u32[]{:S(2)}) collective-permute-start(bf16[1,640,128]{2,1,0:T(8,128)(2,1)S(1)} %get-tuple-element.55), channel_id=1, source_target_pairs={{0,2},{2,4},{4,6},{6,8},{8,10},{10,12},{12,14},{1,3},{3,5},{5,7},{... | collective-permute-start | bytes 491528 | tf_op jit(solution)/shard_map/ppermute | solution.py:512
  6.6 1.3 collective-permute-start.1
  7.9 1.3 convert_reduce_fusion
  9.2 0.1 reduce_sum.32
  9.3 0.1 reduce_sum.45
  9.4 0.1 reduce_sum.36
  9.5 0.1 reduce_sum.46
  9.7 0.1 dynamic_update_slice.3
  9.8 0.1 broadcast_in_dim.22
  9.9 0.6 broadcast_in_dim.23
  10.5 7.0 %all-to-all-start = ((f32[32,1,128]{2,1,0:T(1,128)}), f32[32,1,128]{2,1,0:T(1,128)S(1)}, u32[]{:S(2)}, u32[]{:S(2)}) async-start(f32[32,1,128]{2,1,0:T(1,128)} %broadcast_in_dim.23), calls=%async_computation | async-start | bytes 32768 | tf_op jit(solution)/shard_map/all_to_all | solution.py:43
  17.5 0.7 fusion.8.vector_ref
  18.2 6.4 %all-to-all-done = f32[32,1,128]{2,1,0:T(1,128)S(1)} async-done(((f32[32,1,128]{2,1,0:T(1,128)}), f32[32,1,128]{2,1,0:T(1,128)S(1)}, u32[]{:S(2)}, u32[]{:S(2)}) %all-to-all-start) | async-done | bytes 16416 | tf_op jit(solution)/shard_map/all_to_all | solution.py:43
  24.6 0.5 reduce_sum.47.sums_ref
  25.1 1.1 copy-done.1
  26.2 0.1 rim.1.refs_0_
  26.3 1.3 collective-permute-start.3
  27.6 0.6 collective-permute-start.7
  28.1 1.5 %collective-permute-start.8 = (bf16[2,512,512]{2,1,0:T(8,128)(2,1)}, bf16[2,512,512]{2,1,0:T(8,128)(2,1)S(1)}, u32[]{:S(2)}, u32[]{:S(2)}) collective-permute-start(bf16[2,512,512]{2,1,0:T(8,128)(2,1)} %bitcast.21), channel_id=1, source_target_pairs={{4,0},{8,4},{12,8},{14,12},{10,14},{6,10},{2,6},{0,2},{5,1},{9,5},... | collective-permute-start | bytes 3145736 | tf_op jit(solution)/shard_map/ppermute | solution.py:536
  29.7 4.0 %collective-permute-start.2 = (bf16[6,656,128]{2,1,0:T(8,128)(2,1)S(1)}, bf16[6,656,128]{2,1,0:T(8,128)(2,1)}, u32[]{:S(2)}, u32[]{:S(2)}) collective-permute-start(bf16[6,656,128]{2,1,0:T(8,128)(2,1)S(1)} %rim.1.refs_0_), channel_id=1, source_target_pairs={{0,1},{17,16},{2,3},{19,18},{4,5},{21,20},{6,7},{23,22},{8,9},{25,... | collective-permute-start | bytes 3022856 | tf_op jit(solution)/shard_map/ppermute | solution.py:63
  33.6 9.0 %collective-permute-done.3.refs_0_ = bf16[6,656,128]{2,1,0:T(8,128)(2,1)} collective-permute-done((bf16[6,656,128]{2,1,0:T(8,128)(2,1)S(1)}, bf16[6,656,128]{2,1,0:T(8,128)(2,1)}, u32[]{:S(2)}, u32[]{:S(2)}) %collective-permute-start.3) | collective-permute-done | bytes 1007648 | tf_op jit(solution)/shard_map/ppermute | solution.py:61
  42.6 2.3 %collective-permute-start.4 = (bf16[6,656,128]{2,1,0:T(8,128)(2,1)}, bf16[6,656,128]{2,1,0:T(8,128)(2,1)}, u32[]{:S(2)}, u32[]{:S(2)}) collective-permute-start(bf16[6,656,128]{2,1,0:T(8,128)(2,1)} %collective-permute-done.3.refs_0_), channel_id=1, source_target_pairs={{0,1},{17,16},{2,3},{19,18},{4,5},{21,20},{6,7},{23,22},{8,9},{25,... | collective-permute-start | bytes 3022856 | tf_op jit(solution)/shard_map/ppermute | solution.py:64
  44.9 1.3 copy-done.9
  46.2 1.2 arrange.1.refs_5_
  47.4 0.6 pad_add_fusion.2.order_ref
  48.0 0.1 add_convert_fusion
  48.1 0.7 pad_add_fusion.1
  48.8 10.4 %norm_conv.3 = bf16[4,640,128]{2,1,0:T(8,128)(2,1)} custom-call(s32[4]{0:T(128)} %get-tuple-element.24.flags_ref, f32[128]{0:T(128)} %reduce_sum.47.sums_ref, bf16[6,656,128]{2,1,0:T(8,128)(2,1)} %collective-permute-done.3.refs_0_, bf16[6,656,128]{2,1,0:T(8,128)(2,1)} %collective-permute-done.4.refs_1_, bf16[3,3,640,640]{3,2,1,0:T(8,128)(2,1)} %refs_2_.3), custom_call_target="tpu_custom_call" | custom-call | flops 180000000 | bytes 1000 | tf_op jit(solution)/shard_map/norm_conv/pallas_call | solution.py:136
  59.2 0.6 collective-permute-start.10
  59.8 1.5 %collective-permute-start.9 = (bf16[2,512,512]{2,1,0:T(8,128)(2,1)S(1)}, bf16[2,512,512]{2,1,0:T(8,128)(2,1)}, u32[]{:S(2)}, u32[]{:S(2)}) collective-permute-start(bf16[2,512,512]{2,1,0:T(8,128)(2,1)S(1)} %collective-permute-done.7.refs_3_.refs_4_), channel_id=1, source_target_pairs={{0,4},{4,8},{8,12},{12,14},{14,10},{10,6},{6,2},{2,0},{1,5},{5,9},... | collective-permute-start | bytes 3145736 | tf_op jit(solution)/shard_map/ppermute | solution.py:536
  61.9 0.1 collective-permute-start.5
  62.1 0.1 divide_multiply_fusion
  62.2 0.3 convolution_reduce_fusion
  62.5 0.1 broadcast_in_dim.26.bias_ref
  62.7 10.7 %norm_conv.2.own_ref = f32[4,640,128]{2,1,0:T(8,128)} custom-call(s32[4]{0:T(128)} %get-tuple-element.57.flags_ref, f32[128]{0:T(128)} %reduce_sum.47.sums_ref, bf16[6,656,128]{2,1,0:T(8,128)(2,1)} %copy-done.8, bf16[6,656,128]{2,1,0:T(8,128)(2,1)} %collective-permute-done.2.refs_1_, bf16[3,3,640,640]{3,2,1,0:T(8,128)(2,1)} %refs_2_.3), custom_call_target="tpu_custom_call" | custom-call | flops 180000000 | bytes 1000 | tf_op jit(solution)/shard_map/norm_conv/pallas_call | solution.py:136
  73.4 3.8 %collective-permute-done.5.received_ref = bf16[4,640,128]{2,1,0:T(8,128)(2,1)S(1)} collective-permute-done((bf16[4,640,128]{2,1,0:T(8,128)(2,1)}, bf16[4,640,128]{2,1,0:T(8,128)(2,1)S(1)}, u32[]{:S(2)}, u32[]{:S(2)}) %collective-permute-start.5) | collective-permute-done | bytes 655392 | tf_op jit(solution)/shard_map/ppermute | solution.py:30
  77.1 1.3 copy-done.5
  78.4 0.4 residual.1.own_ref.refs_0_
  78.9 3.5 %collective-permute-done.10.refs_9_.refs_10_ = bf16[2,512,512]{2,1,0:T(8,128)(2,1)S(1)} collective-permute-done((bf16[2,512,512]{2,1,0:T(8,128)(2,1)S(1)}, bf16[2,512,512]{2,1,0:T(8,128)(2,1)S(1)}, u32[]{:S(2)}, u32[]{:S(2)}) %collective-permute-start.10) | collective-permute-done | bytes 1048608 | tf_op jit(solution)/shard_map/ppermute | solution.py:536
  82.4 0.5 collective-permute-done.9.refs_7_.refs_8_
  82.9 1.5 %collective-permute-start.11 = (bf16[2,512,512]{2,1,0:T(8,128)(2,1)}, bf16[2,512,512]{2,1,0:T(8,128)(2,1)S(1)}, u32[]{:S(2)}, u32[]{:S(2)}) collective-permute-start(bf16[2,512,512]{2,1,0:T(8,128)(2,1)} %collective-permute-done.9.refs_7_.refs_8_), channel_id=1, source_target_pairs={{0,4},{4,8},{8,12},{12,14},{14,10},{10,6},{6,2},{2,0},{1,5},{5,9},... | collective-permute-start | bytes 3145736 | tf_op jit(solution)/shard_map/ppermute | solution.py:536
  84.4 0.5 collective-permute-start.12
  84.9 2.1 %collective-permute-done.6.refs_1_ = bf16[4,656,128]{2,1,0:T(8,128)(2,1)S(1)} collective-permute-done((bf16[4,656,128]{2,1,0:T(8,128)(2,1)S(1)}, bf16[4,656,128]{2,1,0:T(8,128)(2,1)S(1)}, u32[]{:S(2)}, u32[]{:S(2)}) %collective-permute-start.6) | collective-permute-done | bytes 671776 | tf_op jit(solution)/shard_map/ppermute | solution.py:30
  87.0 0.8 copy-done.10
  87.9 6.3 %norm_project.1 = (bf16[512,512]{1,0:T(8,128)(2,1)}, bf16[2,512,512]{2,1,0:T(8,128)(2,1)}) custom-call(s32[2]{0:T(128)} %pad_add_fusion.2.order_ref, bf16[4,656,128]{2,1,0:T(8,128)(2,1)} %copy-done.3, bf16[4,656,128]{2,1,0:T(8,128)(2,1)} %copy-done.10, bf16[3,1280,512]{2,1,0:T(8,128)(2,1)} %bitcast.37), custom_call_target="tpu_custom_call" | custom-call | flops 130000000 | bytes 1000 | tf_op jit(solution)/shard_map/norm_project/pallas_call | solution.py:290
  94.2 1.0 copy-done.6
  95.2 1.2 copy-done.7
  96.5 15.1 %attend.3 = (f32[4,2,512,128]{3,2,1,0:T(8,128)S(1)}, f32[4,2,512,128]{3,2,1,0:T(8,128)S(1)}) custom-call(bf16[512,512]{1,0:T(8,128)(2,1)S(1)} %copy-done.6, bf16[2,512,512]{2,1,0:T(8,128)(2,1)S(1)} %copy-done.7, bf16[2,512,512]{2,1,0:T(8,128)(2,1)S(1)} %copy-done.7, bf16[2,512,512]{2,1,0:T(8,128)(2,1)S(1)} %collective-permute-done.7.refs_3_.refs_4_, ...), custom_call_target="tpu_custom_call" | custom-call | flops 340000000 | bytes 1000 | tf_op jit(solution)/shard_map/attend/pallas_call | solution.py:463
  111.7 1.6 %collective-permute-start.13 = (bf16[1,512,512]{2,1,0:T(8,128)(2,1)S(1)}, bf16[1,512,512]{2,1,0:T(8,128)(2,1)S(1)}, u32[]{:S(2)}, u32[]{:S(2)}) collective-permute-start(bf16[1,512,512]{2,1,0:T(8,128)(2,1)S(1)} %slice.24), channel_id=1, source_target_pairs={{0,4},{4,8},{8,12},{12,14},{14,10},{10,6},{6,2},{2,0},{1,5},{5,9},... | collective-permute-start | bytes 1572872 | tf_op jit(solution)/shard_map/ppermute | solution.py:536
  113.2 0.5 collective-permute-start.14
  113.7 6.8 %attend.4 = (f32[4,2,512,128]{3,2,1,0:T(8,128)S(1)}, f32[4,2,512,128]{3,2,1,0:T(8,128)S(1)}) custom-call(bf16[512,512]{1,0:T(8,128)(2,1)S(1)} %copy-done.6, bf16[2,512,512]{2,1,0:T(8,128)(2,1)S(1)} %collective-permute-done.11.refs_1_.refs_2_, bf16[2,512,512]{2,1,0:T(8,128)(2,1)S(1)} %collective-permute-done.11.refs_1_.refs_2_, ...), custom_call_target="tpu_custom_call" | custom-call | flops 148000000 | bytes 1000 | tf_op jit(solution)/shard_map/attend/pallas_call | solution.py:463
  120.6 5.1 %collective-permute-done.13.refs_1_ = bf16[1,512,512]{2,1,0:T(8,128)(2,1)S(1)} collective-permute-done((bf16[1,512,512]{2,1,0:T(8,128)(2,1)S(1)}, bf16[1,512,512]{2,1,0:T(8,128)(2,1)S(1)}, u32[]{:S(2)}, u32[]{:S(2)}) %collective-permute-start.13) | collective-permute-done | bytes 524320 | tf_op jit(solution)/shard_map/ppermute | solution.py:536
  125.7 1.2 collective-permute-done.14.refs_2_
  126.9 5.4 %attend.5 = (bf16[2,4,320,128]{3,2,1,0:T(8,128)(2,1)S(1)}, f32[2,4,320,128]{3,2,1,0:T(8,128)S(1)}) custom-call(bf16[512,512]{1,0:T(8,128)(2,1)S(1)} %copy-done.6, bf16[1,512,512]{2,1,0:T(8,128)(2,1)S(1)} %collective-permute-done.13.refs_1_, bf16[1,512,512]{2,1,0:T(8,128)(2,1)S(1)} %collective-permute-done.14.refs_2_, ...), custom_call_target="tpu_custom_call" | custom-call | flops 84000000 | bytes 1000 | tf_op jit(solution)/shard_map/attend/pallas_call | solution.py:463
  132.4 0.1 collective-permute-start.15
  132.5 1.0 parity_split.1.resid_ref
  133.5 1.1 collective-permute-done.15.refs_1_
  134.5 0.1 branch_out.2
  134.6 0.8 collective-permute-start.16
  135.5 0.1 branch_out.3
  135.6 9.0 %collective-permute-done.16 = bf16[4,320,128]{2,1,0:T(8,128)(2,1)} collective-permute-done((bf16[4,320,128]{2,1,0:T(8,128)(2,1)S(1)}, bf16[4,320,128]{2,1,0:T(8,128)(2,1)}, u32[]{:S(2)}, u32[]{:S(2)}) %collective-permute-start.16) | collective-permute-done | bytes 327712 | tf_op jit(solution)/shard_map/ppermute | solution.py:30
  144.6 1.9 %fusion.3 = bf16[4,320,1,128]{3,1,2,0:T(8,128)(2,1)} fusion(bf16[4,320,128]{2,1,0:T(8,128)(2,1)S(1)} %branch_out.3, bf16[4,320,128]{2,1,0:T(8,128)(2,1)} %collective-permute-done.16, pred[]{:T(512)S(6)} %eq.9), kind=kLoop, calls=%fused_computation.8 | loop fusion | flops 1310720 | bytes 983041
  (38 shorter events, 0.2 us)
Async XLA Ops:
  0.6 61.5 %copy-start = (bf16[320,640]{1,0:T(8,128)(2,1)S(1)}, bf16[320,640]{1,0:T(8,128)(2,1)}, u32[]{:S(2)}) copy-start(bf16[320,640]{1,0:T(8,128)(2,1)} %param.15) | copy-start | bytes 1228804
  1.7 23.4 %collective-permute-start = (bf16[1,640,128]{2,1,0:T(8,128)(2,1)S(1)}, bf16[1,640,128]{2,1,0:T(8,128)(2,1)S(1)}, u32[]{:S(2)}, u32[]{:S(2)}) collective-permute-start(bf16[1,640,128]{2,1,0:T(8,128)(2,1)S(1)} %get-tuple-element.55), channel_id=1, source_target_pairs={{0,2},{2,4},{4,6},{6,8},{8,10},{10,12},{12,14},{1,3},{3,5},{5,7},{... | collective-permute-start | bytes 491528 | tf_op jit(solution)/shard_map/ppermute | solution.py:512
  6.6 18.5 %collective-permute-start.1 = (bf16[1,640,128]{2,1,0:T(8,128)(2,1)S(1)}, bf16[1,640,128]{2,1,0:T(8,128)(2,1)S(1)}, u32[]{:S(2)}, u32[]{:S(2)}) collective-permute-start(bf16[1,640,128]{2,1,0:T(8,128)(2,1)S(1)} %get-tuple-element.54), channel_id=1, source_target_pairs={{2,0},{4,2},{6,4},{8,6},{10,8},{12,10},{14,12},{3,1},{5,3},{7,5},{... | collective-permute-start | bytes 491528 | tf_op jit(solution)/shard_map/ppermute | solution.py:513
  10.5 14.1 %all-to-all-start = ((f32[32,1,128]{2,1,0:T(1,128)}), f32[32,1,128]{2,1,0:T(1,128)S(1)}, u32[]{:S(2)}, u32[]{:S(2)}) async-start(f32[32,1,128]{2,1,0:T(1,128)} %broadcast_in_dim.23), calls=%async_computation | async-start | bytes 32768 | tf_op jit(solution)/shard_map/all_to_all | solution.py:43
  25.1 1.1 copy-start.1
  26.3 32.9 %copy-start.8 = (bf16[6,656,128]{2,1,0:T(8,128)(2,1)}, bf16[6,656,128]{2,1,0:T(8,128)(2,1)S(1)}, u32[]{:S(2)}) copy-start(bf16[6,656,128]{2,1,0:T(8,128)(2,1)S(1)} %rim.1.refs_0_) | copy-start | bytes 3022852
  26.3 16.4 %collective-permute-start.3 = (bf16[6,656,128]{2,1,0:T(8,128)(2,1)S(1)}, bf16[6,656,128]{2,1,0:T(8,128)(2,1)}, u32[]{:S(2)}, u32[]{:S(2)}) collective-permute-start(bf16[6,656,128]{2,1,0:T(8,128)(2,1)S(1)} %rim.1.refs_0_), channel_id=1, source_target_pairs={{1,17},{16,0},{3,19},{18,2},{5,21},{20,4},{7,23},{22,6},{9,25},{24... | collective-permute-start | bytes 3022856 | tf_op jit(solution)/shard_map/ppermute | solution.py:61
  27.6 31.6 %collective-permute-start.7 = (bf16[2,512,512]{2,1,0:T(8,128)(2,1)}, bf16[2,512,512]{2,1,0:T(8,128)(2,1)S(1)}, u32[]{:S(2)}, u32[]{:S(2)}) collective-permute-start(bf16[2,512,512]{2,1,0:T(8,128)(2,1)} %bitcast.21), channel_id=1, source_target_pairs={{0,4},{4,8},{8,12},{12,14},{14,10},{10,6},{6,2},{2,0},{1,5},{5,9},... | collective-permute-start | bytes 3145736 | tf_op jit(solution)/shard_map/ppermute | solution.py:536
  28.1 31.1 %collective-permute-start.8 = (bf16[2,512,512]{2,1,0:T(8,128)(2,1)}, bf16[2,512,512]{2,1,0:T(8,128)(2,1)S(1)}, u32[]{:S(2)}, u32[]{:S(2)}) collective-permute-start(bf16[2,512,512]{2,1,0:T(8,128)(2,1)} %bitcast.21), channel_id=1, source_target_pairs={{4,0},{8,4},{12,8},{14,12},{10,14},{6,10},{2,6},{0,2},{5,1},{9,5},... | collective-permute-start | bytes 3145736 | tf_op jit(solution)/shard_map/ppermute | solution.py:536
  29.7 19.1 %collective-permute-start.2 = (bf16[6,656,128]{2,1,0:T(8,128)(2,1)S(1)}, bf16[6,656,128]{2,1,0:T(8,128)(2,1)}, u32[]{:S(2)}, u32[]{:S(2)}) collective-permute-start(bf16[6,656,128]{2,1,0:T(8,128)(2,1)S(1)} %rim.1.refs_0_), channel_id=1, source_target_pairs={{0,1},{17,16},{2,3},{19,18},{4,5},{21,20},{6,7},{23,22},{8,9},{25,... | collective-permute-start | bytes 3022856 | tf_op jit(solution)/shard_map/ppermute | solution.py:63
  42.6 6.2 %collective-permute-start.4 = (bf16[6,656,128]{2,1,0:T(8,128)(2,1)}, bf16[6,656,128]{2,1,0:T(8,128)(2,1)}, u32[]{:S(2)}, u32[]{:S(2)}) collective-permute-start(bf16[6,656,128]{2,1,0:T(8,128)(2,1)} %collective-permute-done.3.refs_0_), channel_id=1, source_target_pairs={{0,1},{17,16},{2,3},{19,18},{4,5},{21,20},{6,7},{23,22},{8,9},{25,... | collective-permute-start | bytes 3022856 | tf_op jit(solution)/shard_map/ppermute | solution.py:64
  44.9 1.3 copy-start.9
  48.8 13.7 %copy-start.11 = (bf16[640]{0:T(1024)(128)(2,1)S(1)}, bf16[640]{0:T(1024)(128)(2,1)}, u32[]{:S(2)}) copy-start(bf16[640]{0:T(1024)(128)(2,1)} %param.19) | copy-start | bytes 3844
  48.8 13.9 %copy-start.12 = (bf16[640]{0:T(1024)(128)(2,1)S(1)}, bf16[640]{0:T(1024)(128)(2,1)}, u32[]{:S(2)}) copy-start(bf16[640]{0:T(1024)(128)(2,1)} %param.21) | copy-start | bytes 3844
  48.8 13.9 %copy-start.13 = (bf16[640]{0:T(1024)(128)(2,1)S(1)}, bf16[640]{0:T(1024)(128)(2,1)}, u32[]{:S(2)}) copy-start(bf16[640]{0:T(1024)(128)(2,1)} %param.20) | copy-start | bytes 3844
  59.2 23.2 %collective-permute-start.10 = (bf16[2,512,512]{2,1,0:T(8,128)(2,1)S(1)}, bf16[2,512,512]{2,1,0:T(8,128)(2,1)S(1)}, u32[]{:S(2)}, u32[]{:S(2)}) collective-permute-start(bf16[2,512,512]{2,1,0:T(8,128)(2,1)S(1)} %collective-permute-done.8.refs_5_.refs_6_), channel_id=1, source_target_pairs={{4,0},{8,4},{12,8},{14,12},{10,14},{6,10},{2,6},{0,2},{5,1},{9,5},... | collective-permute-start | bytes 3145736 | tf_op jit(solution)/shard_map/ppermute | solution.py:536
  59.8 23.1 %collective-permute-start.9 = (bf16[2,512,512]{2,1,0:T(8,128)(2,1)S(1)}, bf16[2,512,512]{2,1,0:T(8,128)(2,1)}, u32[]{:S(2)}, u32[]{:S(2)}) collective-permute-start(bf16[2,512,512]{2,1,0:T(8,128)(2,1)S(1)} %collective-permute-done.7.refs_3_.refs_4_), channel_id=1, source_target_pairs={{0,4},{4,8},{8,12},{12,14},{14,10},{10,6},{6,2},{2,0},{1,5},{5,9},... | collective-permute-start | bytes 3145736 | tf_op jit(solution)/shard_map/ppermute | solution.py:536
  61.9 15.2 %collective-permute-start.5 = (bf16[4,640,128]{2,1,0:T(8,128)(2,1)}, bf16[4,640,128]{2,1,0:T(8,128)(2,1)S(1)}, u32[]{:S(2)}, u32[]{:S(2)}) collective-permute-start(bf16[4,640,128]{2,1,0:T(8,128)(2,1)} %norm_conv.3), channel_id=1, source_target_pairs={{0,16},{16,0},{1,17},{17,1},{2,18},{18,2},{3,19},{19,3},{4,20},{20... | collective-permute-start | bytes 1966088 | tf_op jit(solution)/shard_map/ppermute | solution.py:30
  62.7 14.4 %copy-start.2 = (bf16[1,4,640,128]{3,2,1,0:T(8,128)(2,1)S(1)}, bf16[1,4,640,128]{3,2,1,0:T(8,128)(2,1)}, u32[]{:S(2)}) copy-start(bf16[1,4,640,128]{3,2,1,0:T(8,128)(2,1)} %param.12) | copy-start | bytes 1966084
  77.1 1.3 copy-start.5
  78.9 8.2 %copy-start.3 = (bf16[4,656,128]{2,1,0:T(8,128)(2,1)}, bf16[4,656,128]{2,1,0:T(8,128)(2,1)S(1)}, u32[]{:S(2)}) copy-start(bf16[4,656,128]{2,1,0:T(8,128)(2,1)S(1)} %residual.1.own_ref.refs_0_) | copy-start | bytes 2015236
  82.9 28.7 %collective-permute-start.11 = (bf16[2,512,512]{2,1,0:T(8,128)(2,1)}, bf16[2,512,512]{2,1,0:T(8,128)(2,1)S(1)}, u32[]{:S(2)}, u32[]{:S(2)}) collective-permute-start(bf16[2,512,512]{2,1,0:T(8,128)(2,1)} %collective-permute-done.9.refs_7_.refs_8_), channel_id=1, source_target_pairs={{0,4},{4,8},{8,12},{12,14},{14,10},{10,6},{6,2},{2,0},{1,5},{5,9},... | collective-permute-start | bytes 3145736 | tf_op jit(solution)/shard_map/ppermute | solution.py:536
  84.4 27.2 %collective-permute-start.12 = (bf16[2,512,512]{2,1,0:T(8,128)(2,1)S(1)}, bf16[2,512,512]{2,1,0:T(8,128)(2,1)S(1)}, u32[]{:S(2)}, u32[]{:S(2)}) collective-permute-start(bf16[2,512,512]{2,1,0:T(8,128)(2,1)S(1)} %collective-permute-done.10.refs_9_.refs_10_), channel_id=1, source_target_pairs={{4,0},{8,4},{12,8},{14,12},{10,14},{6,10},{2,6},{0,2},{5,1},{9,5},... | collective-permute-start | bytes 3145736 | tf_op jit(solution)/shard_map/ppermute | solution.py:536
  84.9 2.1 %collective-permute-start.6 = (bf16[4,656,128]{2,1,0:T(8,128)(2,1)S(1)}, bf16[4,656,128]{2,1,0:T(8,128)(2,1)S(1)}, u32[]{:S(2)}, u32[]{:S(2)}) collective-permute-start(bf16[4,656,128]{2,1,0:T(8,128)(2,1)S(1)} %residual.1.own_ref.refs_0_), channel_id=1, source_target_pairs={{0,1},{1,0},{2,3},{3,2},{4,5},{5,4},{6,7},{7,6},{8,9},{9,8},{10,11... | collective-permute-start | bytes 2015240 | tf_op jit(solution)/shard_map/ppermute | solution.py:30
  87.0 0.9 copy-start.10
  94.2 1.0 copy-start.6
  95.2 1.2 copy-start.7
  111.7 14.0 %collective-permute-start.13 = (bf16[1,512,512]{2,1,0:T(8,128)(2,1)S(1)}, bf16[1,512,512]{2,1,0:T(8,128)(2,1)S(1)}, u32[]{:S(2)}, u32[]{:S(2)}) collective-permute-start(bf16[1,512,512]{2,1,0:T(8,128)(2,1)S(1)} %slice.24), channel_id=1, source_target_pairs={{0,4},{4,8},{8,12},{12,14},{14,10},{10,6},{6,2},{2,0},{1,5},{5,9},... | collective-permute-start | bytes 1572872 | tf_op jit(solution)/shard_map/ppermute | solution.py:536
  113.2 13.7 %collective-permute-start.14 = (bf16[1,512,512]{2,1,0:T(8,128)(2,1)S(1)}, bf16[1,512,512]{2,1,0:T(8,128)(2,1)S(1)}, u32[]{:S(2)}, u32[]{:S(2)}) collective-permute-start(bf16[1,512,512]{2,1,0:T(8,128)(2,1)S(1)} %slice.25), channel_id=1, source_target_pairs={{4,0},{8,4},{12,8},{14,12},{10,14},{6,10},{2,6},{0,2},{5,1},{9,5},... | collective-permute-start | bytes 1572872 | tf_op jit(solution)/shard_map/ppermute | solution.py:536
  126.9 5.5 %copy-start.4 = (bf16[4,656,128]{2,1,0:T(8,128)(2,1)S(1)}, bf16[4,656,128]{2,1,0:T(8,128)(2,1)}, u32[]{:S(2)}) copy-start(bf16[4,656,128]{2,1,0:T(8,128)(2,1)} %copy-done.3) | copy-start | bytes 2015236
  132.4 2.2 %collective-permute-start.15 = (bf16[2,4,320,128]{3,2,1,0:T(8,128)(2,1)S(1)}, bf16[2,4,320,128]{3,2,1,0:T(8,128)(2,1)S(1)}, u32[]{:S(2)}, u32[]{:S(2)}) collective-permute-start(bf16[2,4,320,128]{3,2,1,0:T(8,128)(2,1)S(1)} %get-tuple-element.43), channel_id=1, source_target_pairs={{0,1},{1,0},{2,3},{3,2},{4,5},{5,4},{6,7},{7,6},{8,9},{9,8},{10,11... | collective-permute-start | bytes 1966088 | tf_op jit(solution)/shard_map/ppermute | solution.py:30
  134.6 9.9 %collective-permute-start.16 = (bf16[4,320,128]{2,1,0:T(8,128)(2,1)S(1)}, bf16[4,320,128]{2,1,0:T(8,128)(2,1)}, u32[]{:S(2)}, u32[]{:S(2)}) collective-permute-start(bf16[4,320,128]{2,1,0:T(8,128)(2,1)S(1)} %branch_out.2), channel_id=1, source_target_pairs={{0,16},{16,0},{1,17},{17,1},{2,18},{18,2},{3,19},{19,3},{4,20},{20... | collective-permute-start | bytes 983048 | tf_op jit(solution)/shard_map/ppermute | solution.py:30

commit v9 on v8

--- a/solution.py
+++ b/solution.py
@@ -47,17 +47,14 @@
     return lax.optimization_barrier((array,) + tuple(others))[0] if others else array
 
 
-def halves_of_inputs(own, gain, bias):
+def halves_of_inputs(own):
     cfg = lax.axis_index("cfg")
     if lax.axis_size("tp") != 2:
         full = lax.all_gather(own, "tp", axis=1, tiled=True)
         half = full.shape[1] // 2
-        vectors = lax.all_gather(jnp.stack([gain, bias]), "tp", axis=1, tiled=True)
-        vectors = lax.dynamic_slice_in_dim(vectors, cfg * half, half, 1)
-        rows = vector_rows(vectors[0], vectors[1])
         mine = lax.dynamic_slice_in_dim(full, cfg * half, half, 1)
         sent = lax.dynamic_slice_in_dim(full, (1 - cfg) * half, half, 1)
-        return [attached(mine, rows)], [attached(swapped(sent, "cfg"), rows)]
+        return [mine], [swapped(sent, "cfg")]
     across = lax.ppermute(own, ("cfg", "tp"), [(1, 3), (2, 0)])
     pairs = [(0, 1), (3, 2)]
     own_side = lax.ppermute(own, ("cfg", "tp"), pairs)
@@ -65,7 +62,7 @@
     return [own, own_side], [across, across_side]
 
 
-def conv_kernel(choices, amount, flags_ref, sums_ref, *refs):
+def conv_kernel(choices, flags_ref, *refs):
     x_refs = refs[:choices]
     w_hbm, out_ref, w_ref, act_ref, sems = refs[choices:]
     rows = out_ref.shape[0]
@@ -77,37 +74,12 @@
                 w_hbm.at[a, b], w_ref.at[b, :, a * ins : (a + 1) * ins], sems.at[a, b]
             )
             copies[a, b].start()
-
-    groups = ins // (D // GROUPS)
-    base = flags_ref[3]
-
-    def column(offset):
-        return jnp.concatenate(
-            [jnp.full((D // GROUPS, 1), sums_ref[base + offset + g], jnp.float32) for g in range(groups)],
-            axis=0,
-        )
-
-    mean = column(0) / amount
-    variance = column(GROUPS) / amount - mean * mean
-
-    def chosen(r, at):
-        x = [ref[r, at] for ref in x_refs]
-        return x[0] if choices == 1 else jnp.where(flags_ref[2] == 1, x[0], x[1])
-
-    gain, shift = columns_of(chosen(0, slice(ins, None)), ins)
-    scale = lax.rsqrt(variance + epsilon) * gain
     for r in range(rows + 2):
-        x = chosen(r, slice(0, ins))
-        z = ((x.astype(jnp.float32) - mean) * scale + shift) * 0.5
-        z = z + z * jnp.tanh(z)
-        if r == 0:
-            z = jnp.where(flags_ref[0] == 1, z, 0.0)
-        if r == rows + 1:
-            z = jnp.where(flags_ref[1] == 1, z, 0.0)
-        z = z.astype(jnp.bfloat16)
+        x = [ref[r] for ref in x_refs]
+        x = x[0] if choices == 1 else jnp.where(flags_ref[2] == 1, x[0], x[1])
         for a in range(3):
             if 0 <= r - a < rows:
-                act_ref[a * ins : (a + 1) * ins, (r - a) * LANES : (r - a + 1) * LANES] = z
+                act_ref[a * ins : (a + 1) * ins, (r - a) * LANES : (r - a + 1) * LANES] = x
 
     width = min(2, rows)
     lane = lax.broadcasted_iota(jnp.int32, (out_ref.shape[1], LANES), 1)
@@ -130,13 +102,12 @@
             out_ref[start + r] = total[r].astype(out_ref.dtype)
 
 
-def conv_call(flags, sums, amount, xs, conv_w, out_dtype):
+def conv_call(flags, xs, conv_w, out_dtype):
     rows = xs[0].shape[0] - 2
     outs, ins = conv_w.shape[2:]
     return pl.pallas_call(
-        functools.partial(conv_kernel, len(xs), amount),
+        functools.partial(conv_kernel, len(xs)),
         in_specs=[
-            pl.BlockSpec(memory_space=pltpu.SMEM),
             pl.BlockSpec(memory_space=pltpu.SMEM),
             *[pl.BlockSpec(memory_space=pltpu.VMEM)] * len(xs),
             pl.BlockSpec(memory_space=pltpu.HBM),
@@ -151,7 +122,7 @@
         compiler_params=pltpu.CompilerParams(vmem_limit_bytes=57 * MIB),
         cost_estimate=cost(9000),
         name="norm_conv",
-    )(flags, sums, *xs, conv_w)
+    )(flags, *xs, conv_w)
 
 
 def extra_rows(channels):
@@ -175,14 +146,44 @@
     return jnp.concatenate([array, jnp.broadcast_to(rows[None], shape)], axis=1)
 
 
-def rim_kernel(before_ref, x_ref, after_ref, vector_ref, out_ref):
+def activate_kernel(amount, flags_ref, sums_ref, before_ref, x_ref, after_ref, affine_ref, out_ref):
     rows, channels, _ = x_ref.shape
-    out_ref[0, :channels] = before_ref[0]
-    out_ref[rows + 1, :channels] = after_ref[0]
-    for r in range(rows):
-        out_ref[r + 1, :channels] = x_ref[r]
+    width = D // GROUPS
+    groups = channels // width
+
+    def column(offset):
+        return jnp.concatenate(
+            [jnp.full((width, 1), sums_ref[offset + g], jnp.float32) for g in range(groups)], axis=0
+        )
+
+    mean = column(0) / amount
+    variance = column(groups) / amount - mean * mean
+    scale = lax.rsqrt(variance + epsilon) * affine_ref[:, 0:1]
+    shift = affine_ref[:, 1:2]
     for r in range(rows + 2):
-        out_ref[r, channels:] = vector_ref[...]
+        x = before_ref[0] if r == 0 else after_ref[0] if r == rows + 1 else x_ref[r - 1]
+        z = ((x.astype(jnp.float32) - mean) * scale + shift) * 0.5
+        z = z + z * jnp.tanh(z)
+        if r == 0:
+            z = jnp.where(flags_ref[0] == 1, z, 0.0)
+        if r == rows + 1:
+            z = jnp.where(flags_ref[1] == 1, z, 0.0)
+        out_ref[r] = z.astype(jnp.bfloat16)
+
+
+def activate_call(flags, sums, amount, before, x, after, affine):
+    rows, channels, _ = x.shape
+    smem = pl.BlockSpec(memory_space=pltpu.SMEM)
+    vmem = pl.BlockSpec(memory_space=pltpu.VMEM)
+    return pl.pallas_call(
+        functools.partial(activate_kernel, amount),
+        in_specs=[smem, smem, vmem, vmem, vmem, vmem],
+        out_specs=vmem,
+        out_shape=jax.ShapeDtypeStruct((rows + 2, channels, LANES), jnp.bfloat16),
+        compiler_params=pltpu.CompilerParams(vmem_limit_bytes=VMEM_LIMIT),
+        cost_estimate=cost(1000),
+        name="activate",
+    )(flags, sums, before, x, after, affine)
 
 
 def small_call(kernel, out_shape, name, *operands):
@@ -503,23 +504,18 @@
     sums = jnp.stack(
         [jnp.sum(values32, axis=(0, 2, 3)), jnp.sum(values32 * values32, axis=(0, 2, 3))]
     )
-    table = jnp.zeros((2, 2, GROUPS), jnp.float32)
-    table = lax.dynamic_update_slice(table, sums[None], (cfg, 0, tp * local_groups))
-    table = summed(table.reshape(-1), ("cfg", "rows", "tp"))
+    table = jnp.pad(sums.reshape(-1), (0, LANES - 2 * local_groups))
+    table = summed(table, "rows")
 
     up_pairs = [(i, i + 1) for i in range(rows_count - 1)]
     down_pairs = [(i + 1, i) for i in range(rows_count - 1)]
     before = lax.ppermute(latent_rows[span_rows - 1 :], "rows", up_pairs)
     after = lax.ppermute(latent_rows[:1], "rows", down_pairs)
-    if tp_count == 2:
-        shape = (span_rows + 2, local_channels + extra_rows(local_channels), grid_width)
-        rimmed = small_call(
-            rim_kernel, shape, "rim", before, latent_rows, after, vector_rows(gn_gain, gn_bias)
-        )
-        rimmed = need(rimmed, (table,))
-    else:
-        rimmed = jnp.concatenate([before, latent_rows, after], axis=0)
-    x_mine, x_other = halves_of_inputs(rimmed, gn_gain, gn_bias)
+    flags = jnp.stack([my_block > 0, my_block < rows_count - 1, tp == cfg]).astype(jnp.int32)
+    affine = jnp.stack([gn_gain, gn_bias], axis=1).astype(jnp.float32)
+    amount = span_rows * rows_count * grid_width * group_width
+    activated = activate_call(flags, table, amount, before, latent_rows, after, affine)
+    x_mine, x_other = halves_of_inputs(activated)
 
     forward, backward = ring_pairs(rows_count)
     last = rows_count // 2
@@ -544,25 +540,19 @@
 
     next_hop(table)
 
-    amount = span_rows * rows_count * grid_width * group_width
-    flags = jnp.stack([my_block > 0, my_block < rows_count - 1, tp == cfg]).astype(jnp.int32)
-    place = cfg * (GROUPS // 2)
-    flags_mine = jnp.append(flags, cfg * 2 * GROUPS + place)
-    flags_other = jnp.append(flags, (1 - cfg) * 2 * GROUPS + place)
-
     local_features = w_qkv.shape[2]
     w_project = w_qkv.transpose(1, 0, 2)
     flip = jnp.logical_and(tp_count == 2, tp == 0)
     w_back = arrange_call(flip, w_out, tp_count)
     order = jnp.stack([tp, 1 - tp]).astype(jnp.int32) if tp_count == 2 else jnp.zeros((1,), jnp.int32)
     flags_other, order, w_back, *_ = lax.optimization_barrier(
-        (flags_other, order, w_back) + tuple(x_mine[1:])
+        (flags, order, w_back) + tuple(x_mine[1:])
     )
 
-    conv_sent = conv_call(flags_other, table, amount, x_other, conv_w, jnp.bfloat16)
+    conv_sent = conv_call(flags_other, x_other, conv_w, jnp.bfloat16)
     conv_received = swapped(conv_sent, "cfg")
     next_hop(conv_sent)
-    conv_own = conv_call(flags_mine, table, amount, x_mine, conv_w, jnp.float32)
+    conv_own = conv_call(flags, x_mine, conv_w, jnp.float32)
 
     half_width = TEMB // 2
     frequencies = jnp.exp(

time: 147 us -> 147 us (level)
  waiting for transfers between devices: 41.7 us -> 36.6 us
  Pallas kernels: 57.6 us -> 62.2 us
  other arithmetic: 6.16 us -> 3.48 us
  local copies, waits for them, and re-layouts: 9.17 us -> 11.3 us
    all_to_all x1, waiting for transfers between devices: 6.36 us -> 0.01 us  [summed(): return jnp.sum(lax.all_to_all(spread, axes, 0, 0, tiled=True), axis=0)]
    ppermute x1, waiting for transfers between devices: 0.01 us -> 4.22 us  [per_device(): after = lax.ppermute(latent_rows[:1], 'rows', down_pairs)]
    ppermute x4, waiting for transfers between devices: 4.75 us -> 2.68 us  [next_hop(): lax.ppermute(behind, 'rows', backward)]
    ppermute x4, starting transfers between devices: 3.1 us -> 5.11 us  [next_hop(): lax.ppermute(behind, 'rows', backward)]
    pallas_call x2, Pallas kernels: 0.2 us -> 2.14 us  [branch_call(): pl.pallas_call(branch_kernel, grid_spec=pltpu.PrefetchScalarGridSpec(num_...]
    pallas_call x2 -> x3, Pallas kernels: 21 us -> 22.9 us  [the longest x2 20.8 us: conv_call(): pl.pallas_call(functools.partial(conv_kernel, len(xs)), in_specs=[pl.Bloc...]
    unnamed x28 -> x30, local copies, waits for them, and re-layouts: 6.87 us -> 7.71 us
  transfers between devices with their start and end apart: 18 -> 18, of which waited for: 10 -> 10; matrix products, arithmetic and copies ran while one was open for 4% -> 3% of each run, Pallas kernels for 36% -> 36%
where the time goes in v9:
time: 147 us; the launch traced here: 146 us
  Pallas kernels  62.2 us (42%)
  waiting for transfers between devices  36.6 us (25%)
  starting transfers between devices  30.9 us (21%)
  local copies, waits for them, and re-layouts  11.3 us (8%)
  other arithmetic  3.48 us (2%)
  between operations  1.63 us (1%)
    pallas_call x3, Pallas kernels, attention_call(): pl.pallas_call(functools.partial(attention_kernel, len(pairs), state is n...  28.2 us
    pallas_call x2, Pallas kernels, conv_call(): pl.pallas_call(functools.partial(conv_kernel, len(xs)), in_specs=[pl.Bloc...  20.8 us
    ppermute x4, waiting for transfers between devices, swapped(): lax.ppermute(array, axis, [(i, i ^ 1) for i in range(lax.axis_size(axis))])  15.9 us
    unnamed x30, local copies, waits for them, and re-layouts  7.71 us
    ppermute x1, waiting for transfers between devices, halves_of_inputs(): across = lax.ppermute(own, ('cfg', 'tp'), [(1, 3), (2, 0)])  7.7 us
    all_to_all x1, starting transfers between devices, summed(): return jnp.sum(lax.all_to_all(spread, axes, 0, 0, tiled=True), axis=0)  7.25 us
    pallas_call x1, Pallas kernels, project_call(): pl.pallas_call(functools.partial(project_kernel, len(parts)), in_specs=[p...  6.31 us
    ppermute x4, waiting for transfers between devices, next_hop(): lax.ppermute(ahead, 'rows', forward)  6.13 us
  transfers between devices with their start and end apart: 18, of which 10 were waited for; matrix products, arithmetic and copies ran while one was open for 3% of the time, Pallas kernels for 36%

profile of v9, /device:TPU:0, one launch (start us, length us, event | category | flops | bytes accessed | tf_op | source)
XLA Modules:
  0.0 146.5 jit_solution(17275960820536042273)
XLA Ops:
  0.6 0.0 copy-start
  0.6 0.0 copy-start.1
  0.7 1.4 convert_reduce_fusion
  2.1 0.1 reduce_sum.32
  2.2 0.1 reduce_sum.45
  2.3 0.1 reduce_sum.36
  2.4 0.1 reduce_sum.46
  2.5 0.1 reshape.46
  2.6 0.6 broadcast_in_dim.6
  3.2 7.3 %all-to-all-start = ((f32[8,1,128]{2,1,0:T(1,128)}), f32[8,1,128]{2,1,0:T(1,128)S(1)}, u32[]{:S(2)}, u32[]{:S(2)}) async-start(f32[8,1,128]{2,1,0:T(1,128)} %broadcast_in_dim.6), calls=%async_computation | async-start | bytes 8192 | tf_op jit(solution)/shard_map/all_to_all | solution.py:43
  10.5 1.0 slice_bitcast_fusion
  11.5 3.9 %collective-permute-start = (bf16[1,640,128]{2,1,0:T(8,128)(2,1)S(1)}, bf16[1,640,128]{2,1,0:T(8,128)(2,1)S(1)}, u32[]{:S(2)}, u32[]{:S(2)}) collective-permute-start(bf16[1,640,128]{2,1,0:T(8,128)(2,1)S(1)} %get-tuple-element.57), channel_id=1, source_target_pairs={{0,2},{2,4},{4,6},{6,8},{8,10},{10,12},{12,14},{1,3},{3,5},{5,7},{... | collective-permute-start | bytes 491528 | tf_op jit(solution)/shard_map/ppermute | solution.py:512
  15.4 1.3 collective-permute-start.1
  16.7 0.7 stack.46
  17.4 0.7 stack.47
  18.1 0.1 add_convert_fusion.flags_ref
  18.2 0.2 copy.30.affine_ref
  18.4 0.0 all-to-all-done
  18.4 4.2 %collective-permute-done.1.after_ref = bf16[1,640,128]{2,1,0:T(8,128)(2,1)S(1)} collective-permute-done((bf16[1,640,128]{2,1,0:T(8,128)(2,1)S(1)}, bf16[1,640,128]{2,1,0:T(8,128)(2,1)S(1)}, u32[]{:S(2)}, u32[]{:S(2)}) %collective-permute-start.1) | collective-permute-done | bytes 163872 | tf_op jit(solution)/shard_map/ppermute | solution.py:513
  22.6 2.2 %activate.1.refs_0_ = bf16[6,640,128]{2,1,0:T(8,128)(2,1)} custom-call(s32[3]{0:T(128)S(1)} %add_convert_fusion.flags_ref, f32[128]{0:T(128)S(1)} %reduce_sum.47.sums_ref, bf16[1,640,128]{2,1,0:T(8,128)(2,1)S(1)} %collective-permute-done.before_ref, bf16[4,640,128]{2,1,0:T(8,128)(2,1)S(1)} %bitcast.28, ...), custom_call_target="tpu_custom_call" | custom-call | flops 20000000 | bytes 1000 | tf_op jit(solution)/shard_map/activate/pallas_call | solution.py:178
  24.8 1.3 collective-permute-start.3
  26.1 2.6 %collective-permute-start.7 = (bf16[2,512,512]{2,1,0:T(8,128)(2,1)}, bf16[2,512,512]{2,1,0:T(8,128)(2,1)S(1)}, u32[]{:S(2)}, u32[]{:S(2)}) collective-permute-start(bf16[2,512,512]{2,1,0:T(8,128)(2,1)} %bitcast.16), channel_id=1, source_target_pairs={{0,4},{4,8},{8,12},{12,14},{14,10},{10,6},{6,2},{2,0},{1,5},{5,9},... | collective-permute-start | bytes 3145736 | tf_op jit(solution)/shard_map/ppermute | solution.py:532
  28.7 4.7 %collective-permute-start.2 = (bf16[6,640,128]{2,1,0:T(8,128)(2,1)}, bf16[6,640,128]{2,1,0:T(8,128)(2,1)}, u32[]{:S(2)}, u32[]{:S(2)}) collective-permute-start(bf16[6,640,128]{2,1,0:T(8,128)(2,1)} %activate.1.refs_0_), channel_id=1, source_target_pairs={{0,1},{17,16},{2,3},{19,18},{4,5},{21,20},{6,7},{23,22},{8,9},{25,... | collective-permute-start | bytes 2949128 | tf_op jit(solution)/shard_map/ppermute | solution.py:60
  33.4 7.7 %collective-permute-done.3.refs_0_ = bf16[6,640,128]{2,1,0:T(8,128)(2,1)} collective-permute-done((bf16[6,640,128]{2,1,0:T(8,128)(2,1)}, bf16[6,640,128]{2,1,0:T(8,128)(2,1)}, u32[]{:S(2)}, u32[]{:S(2)}) %collective-permute-start.3) | collective-permute-done | bytes 983072 | tf_op jit(solution)/shard_map/ppermute | solution.py:58
  41.1 2.3 %collective-permute-start.4 = (bf16[6,640,128]{2,1,0:T(8,128)(2,1)}, bf16[6,640,128]{2,1,0:T(8,128)(2,1)}, u32[]{:S(2)}, u32[]{:S(2)}) collective-permute-start(bf16[6,640,128]{2,1,0:T(8,128)(2,1)} %collective-permute-done.3.refs_0_), channel_id=1, source_target_pairs={{0,1},{17,16},{2,3},{19,18},{4,5},{21,20},{6,7},{23,22},{8,9},{25,... | collective-permute-start | bytes 2949128 | tf_op jit(solution)/shard_map/ppermute | solution.py:61
  43.4 1.3 copy-done.7
  44.7 1.2 arrange.1.refs_5_
  45.9 0.7 pad_add_fusion.order_ref
  46.6 10.3 %norm_conv.3 = bf16[4,640,128]{2,1,0:T(8,128)(2,1)} custom-call(s32[3]{0:T(128)} %copy-done.10, bf16[6,640,128]{2,1,0:T(8,128)(2,1)} %collective-permute-done.3.refs_0_, bf16[6,640,128]{2,1,0:T(8,128)(2,1)} %collective-permute-done.4.refs_1_, bf16[3,3,640,640]{3,2,1,0:T(8,128)(2,1)} %refs_2_.3), custom_call_target="tpu_custom_call" | custom-call | flops 180000000 | bytes 1000 | tf_op jit(solution)/shard_map/norm_conv/pallas_call | solution.py:108
  56.9 2.4 %collective-permute-start.10 = (bf16[2,512,512]{2,1,0:T(8,128)(2,1)}, bf16[2,512,512]{2,1,0:T(8,128)(2,1)S(1)}, u32[]{:S(2)}, u32[]{:S(2)}) collective-permute-start(bf16[2,512,512]{2,1,0:T(8,128)(2,1)} %collective-permute-done.8.refs_5_.refs_6_), channel_id=1, source_target_pairs={{4,0},{8,4},{12,8},{14,12},{10,14},{6,10},{2,6},{0,2},{5,1},{9,5},... | collective-permute-start | bytes 3145736 | tf_op jit(solution)/shard_map/ppermute | solution.py:532
  59.3 0.3 collective-permute-start.9
  60.2 0.1 collective-permute-start.5
  60.4 0.1 divide_multiply_fusion
  60.5 0.3 convolution_reduce_fusion
  60.8 0.1 broadcast_in_dim.16.bias_ref
  61.0 10.5 %norm_conv.2.own_ref = f32[4,640,128]{2,1,0:T(8,128)} custom-call(s32[3]{0:T(128)} %copy-done.10, bf16[6,640,128]{2,1,0:T(8,128)(2,1)} %activate.1.refs_0_, bf16[6,640,128]{2,1,0:T(8,128)(2,1)} %collective-permute-done.2.refs_1_, bf16[3,3,640,640]{3,2,1,0:T(8,128)(2,1)} %refs_2_.3), custom_call_target="tpu_custom_call" | custom-call | flops 180000000 | bytes 1000 | tf_op jit(solution)/shard_map/norm_conv/pallas_call | solution.py:108
  71.5 4.3 %collective-permute-done.5.received_ref = bf16[4,640,128]{2,1,0:T(8,128)(2,1)S(1)} collective-permute-done((bf16[4,640,128]{2,1,0:T(8,128)(2,1)}, bf16[4,640,128]{2,1,0:T(8,128)(2,1)S(1)}, u32[]{:S(2)}, u32[]{:S(2)}) %collective-permute-start.5) | collective-permute-done | bytes 655392 | tf_op jit(solution)/shard_map/ppermute | solution.py:30
  75.8 0.8 copy-done.8
  76.6 1.3 copy-done.4
  77.9 1.1 copy-done.9
  79.0 0.4 residual.1.own_ref.refs_0_
  79.5 2.3 %collective-permute-done.10.refs_9_.refs_10_ = bf16[2,512,512]{2,1,0:T(8,128)(2,1)S(1)} collective-permute-done((bf16[2,512,512]{2,1,0:T(8,128)(2,1)}, bf16[2,512,512]{2,1,0:T(8,128)(2,1)S(1)}, u32[]{:S(2)}, u32[]{:S(2)}) %collective-permute-start.10) | collective-permute-done | bytes 1048608 | tf_op jit(solution)/shard_map/ppermute | solution.py:532
  81.7 1.1 collective-permute-done.9.refs_7_.refs_8_
  82.8 0.7 collective-permute-start.11
  83.5 1.3 collective-permute-start.12
  84.8 2.1 %collective-permute-done.6.refs_1_ = bf16[4,656,128]{2,1,0:T(8,128)(2,1)S(1)} collective-permute-done((bf16[4,656,128]{2,1,0:T(8,128)(2,1)S(1)}, bf16[4,656,128]{2,1,0:T(8,128)(2,1)S(1)}, u32[]{:S(2)}, u32[]{:S(2)}) %collective-permute-start.6) | collective-permute-done | bytes 671776 | tf_op jit(solution)/shard_map/ppermute | solution.py:30
  86.9 0.9 copy-done.11
  87.8 6.3 %norm_project.1 = (bf16[512,512]{1,0:T(8,128)(2,1)}, bf16[2,512,512]{2,1,0:T(8,128)(2,1)}) custom-call(s32[2]{0:T(128)} %pad_add_fusion.order_ref, bf16[4,656,128]{2,1,0:T(8,128)(2,1)} %copy-done.2, bf16[4,656,128]{2,1,0:T(8,128)(2,1)} %copy-done.11, bf16[3,1280,512]{2,1,0:T(8,128)(2,1)} %bitcast.31), custom_call_target="tpu_custom_call" | custom-call | flops 130000000 | bytes 1000 | tf_op jit(solution)/shard_map/norm_project/pallas_call | solution.py:291
  94.1 1.0 copy-done.5
  95.2 1.2 copy-done.6
  96.4 15.0 %attend.3 = (f32[4,2,512,128]{3,2,1,0:T(8,128)S(1)}, f32[4,2,512,128]{3,2,1,0:T(8,128)S(1)}) custom-call(bf16[512,512]{1,0:T(8,128)(2,1)S(1)} %copy-done.5, bf16[2,512,512]{2,1,0:T(8,128)(2,1)S(1)} %copy-done.6, bf16[2,512,512]{2,1,0:T(8,128)(2,1)S(1)} %copy-done.6, bf16[2,512,512]{2,1,0:T(8,128)(2,1)S(1)} %collective-permute-done.7.refs_3_.refs_4_, ...), custom_call_target="tpu_custom_call" | custom-call | flops 340000000 | bytes 1000 | tf_op jit(solution)/shard_map/attend/pallas_call | solution.py:464
  111.5 0.7 collective-permute-start.13
  112.2 1.3 collective-permute-start.14
  113.6 6.9 %attend.4 = (f32[4,2,512,128]{3,2,1,0:T(8,128)S(1)}, f32[4,2,512,128]{3,2,1,0:T(8,128)S(1)}) custom-call(bf16[512,512]{1,0:T(8,128)(2,1)S(1)} %copy-done.5, bf16[2,512,512]{2,1,0:T(8,128)(2,1)S(1)} %collective-permute-done.11.refs_1_.refs_2_, bf16[2,512,512]{2,1,0:T(8,128)(2,1)S(1)} %collective-permute-done.11.refs_1_.refs_2_, ...), custom_call_target="tpu_custom_call" | custom-call | flops 148000000 | bytes 1000 | tf_op jit(solution)/shard_map/attend/pallas_call | solution.py:464
  120.5 5.1 %collective-permute-done.13.refs_1_ = bf16[1,512,512]{2,1,0:T(8,128)(2,1)S(1)} collective-permute-done((bf16[1,512,512]{2,1,0:T(8,128)(2,1)S(1)}, bf16[1,512,512]{2,1,0:T(8,128)(2,1)S(1)}, u32[]{:S(2)}, u32[]{:S(2)}) %collective-permute-start.13) | collective-permute-done | bytes 524320 | tf_op jit(solution)/shard_map/ppermute | solution.py:532
  125.5 0.4 collective-permute-done.14.refs_2_
  125.9 6.3 %attend.5 = (bf16[2,4,320,128]{3,2,1,0:T(8,128)(2,1)}, f32[2,4,320,128]{3,2,1,0:T(8,128)S(1)}) custom-call(bf16[512,512]{1,0:T(8,128)(2,1)S(1)} %copy-done.5, bf16[1,512,512]{2,1,0:T(8,128)(2,1)S(1)} %collective-permute-done.13.refs_1_, bf16[1,512,512]{2,1,0:T(8,128)(2,1)S(1)} %collective-permute-done.14.refs_2_, ...), custom_call_target="tpu_custom_call" | custom-call | flops 84000000 | bytes 1000 | tf_op jit(solution)/shard_map/attend/pallas_call | solution.py:464
  132.2 1.0 parity_split.1.resid_ref
  133.2 1.4 collective-permute-done.15.refs_1_
  134.7 1.1 branch_out.2
  135.7 0.7 collective-permute-start.16
  136.5 1.1 branch_out.3
  137.5 8.0 %collective-permute-done.16 = bf16[4,320,128]{2,1,0:T(8,128)(2,1)S(1)} collective-permute-done((bf16[4,320,128]{2,1,0:T(8,128)(2,1)S(1)}, bf16[4,320,128]{2,1,0:T(8,128)(2,1)S(1)}, u32[]{:S(2)}, u32[]{:S(2)}) %collective-permute-start.16) | collective-permute-done | bytes 327712 | tf_op jit(solution)/shard_map/ppermute | solution.py:30
  145.6 0.9 fusion.3
  (41 shorter events, 0.3 us)
Async XLA Ops:
  0.6 59.8 %copy-start = (bf16[320,640]{1,0:T(8,128)(2,1)S(1)}, bf16[320,640]{1,0:T(8,128)(2,1)}, u32[]{:S(2)}) copy-start(bf16[320,640]{1,0:T(8,128)(2,1)} %param.15) | copy-start | bytes 1228804
  0.6 22.0 %copy-start.1 = (bf16[1,4,640,128]{3,2,1,0:T(8,128)(2,1)S(1)}, bf16[1,4,640,128]{3,2,1,0:T(8,128)(2,1)}, u32[]{:S(2)}) copy-start(bf16[1,4,640,128]{3,2,1,0:T(8,128)(2,1)} %param.12) | copy-start | bytes 1966084
  3.2 15.2 %all-to-all-start = ((f32[8,1,128]{2,1,0:T(1,128)}), f32[8,1,128]{2,1,0:T(1,128)S(1)}, u32[]{:S(2)}, u32[]{:S(2)}) async-start(f32[8,1,128]{2,1,0:T(1,128)} %broadcast_in_dim.6), calls=%async_computation | async-start | bytes 8192 | tf_op jit(solution)/shard_map/all_to_all | solution.py:43
  11.5 6.9 %collective-permute-start = (bf16[1,640,128]{2,1,0:T(8,128)(2,1)S(1)}, bf16[1,640,128]{2,1,0:T(8,128)(2,1)S(1)}, u32[]{:S(2)}, u32[]{:S(2)}) collective-permute-start(bf16[1,640,128]{2,1,0:T(8,128)(2,1)S(1)} %get-tuple-element.57), channel_id=1, source_target_pairs={{0,2},{2,4},{4,6},{6,8},{8,10},{10,12},{12,14},{1,3},{3,5},{5,7},{... | collective-permute-start | bytes 491528 | tf_op jit(solution)/shard_map/ppermute | solution.py:512
  15.4 7.2 %collective-permute-start.1 = (bf16[1,640,128]{2,1,0:T(8,128)(2,1)S(1)}, bf16[1,640,128]{2,1,0:T(8,128)(2,1)S(1)}, u32[]{:S(2)}, u32[]{:S(2)}) collective-permute-start(bf16[1,640,128]{2,1,0:T(8,128)(2,1)S(1)} %get-tuple-element.56), channel_id=1, source_target_pairs={{2,0},{4,2},{6,4},{8,6},{10,8},{12,10},{14,12},{3,1},{5,3},{7,5},{... | collective-permute-start | bytes 491528 | tf_op jit(solution)/shard_map/ppermute | solution.py:513
  18.2 27.7 %copy-start.10 = (s32[3]{0:T(128)}, s32[3]{0:T(128)S(1)}, u32[]{:S(2)}) copy-start(s32[3]{0:T(128)S(1)} %add_convert_fusion.flags_ref) | copy-start | bytes 40
  24.8 16.3 %collective-permute-start.3 = (bf16[6,640,128]{2,1,0:T(8,128)(2,1)}, bf16[6,640,128]{2,1,0:T(8,128)(2,1)}, u32[]{:S(2)}, u32[]{:S(2)}) collective-permute-start(bf16[6,640,128]{2,1,0:T(8,128)(2,1)} %activate.1.refs_0_), channel_id=1, source_target_pairs={{1,17},{16,0},{3,19},{18,2},{5,21},{20,4},{7,23},{22,6},{9,25},{24... | collective-permute-start | bytes 2949128 | tf_op jit(solution)/shard_map/ppermute | solution.py:58
  26.1 30.8 %collective-permute-start.7 = (bf16[2,512,512]{2,1,0:T(8,128)(2,1)}, bf16[2,512,512]{2,1,0:T(8,128)(2,1)S(1)}, u32[]{:S(2)}, u32[]{:S(2)}) collective-permute-start(bf16[2,512,512]{2,1,0:T(8,128)(2,1)} %bitcast.16), channel_id=1, source_target_pairs={{0,4},{4,8},{8,12},{12,14},{14,10},{10,6},{6,2},{2,0},{1,5},{5,9},... | collective-permute-start | bytes 3145736 | tf_op jit(solution)/shard_map/ppermute | solution.py:532
  28.7 28.2 %collective-permute-start.8 = (bf16[2,512,512]{2,1,0:T(8,128)(2,1)}, bf16[2,512,512]{2,1,0:T(8,128)(2,1)}, u32[]{:S(2)}, u32[]{:S(2)}) collective-permute-start(bf16[2,512,512]{2,1,0:T(8,128)(2,1)} %bitcast.16), channel_id=1, source_target_pairs={{4,0},{8,4},{12,8},{14,12},{10,14},{6,10},{2,6},{0,2},{5,1},{9,5},... | collective-permute-start | bytes 3145736 | tf_op jit(solution)/shard_map/ppermute | solution.py:532
  28.7 17.9 %collective-permute-start.2 = (bf16[6,640,128]{2,1,0:T(8,128)(2,1)}, bf16[6,640,128]{2,1,0:T(8,128)(2,1)}, u32[]{:S(2)}, u32[]{:S(2)}) collective-permute-start(bf16[6,640,128]{2,1,0:T(8,128)(2,1)} %activate.1.refs_0_), channel_id=1, source_target_pairs={{0,1},{17,16},{2,3},{19,18},{4,5},{21,20},{6,7},{23,22},{8,9},{25,... | collective-permute-start | bytes 2949128 | tf_op jit(solution)/shard_map/ppermute | solution.py:60
  41.1 5.5 %collective-permute-start.4 = (bf16[6,640,128]{2,1,0:T(8,128)(2,1)}, bf16[6,640,128]{2,1,0:T(8,128)(2,1)}, u32[]{:S(2)}, u32[]{:S(2)}) collective-permute-start(bf16[6,640,128]{2,1,0:T(8,128)(2,1)} %collective-permute-done.3.refs_0_), channel_id=1, source_target_pairs={{0,1},{17,16},{2,3},{19,18},{4,5},{21,20},{6,7},{23,22},{8,9},{25,... | collective-permute-start | bytes 2949128 | tf_op jit(solution)/shard_map/ppermute | solution.py:61
  43.4 1.3 copy-start.7
  46.6 14.2 %copy-start.12 = (bf16[640]{0:T(1024)(128)(2,1)S(1)}, bf16[640]{0:T(1024)(128)(2,1)}, u32[]{:S(2)}) copy-start(bf16[640]{0:T(1024)(128)(2,1)} %param.19) | copy-start | bytes 3844
  46.6 14.3 %copy-start.13 = (bf16[640]{0:T(1024)(128)(2,1)S(1)}, bf16[640]{0:T(1024)(128)(2,1)}, u32[]{:S(2)}) copy-start(bf16[640]{0:T(1024)(128)(2,1)} %param.21) | copy-start | bytes 3844
  46.6 14.4 %copy-start.14 = (bf16[640]{0:T(1024)(128)(2,1)S(1)}, bf16[640]{0:T(1024)(128)(2,1)}, u32[]{:S(2)}) copy-start(bf16[640]{0:T(1024)(128)(2,1)} %param.20) | copy-start | bytes 3844
  56.9 24.8 %collective-permute-start.10 = (bf16[2,512,512]{2,1,0:T(8,128)(2,1)}, bf16[2,512,512]{2,1,0:T(8,128)(2,1)S(1)}, u32[]{:S(2)}, u32[]{:S(2)}) collective-permute-start(bf16[2,512,512]{2,1,0:T(8,128)(2,1)} %collective-permute-done.8.refs_5_.refs_6_), channel_id=1, source_target_pairs={{4,0},{8,4},{12,8},{14,12},{10,14},{6,10},{2,6},{0,2},{5,1},{9,5},... | collective-permute-start | bytes 3145736 | tf_op jit(solution)/shard_map/ppermute | solution.py:532
  59.3 23.5 %collective-permute-start.9 = (bf16[2,512,512]{2,1,0:T(8,128)(2,1)S(1)}, bf16[2,512,512]{2,1,0:T(8,128)(2,1)S(1)}, u32[]{:S(2)}, u32[]{:S(2)}) collective-permute-start(bf16[2,512,512]{2,1,0:T(8,128)(2,1)S(1)} %collective-permute-done.7.refs_3_.refs_4_), channel_id=1, source_target_pairs={{0,4},{4,8},{8,12},{12,14},{14,10},{10,6},{6,2},{2,0},{1,5},{5,9},... | collective-permute-start | bytes 3145736 | tf_op jit(solution)/shard_map/ppermute | solution.py:532
  60.2 15.6 %collective-permute-start.5 = (bf16[4,640,128]{2,1,0:T(8,128)(2,1)}, bf16[4,640,128]{2,1,0:T(8,128)(2,1)S(1)}, u32[]{:S(2)}, u32[]{:S(2)}) collective-permute-start(bf16[4,640,128]{2,1,0:T(8,128)(2,1)} %norm_conv.3), channel_id=1, source_target_pairs={{0,16},{16,0},{1,17},{17,1},{2,18},{18,2},{3,19},{19,3},{4,20},{20... | collective-permute-start | bytes 1966088 | tf_op jit(solution)/shard_map/ppermute | solution.py:30
  75.8 0.8 copy-start.8
  76.6 1.3 copy-start.4
  77.9 1.1 copy-start.9
  79.4 7.5 %copy-start.2 = (bf16[4,656,128]{2,1,0:T(8,128)(2,1)}, bf16[4,656,128]{2,1,0:T(8,128)(2,1)S(1)}, u32[]{:S(2)}) copy-start(bf16[4,656,128]{2,1,0:T(8,128)(2,1)S(1)} %residual.1.own_ref.refs_0_) | copy-start | bytes 2015236
  82.8 28.6 %collective-permute-start.11 = (bf16[2,512,512]{2,1,0:T(8,128)(2,1)S(1)}, bf16[2,512,512]{2,1,0:T(8,128)(2,1)S(1)}, u32[]{:S(2)}, u32[]{:S(2)}) collective-permute-start(bf16[2,512,512]{2,1,0:T(8,128)(2,1)S(1)} %collective-permute-done.9.refs_7_.refs_8_), channel_id=1, source_target_pairs={{0,4},{4,8},{8,12},{12,14},{14,10},{10,6},{6,2},{2,0},{1,5},{5,9},... | collective-permute-start | bytes 3145736 | tf_op jit(solution)/shard_map/ppermute | solution.py:532
  83.5 28.0 %collective-permute-start.12 = (bf16[2,512,512]{2,1,0:T(8,128)(2,1)S(1)}, bf16[2,512,512]{2,1,0:T(8,128)(2,1)S(1)}, u32[]{:S(2)}, u32[]{:S(2)}) collective-permute-start(bf16[2,512,512]{2,1,0:T(8,128)(2,1)S(1)} %collective-permute-done.10.refs_9_.refs_10_), channel_id=1, source_target_pairs={{4,0},{8,4},{12,8},{14,12},{10,14},{6,10},{2,6},{0,2},{5,1},{9,5},... | collective-permute-start | bytes 3145736 | tf_op jit(solution)/shard_map/ppermute | solution.py:532
  84.8 2.1 %collective-permute-start.6 = (bf16[4,656,128]{2,1,0:T(8,128)(2,1)S(1)}, bf16[4,656,128]{2,1,0:T(8,128)(2,1)S(1)}, u32[]{:S(2)}, u32[]{:S(2)}) collective-permute-start(bf16[4,656,128]{2,1,0:T(8,128)(2,1)S(1)} %residual.1.own_ref.refs_0_), channel_id=1, source_target_pairs={{0,1},{1,0},{2,3},{3,2},{4,5},{5,4},{6,7},{7,6},{8,9},{9,8},{10,11... | collective-permute-start | bytes 2015240 | tf_op jit(solution)/shard_map/ppermute | solution.py:30
  86.9 0.9 copy-start.11
  94.1 1.0 copy-start.5
  95.1 1.2 copy-start.6
  111.5 14.0 %collective-permute-start.13 = (bf16[1,512,512]{2,1,0:T(8,128)(2,1)S(1)}, bf16[1,512,512]{2,1,0:T(8,128)(2,1)S(1)}, u32[]{:S(2)}, u32[]{:S(2)}) collective-permute-start(bf16[1,512,512]{2,1,0:T(8,128)(2,1)S(1)} %slice.24), channel_id=1, source_target_pairs={{0,4},{4,8},{8,12},{12,14},{14,10},{10,6},{6,2},{2,0},{1,5},{5,9},... | collective-permute-start | bytes 1572872 | tf_op jit(solution)/shard_map/ppermute | solution.py:532
  112.2 13.7 %collective-permute-start.14 = (bf16[1,512,512]{2,1,0:T(8,128)(2,1)S(1)}, bf16[1,512,512]{2,1,0:T(8,128)(2,1)S(1)}, u32[]{:S(2)}, u32[]{:S(2)}) collective-permute-start(bf16[1,512,512]{2,1,0:T(8,128)(2,1)S(1)} %slice.25), channel_id=1, source_target_pairs={{4,0},{8,4},{12,8},{14,12},{10,14},{6,10},{2,6},{0,2},{5,1},{9,5},... | collective-permute-start | bytes 1572872 | tf_op jit(solution)/shard_map/ppermute | solution.py:532
  125.9 6.3 %copy-start.3 = (bf16[4,656,128]{2,1,0:T(8,128)(2,1)S(1)}, bf16[4,656,128]{2,1,0:T(8,128)(2,1)}, u32[]{:S(2)}) copy-start(bf16[4,656,128]{2,1,0:T(8,128)(2,1)} %copy-done.2) | copy-start | bytes 2015236
  132.2 2.4 %collective-permute-start.15 = (bf16[2,4,320,128]{3,2,1,0:T(8,128)(2,1)}, bf16[2,4,320,128]{3,2,1,0:T(8,128)(2,1)}, u32[]{:S(2)}, u32[]{:S(2)}) collective-permute-start(bf16[2,4,320,128]{3,2,1,0:T(8,128)(2,1)} %get-tuple-element.41), channel_id=1, source_target_pairs={{0,1},{1,0},{2,3},{3,2},{4,5},{5,4},{6,7},{7,6},{8,9},{9,8},{10,11... | collective-permute-start | bytes 1966088 | tf_op jit(solution)/shard_map/ppermute | solution.py:30
  135.7 9.8 %collective-permute-start.16 = (bf16[4,320,128]{2,1,0:T(8,128)(2,1)S(1)}, bf16[4,320,128]{2,1,0:T(8,128)(2,1)S(1)}, u32[]{:S(2)}, u32[]{:S(2)}) collective-permute-start(bf16[4,320,128]{2,1,0:T(8,128)(2,1)S(1)} %branch_out.2), channel_id=1, source_target_pairs={{0,16},{16,0},{1,17},{17,1},{2,18},{18,2},{3,19},{19,3},{4,20},{20... | collective-permute-start | bytes 983048 | tf_op jit(solution)/shard_map/ppermute | solution.py:30

commit v10 on v9

--- a/solution.py
+++ b/solution.py
@@ -546,12 +546,12 @@
     w_back = arrange_call(flip, w_out, tp_count)
     order = jnp.stack([tp, 1 - tp]).astype(jnp.int32) if tp_count == 2 else jnp.zeros((1,), jnp.int32)
     flags_other, order, w_back, *_ = lax.optimization_barrier(
-        (flags, order, w_back) + tuple(x_mine[1:])
+        (flags, order, w_back) + tuple(x_mine[1:]) + hops[1]
     )
+    next_hop()
 
     conv_sent = conv_call(flags_other, x_other, conv_w, jnp.bfloat16)
     conv_received = swapped(conv_sent, "cfg")
-    next_hop(conv_sent)
     conv_own = conv_call(flags, x_mine, conv_w, jnp.float32)
 
     half_width = TEMB // 2
@@ -589,9 +589,9 @@
     )
     fresh_kv = fresh.reshape(1, 2, span_rows, grid_width, local_features)
 
-    group = [((fresh, 0), (fresh, 1))] + blocks_of(1) + blocks_of(2)
+    group = [((fresh, 0), (fresh, 1))] + blocks_of(1)
     state = None
-    for hop in range(3, last + 1):
+    for hop in range(2, last + 1):
         state = attention_call(queries, group, state)
         while len(hops) <= last:
             next_hop(state[0])

time: 147 us -> 152 us (1.034)
  waiting for transfers between devices: 36.6 us -> 40 us
  Pallas kernels: 62.2 us -> 64.7 us
  local copies, waits for them, and re-layouts: 11.3 us -> 9.41 us
    ppermute x4, waiting for transfers between devices: 2.68 us -> 10.1 us  [next_hop(): lax.ppermute(behind, 'rows', backward)]
    ppermute x4, waiting for transfers between devices: 6.13 us -> 1.03 us  [next_hop(): lax.ppermute(ahead, 'rows', forward)]
    pallas_call x3 -> x4, Pallas kernels: 28.2 us -> 30.7 us  [attention_call(): pl.pallas_call(functools.partial(attention_kernel, len(pairs), state is n...]
    unnamed x30 -> x28, local copies, waits for them, and re-layouts: 7.71 us -> 5.78 us
  transfers between devices with their start and end apart: 18 -> 18, of which waited for: 10 -> 9; matrix products, arithmetic and copies ran while one was open for 3% -> 3% of each run, Pallas kernels for 36% -> 37%
where the time goes in v10:
time: 152 us; the launch traced here: 151 us
  Pallas kernels  64.7 us (43%)
  waiting for transfers between devices  40 us (26%)
  starting transfers between devices  31.3 us (21%)
  local copies, waits for them, and re-layouts  9.41 us (6%)
  other arithmetic  3.56 us (2%)
  between operations  1.66 us (1%)
    pallas_call x4, Pallas kernels, attention_call(): pl.pallas_call(functools.partial(attention_kernel, len(pairs), state is n...  30.7 us
    pallas_call x2, Pallas kernels, conv_call(): pl.pallas_call(functools.partial(conv_kernel, len(xs)), in_specs=[pl.Bloc...  20.8 us
    ppermute x4, waiting for transfers between devices, swapped(): lax.ppermute(array, axis, [(i, i ^ 1) for i in range(lax.axis_size(axis))])  17 us
    ppermute x4, waiting for transfers between devices, next_hop(): lax.ppermute(behind, 'rows', backward)  10.1 us
    ppermute x1, waiting for transfers between devices, halves_of_inputs(): across = lax.ppermute(own, ('cfg', 'tp'), [(1, 3), (2, 0)])  7.7 us
    all_to_all x1, starting transfers between devices, summed(): return jnp.sum(lax.all_to_all(spread, axes, 0, 0, tiled=True), axis=0)  7.25 us
    pallas_call x1, Pallas kernels, project_call(): pl.pallas_call(functools.partial(project_kernel, len(parts)), in_specs=[p...  6.31 us
    unnamed x28, local copies, waits for them, and re-layouts  5.78 us
  transfers between devices with their start and end apart: 18, of which 9 were waited for; matrix products, arithmetic and copies ran while one was open for 3% of the time, Pallas kernels for 37%

profile of v10, /device:TPU:0, one launch (start us, length us, event | category | flops | bytes accessed | tf_op | source)
XLA Modules:
  0.0 150.9 jit_solution(8650357841260431373)
XLA Ops:
  0.6 0.0 copy-start
  0.6 0.0 copy-start.2
  0.7 1.5 convert_reduce_fusion
  2.2 0.1 reduce_sum.32
  2.2 0.1 reduce_sum.45
  2.3 0.1 reduce_sum.36
  2.5 0.1 reduce_sum.46
  2.6 0.1 reshape.46
  2.7 0.6 broadcast_in_dim.6
  3.3 7.3 %all-to-all-start = ((f32[8,1,128]{2,1,0:T(1,128)}), f32[8,1,128]{2,1,0:T(1,128)S(1)}, u32[]{:S(2)}, u32[]{:S(2)}) async-start(f32[8,1,128]{2,1,0:T(1,128)} %broadcast_in_dim.6), calls=%async_computation | async-start | bytes 8192 | tf_op jit(solution)/shard_map/all_to_all | solution.py:43
  10.5 1.0 slice_bitcast_fusion
  11.5 3.9 %collective-permute-start = (bf16[1,640,128]{2,1,0:T(8,128)(2,1)S(1)}, bf16[1,640,128]{2,1,0:T(8,128)(2,1)S(1)}, u32[]{:S(2)}, u32[]{:S(2)}) collective-permute-start(bf16[1,640,128]{2,1,0:T(8,128)(2,1)S(1)} %get-tuple-element.57), channel_id=1, source_target_pairs={{0,2},{2,4},{4,6},{6,8},{8,10},{10,12},{12,14},{1,3},{3,5},{5,7},{... | collective-permute-start | bytes 491528 | tf_op jit(solution)/shard_map/ppermute | solution.py:512
  15.5 1.3 collective-permute-start.1
  16.8 0.7 stack.46
  17.5 0.7 stack.47
  18.2 0.1 add_convert_fusion.flags_ref
  18.3 0.2 copy.30.affine_ref
  18.4 0.0 all-to-all-done
  18.5 0.0 collective-permute-done.before_ref
  18.5 4.2 %collective-permute-done.1.after_ref = bf16[1,640,128]{2,1,0:T(8,128)(2,1)S(1)} collective-permute-done((bf16[1,640,128]{2,1,0:T(8,128)(2,1)S(1)}, bf16[1,640,128]{2,1,0:T(8,128)(2,1)S(1)}, u32[]{:S(2)}, u32[]{:S(2)}) %collective-permute-start.1) | collective-permute-done | bytes 163872 | tf_op jit(solution)/shard_map/ppermute | solution.py:513
  22.7 2.2 %activate.1.refs_0_ = bf16[6,640,128]{2,1,0:T(8,128)(2,1)} custom-call(s32[3]{0:T(128)S(1)} %add_convert_fusion.flags_ref, f32[128]{0:T(128)S(1)} %reduce_sum.47.sums_ref, bf16[1,640,128]{2,1,0:T(8,128)(2,1)S(1)} %collective-permute-done.before_ref, bf16[4,640,128]{2,1,0:T(8,128)(2,1)S(1)} %bitcast.28, ...), custom_call_target="tpu_custom_call" | custom-call | flops 20000000 | bytes 1000 | tf_op jit(solution)/shard_map/activate/pallas_call | solution.py:178
  24.9 1.3 collective-permute-start.5
  26.2 2.4 %collective-permute-start.4 = (bf16[2,512,512]{2,1,0:T(8,128)(2,1)S(1)}, bf16[2,512,512]{2,1,0:T(8,128)(2,1)}, u32[]{:S(2)}, u32[]{:S(2)}) collective-permute-start(bf16[2,512,512]{2,1,0:T(8,128)(2,1)S(1)} %bitcast.37), channel_id=1, source_target_pairs={{4,0},{8,4},{12,8},{14,12},{10,14},{6,10},{2,6},{0,2},{5,1},{9,5},... | collective-permute-start | bytes 3145736 | tf_op jit(solution)/shard_map/ppermute | solution.py:532
  28.6 0.3 collective-permute-start.3
  28.9 4.6 %collective-permute-start.2 = (bf16[6,640,128]{2,1,0:T(8,128)(2,1)}, bf16[6,640,128]{2,1,0:T(8,128)(2,1)}, u32[]{:S(2)}, u32[]{:S(2)}) collective-permute-start(bf16[6,640,128]{2,1,0:T(8,128)(2,1)} %activate.1.refs_0_), channel_id=1, source_target_pairs={{0,1},{17,16},{2,3},{19,18},{4,5},{21,20},{6,7},{23,22},{8,9},{25,... | collective-permute-start | bytes 2949128 | tf_op jit(solution)/shard_map/ppermute | solution.py:60
  33.5 7.7 %collective-permute-done.5.refs_0_ = bf16[6,640,128]{2,1,0:T(8,128)(2,1)} collective-permute-done((bf16[6,640,128]{2,1,0:T(8,128)(2,1)}, bf16[6,640,128]{2,1,0:T(8,128)(2,1)}, u32[]{:S(2)}, u32[]{:S(2)}) %collective-permute-start.5) | collective-permute-done | bytes 983072 | tf_op jit(solution)/shard_map/ppermute | solution.py:58
  41.2 2.3 %collective-permute-start.6 = (bf16[6,640,128]{2,1,0:T(8,128)(2,1)}, bf16[6,640,128]{2,1,0:T(8,128)(2,1)}, u32[]{:S(2)}, u32[]{:S(2)}) collective-permute-start(bf16[6,640,128]{2,1,0:T(8,128)(2,1)} %collective-permute-done.5.refs_0_), channel_id=1, source_target_pairs={{0,1},{17,16},{2,3},{19,18},{4,5},{21,20},{6,7},{23,22},{8,9},{25,... | collective-permute-start | bytes 2949128 | tf_op jit(solution)/shard_map/ppermute | solution.py:61
  43.5 8.3 %collective-permute-done.4.refs_5_.refs_6_ = bf16[2,512,512]{2,1,0:T(8,128)(2,1)} collective-permute-done((bf16[2,512,512]{2,1,0:T(8,128)(2,1)S(1)}, bf16[2,512,512]{2,1,0:T(8,128)(2,1)}, u32[]{:S(2)}, u32[]{:S(2)}) %collective-permute-start.4) | collective-permute-done | bytes 1048608 | tf_op jit(solution)/shard_map/ppermute | solution.py:532
  51.8 2.6 %collective-permute-start.10 = (bf16[2,512,512]{2,1,0:T(8,128)(2,1)}, bf16[2,512,512]{2,1,0:T(8,128)(2,1)S(1)}, u32[]{:S(2)}, u32[]{:S(2)}) collective-permute-start(bf16[2,512,512]{2,1,0:T(8,128)(2,1)} %collective-permute-done.4.refs_5_.refs_6_), channel_id=1, source_target_pairs={{4,0},{8,4},{12,8},{14,12},{10,14},{6,10},{2,6},{0,2},{5,1},{9,5},... | collective-permute-start | bytes 3145736 | tf_op jit(solution)/shard_map/ppermute | solution.py:532
  55.0 0.0 copy-start.7
  55.0 1.3 copy-done.7
  56.3 1.2 arrange.1.refs_5_
  57.6 0.7 pad_add_fusion.order_ref
  58.3 10.3 %norm_conv.3 = bf16[4,640,128]{2,1,0:T(8,128)(2,1)} custom-call(s32[3]{0:T(128)} %copy-done.8, bf16[6,640,128]{2,1,0:T(8,128)(2,1)} %collective-permute-done.5.refs_0_, bf16[6,640,128]{2,1,0:T(8,128)(2,1)} %collective-permute-done.6.refs_1_, bf16[3,3,640,640]{3,2,1,0:T(8,128)(2,1)} %refs_2_.3), custom_call_target="tpu_custom_call" | custom-call | flops 180000000 | bytes 1000 | tf_op jit(solution)/shard_map/norm_conv/pallas_call | solution.py:108
  68.5 1.1 collective-permute-start.7
  69.7 0.1 divide_multiply_fusion
  69.8 0.3 convolution_reduce_fusion
  70.2 0.1 broadcast_in_dim.16.bias_ref
  70.3 10.5 %norm_conv.2.own_ref = f32[4,640,128]{2,1,0:T(8,128)} custom-call(s32[3]{0:T(128)} %copy-done.8, bf16[6,640,128]{2,1,0:T(8,128)(2,1)} %activate.1.refs_0_, bf16[6,640,128]{2,1,0:T(8,128)(2,1)} %collective-permute-done.2.refs_1_, bf16[3,3,640,640]{3,2,1,0:T(8,128)(2,1)} %refs_2_.3), custom_call_target="tpu_custom_call" | custom-call | flops 180000000 | bytes 1000 | tf_op jit(solution)/shard_map/norm_conv/pallas_call | solution.py:108
  80.9 4.8 %collective-permute-done.7.received_ref = bf16[4,640,128]{2,1,0:T(8,128)(2,1)S(1)} collective-permute-done((bf16[4,640,128]{2,1,0:T(8,128)(2,1)}, bf16[4,640,128]{2,1,0:T(8,128)(2,1)S(1)}, u32[]{:S(2)}, u32[]{:S(2)}) %collective-permute-start.7) | collective-permute-done | bytes 655392 | tf_op jit(solution)/shard_map/ppermute | solution.py:30
  85.6 1.3 copy-done.5
  86.9 0.4 residual.1.own_ref.refs_0_
  87.4 2.0 %collective-permute-start.11 = (bf16[2,512,512]{2,1,0:T(8,128)(2,1)}, bf16[2,512,512]{2,1,0:T(8,128)(2,1)S(1)}, u32[]{:S(2)}, u32[]{:S(2)}) collective-permute-start(bf16[2,512,512]{2,1,0:T(8,128)(2,1)} %collective-permute-done.9.refs_1_.refs_2_), channel_id=1, source_target_pairs={{0,4},{4,8},{8,12},{12,14},{14,10},{10,6},{6,2},{2,0},{1,5},{5,9},... | collective-permute-start | bytes 3145736 | tf_op jit(solution)/shard_map/ppermute | solution.py:532
  89.4 0.0 collective-permute-start.12
  89.5 2.1 %collective-permute-done.8.refs_1_ = bf16[4,656,128]{2,1,0:T(8,128)(2,1)S(1)} collective-permute-done((bf16[4,656,128]{2,1,0:T(8,128)(2,1)S(1)}, bf16[4,656,128]{2,1,0:T(8,128)(2,1)S(1)}, u32[]{:S(2)}, u32[]{:S(2)}) %collective-permute-start.8) | collective-permute-done | bytes 671776 | tf_op jit(solution)/shard_map/ppermute | solution.py:30
  91.6 0.9 copy-done.9
  92.4 6.3 %norm_project.1 = (bf16[512,512]{1,0:T(8,128)(2,1)}, bf16[2,512,512]{2,1,0:T(8,128)(2,1)}) custom-call(s32[2]{0:T(128)} %pad_add_fusion.order_ref, bf16[4,656,128]{2,1,0:T(8,128)(2,1)} %copy-done.3, bf16[4,656,128]{2,1,0:T(8,128)(2,1)} %copy-done.9, bf16[3,1280,512]{2,1,0:T(8,128)(2,1)} %bitcast.31), custom_call_target="tpu_custom_call" | custom-call | flops 130000000 | bytes 1000 | tf_op jit(solution)/shard_map/norm_project/pallas_call | solution.py:291
  98.8 1.0 copy-done.1
  99.8 1.2 copy-done.6
  101.0 10.0 %attend.4 = (f32[4,2,512,128]{3,2,1,0:T(8,128)S(1)}, f32[4,2,512,128]{3,2,1,0:T(8,128)S(1)}) custom-call(bf16[512,512]{1,0:T(8,128)(2,1)S(1)} %copy-done.1, bf16[2,512,512]{2,1,0:T(8,128)(2,1)S(1)} %copy-done.6, bf16[2,512,512]{2,1,0:T(8,128)(2,1)S(1)} %copy-done.6, bf16[2,512,512]{2,1,0:T(8,128)(2,1)} %collective-permute-done.3.refs_3_.refs_4_, ...), custom_call_target="tpu_custom_call" | custom-call | flops 212000000 | bytes 1000 | tf_op jit(solution)/shard_map/attend/pallas_call | solution.py:464
  111.0 1.0 collective-permute-done.11.refs_1_.refs_2_
  112.1 1.8 %collective-permute-done.12.refs_3_.refs_4_ = bf16[2,512,512]{2,1,0:T(8,128)(2,1)S(1)} collective-permute-done((bf16[2,512,512]{2,1,0:T(8,128)(2,1)S(1)}, bf16[2,512,512]{2,1,0:T(8,128)(2,1)S(1)}, u32[]{:S(2)}, u32[]{:S(2)}) %collective-permute-start.12) | collective-permute-done | bytes 1048608 | tf_op jit(solution)/shard_map/ppermute | solution.py:532
  113.9 1.5 %collective-permute-start.13 = (bf16[1,512,512]{2,1,0:T(8,128)(2,1)S(1)}, bf16[1,512,512]{2,1,0:T(8,128)(2,1)S(1)}, u32[]{:S(2)}, u32[]{:S(2)}) collective-permute-start(bf16[1,512,512]{2,1,0:T(8,128)(2,1)S(1)} %slice.24), channel_id=1, source_target_pairs={{0,4},{4,8},{8,12},{12,14},{14,10},{10,6},{6,2},{2,0},{1,5},{5,9},... | collective-permute-start | bytes 1572872 | tf_op jit(solution)/shard_map/ppermute | solution.py:532
  115.4 0.6 collective-permute-start.14
  116.0 7.5 %attend.5 = (f32[4,2,512,128]{3,2,1,0:T(8,128)S(1)}, f32[4,2,512,128]{3,2,1,0:T(8,128)S(1)}) custom-call(bf16[512,512]{1,0:T(8,128)(2,1)S(1)} %copy-done.1, bf16[2,512,512]{2,1,0:T(8,128)(2,1)} %collective-permute-done.9.refs_1_.refs_2_, bf16[2,512,512]{2,1,0:T(8,128)(2,1)} %collective-permute-done.9.refs_1_.refs_2_, ...), custom_call_target="tpu_custom_call" | custom-call | flops 148000000 | bytes 1000 | tf_op jit(solution)/shard_map/attend/pallas_call | solution.py:464
  123.5 6.9 %attend.6 = (f32[4,2,512,128]{3,2,1,0:T(8,128)S(1)}, f32[4,2,512,128]{3,2,1,0:T(8,128)S(1)}) custom-call(bf16[512,512]{1,0:T(8,128)(2,1)S(1)} %copy-done.1, bf16[2,512,512]{2,1,0:T(8,128)(2,1)S(1)} %collective-permute-done.11.refs_1_.refs_2_, bf16[2,512,512]{2,1,0:T(8,128)(2,1)S(1)} %collective-permute-done.11.refs_1_.refs_2_, ...), custom_call_target="tpu_custom_call" | custom-call | flops 148000000 | bytes 1000 | tf_op jit(solution)/shard_map/attend/pallas_call | solution.py:464
  130.4 6.3 %attend.7 = (bf16[2,4,320,128]{3,2,1,0:T(8,128)(2,1)}, f32[2,4,320,128]{3,2,1,0:T(8,128)S(1)}) custom-call(bf16[512,512]{1,0:T(8,128)(2,1)S(1)} %copy-done.1, bf16[1,512,512]{2,1,0:T(8,128)(2,1)S(1)} %collective-permute-done.13.refs_1_, bf16[1,512,512]{2,1,0:T(8,128)(2,1)S(1)} %collective-permute-done.14.refs_2_, ...), custom_call_target="tpu_custom_call" | custom-call | flops 84000000 | bytes 1000 | tf_op jit(solution)/shard_map/attend/pallas_call | solution.py:464
  136.7 1.0 parity_split.1.resid_ref
  137.7 1.4 collective-permute-done.15.refs_1_
  139.1 1.1 branch_out.2
  140.2 0.1 collective-permute-start.16
  140.3 1.1 branch_out.3
  141.4 8.7 %collective-permute-done.16 = bf16[4,320,128]{2,1,0:T(8,128)(2,1)S(1)} collective-permute-done((bf16[4,320,128]{2,1,0:T(8,128)(2,1)S(1)}, bf16[4,320,128]{2,1,0:T(8,128)(2,1)S(1)}, u32[]{:S(2)}, u32[]{:S(2)}) %collective-permute-start.16) | collective-permute-done | bytes 327712 | tf_op jit(solution)/shard_map/ppermute | solution.py:30
  150.0 0.9 fusion.3
  (40 shorter events, 0.3 us)
Async XLA Ops:
  0.6 69.2 %copy-start = (bf16[320,640]{1,0:T(8,128)(2,1)S(1)}, bf16[320,640]{1,0:T(8,128)(2,1)}, u32[]{:S(2)}) copy-start(bf16[320,640]{1,0:T(8,128)(2,1)} %param.15) | copy-start | bytes 1228804
  0.6 22.1 %copy-start.2 = (bf16[1,4,640,128]{3,2,1,0:T(8,128)(2,1)S(1)}, bf16[1,4,640,128]{3,2,1,0:T(8,128)(2,1)}, u32[]{:S(2)}) copy-start(bf16[1,4,640,128]{3,2,1,0:T(8,128)(2,1)} %param.12) | copy-start | bytes 1966084
  0.7 25.5 %copy-start.13 = (bf16[1,2,4,128,512]{4,3,2,1,0:T(8,128)(2,1)S(1)}, bf16[1,2,4,128,512]{4,3,2,1,0:T(8,128)(2,1)}, u32[]{:S(2)}) copy-start(bf16[1,2,4,128,512]{4,3,2,1,0:T(8,128)(2,1)} %param.13) | copy-start | bytes 3145732
  3.3 15.2 %all-to-all-start = ((f32[8,1,128]{2,1,0:T(1,128)}), f32[8,1,128]{2,1,0:T(1,128)S(1)}, u32[]{:S(2)}, u32[]{:S(2)}) async-start(f32[8,1,128]{2,1,0:T(1,128)} %broadcast_in_dim.6), calls=%async_computation | async-start | bytes 8192 | tf_op jit(solution)/shard_map/all_to_all | solution.py:43
  11.5 6.9 %collective-permute-start = (bf16[1,640,128]{2,1,0:T(8,128)(2,1)S(1)}, bf16[1,640,128]{2,1,0:T(8,128)(2,1)S(1)}, u32[]{:S(2)}, u32[]{:S(2)}) collective-permute-start(bf16[1,640,128]{2,1,0:T(8,128)(2,1)S(1)} %get-tuple-element.57), channel_id=1, source_target_pairs={{0,2},{2,4},{4,6},{6,8},{8,10},{10,12},{12,14},{1,3},{3,5},{5,7},{... | collective-permute-start | bytes 491528 | tf_op jit(solution)/shard_map/ppermute | solution.py:512
  15.5 7.2 %collective-permute-start.1 = (bf16[1,640,128]{2,1,0:T(8,128)(2,1)S(1)}, bf16[1,640,128]{2,1,0:T(8,128)(2,1)S(1)}, u32[]{:S(2)}, u32[]{:S(2)}) collective-permute-start(bf16[1,640,128]{2,1,0:T(8,128)(2,1)S(1)} %get-tuple-element.56), channel_id=1, source_target_pairs={{2,0},{4,2},{6,4},{8,6},{10,8},{12,10},{14,12},{3,1},{5,3},{7,5},{... | collective-permute-start | bytes 491528 | tf_op jit(solution)/shard_map/ppermute | solution.py:513
  18.3 39.3 %copy-start.8 = (s32[3]{0:T(128)}, s32[3]{0:T(128)S(1)}, u32[]{:S(2)}) copy-start(s32[3]{0:T(128)S(1)} %add_convert_fusion.flags_ref) | copy-start | bytes 40
  24.9 16.3 %collective-permute-start.5 = (bf16[6,640,128]{2,1,0:T(8,128)(2,1)}, bf16[6,640,128]{2,1,0:T(8,128)(2,1)}, u32[]{:S(2)}, u32[]{:S(2)}) collective-permute-start(bf16[6,640,128]{2,1,0:T(8,128)(2,1)} %activate.1.refs_0_), channel_id=1, source_target_pairs={{1,17},{16,0},{3,19},{18,2},{5,21},{20,4},{7,23},{22,6},{9,25},{24... | collective-permute-start | bytes 2949128 | tf_op jit(solution)/shard_map/ppermute | solution.py:58
  26.2 25.6 %collective-permute-start.4 = (bf16[2,512,512]{2,1,0:T(8,128)(2,1)S(1)}, bf16[2,512,512]{2,1,0:T(8,128)(2,1)}, u32[]{:S(2)}, u32[]{:S(2)}) collective-permute-start(bf16[2,512,512]{2,1,0:T(8,128)(2,1)S(1)} %bitcast.37), channel_id=1, source_target_pairs={{4,0},{8,4},{12,8},{14,12},{10,14},{6,10},{2,6},{0,2},{5,1},{9,5},... | collective-permute-start | bytes 3145736 | tf_op jit(solution)/shard_map/ppermute | solution.py:532
  28.6 25.8 %collective-permute-start.3 = (bf16[2,512,512]{2,1,0:T(8,128)(2,1)S(1)}, bf16[2,512,512]{2,1,0:T(8,128)(2,1)}, u32[]{:S(2)}, u32[]{:S(2)}) collective-permute-start(bf16[2,512,512]{2,1,0:T(8,128)(2,1)S(1)} %bitcast.38), channel_id=1, source_target_pairs={{0,4},{4,8},{8,12},{12,14},{14,10},{10,6},{6,2},{2,0},{1,5},{5,9},... | collective-permute-start | bytes 3145736 | tf_op jit(solution)/shard_map/ppermute | solution.py:532
  28.9 29.4 %collective-permute-start.2 = (bf16[6,640,128]{2,1,0:T(8,128)(2,1)}, bf16[6,640,128]{2,1,0:T(8,128)(2,1)}, u32[]{:S(2)}, u32[]{:S(2)}) collective-permute-start(bf16[6,640,128]{2,1,0:T(8,128)(2,1)} %activate.1.refs_0_), channel_id=1, source_target_pairs={{0,1},{17,16},{2,3},{19,18},{4,5},{21,20},{6,7},{23,22},{8,9},{25,... | collective-permute-start | bytes 2949128 | tf_op jit(solution)/shard_map/ppermute | solution.py:60
  41.2 17.1 %collective-permute-start.6 = (bf16[6,640,128]{2,1,0:T(8,128)(2,1)}, bf16[6,640,128]{2,1,0:T(8,128)(2,1)}, u32[]{:S(2)}, u32[]{:S(2)}) collective-permute-start(bf16[6,640,128]{2,1,0:T(8,128)(2,1)} %collective-permute-done.5.refs_0_), channel_id=1, source_target_pairs={{0,1},{17,16},{2,3},{19,18},{4,5},{21,20},{6,7},{23,22},{8,9},{25,... | collective-permute-start | bytes 2949128 | tf_op jit(solution)/shard_map/ppermute | solution.py:61
  51.8 35.6 %collective-permute-start.10 = (bf16[2,512,512]{2,1,0:T(8,128)(2,1)}, bf16[2,512,512]{2,1,0:T(8,128)(2,1)S(1)}, u32[]{:S(2)}, u32[]{:S(2)}) collective-permute-start(bf16[2,512,512]{2,1,0:T(8,128)(2,1)} %collective-permute-done.4.refs_5_.refs_6_), channel_id=1, source_target_pairs={{4,0},{8,4},{12,8},{14,12},{10,14},{6,10},{2,6},{0,2},{5,1},{9,5},... | collective-permute-start | bytes 3145736 | tf_op jit(solution)/shard_map/ppermute | solution.py:532
  54.4 33.0 %collective-permute-start.9 = (bf16[2,512,512]{2,1,0:T(8,128)(2,1)}, bf16[2,512,512]{2,1,0:T(8,128)(2,1)}, u32[]{:S(2)}, u32[]{:S(2)}) collective-permute-start(bf16[2,512,512]{2,1,0:T(8,128)(2,1)} %collective-permute-done.3.refs_3_.refs_4_), channel_id=1, source_target_pairs={{0,4},{4,8},{8,12},{12,14},{14,10},{10,6},{6,2},{2,0},{1,5},{5,9},... | collective-permute-start | bytes 3145736 | tf_op jit(solution)/shard_map/ppermute | solution.py:532
  55.0 1.3 copy-start.7
  58.2 11.9 %copy-start.10 = (bf16[640]{0:T(1024)(128)(2,1)S(1)}, bf16[640]{0:T(1024)(128)(2,1)}, u32[]{:S(2)}) copy-start(bf16[640]{0:T(1024)(128)(2,1)} %param.19) | copy-start | bytes 3844
  58.2 12.1 %copy-start.11 = (bf16[640]{0:T(1024)(128)(2,1)S(1)}, bf16[640]{0:T(1024)(128)(2,1)}, u32[]{:S(2)}) copy-start(bf16[640]{0:T(1024)(128)(2,1)} %param.21) | copy-start | bytes 3844
  58.2 12.1 %copy-start.12 = (bf16[640]{0:T(1024)(128)(2,1)S(1)}, bf16[640]{0:T(1024)(128)(2,1)}, u32[]{:S(2)}) copy-start(bf16[640]{0:T(1024)(128)(2,1)} %param.20) | copy-start | bytes 3844
  68.5 17.1 %collective-permute-start.7 = (bf16[4,640,128]{2,1,0:T(8,128)(2,1)}, bf16[4,640,128]{2,1,0:T(8,128)(2,1)S(1)}, u32[]{:S(2)}, u32[]{:S(2)}) collective-permute-start(bf16[4,640,128]{2,1,0:T(8,128)(2,1)} %norm_conv.3), channel_id=1, source_target_pairs={{0,16},{16,0},{1,17},{17,1},{2,18},{18,2},{3,19},{19,3},{4,20},{20... | collective-permute-start | bytes 1966088 | tf_op jit(solution)/shard_map/ppermute | solution.py:30
  85.6 1.3 copy-start.5
  87.4 4.2 %copy-start.3 = (bf16[4,656,128]{2,1,0:T(8,128)(2,1)}, bf16[4,656,128]{2,1,0:T(8,128)(2,1)S(1)}, u32[]{:S(2)}) copy-start(bf16[4,656,128]{2,1,0:T(8,128)(2,1)S(1)} %residual.1.own_ref.refs_0_) | copy-start | bytes 2015236
  87.4 24.7 %collective-permute-start.11 = (bf16[2,512,512]{2,1,0:T(8,128)(2,1)}, bf16[2,512,512]{2,1,0:T(8,128)(2,1)S(1)}, u32[]{:S(2)}, u32[]{:S(2)}) collective-permute-start(bf16[2,512,512]{2,1,0:T(8,128)(2,1)} %collective-permute-done.9.refs_1_.refs_2_), channel_id=1, source_target_pairs={{0,4},{4,8},{8,12},{12,14},{14,10},{10,6},{6,2},{2,0},{1,5},{5,9},... | collective-permute-start | bytes 3145736 | tf_op jit(solution)/shard_map/ppermute | solution.py:532
  89.4 24.4 %collective-permute-start.12 = (bf16[2,512,512]{2,1,0:T(8,128)(2,1)S(1)}, bf16[2,512,512]{2,1,0:T(8,128)(2,1)S(1)}, u32[]{:S(2)}, u32[]{:S(2)}) collective-permute-start(bf16[2,512,512]{2,1,0:T(8,128)(2,1)S(1)} %collective-permute-done.10.refs_3_.refs_4_), channel_id=1, source_target_pairs={{4,0},{8,4},{12,8},{14,12},{10,14},{6,10},{2,6},{0,2},{5,1},{9,5},... | collective-permute-start | bytes 3145736 | tf_op jit(solution)/shard_map/ppermute | solution.py:532
  89.5 2.1 %collective-permute-start.8 = (bf16[4,656,128]{2,1,0:T(8,128)(2,1)S(1)}, bf16[4,656,128]{2,1,0:T(8,128)(2,1)S(1)}, u32[]{:S(2)}, u32[]{:S(2)}) collective-permute-start(bf16[4,656,128]{2,1,0:T(8,128)(2,1)S(1)} %residual.1.own_ref.refs_0_), channel_id=1, source_target_pairs={{0,1},{1,0},{2,3},{3,2},{4,5},{5,4},{6,7},{7,6},{8,9},{9,8},{10,11... | collective-permute-start | bytes 2015240 | tf_op jit(solution)/shard_map/ppermute | solution.py:30
  91.6 0.9 copy-start.9
  98.8 1.0 copy-start.1
  99.8 1.2 copy-start.6
  113.9 16.5 %collective-permute-start.13 = (bf16[1,512,512]{2,1,0:T(8,128)(2,1)S(1)}, bf16[1,512,512]{2,1,0:T(8,128)(2,1)S(1)}, u32[]{:S(2)}, u32[]{:S(2)}) collective-permute-start(bf16[1,512,512]{2,1,0:T(8,128)(2,1)S(1)} %slice.24), channel_id=1, source_target_pairs={{0,4},{4,8},{8,12},{12,14},{14,10},{10,6},{6,2},{2,0},{1,5},{5,9},... | collective-permute-start | bytes 1572872 | tf_op jit(solution)/shard_map/ppermute | solution.py:532
  115.4 15.0 %collective-permute-start.14 = (bf16[1,512,512]{2,1,0:T(8,128)(2,1)S(1)}, bf16[1,512,512]{2,1,0:T(8,128)(2,1)S(1)}, u32[]{:S(2)}, u32[]{:S(2)}) collective-permute-start(bf16[1,512,512]{2,1,0:T(8,128)(2,1)S(1)} %slice.25), channel_id=1, source_target_pairs={{4,0},{8,4},{12,8},{14,12},{10,14},{6,10},{2,6},{0,2},{5,1},{9,5},... | collective-permute-start | bytes 1572872 | tf_op jit(solution)/shard_map/ppermute | solution.py:532
  130.4 6.3 %copy-start.4 = (bf16[4,656,128]{2,1,0:T(8,128)(2,1)S(1)}, bf16[4,656,128]{2,1,0:T(8,128)(2,1)}, u32[]{:S(2)}) copy-start(bf16[4,656,128]{2,1,0:T(8,128)(2,1)} %copy-done.3) | copy-start | bytes 2015236
  136.7 2.4 %collective-permute-start.15 = (bf16[2,4,320,128]{3,2,1,0:T(8,128)(2,1)}, bf16[2,4,320,128]{3,2,1,0:T(8,128)(2,1)}, u32[]{:S(2)}, u32[]{:S(2)}) collective-permute-start(bf16[2,4,320,128]{3,2,1,0:T(8,128)(2,1)} %get-tuple-element.41), channel_id=1, source_target_pairs={{0,1},{1,0},{2,3},{3,2},{4,5},{5,4},{6,7},{7,6},{8,9},{9,8},{10,11... | collective-permute-start | bytes 1966088 | tf_op jit(solution)/shard_map/ppermute | solution.py:30
  140.2 9.8 %collective-permute-start.16 = (bf16[4,320,128]{2,1,0:T(8,128)(2,1)S(1)}, bf16[4,320,128]{2,1,0:T(8,128)(2,1)S(1)}, u32[]{:S(2)}, u32[]{:S(2)}) collective-permute-start(bf16[4,320,128]{2,1,0:T(8,128)(2,1)S(1)} %branch_out.2), channel_id=1, source_target_pairs={{0,16},{16,0},{1,17},{17,1},{2,18},{18,2},{3,19},{19,3},{4,20},{20... | collective-permute-start | bytes 983048 | tf_op jit(solution)/shard_map/ppermute | solution.py:30

commit v11 on v5

--- a/solution.py
+++ b/solution.py
@@ -102,8 +102,8 @@
         x = x_refs[0][r]
         if choices == 2:
             x = jnp.where(flags_ref[2] == 1, x, x_refs[1][r])
-        z = (x.astype(jnp.float32) - mean) * scale + shift
-        z = z * jax.nn.sigmoid(z)
+        z = ((x.astype(jnp.float32) - mean) * scale + shift) * 0.5
+        z = z + z * jnp.tanh(z)
         if r == 0:
             z = jnp.where(flags_ref[0] == 1, z, 0.0)
         if r == rows + 1:
@@ -268,7 +268,7 @@
             pltpu.VMEM((positions, depth), jnp.bfloat16),
             pltpu.SemaphoreType.DMA((3,)),
         ],
-        compiler_params=pltpu.CompilerParams(vmem_limit_bytes=60 * MIB),
+        compiler_params=pltpu.CompilerParams(vmem_limit_bytes=55 * MIB),
         cost_estimate=cost(6500),
         name="norm_project",
     )(order, *parts, affine, w)
@@ -516,7 +516,10 @@
     w_project = w_qkv.transpose(1, 0, 2)
     flip = jnp.logical_and(tp_count == 2, tp == 0)
     w_back = arrange_call(flip, w_out, tp_count)
-    gn_affine, w_back = lax.optimization_barrier((gn_affine, w_back))
+    order = jnp.stack([tp, 1 - tp]).astype(jnp.int32) if tp_count == 2 else jnp.zeros((1,), jnp.int32)
+    gn_affine, ln_affine, order, w_back = lax.optimization_barrier(
+        (gn_affine, ln_affine, order, w_back)
+    )
 
     flags_other = need(flags_other, hops[1])
     conv_sent = conv_call(flags_other, table, amount, x_other, gn_affine, conv_w, jnp.bfloat16)
@@ -540,10 +543,8 @@
 
     if tp_count == 2:
         parts = [resid, need(swapped(resid, "tp"), hops[2])]
-        order = jnp.stack([tp, 1 - tp]).astype(jnp.int32)
     else:
         parts = [lax.all_gather(resid, "tp", axis=1, tiled=True)]
-        order = jnp.zeros((1,), jnp.int32)
     next_hop(resid)
     queries, fresh = project_call(order, parts, ln_affine, w_project)
     resid_split = split_call(resid)

time: 142 us -> 142 us (level)
  local copies, waits for them, and re-layouts: 12.3 us -> 7.4 us
  waiting for transfers between devices: 26 us -> 30.8 us
    unnamed x41 -> x29, local copies, waits for them, and re-layouts: 9.01 us -> 4.09 us
    ppermute x5, waiting for transfers between devices: 12.6 us -> 16.3 us  [swapped(): lax.ppermute(array, axis, [(i, i ^ 1) for i in range(lax.axis_size(axis))])]
    ppermute x4, starting transfers between devices: 3.46 us -> 1.55 us  [next_hop(): lax.ppermute(behind, 'rows', backward)]
    ppermute x4, starting transfers between devices: 5.9 us -> 7.57 us  [next_hop(): lax.ppermute(ahead, 'rows', forward)]
  transfers between devices with their start and end apart: 19 -> 19, of which waited for: 9 -> 11; matrix products, arithmetic and copies ran while one was open for 5% -> 5% of each run, Pallas kernels for 39% -> 40%
where the time goes in v11:
time: 142 us; the launch traced here: 141 us
  Pallas kernels  61.6 us (43%)
  starting transfers between devices  31.4 us (22%)
  waiting for transfers between devices  30.8 us (22%)
  other arithmetic  8.21 us (6%)
  local copies, waits for them, and re-layouts  7.4 us (5%)
  between operations  1.73 us (1%)
    pallas_call x4, Pallas kernels, attention_call(): pl.pallas_call(functools.partial(attention_kernel, len(pairs), state is n...  29.9 us
    pallas_call x2, Pallas kernels, conv_call(): pl.pallas_call(functools.partial(conv_kernel, len(xs), amount), in_specs=...  21 us
    ppermute x5, waiting for transfers between devices, swapped(): lax.ppermute(array, axis, [(i, i ^ 1) for i in range(lax.axis_size(axis))])  16.3 us
    pallas_call x1, Pallas kernels, project_call(): pl.pallas_call(functools.partial(project_kernel, len(parts)), in_specs=[p...  8.31 us
    ppermute x4, starting transfers between devices, next_hop(): lax.ppermute(ahead, 'rows', forward)  7.57 us
    ppermute x4, waiting for transfers between devices, next_hop(): lax.ppermute(ahead, 'rows', forward)  5.9 us
    all_to_all x1, starting transfers between devices, summed(): return jnp.sum(lax.all_to_all(spread, axes, 0, 0, tiled=True), axis=0)  5.15 us
    ppermute x1, starting transfers between devices, per_device(): before = lax.ppermute(latent_rows[span_rows - 1:], 'rows', up_pairs)  4.85 us
  transfers between devices with their start and end apart: 19, of which 11 were waited for; matrix products, arithmetic and copies ran while one was open for 5% of the time, Pallas kernels for 40%

profile of v11, /device:TPU:0, one launch (start us, length us, event | category | flops | bytes accessed | tf_op | source)
XLA Modules:
  0.0 141.5 jit_solution(8033372040801376798)
XLA Ops:
  0.6 0.0 copy-start
  0.6 0.0 copy-start.6
  0.7 1.1 slice_bitcast_fusion.1
  1.8 4.9 %collective-permute-start = (bf16[1,640,128]{2,1,0:T(8,128)(2,1)S(1)}, bf16[1,640,128]{2,1,0:T(8,128)(2,1)S(1)}, u32[]{:S(2)}, u32[]{:S(2)}) collective-permute-start(bf16[1,640,128]{2,1,0:T(8,128)(2,1)S(1)} %get-tuple-element.54), channel_id=1, source_target_pairs={{0,2},{2,4},{4,6},{6,8},{8,10},{10,12},{12,14},{1,3},{3,5},{5,7},{... | collective-permute-start | bytes 491528 | tf_op jit(solution)/shard_map/ppermute | solution.py:476
  6.7 1.3 collective-permute-start.1
  8.0 2.1 %collective-permute-done = bf16[1,640,128]{2,1,0:T(8,128)(2,1)S(1)} collective-permute-done((bf16[1,640,128]{2,1,0:T(8,128)(2,1)S(1)}, bf16[1,640,128]{2,1,0:T(8,128)(2,1)S(1)}, u32[]{:S(2)}, u32[]{:S(2)}) %collective-permute-start) | collective-permute-done | bytes 163872 | tf_op jit(solution)/shard_map/ppermute | solution.py:476
  10.1 4.1 %collective-permute-done.1 = bf16[1,640,128]{2,1,0:T(8,128)(2,1)S(1)} collective-permute-done((bf16[1,640,128]{2,1,0:T(8,128)(2,1)S(1)}, bf16[1,640,128]{2,1,0:T(8,128)(2,1)S(1)}, u32[]{:S(2)}, u32[]{:S(2)}) %collective-permute-start.1) | collective-permute-done | bytes 163872 | tf_op jit(solution)/shard_map/ppermute | solution.py:477
  14.2 2.3 %pad_maximum_fusion.refs_0_ = bf16[6,640,128]{2,1,0:T(8,128)(2,1)} fusion(bf16[1,640,128]{2,1,0:T(8,128)(2,1)S(1)} %collective-permute-done.1, bf16[4,640,128]{2,1,0:T(8,128)(2,1)} %bitcast.34, bf16[1,640,128]{2,1,0:T(8,128)(2,1)S(1)} %collective-permute-done), kind=kLoop, calls=%fused_computation.5 | loop fusion | flops 983040 | bytes 1966080 | tf_op jit(solution)/shard_map/concatenate | solution.py:478
  16.5 1.3 collective-permute-start.6
  17.8 2.9 %collective-permute-start.4 = (bf16[2,512,512]{2,1,0:T(8,128)(2,1)}, bf16[2,512,512]{2,1,0:T(8,128)(2,1)}, u32[]{:S(2)}, u32[]{:S(2)}) collective-permute-start(bf16[2,512,512]{2,1,0:T(8,128)(2,1)} %bitcast.18), channel_id=1, source_target_pairs={{0,4},{4,8},{8,12},{12,14},{14,10},{10,6},{6,2},{2,0},{1,5},{5,9},... | collective-permute-start | bytes 3145736 | tf_op jit(solution)/shard_map/ppermute | solution.py:494
  20.8 2.5 %collective-permute-start.3 = (bf16[4,640]{1,0:T(4,128)(2,1)S(1)}, bf16[4,640]{1,0:T(4,128)(2,1)S(1)}, u32[]{:S(2)}, u32[]{:S(2)}) collective-permute-start(bf16[4,640]{1,0:T(4,128)(2,1)S(1)} %pad_maximum_fusion.1), channel_id=1, source_target_pairs={{0,1},{1,0},{2,3},{3,2},{4,5},{5,4},{6,7},{7,6},{8,9},{9,8},{10,11... | collective-permute-start | bytes 15368 | tf_op jit(solution)/shard_map/ppermute | solution.py:30
  23.3 0.3 convert_reduce_fusion
  23.6 0.1 reduce_sum.32
  23.7 0.1 reduce_sum.45
  23.7 0.1 reduce_sum.36
  23.9 0.1 reduce_sum.46
  24.0 0.1 dynamic_update_slice.3
  24.2 0.1 broadcast_in_dim.20
  24.2 0.6 broadcast_in_dim.21
  24.9 5.1 %all-to-all-start = ((f32[32,1,128]{2,1,0:T(1,128)}), f32[32,1,128]{2,1,0:T(1,128)S(1)}, u32[]{:S(2)}, u32[]{:S(2)}) async-start(f32[32,1,128]{2,1,0:T(1,128)} %broadcast_in_dim.21), calls=%async_computation | async-start | bytes 32768 | tf_op jit(solution)/shard_map/all_to_all | solution.py:53
  30.0 0.1 add_convert_fusion.1
  30.1 0.6 pad_add_fusion.2
  30.7 0.6 pad_add_fusion.1.order_ref
  31.3 1.2 arrange.1.refs_5_
  32.5 0.2 collective-permute-done.6.refs_0_
  32.8 2.9 %collective-permute-start.7 = (bf16[6,640,128]{2,1,0:T(8,128)(2,1)}, bf16[6,640,128]{2,1,0:T(8,128)(2,1)}, u32[]{:S(2)}, u32[]{:S(2)}) collective-permute-start(bf16[6,640,128]{2,1,0:T(8,128)(2,1)} %collective-permute-done.6.refs_0_), channel_id=1, source_target_pairs={{0,1},{17,16},{2,3},{19,18},{4,5},{21,20},{6,7},{23,22},{8,9},{25,... | collective-permute-start | bytes 2949128 | tf_op jit(solution)/shard_map/ppermute | solution.py:71
  35.7 2.3 %collective-permute-start.2 = (bf16[6,640,128]{2,1,0:T(8,128)(2,1)}, bf16[6,640,128]{2,1,0:T(8,128)(2,1)}, u32[]{:S(2)}, u32[]{:S(2)}) collective-permute-start(bf16[6,640,128]{2,1,0:T(8,128)(2,1)} %pad_maximum_fusion.refs_0_), channel_id=1, source_target_pairs={{0,1},{17,16},{2,3},{19,18},{4,5},{21,20},{6,7},{23,22},{8,9},{25,... | collective-permute-start | bytes 2949128 | tf_op jit(solution)/shard_map/ppermute | solution.py:70
  38.0 5.9 %collective-permute-done.4.refs_3_.refs_4_ = bf16[2,512,512]{2,1,0:T(8,128)(2,1)} collective-permute-done((bf16[2,512,512]{2,1,0:T(8,128)(2,1)}, bf16[2,512,512]{2,1,0:T(8,128)(2,1)}, u32[]{:S(2)}, u32[]{:S(2)}) %collective-permute-start.4) | collective-permute-done | bytes 1048608 | tf_op jit(solution)/shard_map/ppermute | solution.py:494
  43.9 1.3 collective-permute-start.10
  45.2 0.3 collective-permute-done.5.refs_5_.refs_6_
  45.4 0.8 collective-permute-start.11
  46.2 0.9 copy.30
  47.1 1.1 copy.28
  48.2 0.8 all-to-all-done
  49.1 0.5 reduce_sum.47.sums_ref
  49.6 10.3 %norm_conv.3 = bf16[4,640,128]{2,1,0:T(8,128)(2,1)} custom-call(s32[4]{0:T(128)} %get-tuple-element.23.flags_ref, f32[128]{0:T(128)} %reduce_sum.47.sums_ref, bf16[6,640,128]{2,1,0:T(8,128)(2,1)} %collective-permute-done.6.refs_0_, bf16[6,640,128]{2,1,0:T(8,128)(2,1)} %collective-permute-done.7.refs_1_, f32[640,2]{1,0:T(8,128)} %bitcast.36, ...), custom_call_target="tpu_custom_call" | custom-call | flops 180000000 | bytes 1000 | tf_op jit(solution)/shard_map/norm_conv/pallas_call | solution.py:141
  59.9 1.6 %collective-permute-start.8 = (bf16[4,640,128]{2,1,0:T(8,128)(2,1)}, bf16[4,640,128]{2,1,0:T(8,128)(2,1)S(1)}, u32[]{:S(2)}, u32[]{:S(2)}) collective-permute-start(bf16[4,640,128]{2,1,0:T(8,128)(2,1)} %norm_conv.3), channel_id=1, source_target_pairs={{0,16},{16,0},{1,17},{17,1},{2,18},{18,2},{3,19},{19,3},{4,20},{20... | collective-permute-start | bytes 1966088 | tf_op jit(solution)/shard_map/ppermute | solution.py:30
  62.3 0.1 divide_multiply_fusion
  62.4 0.3 convolution_reduce_fusion
  62.7 10.6 %norm_conv.2 = f32[4,640,128]{2,1,0:T(8,128)} custom-call(s32[4]{0:T(128)} %get-tuple-element.61.flags_ref, f32[128]{0:T(128)} %reduce_sum.47.sums_ref, bf16[6,640,128]{2,1,0:T(8,128)(2,1)} %pad_maximum_fusion.refs_0_, bf16[6,640,128]{2,1,0:T(8,128)(2,1)} %collective-permute-done.2.refs_1_, f32[640,2]{1,0:T(8,128)} %bitcast.37, bf16[3,3,640,640]{3,2,1,0:T(8,128)(2,1)} %refs_3_.3), custom_call_target="tpu_custom_call" | custom-call | flops 180000000 | bytes 1000 | tf_op jit(solution)/shard_map/norm_conv/pallas_call | solution.py:141
  73.4 3.6 %collective-permute-done.8 = bf16[4,640,128]{2,1,0:T(8,128)(2,1)S(1)} collective-permute-done((bf16[4,640,128]{2,1,0:T(8,128)(2,1)}, bf16[4,640,128]{2,1,0:T(8,128)(2,1)S(1)}, u32[]{:S(2)}, u32[]{:S(2)}) %collective-permute-start.8) | collective-permute-done | bytes 655392 | tf_op jit(solution)/shard_map/ppermute | solution.py:30
  76.9 1.6 %add_convert_fusion.own_ref.refs_0_ = bf16[4,640,128]{2,1,0:T(8,128)(2,1)S(1)} fusion(f32[4,640,128]{2,1,0:T(8,128)} %norm_conv.2, bf16[4,640,128]{2,1,0:T(8,128)(2,1)S(1)} %collective-permute-done.8, f32[640]{0:T(1024)S(1)} %convert_add_fusion.1, bf16[1,4,640,128]{3,2,1,0:T(8,128)(2,1)S(1)} %copy-done.7), kind=kLoop, calls=%fused_computation.3 | loop fusion | flops 1966080 | bytes 3279360 | tf_op jit(solution)/shard_map/convert_element_type | solution.py:542
  78.6 1.7 %collective-permute-start.12 = (bf16[2,512,512]{2,1,0:T(8,128)(2,1)S(1)}, bf16[2,512,512]{2,1,0:T(8,128)(2,1)S(1)}, u32[]{:S(2)}, u32[]{:S(2)}) collective-permute-start(bf16[2,512,512]{2,1,0:T(8,128)(2,1)S(1)} %collective-permute-done.10.refs_1_.refs_2_), channel_id=1, source_target_pairs={{0,4},{4,8},{8,12},{12,14},{14,10},{10,6},{6,2},{2,0},{1,5},{5,9},... | collective-permute-start | bytes 3145736 | tf_op jit(solution)/shard_map/ppermute | solution.py:494
  80.3 0.4 collective-permute-start.13
  80.7 2.1 %collective-permute-done.9.refs_1_ = bf16[4,640,128]{2,1,0:T(8,128)(2,1)S(1)} collective-permute-done((bf16[4,640,128]{2,1,0:T(8,128)(2,1)S(1)}, bf16[4,640,128]{2,1,0:T(8,128)(2,1)S(1)}, u32[]{:S(2)}, u32[]{:S(2)}) %collective-permute-start.9) | collective-permute-done | bytes 655392 | tf_op jit(solution)/shard_map/ppermute | solution.py:30
  82.8 0.9 copy-done.8
  83.6 8.3 %norm_project.1 = (bf16[512,512]{1,0:T(8,128)(2,1)}, bf16[2,512,512]{2,1,0:T(8,128)(2,1)}) custom-call(s32[2]{0:T(128)} %pad_add_fusion.1.order_ref, bf16[4,640,128]{2,1,0:T(8,128)(2,1)} %copy-done.2, bf16[4,640,128]{2,1,0:T(8,128)(2,1)} %copy-done.8, f32[1280,2]{1,0:T(8,128)} %bitcast.38, bf16[3,1280,512]{2,1,0:T(8,128)(2,1)} %bitcast.35), custom_call_target="tpu_custom_call" | custom-call | flops 130000000 | bytes 1000 | tf_op jit(solution)/shard_map/norm_project/pallas_call | solution.py:254
  92.0 1.0 copy-done.1
  93.0 1.2 copy-done.4
  94.2 10.0 %attend.4 = (f32[4,2,512,128]{3,2,1,0:T(8,128)S(1)}, f32[4,2,512,128]{3,2,1,0:T(8,128)S(1)}) custom-call(bf16[512,512]{1,0:T(8,128)(2,1)S(1)} %copy-done.1, bf16[2,512,512]{2,1,0:T(8,128)(2,1)S(1)} %copy-done.4, bf16[2,512,512]{2,1,0:T(8,128)(2,1)S(1)} %copy-done.4, bf16[2,512,512]{2,1,0:T(8,128)(2,1)} %collective-permute-done.4.refs_3_.refs_4_, ...), custom_call_target="tpu_custom_call" | custom-call | flops 212000000 | bytes 1000 | tf_op jit(solution)/shard_map/attend/pallas_call | solution.py:427
  104.3 1.1 collective-permute-done.13.refs_3_.refs_4_
  105.4 1.7 %collective-permute-start.14 = (bf16[1,512,512]{2,1,0:T(8,128)(2,1)S(1)}, bf16[1,512,512]{2,1,0:T(8,128)(2,1)S(1)}, u32[]{:S(2)}, u32[]{:S(2)}) collective-permute-start(bf16[1,512,512]{2,1,0:T(8,128)(2,1)S(1)} %slice.34), channel_id=1, source_target_pairs={{0,4},{4,8},{8,12},{12,14},{14,10},{10,6},{6,2},{2,0},{1,5},{5,9},... | collective-permute-start | bytes 1572872 | tf_op jit(solution)/shard_map/ppermute | solution.py:494
  107.1 0.3 collective-permute-start.15
  107.5 7.6 %attend.5 = (f32[4,2,512,128]{3,2,1,0:T(8,128)S(1)}, f32[4,2,512,128]{3,2,1,0:T(8,128)S(1)}) custom-call(bf16[512,512]{1,0:T(8,128)(2,1)S(1)} %copy-done.1, bf16[2,512,512]{2,1,0:T(8,128)(2,1)S(1)} %collective-permute-done.10.refs_1_.refs_2_, bf16[2,512,512]{2,1,0:T(8,128)(2,1)S(1)} %collective-permute-done.10.refs_1_.refs_2_, ...), custom_call_target="tpu_custom_call" | custom-call | flops 148000000 | bytes 1000 | tf_op jit(solution)/shard_map/attend/pallas_call | solution.py:427
  115.1 6.9 %attend.6 = (f32[4,2,512,128]{3,2,1,0:T(8,128)S(1)}, f32[4,2,512,128]{3,2,1,0:T(8,128)S(1)}) custom-call(bf16[512,512]{1,0:T(8,128)(2,1)S(1)} %copy-done.1, bf16[2,512,512]{2,1,0:T(8,128)(2,1)S(1)} %collective-permute-done.12.refs_1_.refs_2_, bf16[2,512,512]{2,1,0:T(8,128)(2,1)S(1)} %collective-permute-done.12.refs_1_.refs_2_, ...), custom_call_target="tpu_custom_call" | custom-call | flops 148000000 | bytes 1000 | tf_op jit(solution)/shard_map/attend/pallas_call | solution.py:427
  122.0 5.4 %attend.7 = (bf16[2,4,320,128]{3,2,1,0:T(8,128)(2,1)S(1)}, f32[2,4,320,128]{3,2,1,0:T(8,128)S(1)}) custom-call(bf16[512,512]{1,0:T(8,128)(2,1)S(1)} %copy-done.1, bf16[1,512,512]{2,1,0:T(8,128)(2,1)S(1)} %collective-permute-done.14.refs_1_, bf16[1,512,512]{2,1,0:T(8,128)(2,1)S(1)} %collective-permute-done.15.refs_2_, ...), custom_call_target="tpu_custom_call" | custom-call | flops 84000000 | bytes 1000 | tf_op jit(solution)/shard_map/attend/pallas_call | solution.py:427
  127.4 0.1 collective-permute-start.16
  127.5 1.0 parity_split.1.resid_ref
  128.5 1.1 collective-permute-done.16.refs_1_
  129.6 0.1 branch_out.2
  129.7 0.3 collective-permute-start.17
  129.9 0.1 branch_out.3
  130.0 9.6 %collective-permute-done.17 = bf16[4,320,128]{2,1,0:T(8,128)(2,1)} collective-permute-done((bf16[4,320,128]{2,1,0:T(8,128)(2,1)S(1)}, bf16[4,320,128]{2,1,0:T(8,128)(2,1)}, u32[]{:S(2)}, u32[]{:S(2)}) %collective-permute-start.17) | collective-permute-done | bytes 327712 | tf_op jit(solution)/shard_map/ppermute | solution.py:30
  139.6 1.9 %fusion.3 = bf16[4,320,1,128]{3,1,2,0:T(8,128)(2,1)} fusion(bf16[4,320,128]{2,1,0:T(8,128)(2,1)S(1)} %branch_out.3, bf16[4,320,128]{2,1,0:T(8,128)(2,1)} %collective-permute-done.17, pred[]{:T(512)S(6)} %eq.10), kind=kLoop, calls=%fused_computation.10 | loop fusion | flops 1310720 | bytes 983041
  (49 shorter events, 0.3 us)
Async XLA Ops:
  0.6 61.7 %copy-start = (bf16[320,640]{1,0:T(8,128)(2,1)S(1)}, bf16[320,640]{1,0:T(8,128)(2,1)}, u32[]{:S(2)}) copy-start(bf16[320,640]{1,0:T(8,128)(2,1)} %param.15) | copy-start | bytes 1228804
  0.6 22.7 %copy-start.6 = (bf16[1,4,640,128]{3,2,1,0:T(8,128)(2,1)S(1)}, bf16[1,4,640,128]{3,2,1,0:T(8,128)(2,1)}, u32[]{:S(2)}) copy-start(bf16[1,4,640,128]{3,2,1,0:T(8,128)(2,1)} %param.12) | copy-start | bytes 1966084
  0.7 20.0 %copy-start.10 = (bf16[640]{0:T(1024)(128)(2,1)S(1)}, bf16[640]{0:T(1024)(128)(2,1)}, u32[]{:S(2)}) copy-start(bf16[640]{0:T(1024)(128)(2,1)} %param.16) | copy-start | bytes 3844
  0.7 20.0 %copy-start.11 = (bf16[640]{0:T(1024)(128)(2,1)S(1)}, bf16[640]{0:T(1024)(128)(2,1)}, u32[]{:S(2)}) copy-start(bf16[640]{0:T(1024)(128)(2,1)} %param.17) | copy-start | bytes 3844
  0.7 20.0 %copy-start.12 = (bf16[640]{0:T(1024)(128)(2,1)S(1)}, bf16[640]{0:T(1024)(128)(2,1)}, u32[]{:S(2)}) copy-start(bf16[640]{0:T(1024)(128)(2,1)} %param.20) | copy-start | bytes 3844
  0.7 20.0 %copy-start.13 = (bf16[640]{0:T(1024)(128)(2,1)S(1)}, bf16[640]{0:T(1024)(128)(2,1)}, u32[]{:S(2)}) copy-start(bf16[640]{0:T(1024)(128)(2,1)} %param.21) | copy-start | bytes 3844
  1.8 8.3 %collective-permute-start = (bf16[1,640,128]{2,1,0:T(8,128)(2,1)S(1)}, bf16[1,640,128]{2,1,0:T(8,128)(2,1)S(1)}, u32[]{:S(2)}, u32[]{:S(2)}) collective-permute-start(bf16[1,640,128]{2,1,0:T(8,128)(2,1)S(1)} %get-tuple-element.54), channel_id=1, source_target_pairs={{0,2},{2,4},{4,6},{6,8},{8,10},{10,12},{12,14},{1,3},{3,5},{5,7},{... | collective-permute-start | bytes 491528 | tf_op jit(solution)/shard_map/ppermute | solution.py:476
  6.7 7.6 %collective-permute-start.1 = (bf16[1,640,128]{2,1,0:T(8,128)(2,1)S(1)}, bf16[1,640,128]{2,1,0:T(8,128)(2,1)S(1)}, u32[]{:S(2)}, u32[]{:S(2)}) collective-permute-start(bf16[1,640,128]{2,1,0:T(8,128)(2,1)S(1)} %get-tuple-element.55), channel_id=1, source_target_pairs={{2,0},{4,2},{6,4},{8,6},{10,8},{12,10},{14,12},{3,1},{5,3},{7,5},{... | collective-permute-start | bytes 491528 | tf_op jit(solution)/shard_map/ppermute | solution.py:477
  14.2 17.1 %copy-start.5 = (bf16[512,1280]{1,0:T(8,128)(2,1)S(1)}, bf16[512,1280]{1,0:T(8,128)(2,1)}, u32[]{:S(2)}) copy-start(bf16[512,1280]{1,0:T(8,128)(2,1)} %w_ref.1) | copy-start | bytes 3932164
  16.5 16.3 %collective-permute-start.6 = (bf16[6,640,128]{2,1,0:T(8,128)(2,1)}, bf16[6,640,128]{2,1,0:T(8,128)(2,1)}, u32[]{:S(2)}, u32[]{:S(2)}) collective-permute-start(bf16[6,640,128]{2,1,0:T(8,128)(2,1)} %pad_maximum_fusion.refs_0_), channel_id=1, source_target_pairs={{1,17},{16,0},{3,19},{18,2},{5,21},{20,4},{7,23},{22,6},{9,25},{24... | collective-permute-start | bytes 2949128 | tf_op jit(solution)/shard_map/ppermute | solution.py:68
  17.8 26.1 %collective-permute-start.4 = (bf16[2,512,512]{2,1,0:T(8,128)(2,1)}, bf16[2,512,512]{2,1,0:T(8,128)(2,1)}, u32[]{:S(2)}, u32[]{:S(2)}) collective-permute-start(bf16[2,512,512]{2,1,0:T(8,128)(2,1)} %bitcast.18), channel_id=1, source_target_pairs={{0,4},{4,8},{8,12},{12,14},{14,10},{10,6},{6,2},{2,0},{1,5},{5,9},... | collective-permute-start | bytes 3145736 | tf_op jit(solution)/shard_map/ppermute | solution.py:494
  20.7 24.8 %collective-permute-start.5 = (bf16[2,512,512]{2,1,0:T(8,128)(2,1)}, bf16[2,512,512]{2,1,0:T(8,128)(2,1)}, u32[]{:S(2)}, u32[]{:S(2)}) collective-permute-start(bf16[2,512,512]{2,1,0:T(8,128)(2,1)} %bitcast.18), channel_id=1, source_target_pairs={{4,0},{8,4},{12,8},{14,12},{10,14},{6,10},{2,6},{0,2},{5,1},{9,5},... | collective-permute-start | bytes 3145736 | tf_op jit(solution)/shard_map/ppermute | solution.py:494
  20.8 14.9 %collective-permute-start.3 = (bf16[4,640]{1,0:T(4,128)(2,1)S(1)}, bf16[4,640]{1,0:T(4,128)(2,1)S(1)}, u32[]{:S(2)}, u32[]{:S(2)}) collective-permute-start(bf16[4,640]{1,0:T(4,128)(2,1)S(1)} %pad_maximum_fusion.1), channel_id=1, source_target_pairs={{0,1},{1,0},{2,3},{3,2},{4,5},{5,4},{6,7},{7,6},{8,9},{9,8},{10,11... | collective-permute-start | bytes 15368 | tf_op jit(solution)/shard_map/ppermute | solution.py:30
  24.9 24.2 %all-to-all-start = ((f32[32,1,128]{2,1,0:T(1,128)}), f32[32,1,128]{2,1,0:T(1,128)S(1)}, u32[]{:S(2)}, u32[]{:S(2)}) async-start(f32[32,1,128]{2,1,0:T(1,128)} %broadcast_in_dim.21), calls=%async_computation | async-start | bytes 32768 | tf_op jit(solution)/shard_map/all_to_all | solution.py:53
  32.8 16.8 %collective-permute-start.7 = (bf16[6,640,128]{2,1,0:T(8,128)(2,1)}, bf16[6,640,128]{2,1,0:T(8,128)(2,1)}, u32[]{:S(2)}, u32[]{:S(2)}) collective-permute-start(bf16[6,640,128]{2,1,0:T(8,128)(2,1)} %collective-permute-done.6.refs_0_), channel_id=1, source_target_pairs={{0,1},{17,16},{2,3},{19,18},{4,5},{21,20},{6,7},{23,22},{8,9},{25,... | collective-permute-start | bytes 2949128 | tf_op jit(solution)/shard_map/ppermute | solution.py:71
  35.7 27.0 %collective-permute-start.2 = (bf16[6,640,128]{2,1,0:T(8,128)(2,1)}, bf16[6,640,128]{2,1,0:T(8,128)(2,1)}, u32[]{:S(2)}, u32[]{:S(2)}) collective-permute-start(bf16[6,640,128]{2,1,0:T(8,128)(2,1)} %pad_maximum_fusion.refs_0_), channel_id=1, source_target_pairs={{0,1},{17,16},{2,3},{19,18},{4,5},{21,20},{6,7},{23,22},{8,9},{25,... | collective-permute-start | bytes 2949128 | tf_op jit(solution)/shard_map/ppermute | solution.py:70
  43.9 34.7 %collective-permute-start.10 = (bf16[2,512,512]{2,1,0:T(8,128)(2,1)}, bf16[2,512,512]{2,1,0:T(8,128)(2,1)S(1)}, u32[]{:S(2)}, u32[]{:S(2)}) collective-permute-start(bf16[2,512,512]{2,1,0:T(8,128)(2,1)} %collective-permute-done.4.refs_3_.refs_4_), channel_id=1, source_target_pairs={{0,4},{4,8},{8,12},{12,14},{14,10},{10,6},{6,2},{2,0},{1,5},{5,9},... | collective-permute-start | bytes 3145736 | tf_op jit(solution)/shard_map/ppermute | solution.py:494
  45.4 33.1 %collective-permute-start.11 = (bf16[2,512,512]{2,1,0:T(8,128)(2,1)}, bf16[2,512,512]{2,1,0:T(8,128)(2,1)}, u32[]{:S(2)}, u32[]{:S(2)}) collective-permute-start(bf16[2,512,512]{2,1,0:T(8,128)(2,1)} %collective-permute-done.5.refs_5_.refs_6_), channel_id=1, source_target_pairs={{4,0},{8,4},{12,8},{14,12},{10,14},{6,10},{2,6},{0,2},{5,1},{9,5},... | collective-permute-start | bytes 3145736 | tf_op jit(solution)/shard_map/ppermute | solution.py:494
  49.6 13.1 %copy-start.9 = (bf16[640]{0:T(1024)(128)(2,1)S(1)}, bf16[640]{0:T(1024)(128)(2,1)}, u32[]{:S(2)}) copy-start(bf16[640]{0:T(1024)(128)(2,1)} %param.19) | copy-start | bytes 3844
  59.9 17.0 %collective-permute-start.8 = (bf16[4,640,128]{2,1,0:T(8,128)(2,1)}, bf16[4,640,128]{2,1,0:T(8,128)(2,1)S(1)}, u32[]{:S(2)}, u32[]{:S(2)}) collective-permute-start(bf16[4,640,128]{2,1,0:T(8,128)(2,1)} %norm_conv.3), channel_id=1, source_target_pairs={{0,16},{16,0},{1,17},{17,1},{2,18},{18,2},{3,19},{19,3},{4,20},{20... | collective-permute-start | bytes 1966088 | tf_op jit(solution)/shard_map/ppermute | solution.py:30
  62.7 14.2 %copy-start.7 = (bf16[1,4,640,128]{3,2,1,0:T(8,128)(2,1)S(1)}, bf16[1,4,640,128]{3,2,1,0:T(8,128)(2,1)}, u32[]{:S(2)}) copy-start(bf16[1,4,640,128]{3,2,1,0:T(8,128)(2,1)} %param.12) | copy-start | bytes 1966084
  78.6 4.2 %copy-start.2 = (bf16[4,640,128]{2,1,0:T(8,128)(2,1)}, bf16[4,640,128]{2,1,0:T(8,128)(2,1)S(1)}, u32[]{:S(2)}) copy-start(bf16[4,640,128]{2,1,0:T(8,128)(2,1)S(1)} %add_convert_fusion.own_ref.refs_0_) | copy-start | bytes 1966084
  78.6 25.6 %collective-permute-start.12 = (bf16[2,512,512]{2,1,0:T(8,128)(2,1)S(1)}, bf16[2,512,512]{2,1,0:T(8,128)(2,1)S(1)}, u32[]{:S(2)}, u32[]{:S(2)}) collective-permute-start(bf16[2,512,512]{2,1,0:T(8,128)(2,1)S(1)} %collective-permute-done.10.refs_1_.refs_2_), channel_id=1, source_target_pairs={{0,4},{4,8},{8,12},{12,14},{14,10},{10,6},{6,2},{2,0},{1,5},{5,9},... | collective-permute-start | bytes 3145736 | tf_op jit(solution)/shard_map/ppermute | solution.py:494
  80.3 25.1 %collective-permute-start.13 = (bf16[2,512,512]{2,1,0:T(8,128)(2,1)}, bf16[2,512,512]{2,1,0:T(8,128)(2,1)S(1)}, u32[]{:S(2)}, u32[]{:S(2)}) collective-permute-start(bf16[2,512,512]{2,1,0:T(8,128)(2,1)} %collective-permute-done.11.refs_3_.refs_4_), channel_id=1, source_target_pairs={{4,0},{8,4},{12,8},{14,12},{10,14},{6,10},{2,6},{0,2},{5,1},{9,5},... | collective-permute-start | bytes 3145736 | tf_op jit(solution)/shard_map/ppermute | solution.py:494
  80.7 2.1 %collective-permute-start.9 = (bf16[4,640,128]{2,1,0:T(8,128)(2,1)S(1)}, bf16[4,640,128]{2,1,0:T(8,128)(2,1)S(1)}, u32[]{:S(2)}, u32[]{:S(2)}) collective-permute-start(bf16[4,640,128]{2,1,0:T(8,128)(2,1)S(1)} %add_convert_fusion.own_ref.refs_0_), channel_id=1, source_target_pairs={{0,1},{1,0},{2,3},{3,2},{4,5},{5,4},{6,7},{7,6},{8,9},{9,8},{10,11... | collective-permute-start | bytes 1966088 | tf_op jit(solution)/shard_map/ppermute | solution.py:30
  82.8 0.9 copy-start.8
  91.9 1.0 copy-start.1
  93.0 1.2 copy-start.4
  105.4 16.5 %collective-permute-start.14 = (bf16[1,512,512]{2,1,0:T(8,128)(2,1)S(1)}, bf16[1,512,512]{2,1,0:T(8,128)(2,1)S(1)}, u32[]{:S(2)}, u32[]{:S(2)}) collective-permute-start(bf16[1,512,512]{2,1,0:T(8,128)(2,1)S(1)} %slice.34), channel_id=1, source_target_pairs={{0,4},{4,8},{8,12},{12,14},{14,10},{10,6},{6,2},{2,0},{1,5},{5,9},... | collective-permute-start | bytes 1572872 | tf_op jit(solution)/shard_map/ppermute | solution.py:494
  107.1 14.8 %collective-permute-start.15 = (bf16[1,512,512]{2,1,0:T(8,128)(2,1)S(1)}, bf16[1,512,512]{2,1,0:T(8,128)(2,1)S(1)}, u32[]{:S(2)}, u32[]{:S(2)}) collective-permute-start(bf16[1,512,512]{2,1,0:T(8,128)(2,1)S(1)} %slice.35), channel_id=1, source_target_pairs={{4,0},{8,4},{12,8},{14,12},{10,14},{6,10},{2,6},{0,2},{5,1},{9,5},... | collective-permute-start | bytes 1572872 | tf_op jit(solution)/shard_map/ppermute | solution.py:494
  122.0 5.5 %copy-start.3 = (bf16[4,640,128]{2,1,0:T(8,128)(2,1)S(1)}, bf16[4,640,128]{2,1,0:T(8,128)(2,1)}, u32[]{:S(2)}) copy-start(bf16[4,640,128]{2,1,0:T(8,128)(2,1)} %copy-done.2) | copy-start | bytes 1966084
  127.4 2.2 %collective-permute-start.16 = (bf16[2,4,320,128]{3,2,1,0:T(8,128)(2,1)S(1)}, bf16[2,4,320,128]{3,2,1,0:T(8,128)(2,1)S(1)}, u32[]{:S(2)}, u32[]{:S(2)}) collective-permute-start(bf16[2,4,320,128]{3,2,1,0:T(8,128)(2,1)S(1)} %get-tuple-element.41), channel_id=1, source_target_pairs={{0,1},{1,0},{2,3},{3,2},{4,5},{5,4},{6,7},{7,6},{8,9},{9,8},{10,11... | collective-permute-start | bytes 1966088 | tf_op jit(solution)/shard_map/ppermute | solution.py:30
  129.7 9.9 %collective-permute-start.17 = (bf16[4,320,128]{2,1,0:T(8,128)(2,1)S(1)}, bf16[4,320,128]{2,1,0:T(8,128)(2,1)}, u32[]{:S(2)}, u32[]{:S(2)}) collective-permute-start(bf16[4,320,128]{2,1,0:T(8,128)(2,1)S(1)} %branch_out.2), channel_id=1, source_target_pairs={{0,16},{16,0},{1,17},{17,1},{2,18},{18,2},{3,19},{19,3},{4,20},{20... | collective-permute-start | bytes 983048 | tf_op jit(solution)/shard_map/ppermute | solution.py:30

commit v12 on v11

--- a/solution.py
+++ b/solution.py
@@ -553,6 +553,9 @@
     group = [((fresh, 0), (fresh, 1))] + blocks_of(1)
     state = None
     for hop in range(2, last + 1):
+        if hop == 3:
+            group = group + blocks_of(3)
+            continue
         state = attention_call(queries, group, state)
         while len(hops) <= last:
             next_hop(state[0])

time: 142 us -> 140 us (0.986)
  Pallas kernels: 61.6 us -> 59.7 us
    pallas_call x4 -> x3, Pallas kernels: 29.9 us -> 28 us  [attention_call(): pl.pallas_call(functools.partial(attention_kernel, len(pairs), state is n...]
  transfers between devices with their start and end apart: 19 -> 19, of which waited for: 11 -> 11; matrix products, arithmetic and copies ran while one was open for 5% -> 5% of each run, Pallas kernels for 40% -> 39%
where the time goes in v12:
time: 140 us
  Pallas kernels  59.7 us (43%)
  starting transfers between devices  31.4 us (22%)
  waiting for transfers between devices  30.8 us (22%)
  other arithmetic  8.21 us (6%)
  local copies, waits for them, and re-layouts  7.41 us (5%)
  between operations  1.72 us (1%)
    pallas_call x3, Pallas kernels, attention_call(): pl.pallas_call(functools.partial(attention_kernel, len(pairs), state is n...  28 us
    pallas_call x2, Pallas kernels, conv_call(): pl.pallas_call(functools.partial(conv_kernel, len(xs), amount), in_specs=...  21 us
    ppermute x5, waiting for transfers between devices, swapped(): lax.ppermute(array, axis, [(i, i ^ 1) for i in range(lax.axis_size(axis))])  16.3 us
    pallas_call x1, Pallas kernels, project_call(): pl.pallas_call(functools.partial(project_kernel, len(parts)), in_specs=[p...  8.31 us
    ppermute x4, starting transfers between devices, next_hop(): lax.ppermute(ahead, 'rows', forward)  7.59 us
    ppermute x4, waiting for transfers between devices, next_hop(): lax.ppermute(ahead, 'rows', forward)  5.85 us
    all_to_all x1, starting transfers between devices, summed(): return jnp.sum(lax.all_to_all(spread, axes, 0, 0, tiled=True), axis=0)  5.15 us
    ppermute x1, starting transfers between devices, per_device(): before = lax.ppermute(latent_rows[span_rows - 1:], 'rows', up_pairs)  4.85 us
  transfers between devices with their start and end apart: 19, of which 11 were waited for; matrix products, arithmetic and copies ran while one was open for 5% of the time, Pallas kernels for 39%

profile of v12, /device:TPU:0, one launch (start us, length us, event | category | flops | bytes accessed | tf_op | source)
XLA Modules:
  0.0 139.6 jit_solution(5632473113648702374)
XLA Ops:
  0.6 0.0 copy-start
  0.6 0.0 copy-start.6
  0.7 1.1 slice_bitcast_fusion.1
  1.8 4.9 %collective-permute-start = (bf16[1,640,128]{2,1,0:T(8,128)(2,1)S(1)}, bf16[1,640,128]{2,1,0:T(8,128)(2,1)S(1)}, u32[]{:S(2)}, u32[]{:S(2)}) collective-permute-start(bf16[1,640,128]{2,1,0:T(8,128)(2,1)S(1)} %get-tuple-element.50), channel_id=1, source_target_pairs={{0,2},{2,4},{4,6},{6,8},{8,10},{10,12},{12,14},{1,3},{3,5},{5,7},{... | collective-permute-start | bytes 491528 | tf_op jit(solution)/shard_map/ppermute | solution.py:476
  6.7 1.3 collective-permute-start.1
  8.0 2.1 %collective-permute-done = bf16[1,640,128]{2,1,0:T(8,128)(2,1)S(1)} collective-permute-done((bf16[1,640,128]{2,1,0:T(8,128)(2,1)S(1)}, bf16[1,640,128]{2,1,0:T(8,128)(2,1)S(1)}, u32[]{:S(2)}, u32[]{:S(2)}) %collective-permute-start) | collective-permute-done | bytes 163872 | tf_op jit(solution)/shard_map/ppermute | solution.py:476
  10.1 4.1 %collective-permute-done.1 = bf16[1,640,128]{2,1,0:T(8,128)(2,1)S(1)} collective-permute-done((bf16[1,640,128]{2,1,0:T(8,128)(2,1)S(1)}, bf16[1,640,128]{2,1,0:T(8,128)(2,1)S(1)}, u32[]{:S(2)}, u32[]{:S(2)}) %collective-permute-start.1) | collective-permute-done | bytes 163872 | tf_op jit(solution)/shard_map/ppermute | solution.py:477
  14.2 2.3 %pad_maximum_fusion.refs_0_ = bf16[6,640,128]{2,1,0:T(8,128)(2,1)} fusion(bf16[1,640,128]{2,1,0:T(8,128)(2,1)S(1)} %collective-permute-done.1, bf16[4,640,128]{2,1,0:T(8,128)(2,1)} %bitcast.34, bf16[1,640,128]{2,1,0:T(8,128)(2,1)S(1)} %collective-permute-done), kind=kLoop, calls=%fused_computation.5 | loop fusion | flops 983040 | bytes 1966080 | tf_op jit(solution)/shard_map/concatenate | solution.py:478
  16.5 1.3 collective-permute-start.6
  17.8 2.9 %collective-permute-start.4 = (bf16[2,512,512]{2,1,0:T(8,128)(2,1)}, bf16[2,512,512]{2,1,0:T(8,128)(2,1)}, u32[]{:S(2)}, u32[]{:S(2)}) collective-permute-start(bf16[2,512,512]{2,1,0:T(8,128)(2,1)} %bitcast.18), channel_id=1, source_target_pairs={{0,4},{4,8},{8,12},{12,14},{14,10},{10,6},{6,2},{2,0},{1,5},{5,9},... | collective-permute-start | bytes 3145736 | tf_op jit(solution)/shard_map/ppermute | solution.py:494
  20.8 2.5 %collective-permute-start.3 = (bf16[4,640]{1,0:T(4,128)(2,1)S(1)}, bf16[4,640]{1,0:T(4,128)(2,1)S(1)}, u32[]{:S(2)}, u32[]{:S(2)}) collective-permute-start(bf16[4,640]{1,0:T(4,128)(2,1)S(1)} %pad_maximum_fusion.1), channel_id=1, source_target_pairs={{0,1},{1,0},{2,3},{3,2},{4,5},{5,4},{6,7},{7,6},{8,9},{9,8},{10,11... | collective-permute-start | bytes 15368 | tf_op jit(solution)/shard_map/ppermute | solution.py:30
  23.3 0.3 convert_reduce_fusion
  23.6 0.1 reduce_sum.32
  23.7 0.1 reduce_sum.45
  23.8 0.1 reduce_sum.36
  23.9 0.1 reduce_sum.46
  24.0 0.1 dynamic_update_slice.3
  24.2 0.1 broadcast_in_dim.20
  24.2 0.6 broadcast_in_dim.21
  24.9 5.1 %all-to-all-start = ((f32[32,1,128]{2,1,0:T(1,128)}), f32[32,1,128]{2,1,0:T(1,128)S(1)}, u32[]{:S(2)}, u32[]{:S(2)}) async-start(f32[32,1,128]{2,1,0:T(1,128)} %broadcast_in_dim.21), calls=%async_computation | async-start | bytes 32768 | tf_op jit(solution)/shard_map/all_to_all | solution.py:53
  30.0 0.1 add_convert_fusion.1
  30.1 0.7 pad_add_fusion.2
  30.8 0.6 pad_add_fusion.1.order_ref
  31.3 1.2 arrange.1.refs_5_
  32.5 0.2 collective-permute-done.6.refs_0_
  32.8 2.9 %collective-permute-start.7 = (bf16[6,640,128]{2,1,0:T(8,128)(2,1)}, bf16[6,640,128]{2,1,0:T(8,128)(2,1)}, u32[]{:S(2)}, u32[]{:S(2)}) collective-permute-start(bf16[6,640,128]{2,1,0:T(8,128)(2,1)} %collective-permute-done.6.refs_0_), channel_id=1, source_target_pairs={{0,1},{17,16},{2,3},{19,18},{4,5},{21,20},{6,7},{23,22},{8,9},{25,... | collective-permute-start | bytes 2949128 | tf_op jit(solution)/shard_map/ppermute | solution.py:71
  35.7 2.3 %collective-permute-start.2 = (bf16[6,640,128]{2,1,0:T(8,128)(2,1)}, bf16[6,640,128]{2,1,0:T(8,128)(2,1)}, u32[]{:S(2)}, u32[]{:S(2)}) collective-permute-start(bf16[6,640,128]{2,1,0:T(8,128)(2,1)} %pad_maximum_fusion.refs_0_), channel_id=1, source_target_pairs={{0,1},{17,16},{2,3},{19,18},{4,5},{21,20},{6,7},{23,22},{8,9},{25,... | collective-permute-start | bytes 2949128 | tf_op jit(solution)/shard_map/ppermute | solution.py:70
  38.0 5.8 %collective-permute-done.4.refs_3_.refs_4_ = bf16[2,512,512]{2,1,0:T(8,128)(2,1)} collective-permute-done((bf16[2,512,512]{2,1,0:T(8,128)(2,1)}, bf16[2,512,512]{2,1,0:T(8,128)(2,1)}, u32[]{:S(2)}, u32[]{:S(2)}) %collective-permute-start.4) | collective-permute-done | bytes 1048608 | tf_op jit(solution)/shard_map/ppermute | solution.py:494
  43.9 1.3 collective-permute-start.10
  45.2 0.3 collective-permute-done.5.refs_5_.refs_6_
  45.4 0.8 collective-permute-start.11
  46.2 0.9 copy.30
  47.1 1.1 copy.28
  48.2 0.8 all-to-all-done
  49.1 0.5 reduce_sum.47.sums_ref
  49.6 10.3 %norm_conv.3 = bf16[4,640,128]{2,1,0:T(8,128)(2,1)} custom-call(s32[4]{0:T(128)} %get-tuple-element.21.flags_ref, f32[128]{0:T(128)} %reduce_sum.47.sums_ref, bf16[6,640,128]{2,1,0:T(8,128)(2,1)} %collective-permute-done.6.refs_0_, bf16[6,640,128]{2,1,0:T(8,128)(2,1)} %collective-permute-done.7.refs_1_, f32[640,2]{1,0:T(8,128)} %bitcast.36, ...), custom_call_target="tpu_custom_call" | custom-call | flops 180000000 | bytes 1000 | tf_op jit(solution)/shard_map/norm_conv/pallas_call | solution.py:141
  59.9 1.6 %collective-permute-start.8 = (bf16[4,640,128]{2,1,0:T(8,128)(2,1)}, bf16[4,640,128]{2,1,0:T(8,128)(2,1)S(1)}, u32[]{:S(2)}, u32[]{:S(2)}) collective-permute-start(bf16[4,640,128]{2,1,0:T(8,128)(2,1)} %norm_conv.3), channel_id=1, source_target_pairs={{0,16},{16,0},{1,17},{17,1},{2,18},{18,2},{3,19},{19,3},{4,20},{20... | collective-permute-start | bytes 1966088 | tf_op jit(solution)/shard_map/ppermute | solution.py:30
  62.3 0.1 divide_multiply_fusion
  62.4 0.3 convolution_reduce_fusion
  62.7 0.0 copy-start.7
  62.7 10.6 %norm_conv.2 = f32[4,640,128]{2,1,0:T(8,128)} custom-call(s32[4]{0:T(128)} %get-tuple-element.57.flags_ref, f32[128]{0:T(128)} %reduce_sum.47.sums_ref, bf16[6,640,128]{2,1,0:T(8,128)(2,1)} %pad_maximum_fusion.refs_0_, bf16[6,640,128]{2,1,0:T(8,128)(2,1)} %collective-permute-done.2.refs_1_, f32[640,2]{1,0:T(8,128)} %bitcast.37, bf16[3,3,640,640]{3,2,1,0:T(8,128)(2,1)} %refs_3_.3), custom_call_target="tpu_custom_call" | custom-call | flops 180000000 | bytes 1000 | tf_op jit(solution)/shard_map/norm_conv/pallas_call | solution.py:141
  73.4 3.6 %collective-permute-done.8 = bf16[4,640,128]{2,1,0:T(8,128)(2,1)S(1)} collective-permute-done((bf16[4,640,128]{2,1,0:T(8,128)(2,1)}, bf16[4,640,128]{2,1,0:T(8,128)(2,1)S(1)}, u32[]{:S(2)}, u32[]{:S(2)}) %collective-permute-start.8) | collective-permute-done | bytes 655392 | tf_op jit(solution)/shard_map/ppermute | solution.py:30
  76.9 1.6 %add_convert_fusion.own_ref.refs_0_ = bf16[4,640,128]{2,1,0:T(8,128)(2,1)S(1)} fusion(f32[4,640,128]{2,1,0:T(8,128)} %norm_conv.2, bf16[4,640,128]{2,1,0:T(8,128)(2,1)S(1)} %collective-permute-done.8, f32[640]{0:T(1024)S(1)} %convert_add_fusion.1, bf16[1,4,640,128]{3,2,1,0:T(8,128)(2,1)S(1)} %copy-done.7), kind=kLoop, calls=%fused_computation.3 | loop fusion | flops 1966080 | bytes 3279360 | tf_op jit(solution)/shard_map/convert_element_type | solution.py:542
  78.6 1.7 %collective-permute-start.12 = (bf16[2,512,512]{2,1,0:T(8,128)(2,1)S(1)}, bf16[2,512,512]{2,1,0:T(8,128)(2,1)S(1)}, u32[]{:S(2)}, u32[]{:S(2)}) collective-permute-start(bf16[2,512,512]{2,1,0:T(8,128)(2,1)S(1)} %collective-permute-done.10.refs_1_.refs_2_), channel_id=1, source_target_pairs={{0,4},{4,8},{8,12},{12,14},{14,10},{10,6},{6,2},{2,0},{1,5},{5,9},... | collective-permute-start | bytes 3145736 | tf_op jit(solution)/shard_map/ppermute | solution.py:494
  80.2 0.4 collective-permute-start.13
  80.7 2.1 %collective-permute-done.9.refs_1_ = bf16[4,640,128]{2,1,0:T(8,128)(2,1)S(1)} collective-permute-done((bf16[4,640,128]{2,1,0:T(8,128)(2,1)S(1)}, bf16[4,640,128]{2,1,0:T(8,128)(2,1)S(1)}, u32[]{:S(2)}, u32[]{:S(2)}) %collective-permute-start.9) | collective-permute-done | bytes 655392 | tf_op jit(solution)/shard_map/ppermute | solution.py:30
  82.8 0.9 copy-done.8
  83.6 8.3 %norm_project.1 = (bf16[512,512]{1,0:T(8,128)(2,1)}, bf16[2,512,512]{2,1,0:T(8,128)(2,1)}) custom-call(s32[2]{0:T(128)} %pad_add_fusion.1.order_ref, bf16[4,640,128]{2,1,0:T(8,128)(2,1)} %copy-done.1, bf16[4,640,128]{2,1,0:T(8,128)(2,1)} %copy-done.8, f32[1280,2]{1,0:T(8,128)} %bitcast.38, bf16[3,1280,512]{2,1,0:T(8,128)(2,1)} %bitcast.35), custom_call_target="tpu_custom_call" | custom-call | flops 130000000 | bytes 1000 | tf_op jit(solution)/shard_map/norm_project/pallas_call | solution.py:254
  91.9 1.0 copy-done.3
  93.0 1.2 copy-done.4
  94.2 10.0 %attend.3 = (f32[4,2,512,128]{3,2,1,0:T(8,128)S(1)}, f32[4,2,512,128]{3,2,1,0:T(8,128)S(1)}) custom-call(bf16[512,512]{1,0:T(8,128)(2,1)S(1)} %copy-done.3, bf16[2,512,512]{2,1,0:T(8,128)(2,1)S(1)} %copy-done.4, bf16[2,512,512]{2,1,0:T(8,128)(2,1)S(1)} %copy-done.4, bf16[2,512,512]{2,1,0:T(8,128)(2,1)} %collective-permute-done.4.refs_3_.refs_4_, ...), custom_call_target="tpu_custom_call" | custom-call | flops 212000000 | bytes 1000 | tf_op jit(solution)/shard_map/attend/pallas_call | solution.py:427
  104.3 1.1 collective-permute-done.13.refs_7_.refs_8_
  105.4 1.7 %collective-permute-start.14 = (bf16[1,512,512]{2,1,0:T(8,128)(2,1)S(1)}, bf16[1,512,512]{2,1,0:T(8,128)(2,1)S(1)}, u32[]{:S(2)}, u32[]{:S(2)}) collective-permute-start(bf16[1,512,512]{2,1,0:T(8,128)(2,1)S(1)} %slice.34), channel_id=1, source_target_pairs={{0,4},{4,8},{8,12},{12,14},{14,10},{10,6},{6,2},{2,0},{1,5},{5,9},... | collective-permute-start | bytes 1572872 | tf_op jit(solution)/shard_map/ppermute | solution.py:494
  107.1 0.3 collective-permute-start.15
  107.5 12.6 %attend.4 = (f32[4,2,512,128]{3,2,1,0:T(8,128)S(1)}, f32[4,2,512,128]{3,2,1,0:T(8,128)S(1)}) custom-call(bf16[512,512]{1,0:T(8,128)(2,1)S(1)} %copy-done.3, bf16[2,512,512]{2,1,0:T(8,128)(2,1)S(1)} %collective-permute-done.10.refs_1_.refs_2_, bf16[2,512,512]{2,1,0:T(8,128)(2,1)S(1)} %collective-permute-done.10.refs_1_.refs_2_, ...), custom_call_target="tpu_custom_call" | custom-call | flops 276000000 | bytes 1000 | tf_op jit(solution)/shard_map/attend/pallas_call | solution.py:427
  120.1 5.5 %attend.5 = (bf16[2,4,320,128]{3,2,1,0:T(8,128)(2,1)S(1)}, f32[2,4,320,128]{3,2,1,0:T(8,128)S(1)}) custom-call(bf16[512,512]{1,0:T(8,128)(2,1)S(1)} %copy-done.3, bf16[1,512,512]{2,1,0:T(8,128)(2,1)S(1)} %collective-permute-done.14.refs_1_, bf16[1,512,512]{2,1,0:T(8,128)(2,1)S(1)} %collective-permute-done.15.refs_2_, ...), custom_call_target="tpu_custom_call" | custom-call | flops 84000000 | bytes 1000 | tf_op jit(solution)/shard_map/attend/pallas_call | solution.py:427
  125.5 0.1 collective-permute-start.16
  125.6 1.0 parity_split.1.resid_ref
  126.7 1.1 collective-permute-done.16.refs_1_
  127.7 0.1 branch_out.2
  127.8 0.2 collective-permute-start.17
  128.0 0.1 branch_out.3
  128.1 9.6 %collective-permute-done.17 = bf16[4,320,128]{2,1,0:T(8,128)(2,1)} collective-permute-done((bf16[4,320,128]{2,1,0:T(8,128)(2,1)S(1)}, bf16[4,320,128]{2,1,0:T(8,128)(2,1)}, u32[]{:S(2)}, u32[]{:S(2)}) %collective-permute-start.17) | collective-permute-done | bytes 327712 | tf_op jit(solution)/shard_map/ppermute | solution.py:30
  137.7 1.9 %fusion.3 = bf16[4,320,1,128]{3,1,2,0:T(8,128)(2,1)} fusion(bf16[4,320,128]{2,1,0:T(8,128)(2,1)S(1)} %branch_out.3, bf16[4,320,128]{2,1,0:T(8,128)(2,1)} %collective-permute-done.17, pred[]{:T(512)S(6)} %eq.10), kind=kLoop, calls=%fused_computation.10 | loop fusion | flops 1310720 | bytes 983041
  (48 shorter events, 0.3 us)
Async XLA Ops:
  0.6 61.7 %copy-start = (bf16[320,640]{1,0:T(8,128)(2,1)S(1)}, bf16[320,640]{1,0:T(8,128)(2,1)}, u32[]{:S(2)}) copy-start(bf16[320,640]{1,0:T(8,128)(2,1)} %param.15) | copy-start | bytes 1228804
  0.6 22.7 %copy-start.6 = (bf16[1,4,640,128]{3,2,1,0:T(8,128)(2,1)S(1)}, bf16[1,4,640,128]{3,2,1,0:T(8,128)(2,1)}, u32[]{:S(2)}) copy-start(bf16[1,4,640,128]{3,2,1,0:T(8,128)(2,1)} %param.12) | copy-start | bytes 1966084
  0.7 20.0 %copy-start.10 = (bf16[640]{0:T(1024)(128)(2,1)S(1)}, bf16[640]{0:T(1024)(128)(2,1)}, u32[]{:S(2)}) copy-start(bf16[640]{0:T(1024)(128)(2,1)} %param.16) | copy-start | bytes 3844
  0.7 20.0 %copy-start.11 = (bf16[640]{0:T(1024)(128)(2,1)S(1)}, bf16[640]{0:T(1024)(128)(2,1)}, u32[]{:S(2)}) copy-start(bf16[640]{0:T(1024)(128)(2,1)} %param.17) | copy-start | bytes 3844
  0.7 20.0 %copy-start.12 = (bf16[640]{0:T(1024)(128)(2,1)S(1)}, bf16[640]{0:T(1024)(128)(2,1)}, u32[]{:S(2)}) copy-start(bf16[640]{0:T(1024)(128)(2,1)} %param.20) | copy-start | bytes 3844
  0.7 20.0 %copy-start.13 = (bf16[640]{0:T(1024)(128)(2,1)S(1)}, bf16[640]{0:T(1024)(128)(2,1)}, u32[]{:S(2)}) copy-start(bf16[640]{0:T(1024)(128)(2,1)} %param.21) | copy-start | bytes 3844
  1.8 8.3 %collective-permute-start = (bf16[1,640,128]{2,1,0:T(8,128)(2,1)S(1)}, bf16[1,640,128]{2,1,0:T(8,128)(2,1)S(1)}, u32[]{:S(2)}, u32[]{:S(2)}) collective-permute-start(bf16[1,640,128]{2,1,0:T(8,128)(2,1)S(1)} %get-tuple-element.50), channel_id=1, source_target_pairs={{0,2},{2,4},{4,6},{6,8},{8,10},{10,12},{12,14},{1,3},{3,5},{5,7},{... | collective-permute-start | bytes 491528 | tf_op jit(solution)/shard_map/ppermute | solution.py:476
  6.7 7.6 %collective-permute-start.1 = (bf16[1,640,128]{2,1,0:T(8,128)(2,1)S(1)}, bf16[1,640,128]{2,1,0:T(8,128)(2,1)S(1)}, u32[]{:S(2)}, u32[]{:S(2)}) collective-permute-start(bf16[1,640,128]{2,1,0:T(8,128)(2,1)S(1)} %get-tuple-element.51), channel_id=1, source_target_pairs={{2,0},{4,2},{6,4},{8,6},{10,8},{12,10},{14,12},{3,1},{5,3},{7,5},{... | collective-permute-start | bytes 491528 | tf_op jit(solution)/shard_map/ppermute | solution.py:477
  14.2 17.1 %copy-start.5 = (bf16[512,1280]{1,0:T(8,128)(2,1)S(1)}, bf16[512,1280]{1,0:T(8,128)(2,1)}, u32[]{:S(2)}) copy-start(bf16[512,1280]{1,0:T(8,128)(2,1)} %w_ref.1) | copy-start | bytes 3932164
  16.5 16.3 %collective-permute-start.6 = (bf16[6,640,128]{2,1,0:T(8,128)(2,1)}, bf16[6,640,128]{2,1,0:T(8,128)(2,1)}, u32[]{:S(2)}, u32[]{:S(2)}) collective-permute-start(bf16[6,640,128]{2,1,0:T(8,128)(2,1)} %pad_maximum_fusion.refs_0_), channel_id=1, source_target_pairs={{1,17},{16,0},{3,19},{18,2},{5,21},{20,4},{7,23},{22,6},{9,25},{24... | collective-permute-start | bytes 2949128 | tf_op jit(solution)/shard_map/ppermute | solution.py:68
  17.8 26.1 %collective-permute-start.4 = (bf16[2,512,512]{2,1,0:T(8,128)(2,1)}, bf16[2,512,512]{2,1,0:T(8,128)(2,1)}, u32[]{:S(2)}, u32[]{:S(2)}) collective-permute-start(bf16[2,512,512]{2,1,0:T(8,128)(2,1)} %bitcast.18), channel_id=1, source_target_pairs={{0,4},{4,8},{8,12},{12,14},{14,10},{10,6},{6,2},{2,0},{1,5},{5,9},... | collective-permute-start | bytes 3145736 | tf_op jit(solution)/shard_map/ppermute | solution.py:494
  20.7 24.8 %collective-permute-start.5 = (bf16[2,512,512]{2,1,0:T(8,128)(2,1)}, bf16[2,512,512]{2,1,0:T(8,128)(2,1)}, u32[]{:S(2)}, u32[]{:S(2)}) collective-permute-start(bf16[2,512,512]{2,1,0:T(8,128)(2,1)} %bitcast.18), channel_id=1, source_target_pairs={{4,0},{8,4},{12,8},{14,12},{10,14},{6,10},{2,6},{0,2},{5,1},{9,5},... | collective-permute-start | bytes 3145736 | tf_op jit(solution)/shard_map/ppermute | solution.py:494
  20.8 14.9 %collective-permute-start.3 = (bf16[4,640]{1,0:T(4,128)(2,1)S(1)}, bf16[4,640]{1,0:T(4,128)(2,1)S(1)}, u32[]{:S(2)}, u32[]{:S(2)}) collective-permute-start(bf16[4,640]{1,0:T(4,128)(2,1)S(1)} %pad_maximum_fusion.1), channel_id=1, source_target_pairs={{0,1},{1,0},{2,3},{3,2},{4,5},{5,4},{6,7},{7,6},{8,9},{9,8},{10,11... | collective-permute-start | bytes 15368 | tf_op jit(solution)/shard_map/ppermute | solution.py:30
  24.9 24.2 %all-to-all-start = ((f32[32,1,128]{2,1,0:T(1,128)}), f32[32,1,128]{2,1,0:T(1,128)S(1)}, u32[]{:S(2)}, u32[]{:S(2)}) async-start(f32[32,1,128]{2,1,0:T(1,128)} %broadcast_in_dim.21), calls=%async_computation | async-start | bytes 32768 | tf_op jit(solution)/shard_map/all_to_all | solution.py:53
  32.8 16.8 %collective-permute-start.7 = (bf16[6,640,128]{2,1,0:T(8,128)(2,1)}, bf16[6,640,128]{2,1,0:T(8,128)(2,1)}, u32[]{:S(2)}, u32[]{:S(2)}) collective-permute-start(bf16[6,640,128]{2,1,0:T(8,128)(2,1)} %collective-permute-done.6.refs_0_), channel_id=1, source_target_pairs={{0,1},{17,16},{2,3},{19,18},{4,5},{21,20},{6,7},{23,22},{8,9},{25,... | collective-permute-start | bytes 2949128 | tf_op jit(solution)/shard_map/ppermute | solution.py:71
  35.7 27.0 %collective-permute-start.2 = (bf16[6,640,128]{2,1,0:T(8,128)(2,1)}, bf16[6,640,128]{2,1,0:T(8,128)(2,1)}, u32[]{:S(2)}, u32[]{:S(2)}) collective-permute-start(bf16[6,640,128]{2,1,0:T(8,128)(2,1)} %pad_maximum_fusion.refs_0_), channel_id=1, source_target_pairs={{0,1},{17,16},{2,3},{19,18},{4,5},{21,20},{6,7},{23,22},{8,9},{25,... | collective-permute-start | bytes 2949128 | tf_op jit(solution)/shard_map/ppermute | solution.py:70
  43.9 34.7 %collective-permute-start.10 = (bf16[2,512,512]{2,1,0:T(8,128)(2,1)}, bf16[2,512,512]{2,1,0:T(8,128)(2,1)S(1)}, u32[]{:S(2)}, u32[]{:S(2)}) collective-permute-start(bf16[2,512,512]{2,1,0:T(8,128)(2,1)} %collective-permute-done.4.refs_3_.refs_4_), channel_id=1, source_target_pairs={{0,4},{4,8},{8,12},{12,14},{14,10},{10,6},{6,2},{2,0},{1,5},{5,9},... | collective-permute-start | bytes 3145736 | tf_op jit(solution)/shard_map/ppermute | solution.py:494
  45.4 33.1 %collective-permute-start.11 = (bf16[2,512,512]{2,1,0:T(8,128)(2,1)}, bf16[2,512,512]{2,1,0:T(8,128)(2,1)}, u32[]{:S(2)}, u32[]{:S(2)}) collective-permute-start(bf16[2,512,512]{2,1,0:T(8,128)(2,1)} %collective-permute-done.5.refs_5_.refs_6_), channel_id=1, source_target_pairs={{4,0},{8,4},{12,8},{14,12},{10,14},{6,10},{2,6},{0,2},{5,1},{9,5},... | collective-permute-start | bytes 3145736 | tf_op jit(solution)/shard_map/ppermute | solution.py:494
  49.6 13.1 %copy-start.9 = (bf16[640]{0:T(1024)(128)(2,1)S(1)}, bf16[640]{0:T(1024)(128)(2,1)}, u32[]{:S(2)}) copy-start(bf16[640]{0:T(1024)(128)(2,1)} %param.19) | copy-start | bytes 3844
  59.9 17.0 %collective-permute-start.8 = (bf16[4,640,128]{2,1,0:T(8,128)(2,1)}, bf16[4,640,128]{2,1,0:T(8,128)(2,1)S(1)}, u32[]{:S(2)}, u32[]{:S(2)}) collective-permute-start(bf16[4,640,128]{2,1,0:T(8,128)(2,1)} %norm_conv.3), channel_id=1, source_target_pairs={{0,16},{16,0},{1,17},{17,1},{2,18},{18,2},{3,19},{19,3},{4,20},{20... | collective-permute-start | bytes 1966088 | tf_op jit(solution)/shard_map/ppermute | solution.py:30
  62.7 14.2 %copy-start.7 = (bf16[1,4,640,128]{3,2,1,0:T(8,128)(2,1)S(1)}, bf16[1,4,640,128]{3,2,1,0:T(8,128)(2,1)}, u32[]{:S(2)}) copy-start(bf16[1,4,640,128]{3,2,1,0:T(8,128)(2,1)} %param.12) | copy-start | bytes 1966084
  78.5 4.2 %copy-start.1 = (bf16[4,640,128]{2,1,0:T(8,128)(2,1)}, bf16[4,640,128]{2,1,0:T(8,128)(2,1)S(1)}, u32[]{:S(2)}) copy-start(bf16[4,640,128]{2,1,0:T(8,128)(2,1)S(1)} %add_convert_fusion.own_ref.refs_0_) | copy-start | bytes 1966084
  78.6 25.6 %collective-permute-start.12 = (bf16[2,512,512]{2,1,0:T(8,128)(2,1)S(1)}, bf16[2,512,512]{2,1,0:T(8,128)(2,1)S(1)}, u32[]{:S(2)}, u32[]{:S(2)}) collective-permute-start(bf16[2,512,512]{2,1,0:T(8,128)(2,1)S(1)} %collective-permute-done.10.refs_1_.refs_2_), channel_id=1, source_target_pairs={{0,4},{4,8},{8,12},{12,14},{14,10},{10,6},{6,2},{2,0},{1,5},{5,9},... | collective-permute-start | bytes 3145736 | tf_op jit(solution)/shard_map/ppermute | solution.py:494
  80.2 25.1 %collective-permute-start.13 = (bf16[2,512,512]{2,1,0:T(8,128)(2,1)}, bf16[2,512,512]{2,1,0:T(8,128)(2,1)S(1)}, u32[]{:S(2)}, u32[]{:S(2)}) collective-permute-start(bf16[2,512,512]{2,1,0:T(8,128)(2,1)} %collective-permute-done.11.refs_3_.refs_4_), channel_id=1, source_target_pairs={{4,0},{8,4},{12,8},{14,12},{10,14},{6,10},{2,6},{0,2},{5,1},{9,5},... | collective-permute-start | bytes 3145736 | tf_op jit(solution)/shard_map/ppermute | solution.py:494
  80.6 2.1 %collective-permute-start.9 = (bf16[4,640,128]{2,1,0:T(8,128)(2,1)S(1)}, bf16[4,640,128]{2,1,0:T(8,128)(2,1)S(1)}, u32[]{:S(2)}, u32[]{:S(2)}) collective-permute-start(bf16[4,640,128]{2,1,0:T(8,128)(2,1)S(1)} %add_convert_fusion.own_ref.refs_0_), channel_id=1, source_target_pairs={{0,1},{1,0},{2,3},{3,2},{4,5},{5,4},{6,7},{7,6},{8,9},{9,8},{10,11... | collective-permute-start | bytes 1966088 | tf_op jit(solution)/shard_map/ppermute | solution.py:30
  82.7 0.9 copy-start.8
  91.9 1.0 copy-start.3
  93.0 1.2 copy-start.4
  105.4 14.7 %collective-permute-start.14 = (bf16[1,512,512]{2,1,0:T(8,128)(2,1)S(1)}, bf16[1,512,512]{2,1,0:T(8,128)(2,1)S(1)}, u32[]{:S(2)}, u32[]{:S(2)}) collective-permute-start(bf16[1,512,512]{2,1,0:T(8,128)(2,1)S(1)} %slice.34), channel_id=1, source_target_pairs={{0,4},{4,8},{8,12},{12,14},{14,10},{10,6},{6,2},{2,0},{1,5},{5,9},... | collective-permute-start | bytes 1572872 | tf_op jit(solution)/shard_map/ppermute | solution.py:494
  107.1 12.9 %collective-permute-start.15 = (bf16[1,512,512]{2,1,0:T(8,128)(2,1)S(1)}, bf16[1,512,512]{2,1,0:T(8,128)(2,1)S(1)}, u32[]{:S(2)}, u32[]{:S(2)}) collective-permute-start(bf16[1,512,512]{2,1,0:T(8,128)(2,1)S(1)} %slice.35), channel_id=1, source_target_pairs={{4,0},{8,4},{12,8},{14,12},{10,14},{6,10},{2,6},{0,2},{5,1},{9,5},... | collective-permute-start | bytes 1572872 | tf_op jit(solution)/shard_map/ppermute | solution.py:494
  120.1 5.6 %copy-start.2 = (bf16[4,640,128]{2,1,0:T(8,128)(2,1)S(1)}, bf16[4,640,128]{2,1,0:T(8,128)(2,1)}, u32[]{:S(2)}) copy-start(bf16[4,640,128]{2,1,0:T(8,128)(2,1)} %copy-done.1) | copy-start | bytes 1966084
  125.5 2.2 %collective-permute-start.16 = (bf16[2,4,320,128]{3,2,1,0:T(8,128)(2,1)S(1)}, bf16[2,4,320,128]{3,2,1,0:T(8,128)(2,1)S(1)}, u32[]{:S(2)}, u32[]{:S(2)}) collective-permute-start(bf16[2,4,320,128]{3,2,1,0:T(8,128)(2,1)S(1)} %get-tuple-element.37), channel_id=1, source_target_pairs={{0,1},{1,0},{2,3},{3,2},{4,5},{5,4},{6,7},{7,6},{8,9},{9,8},{10,11... | collective-permute-start | bytes 1966088 | tf_op jit(solution)/shard_map/ppermute | solution.py:30
  127.8 9.9 %collective-permute-start.17 = (bf16[4,320,128]{2,1,0:T(8,128)(2,1)S(1)}, bf16[4,320,128]{2,1,0:T(8,128)(2,1)}, u32[]{:S(2)}, u32[]{:S(2)}) collective-permute-start(bf16[4,320,128]{2,1,0:T(8,128)(2,1)S(1)} %branch_out.2), channel_id=1, source_target_pairs={{0,16},{16,0},{1,17},{17,1},{2,18},{18,2},{3,19},{19,3},{4,20},{20... | collective-permute-start | bytes 983048 | tf_op jit(solution)/shard_map/ppermute | solution.py:30

commit v13 on v12

--- a/solution.py
+++ b/solution.py
@@ -314,7 +314,7 @@
     else:
         m_out, acc_out = refs[at:]
     positions = q_ref.shape[0]
-    tile = min(256, positions)
+    tile = min(512, positions)
     starts = range(0, positions, tile)
     lanes = lambda array, low: (lax.broadcasted_iota(jnp.int32, array.shape, 1) < HD) == low
 

time: 140 us -> 139 us (level)
  Pallas kernels: 59.7 us -> 57.8 us
    pallas_call x3, Pallas kernels: 28 us -> 26.1 us  [attention_call(): pl.pallas_call(functools.partial(attention_kernel, len(pairs), state is n...]
  transfers between devices with their start and end apart: 19 -> 19, of which waited for: 11 -> 12; matrix products, arithmetic and copies ran while one was open for 5% -> 5% of each run, Pallas kernels for 39% -> 38%
where the time goes in v13:
time: 139 us
  Pallas kernels  57.8 us (42%)
  waiting for transfers between devices  32 us (23%)
  starting transfers between devices  31.2 us (22%)
  other arithmetic  8.21 us (6%)
  local copies, waits for them, and re-layouts  7.41 us (5%)
  between operations  1.72 us (1%)
    pallas_call x3, Pallas kernels, attention_call(): pl.pallas_call(functools.partial(attention_kernel, len(pairs), state is n...  26.1 us
    pallas_call x2, Pallas kernels, conv_call(): pl.pallas_call(functools.partial(conv_kernel, len(xs), amount), in_specs=...  21 us
    ppermute x5, waiting for transfers between devices, swapped(): lax.ppermute(array, axis, [(i, i ^ 1) for i in range(lax.axis_size(axis))])  16.4 us
    pallas_call x1, Pallas kernels, project_call(): pl.pallas_call(functools.partial(project_kernel, len(parts)), in_specs=[p...  8.31 us
    ppermute x4, starting transfers between devices, next_hop(): lax.ppermute(ahead, 'rows', forward)  7.59 us
    ppermute x4, waiting for transfers between devices, next_hop(): lax.ppermute(ahead, 'rows', forward)  5.85 us
    all_to_all x1, starting transfers between devices, summed(): return jnp.sum(lax.all_to_all(spread, axes, 0, 0, tiled=True), axis=0)  5.15 us
    ppermute x1, starting transfers between devices, per_device(): before = lax.ppermute(latent_rows[span_rows - 1:], 'rows', up_pairs)  4.85 us
  transfers between devices with their start and end apart: 19, of which 12 were waited for; matrix products, arithmetic and copies ran while one was open for 5% of the time, Pallas kernels for 38%

profile of v13, /device:TPU:0, one launch (start us, length us, event | category | flops | bytes accessed | tf_op | source)
XLA Modules:
  0.0 138.7 jit_solution(929357744745961345)
XLA Ops:
  0.6 0.0 copy-start
  0.6 0.0 copy-start.6
  0.7 1.1 slice_bitcast_fusion.1
  1.8 4.9 %collective-permute-start = (bf16[1,640,128]{2,1,0:T(8,128)(2,1)S(1)}, bf16[1,640,128]{2,1,0:T(8,128)(2,1)S(1)}, u32[]{:S(2)}, u32[]{:S(2)}) collective-permute-start(bf16[1,640,128]{2,1,0:T(8,128)(2,1)S(1)} %get-tuple-element.50), channel_id=1, source_target_pairs={{0,2},{2,4},{4,6},{6,8},{8,10},{10,12},{12,14},{1,3},{3,5},{5,7},{... | collective-permute-start | bytes 491528 | tf_op jit(solution)/shard_map/ppermute | solution.py:476
  6.7 1.3 collective-permute-start.1
  8.0 2.1 %collective-permute-done = bf16[1,640,128]{2,1,0:T(8,128)(2,1)S(1)} collective-permute-done((bf16[1,640,128]{2,1,0:T(8,128)(2,1)S(1)}, bf16[1,640,128]{2,1,0:T(8,128)(2,1)S(1)}, u32[]{:S(2)}, u32[]{:S(2)}) %collective-permute-start) | collective-permute-done | bytes 163872 | tf_op jit(solution)/shard_map/ppermute | solution.py:476
  10.1 4.1 %collective-permute-done.1 = bf16[1,640,128]{2,1,0:T(8,128)(2,1)S(1)} collective-permute-done((bf16[1,640,128]{2,1,0:T(8,128)(2,1)S(1)}, bf16[1,640,128]{2,1,0:T(8,128)(2,1)S(1)}, u32[]{:S(2)}, u32[]{:S(2)}) %collective-permute-start.1) | collective-permute-done | bytes 163872 | tf_op jit(solution)/shard_map/ppermute | solution.py:477
  14.2 2.3 %pad_maximum_fusion.refs_0_ = bf16[6,640,128]{2,1,0:T(8,128)(2,1)} fusion(bf16[1,640,128]{2,1,0:T(8,128)(2,1)S(1)} %collective-permute-done.1, bf16[4,640,128]{2,1,0:T(8,128)(2,1)} %bitcast.34, bf16[1,640,128]{2,1,0:T(8,128)(2,1)S(1)} %collective-permute-done), kind=kLoop, calls=%fused_computation.5 | loop fusion | flops 983040 | bytes 1966080 | tf_op jit(solution)/shard_map/concatenate | solution.py:478
  16.5 1.3 collective-permute-start.6
  17.8 2.9 %collective-permute-start.4 = (bf16[2,512,512]{2,1,0:T(8,128)(2,1)}, bf16[2,512,512]{2,1,0:T(8,128)(2,1)}, u32[]{:S(2)}, u32[]{:S(2)}) collective-permute-start(bf16[2,512,512]{2,1,0:T(8,128)(2,1)} %bitcast.18), channel_id=1, source_target_pairs={{0,4},{4,8},{8,12},{12,14},{14,10},{10,6},{6,2},{2,0},{1,5},{5,9},... | collective-permute-start | bytes 3145736 | tf_op jit(solution)/shard_map/ppermute | solution.py:494
  20.8 2.5 %collective-permute-start.3 = (bf16[4,640]{1,0:T(4,128)(2,1)S(1)}, bf16[4,640]{1,0:T(4,128)(2,1)S(1)}, u32[]{:S(2)}, u32[]{:S(2)}) collective-permute-start(bf16[4,640]{1,0:T(4,128)(2,1)S(1)} %pad_maximum_fusion.1), channel_id=1, source_target_pairs={{0,1},{1,0},{2,3},{3,2},{4,5},{5,4},{6,7},{7,6},{8,9},{9,8},{10,11... | collective-permute-start | bytes 15368 | tf_op jit(solution)/shard_map/ppermute | solution.py:30
  23.3 0.3 convert_reduce_fusion
  23.6 0.1 reduce_sum.32
  23.7 0.1 reduce_sum.45
  23.8 0.1 reduce_sum.36
  23.9 0.1 reduce_sum.46
  24.0 0.1 dynamic_update_slice.3
  24.2 0.1 broadcast_in_dim.20
  24.2 0.6 broadcast_in_dim.21
  24.9 5.1 %all-to-all-start = ((f32[32,1,128]{2,1,0:T(1,128)}), f32[32,1,128]{2,1,0:T(1,128)S(1)}, u32[]{:S(2)}, u32[]{:S(2)}) async-start(f32[32,1,128]{2,1,0:T(1,128)} %broadcast_in_dim.21), calls=%async_computation | async-start | bytes 32768 | tf_op jit(solution)/shard_map/all_to_all | solution.py:53
  30.0 0.1 add_convert_fusion.1
  30.1 0.7 pad_add_fusion.2
  30.8 0.6 pad_add_fusion.1.order_ref
  31.3 1.2 arrange.1.refs_5_
  32.5 0.2 collective-permute-done.6.refs_0_
  32.8 2.9 %collective-permute-start.7 = (bf16[6,640,128]{2,1,0:T(8,128)(2,1)}, bf16[6,640,128]{2,1,0:T(8,128)(2,1)}, u32[]{:S(2)}, u32[]{:S(2)}) collective-permute-start(bf16[6,640,128]{2,1,0:T(8,128)(2,1)} %collective-permute-done.6.refs_0_), channel_id=1, source_target_pairs={{0,1},{17,16},{2,3},{19,18},{4,5},{21,20},{6,7},{23,22},{8,9},{25,... | collective-permute-start | bytes 2949128 | tf_op jit(solution)/shard_map/ppermute | solution.py:71
  35.7 2.3 %collective-permute-start.2 = (bf16[6,640,128]{2,1,0:T(8,128)(2,1)}, bf16[6,640,128]{2,1,0:T(8,128)(2,1)}, u32[]{:S(2)}, u32[]{:S(2)}) collective-permute-start(bf16[6,640,128]{2,1,0:T(8,128)(2,1)} %pad_maximum_fusion.refs_0_), channel_id=1, source_target_pairs={{0,1},{17,16},{2,3},{19,18},{4,5},{21,20},{6,7},{23,22},{8,9},{25,... | collective-permute-start | bytes 2949128 | tf_op jit(solution)/shard_map/ppermute | solution.py:70
  38.0 5.8 %collective-permute-done.4.refs_3_.refs_4_ = bf16[2,512,512]{2,1,0:T(8,128)(2,1)} collective-permute-done((bf16[2,512,512]{2,1,0:T(8,128)(2,1)}, bf16[2,512,512]{2,1,0:T(8,128)(2,1)}, u32[]{:S(2)}, u32[]{:S(2)}) %collective-permute-start.4) | collective-permute-done | bytes 1048608 | tf_op jit(solution)/shard_map/ppermute | solution.py:494
  43.9 1.3 collective-permute-start.10
  45.2 0.3 collective-permute-done.5.refs_5_.refs_6_
  45.4 0.8 collective-permute-start.11
  46.2 0.9 copy.30
  47.1 1.1 copy.28
  48.2 0.8 all-to-all-done
  49.1 0.5 reduce_sum.47.sums_ref
  49.6 10.3 %norm_conv.3 = bf16[4,640,128]{2,1,0:T(8,128)(2,1)} custom-call(s32[4]{0:T(128)} %get-tuple-element.21.flags_ref, f32[128]{0:T(128)} %reduce_sum.47.sums_ref, bf16[6,640,128]{2,1,0:T(8,128)(2,1)} %collective-permute-done.6.refs_0_, bf16[6,640,128]{2,1,0:T(8,128)(2,1)} %collective-permute-done.7.refs_1_, f32[640,2]{1,0:T(8,128)} %bitcast.36, ...), custom_call_target="tpu_custom_call" | custom-call | flops 180000000 | bytes 1000 | tf_op jit(solution)/shard_map/norm_conv/pallas_call | solution.py:141
  59.9 1.6 %collective-permute-start.8 = (bf16[4,640,128]{2,1,0:T(8,128)(2,1)}, bf16[4,640,128]{2,1,0:T(8,128)(2,1)S(1)}, u32[]{:S(2)}, u32[]{:S(2)}) collective-permute-start(bf16[4,640,128]{2,1,0:T(8,128)(2,1)} %norm_conv.3), channel_id=1, source_target_pairs={{0,16},{16,0},{1,17},{17,1},{2,18},{18,2},{3,19},{19,3},{4,20},{20... | collective-permute-start | bytes 1966088 | tf_op jit(solution)/shard_map/ppermute | solution.py:30
  62.3 0.1 divide_multiply_fusion
  62.4 0.3 convolution_reduce_fusion
  62.7 10.6 %norm_conv.2 = f32[4,640,128]{2,1,0:T(8,128)} custom-call(s32[4]{0:T(128)} %get-tuple-element.57.flags_ref, f32[128]{0:T(128)} %reduce_sum.47.sums_ref, bf16[6,640,128]{2,1,0:T(8,128)(2,1)} %pad_maximum_fusion.refs_0_, bf16[6,640,128]{2,1,0:T(8,128)(2,1)} %collective-permute-done.2.refs_1_, f32[640,2]{1,0:T(8,128)} %bitcast.37, bf16[3,3,640,640]{3,2,1,0:T(8,128)(2,1)} %refs_3_.3), custom_call_target="tpu_custom_call" | custom-call | flops 180000000 | bytes 1000 | tf_op jit(solution)/shard_map/norm_conv/pallas_call | solution.py:141
  73.4 3.6 %collective-permute-done.8 = bf16[4,640,128]{2,1,0:T(8,128)(2,1)S(1)} collective-permute-done((bf16[4,640,128]{2,1,0:T(8,128)(2,1)}, bf16[4,640,128]{2,1,0:T(8,128)(2,1)S(1)}, u32[]{:S(2)}, u32[]{:S(2)}) %collective-permute-start.8) | collective-permute-done | bytes 655392 | tf_op jit(solution)/shard_map/ppermute | solution.py:30
  76.9 1.6 %add_convert_fusion.own_ref.refs_0_ = bf16[4,640,128]{2,1,0:T(8,128)(2,1)S(1)} fusion(f32[4,640,128]{2,1,0:T(8,128)} %norm_conv.2, bf16[4,640,128]{2,1,0:T(8,128)(2,1)S(1)} %collective-permute-done.8, f32[640]{0:T(1024)S(1)} %convert_add_fusion.1, bf16[1,4,640,128]{3,2,1,0:T(8,128)(2,1)S(1)} %copy-done.7), kind=kLoop, calls=%fused_computation.3 | loop fusion | flops 1966080 | bytes 3279360 | tf_op jit(solution)/shard_map/convert_element_type | solution.py:542
  78.6 1.7 %collective-permute-start.12 = (bf16[2,512,512]{2,1,0:T(8,128)(2,1)S(1)}, bf16[2,512,512]{2,1,0:T(8,128)(2,1)S(1)}, u32[]{:S(2)}, u32[]{:S(2)}) collective-permute-start(bf16[2,512,512]{2,1,0:T(8,128)(2,1)S(1)} %collective-permute-done.10.refs_1_.refs_2_), channel_id=1, source_target_pairs={{0,4},{4,8},{8,12},{12,14},{14,10},{10,6},{6,2},{2,0},{1,5},{5,9},... | collective-permute-start | bytes 3145736 | tf_op jit(solution)/shard_map/ppermute | solution.py:494
  80.2 0.4 collective-permute-start.13
  80.7 2.1 %collective-permute-done.9.refs_1_ = bf16[4,640,128]{2,1,0:T(8,128)(2,1)S(1)} collective-permute-done((bf16[4,640,128]{2,1,0:T(8,128)(2,1)S(1)}, bf16[4,640,128]{2,1,0:T(8,128)(2,1)S(1)}, u32[]{:S(2)}, u32[]{:S(2)}) %collective-permute-start.9) | collective-permute-done | bytes 655392 | tf_op jit(solution)/shard_map/ppermute | solution.py:30
  82.8 0.9 copy-done.8
  83.6 8.3 %norm_project.1 = (bf16[512,512]{1,0:T(8,128)(2,1)}, bf16[2,512,512]{2,1,0:T(8,128)(2,1)}) custom-call(s32[2]{0:T(128)} %pad_add_fusion.1.order_ref, bf16[4,640,128]{2,1,0:T(8,128)(2,1)} %copy-done.1, bf16[4,640,128]{2,1,0:T(8,128)(2,1)} %copy-done.8, f32[1280,2]{1,0:T(8,128)} %bitcast.38, bf16[3,1280,512]{2,1,0:T(8,128)(2,1)} %bitcast.35), custom_call_target="tpu_custom_call" | custom-call | flops 130000000 | bytes 1000 | tf_op jit(solution)/shard_map/norm_project/pallas_call | solution.py:254
  91.9 1.0 copy-done.3
  93.0 1.2 copy-done.4
  94.2 9.3 %attend.3 = (f32[4,2,512,128]{3,2,1,0:T(8,128)S(1)}, f32[4,2,512,128]{3,2,1,0:T(8,128)S(1)}) custom-call(bf16[512,512]{1,0:T(8,128)(2,1)S(1)} %copy-done.3, bf16[2,512,512]{2,1,0:T(8,128)(2,1)S(1)} %copy-done.4, bf16[2,512,512]{2,1,0:T(8,128)(2,1)S(1)} %copy-done.4, bf16[2,512,512]{2,1,0:T(8,128)(2,1)} %collective-permute-done.4.refs_3_.refs_4_, ...), custom_call_target="tpu_custom_call" | custom-call | flops 212000000 | bytes 1000 | tf_op jit(solution)/shard_map/attend/pallas_call | solution.py:427
  103.6 1.8 %collective-permute-done.13.refs_7_.refs_8_ = bf16[2,512,512]{2,1,0:T(8,128)(2,1)S(1)} collective-permute-done((bf16[2,512,512]{2,1,0:T(8,128)(2,1)}, bf16[2,512,512]{2,1,0:T(8,128)(2,1)S(1)}, u32[]{:S(2)}, u32[]{:S(2)}) %collective-permute-start.13) | collective-permute-done | bytes 1048608 | tf_op jit(solution)/shard_map/ppermute | solution.py:494
  105.4 1.7 %collective-permute-start.14 = (bf16[1,512,512]{2,1,0:T(8,128)(2,1)S(1)}, bf16[1,512,512]{2,1,0:T(8,128)(2,1)S(1)}, u32[]{:S(2)}, u32[]{:S(2)}) collective-permute-start(bf16[1,512,512]{2,1,0:T(8,128)(2,1)S(1)} %slice.34), channel_id=1, source_target_pairs={{0,4},{4,8},{8,12},{12,14},{14,10},{10,6},{6,2},{2,0},{1,5},{5,9},... | collective-permute-start | bytes 1572872 | tf_op jit(solution)/shard_map/ppermute | solution.py:494
  107.1 0.3 collective-permute-start.15
  107.5 11.8 %attend.4 = (f32[4,2,512,128]{3,2,1,0:T(8,128)S(1)}, f32[4,2,512,128]{3,2,1,0:T(8,128)S(1)}) custom-call(bf16[512,512]{1,0:T(8,128)(2,1)S(1)} %copy-done.3, bf16[2,512,512]{2,1,0:T(8,128)(2,1)S(1)} %collective-permute-done.10.refs_1_.refs_2_, bf16[2,512,512]{2,1,0:T(8,128)(2,1)S(1)} %collective-permute-done.10.refs_1_.refs_2_, ...), custom_call_target="tpu_custom_call" | custom-call | flops 276000000 | bytes 1000 | tf_op jit(solution)/shard_map/attend/pallas_call | solution.py:427
  119.3 0.4 collective-permute-done.15.refs_2_
  119.7 5.0 %attend.5 = (bf16[2,4,320,128]{3,2,1,0:T(8,128)(2,1)S(1)}, f32[2,4,320,128]{3,2,1,0:T(8,128)S(1)}) custom-call(bf16[512,512]{1,0:T(8,128)(2,1)S(1)} %copy-done.3, bf16[1,512,512]{2,1,0:T(8,128)(2,1)S(1)} %collective-permute-done.14.refs_1_, bf16[1,512,512]{2,1,0:T(8,128)(2,1)S(1)} %collective-permute-done.15.refs_2_, ...), custom_call_target="tpu_custom_call" | custom-call | flops 84000000 | bytes 1000 | tf_op jit(solution)/shard_map/attend/pallas_call | solution.py:427
  124.7 0.1 collective-permute-start.16
  124.8 1.0 parity_split.1.resid_ref
  125.8 1.1 collective-permute-done.16.refs_1_
  126.8 0.1 branch_out.2
  126.9 0.1 collective-permute-start.17
  127.0 0.1 branch_out.3
  127.1 9.7 %collective-permute-done.17 = bf16[4,320,128]{2,1,0:T(8,128)(2,1)} collective-permute-done((bf16[4,320,128]{2,1,0:T(8,128)(2,1)S(1)}, bf16[4,320,128]{2,1,0:T(8,128)(2,1)}, u32[]{:S(2)}, u32[]{:S(2)}) %collective-permute-start.17) | collective-permute-done | bytes 327712 | tf_op jit(solution)/shard_map/ppermute | solution.py:30
  136.9 1.9 %fusion.3 = bf16[4,320,1,128]{3,1,2,0:T(8,128)(2,1)} fusion(bf16[4,320,128]{2,1,0:T(8,128)(2,1)S(1)} %branch_out.3, bf16[4,320,128]{2,1,0:T(8,128)(2,1)} %collective-permute-done.17, pred[]{:T(512)S(6)} %eq.10), kind=kLoop, calls=%fused_computation.10 | loop fusion | flops 1310720 | bytes 983041
  (48 shorter events, 0.3 us)
Async XLA Ops:
  0.6 61.7 %copy-start = (bf16[320,640]{1,0:T(8,128)(2,1)S(1)}, bf16[320,640]{1,0:T(8,128)(2,1)}, u32[]{:S(2)}) copy-start(bf16[320,640]{1,0:T(8,128)(2,1)} %param.15) | copy-start | bytes 1228804
  0.6 22.7 %copy-start.6 = (bf16[1,4,640,128]{3,2,1,0:T(8,128)(2,1)S(1)}, bf16[1,4,640,128]{3,2,1,0:T(8,128)(2,1)}, u32[]{:S(2)}) copy-start(bf16[1,4,640,128]{3,2,1,0:T(8,128)(2,1)} %param.12) | copy-start | bytes 1966084
  0.7 20.0 %copy-start.10 = (bf16[640]{0:T(1024)(128)(2,1)S(1)}, bf16[640]{0:T(1024)(128)(2,1)}, u32[]{:S(2)}) copy-start(bf16[640]{0:T(1024)(128)(2,1)} %param.16) | copy-start | bytes 3844
  0.7 20.0 %copy-start.11 = (bf16[640]{0:T(1024)(128)(2,1)S(1)}, bf16[640]{0:T(1024)(128)(2,1)}, u32[]{:S(2)}) copy-start(bf16[640]{0:T(1024)(128)(2,1)} %param.17) | copy-start | bytes 3844
  0.7 20.0 %copy-start.12 = (bf16[640]{0:T(1024)(128)(2,1)S(1)}, bf16[640]{0:T(1024)(128)(2,1)}, u32[]{:S(2)}) copy-start(bf16[640]{0:T(1024)(128)(2,1)} %param.20) | copy-start | bytes 3844
  0.7 20.0 %copy-start.13 = (bf16[640]{0:T(1024)(128)(2,1)S(1)}, bf16[640]{0:T(1024)(128)(2,1)}, u32[]{:S(2)}) copy-start(bf16[640]{0:T(1024)(128)(2,1)} %param.21) | copy-start | bytes 3844
  1.8 8.3 %collective-permute-start = (bf16[1,640,128]{2,1,0:T(8,128)(2,1)S(1)}, bf16[1,640,128]{2,1,0:T(8,128)(2,1)S(1)}, u32[]{:S(2)}, u32[]{:S(2)}) collective-permute-start(bf16[1,640,128]{2,1,0:T(8,128)(2,1)S(1)} %get-tuple-element.50), channel_id=1, source_target_pairs={{0,2},{2,4},{4,6},{6,8},{8,10},{10,12},{12,14},{1,3},{3,5},{5,7},{... | collective-permute-start | bytes 491528 | tf_op jit(solution)/shard_map/ppermute | solution.py:476
  6.7 7.6 %collective-permute-start.1 = (bf16[1,640,128]{2,1,0:T(8,128)(2,1)S(1)}, bf16[1,640,128]{2,1,0:T(8,128)(2,1)S(1)}, u32[]{:S(2)}, u32[]{:S(2)}) collective-permute-start(bf16[1,640,128]{2,1,0:T(8,128)(2,1)S(1)} %get-tuple-element.51), channel_id=1, source_target_pairs={{2,0},{4,2},{6,4},{8,6},{10,8},{12,10},{14,12},{3,1},{5,3},{7,5},{... | collective-permute-start | bytes 491528 | tf_op jit(solution)/shard_map/ppermute | solution.py:477
  14.2 17.1 %copy-start.5 = (bf16[512,1280]{1,0:T(8,128)(2,1)S(1)}, bf16[512,1280]{1,0:T(8,128)(2,1)}, u32[]{:S(2)}) copy-start(bf16[512,1280]{1,0:T(8,128)(2,1)} %w_ref.1) | copy-start | bytes 3932164
  16.5 16.3 %collective-permute-start.6 = (bf16[6,640,128]{2,1,0:T(8,128)(2,1)}, bf16[6,640,128]{2,1,0:T(8,128)(2,1)}, u32[]{:S(2)}, u32[]{:S(2)}) collective-permute-start(bf16[6,640,128]{2,1,0:T(8,128)(2,1)} %pad_maximum_fusion.refs_0_), channel_id=1, source_target_pairs={{1,17},{16,0},{3,19},{18,2},{5,21},{20,4},{7,23},{22,6},{9,25},{24... | collective-permute-start | bytes 2949128 | tf_op jit(solution)/shard_map/ppermute | solution.py:68
  17.8 26.1 %collective-permute-start.4 = (bf16[2,512,512]{2,1,0:T(8,128)(2,1)}, bf16[2,512,512]{2,1,0:T(8,128)(2,1)}, u32[]{:S(2)}, u32[]{:S(2)}) collective-permute-start(bf16[2,512,512]{2,1,0:T(8,128)(2,1)} %bitcast.18), channel_id=1, source_target_pairs={{0,4},{4,8},{8,12},{12,14},{14,10},{10,6},{6,2},{2,0},{1,5},{5,9},... | collective-permute-start | bytes 3145736 | tf_op jit(solution)/shard_map/ppermute | solution.py:494
  20.7 24.8 %collective-permute-start.5 = (bf16[2,512,512]{2,1,0:T(8,128)(2,1)}, bf16[2,512,512]{2,1,0:T(8,128)(2,1)}, u32[]{:S(2)}, u32[]{:S(2)}) collective-permute-start(bf16[2,512,512]{2,1,0:T(8,128)(2,1)} %bitcast.18), channel_id=1, source_target_pairs={{4,0},{8,4},{12,8},{14,12},{10,14},{6,10},{2,6},{0,2},{5,1},{9,5},... | collective-permute-start | bytes 3145736 | tf_op jit(solution)/shard_map/ppermute | solution.py:494
  20.8 14.9 %collective-permute-start.3 = (bf16[4,640]{1,0:T(4,128)(2,1)S(1)}, bf16[4,640]{1,0:T(4,128)(2,1)S(1)}, u32[]{:S(2)}, u32[]{:S(2)}) collective-permute-start(bf16[4,640]{1,0:T(4,128)(2,1)S(1)} %pad_maximum_fusion.1), channel_id=1, source_target_pairs={{0,1},{1,0},{2,3},{3,2},{4,5},{5,4},{6,7},{7,6},{8,9},{9,8},{10,11... | collective-permute-start | bytes 15368 | tf_op jit(solution)/shard_map/ppermute | solution.py:30
  24.9 24.2 %all-to-all-start = ((f32[32,1,128]{2,1,0:T(1,128)}), f32[32,1,128]{2,1,0:T(1,128)S(1)}, u32[]{:S(2)}, u32[]{:S(2)}) async-start(f32[32,1,128]{2,1,0:T(1,128)} %broadcast_in_dim.21), calls=%async_computation | async-start | bytes 32768 | tf_op jit(solution)/shard_map/all_to_all | solution.py:53
  32.8 16.8 %collective-permute-start.7 = (bf16[6,640,128]{2,1,0:T(8,128)(2,1)}, bf16[6,640,128]{2,1,0:T(8,128)(2,1)}, u32[]{:S(2)}, u32[]{:S(2)}) collective-permute-start(bf16[6,640,128]{2,1,0:T(8,128)(2,1)} %collective-permute-done.6.refs_0_), channel_id=1, source_target_pairs={{0,1},{17,16},{2,3},{19,18},{4,5},{21,20},{6,7},{23,22},{8,9},{25,... | collective-permute-start | bytes 2949128 | tf_op jit(solution)/shard_map/ppermute | solution.py:71
  35.7 27.0 %collective-permute-start.2 = (bf16[6,640,128]{2,1,0:T(8,128)(2,1)}, bf16[6,640,128]{2,1,0:T(8,128)(2,1)}, u32[]{:S(2)}, u32[]{:S(2)}) collective-permute-start(bf16[6,640,128]{2,1,0:T(8,128)(2,1)} %pad_maximum_fusion.refs_0_), channel_id=1, source_target_pairs={{0,1},{17,16},{2,3},{19,18},{4,5},{21,20},{6,7},{23,22},{8,9},{25,... | collective-permute-start | bytes 2949128 | tf_op jit(solution)/shard_map/ppermute | solution.py:70
  43.9 34.7 %collective-permute-start.10 = (bf16[2,512,512]{2,1,0:T(8,128)(2,1)}, bf16[2,512,512]{2,1,0:T(8,128)(2,1)S(1)}, u32[]{:S(2)}, u32[]{:S(2)}) collective-permute-start(bf16[2,512,512]{2,1,0:T(8,128)(2,1)} %collective-permute-done.4.refs_3_.refs_4_), channel_id=1, source_target_pairs={{0,4},{4,8},{8,12},{12,14},{14,10},{10,6},{6,2},{2,0},{1,5},{5,9},... | collective-permute-start | bytes 3145736 | tf_op jit(solution)/shard_map/ppermute | solution.py:494
  45.4 33.1 %collective-permute-start.11 = (bf16[2,512,512]{2,1,0:T(8,128)(2,1)}, bf16[2,512,512]{2,1,0:T(8,128)(2,1)}, u32[]{:S(2)}, u32[]{:S(2)}) collective-permute-start(bf16[2,512,512]{2,1,0:T(8,128)(2,1)} %collective-permute-done.5.refs_5_.refs_6_), channel_id=1, source_target_pairs={{4,0},{8,4},{12,8},{14,12},{10,14},{6,10},{2,6},{0,2},{5,1},{9,5},... | collective-permute-start | bytes 3145736 | tf_op jit(solution)/shard_map/ppermute | solution.py:494
  49.6 13.1 %copy-start.9 = (bf16[640]{0:T(1024)(128)(2,1)S(1)}, bf16[640]{0:T(1024)(128)(2,1)}, u32[]{:S(2)}) copy-start(bf16[640]{0:T(1024)(128)(2,1)} %param.19) | copy-start | bytes 3844
  59.9 17.0 %collective-permute-start.8 = (bf16[4,640,128]{2,1,0:T(8,128)(2,1)}, bf16[4,640,128]{2,1,0:T(8,128)(2,1)S(1)}, u32[]{:S(2)}, u32[]{:S(2)}) collective-permute-start(bf16[4,640,128]{2,1,0:T(8,128)(2,1)} %norm_conv.3), channel_id=1, source_target_pairs={{0,16},{16,0},{1,17},{17,1},{2,18},{18,2},{3,19},{19,3},{4,20},{20... | collective-permute-start | bytes 1966088 | tf_op jit(solution)/shard_map/ppermute | solution.py:30
  62.7 14.2 %copy-start.7 = (bf16[1,4,640,128]{3,2,1,0:T(8,128)(2,1)S(1)}, bf16[1,4,640,128]{3,2,1,0:T(8,128)(2,1)}, u32[]{:S(2)}) copy-start(bf16[1,4,640,128]{3,2,1,0:T(8,128)(2,1)} %param.12) | copy-start | bytes 1966084
  78.5 4.2 %copy-start.1 = (bf16[4,640,128]{2,1,0:T(8,128)(2,1)}, bf16[4,640,128]{2,1,0:T(8,128)(2,1)S(1)}, u32[]{:S(2)}) copy-start(bf16[4,640,128]{2,1,0:T(8,128)(2,1)S(1)} %add_convert_fusion.own_ref.refs_0_) | copy-start | bytes 1966084
  78.6 24.9 %collective-permute-start.12 = (bf16[2,512,512]{2,1,0:T(8,128)(2,1)S(1)}, bf16[2,512,512]{2,1,0:T(8,128)(2,1)S(1)}, u32[]{:S(2)}, u32[]{:S(2)}) collective-permute-start(bf16[2,512,512]{2,1,0:T(8,128)(2,1)S(1)} %collective-permute-done.10.refs_1_.refs_2_), channel_id=1, source_target_pairs={{0,4},{4,8},{8,12},{12,14},{14,10},{10,6},{6,2},{2,0},{1,5},{5,9},... | collective-permute-start | bytes 3145736 | tf_op jit(solution)/shard_map/ppermute | solution.py:494
  80.2 25.1 %collective-permute-start.13 = (bf16[2,512,512]{2,1,0:T(8,128)(2,1)}, bf16[2,512,512]{2,1,0:T(8,128)(2,1)S(1)}, u32[]{:S(2)}, u32[]{:S(2)}) collective-permute-start(bf16[2,512,512]{2,1,0:T(8,128)(2,1)} %collective-permute-done.11.refs_3_.refs_4_), channel_id=1, source_target_pairs={{4,0},{8,4},{12,8},{14,12},{10,14},{6,10},{2,6},{0,2},{5,1},{9,5},... | collective-permute-start | bytes 3145736 | tf_op jit(solution)/shard_map/ppermute | solution.py:494
  80.6 2.1 %collective-permute-start.9 = (bf16[4,640,128]{2,1,0:T(8,128)(2,1)S(1)}, bf16[4,640,128]{2,1,0:T(8,128)(2,1)S(1)}, u32[]{:S(2)}, u32[]{:S(2)}) collective-permute-start(bf16[4,640,128]{2,1,0:T(8,128)(2,1)S(1)} %add_convert_fusion.own_ref.refs_0_), channel_id=1, source_target_pairs={{0,1},{1,0},{2,3},{3,2},{4,5},{5,4},{6,7},{7,6},{8,9},{9,8},{10,11... | collective-permute-start | bytes 1966088 | tf_op jit(solution)/shard_map/ppermute | solution.py:30
  82.7 0.9 copy-start.8
  91.9 1.0 copy-start.3
  93.0 1.2 copy-start.4
  105.4 13.9 %collective-permute-start.14 = (bf16[1,512,512]{2,1,0:T(8,128)(2,1)S(1)}, bf16[1,512,512]{2,1,0:T(8,128)(2,1)S(1)}, u32[]{:S(2)}, u32[]{:S(2)}) collective-permute-start(bf16[1,512,512]{2,1,0:T(8,128)(2,1)S(1)} %slice.34), channel_id=1, source_target_pairs={{0,4},{4,8},{8,12},{12,14},{14,10},{10,6},{6,2},{2,0},{1,5},{5,9},... | collective-permute-start | bytes 1572872 | tf_op jit(solution)/shard_map/ppermute | solution.py:494
  107.1 12.5 %collective-permute-start.15 = (bf16[1,512,512]{2,1,0:T(8,128)(2,1)S(1)}, bf16[1,512,512]{2,1,0:T(8,128)(2,1)S(1)}, u32[]{:S(2)}, u32[]{:S(2)}) collective-permute-start(bf16[1,512,512]{2,1,0:T(8,128)(2,1)S(1)} %slice.35), channel_id=1, source_target_pairs={{4,0},{8,4},{12,8},{14,12},{10,14},{6,10},{2,6},{0,2},{5,1},{9,5},... | collective-permute-start | bytes 1572872 | tf_op jit(solution)/shard_map/ppermute | solution.py:494
  119.6 5.1 %copy-start.2 = (bf16[4,640,128]{2,1,0:T(8,128)(2,1)S(1)}, bf16[4,640,128]{2,1,0:T(8,128)(2,1)}, u32[]{:S(2)}) copy-start(bf16[4,640,128]{2,1,0:T(8,128)(2,1)} %copy-done.1) | copy-start | bytes 1966084
  124.7 2.2 %collective-permute-start.16 = (bf16[2,4,320,128]{3,2,1,0:T(8,128)(2,1)S(1)}, bf16[2,4,320,128]{3,2,1,0:T(8,128)(2,1)S(1)}, u32[]{:S(2)}, u32[]{:S(2)}) collective-permute-start(bf16[2,4,320,128]{3,2,1,0:T(8,128)(2,1)S(1)} %get-tuple-element.37), channel_id=1, source_target_pairs={{0,1},{1,0},{2,3},{3,2},{4,5},{5,4},{6,7},{7,6},{8,9},{9,8},{10,11... | collective-permute-start | bytes 1966088 | tf_op jit(solution)/shard_map/ppermute | solution.py:30
  126.9 9.9 %collective-permute-start.17 = (bf16[4,320,128]{2,1,0:T(8,128)(2,1)S(1)}, bf16[4,320,128]{2,1,0:T(8,128)(2,1)}, u32[]{:S(2)}, u32[]{:S(2)}) collective-permute-start(bf16[4,320,128]{2,1,0:T(8,128)(2,1)S(1)} %branch_out.2), channel_id=1, source_target_pairs={{0,16},{16,0},{1,17},{17,1},{2,18},{18,2},{3,19},{19,3},{4,20},{20... | collective-permute-start | bytes 983048 | tf_op jit(solution)/shard_map/ppermute | solution.py:30
